TPU v7x, 32 devices: a whole 2x2x4 slice. The times are simulated.
32 devices in a mesh: dp: 4 (over z), expert: 8 (over y, x, core).
Axes of the slice: x: 2, y: 2, z: 4, core: 2. Of those that a mesh axis runs over, the one named last changes fastest.
Arguments:
- pivot_states: bfloat16 [4096, 2048], P(('dp', 'expert')), may hold values from -6 to 6
- queries: bfloat16 [4096, 2048], P(('dp', 'expert')), may hold values from -8 to 8
- keys: bfloat16 [4096, 2048], P(('dp', 'expert')), may hold values from -8 to 8
- values: bfloat16 [4096, 2048], P(('dp', 'expert')), may hold values from -6 to 6
- pack_pos: int32 [4096], P(('dp', 'expert')), may hold values from 0 to 511, as said below
- segment_ids: int32 [32, 128], P(('dp', 'expert')), may hold values from 0 to 7, never falling along the last dimension, each value on 1 to 64 neighbouring positions
- expert_ids: int32 [4096, 2], P(('dp', 'expert')), may hold values from 0 to 31, all different within a row
- gate_code: int32 [4096, 2], P(('dp', 'expert')), may hold values from 6554 to 65535
- ln_gain: float32 [2048], replicated, may hold values from 0.5 to 1.5
- ln_bias: float32 [2048], replicated, may hold values from -3 to 3
- w_in: bfloat16 [8, 2048, 4096], P('expert', None, 'dp'), may hold values from -0.125 to 0.125
- b_in: float32 [8, 4096], P('expert', 'dp'), may hold values from -3 to 3
- w_out: bfloat16 [8, 4096, 2048], P('expert', 'dp'), may hold values from -0.09375 to 0.09375
- b_out: float32 [8, 2048], replicated, may hold values from -3 to 3
Outputs:
- layer_out: bfloat16 [4096, 2048], P(('dp', 'expert'))
Inputs may be any that keep to these rules, and one draw needn't show every extreme that they name: Within one index of expert, pack_pos over the devices of dp is a permutation, and each device's tokens go exactly 32 to each packed block of its column. `expert_ids`: only ids below 8 belong to the experts of this round.
All inputs are finite; a program needn't handle non-finite values.
Results may differ from a plain program's by a relative error of at most 0.0055.
Values may be sent and summed in bfloat16 or wider, within the bound.
No kernel may reach another device: no remote copies, remote signals or barrier semaphores. Data moves between devices by JAX's collectives and lax.ppermute only.
A program may use at most 64 MiB of HBM per device.

v0:
```python
import math

import jax
import jax.numpy as jnp
from jax import lax
from jax.sharding import PartitionSpec as P

HEAD_DIM = 128
ROUNDS = 4


epsilon = 1e-05
mask_fill = -1e30


def per_device(
    pivot_states,
    queries,
    keys,
    values,
    pack_pos,
    segment_ids,
    expert_ids,
    gate_code,
    ln_gain,
    ln_bias,
    w_in,
    b_in,
    w_out,
    b_out,
):
    tok_count = pivot_states.shape[0]
    model_width = pivot_states.shape[1]
    dp_count = lax.axis_size("dp")
    expert_count = lax.axis_size("expert")
    per_target = tok_count // dp_count
    target_block = pack_pos // tok_count
    offsets = pack_pos % tok_count
    target_hot = (target_block[:, None] == jnp.arange(dp_count, dtype=jnp.int32)[None, :]).astype(
        jnp.int32
    )
    bucket_rank = jnp.sum(jnp.cumsum(target_hot, axis=0) * target_hot, axis=1) - 1
    send_index = target_block * per_target + bucket_rank
    joined = jnp.concatenate([pivot_states, queries, keys, values], axis=1)
    send_rows = jnp.zeros_like(joined).at[send_index].set(joined)
    send_offsets = jnp.zeros_like(offsets).at[send_index].set(offsets)
    recv_rows, recv_offsets = (
        lax.all_to_all(send_rows, "dp", split_axis=0, concat_axis=0, tiled=True),
        lax.all_to_all(send_offsets, "dp", split_axis=0, concat_axis=0, tiled=True),
    )
    packed = jnp.zeros_like(recv_rows).at[recv_offsets].set(recv_rows)
    state_rows = packed[:, :model_width]
    query_rows = packed[:, model_width : 2 * model_width]
    key_rows = packed[:, 2 * model_width : 3 * model_width]
    value_rows = packed[:, 3 * model_width :]
    head_count = model_width // HEAD_DIM
    key_heads = key_rows.reshape(tok_count, head_count, HEAD_DIM)
    value_heads = value_rows.reshape(tok_count, head_count, HEAD_DIM)
    seg_row = segment_ids[0]
    block_rows = min(tok_count, 512)
    block_count = tok_count // block_rows
    score_scale = 1.0 / math.sqrt(HEAD_DIM)

    def attend(block_args):
        query_block, seg_block = block_args
        query_heads = query_block.reshape(block_rows, head_count, HEAD_DIM)
        scores = (
            jnp.einsum("qhd,khd->hqk", query_heads, key_heads, preferred_element_type=jnp.float32)
            * score_scale
        )
        same_doc = seg_block[:, None] == seg_row[None, :]
        scores = jnp.where(same_doc[None, :, :], scores, mask_fill)
        top_score = jnp.max(scores, axis=2, keepdims=True)
        exp_terms = jnp.exp(scores - top_score)
        softmax_weights = (exp_terms / jnp.sum(exp_terms, axis=2, keepdims=True)).astype(
            jnp.bfloat16
        )
        mixed_heads = jnp.einsum(
            "hqk,khd->qhd", softmax_weights, value_heads, preferred_element_type=jnp.float32
        )
        return mixed_heads.reshape(block_rows, model_width)

    attended = lax.map(
        attend,
        (
            query_rows.reshape(block_count, block_rows, model_width),
            seg_row.reshape(block_count, block_rows),
        ),
    )
    hidden_state = state_rows.astype(jnp.float32) + attended.reshape(tok_count, model_width)
    mean_value = jnp.mean(hidden_state, axis=1, keepdims=True)
    centered = hidden_state - mean_value
    variance = jnp.mean(centered * centered, axis=1, keepdims=True)
    normed = (centered * lax.rsqrt(variance + epsilon) * ln_gain + ln_bias).astype(jnp.bfloat16)
    capacity = max(2, 2 * tok_count // (ROUNDS * expert_count))
    assigned = jnp.concatenate([expert_ids[:, 0], expert_ids[:, 1]])
    expert_hot = (assigned[:, None] == jnp.arange(expert_count, dtype=jnp.int32)[None, :]).astype(
        jnp.int32
    )
    slot_rank = jnp.sum(jnp.cumsum(expert_hot, axis=0) * expert_hot, axis=1) - 1
    kept_mask = (assigned < expert_count) & (slot_rank < capacity)
    overflow = expert_count * capacity
    slot_index = jnp.where(kept_mask, assigned * capacity + slot_rank, overflow)
    buffer = jnp.zeros((overflow, model_width), jnp.bfloat16)
    buffer = (
        buffer.at[slot_index[:tok_count]]
        .set(normed, mode="drop")
        .at[slot_index[tok_count:]]
        .set(normed, mode="drop")
    )
    first_matrix = w_in[0]
    bias_in_row = b_in[0]
    second_matrix = w_out[0]
    arrived = lax.all_to_all(
        buffer.reshape(expert_count, capacity, model_width),
        "expert",
        split_axis=0,
        concat_axis=0,
        tiled=True,
    )
    arrived = arrived.reshape(overflow, model_width)
    hidden = jnp.dot(
        lax.all_gather(arrived, "dp", axis=0, tiled=True),
        first_matrix,
        preferred_element_type=jnp.float32,
    )
    hidden = jnp.maximum(hidden + bias_in_row, 0.0).astype(jnp.bfloat16)
    partial_value = jnp.dot(hidden, second_matrix, preferred_element_type=jnp.float32).astype(
        jnp.bfloat16
    )
    summed = lax.psum(partial_value, "dp").astype(jnp.float32)
    summed = lax.dynamic_slice_in_dim(summed, lax.axis_index("dp") * overflow, overflow, 0)
    bias_out_row = lax.dynamic_slice_in_dim(b_out, lax.axis_index("expert"), 1, 0)
    results = (summed + bias_out_row).astype(jnp.bfloat16)
    returned = lax.all_to_all(
        results.reshape(expert_count, capacity, model_width),
        "expert",
        split_axis=0,
        concat_axis=0,
        tiled=True,
    )
    returned = returned.reshape(overflow, model_width)
    gate_values = gate_code.astype(jnp.float32) / 65536.0
    gate_flat = jnp.concatenate([gate_values[:, 0], gate_values[:, 1]])
    weights = jnp.where(kept_mask, gate_flat, 0.0)
    guard_index = jnp.minimum(slot_index, overflow - 1)
    picked = returned[guard_index].astype(jnp.float32) * weights[:, None]
    layer_out = hidden_state + picked[:tok_count] + picked[tok_count:]
    return layer_out.astype(jnp.bfloat16)


def solution(mesh):
    return jax.shard_map(
        per_device,
        mesh=mesh,
        in_specs=(
            P(("dp", "expert"), None),
            P(("dp", "expert"), None),
            P(("dp", "expert"), None),
            P(("dp", "expert"), None),
            P(("dp", "expert")),
            P(("dp", "expert"), None),
            P(("dp", "expert"), None),
            P(("dp", "expert"), None),
            P(),
            P(),
            P("expert", None, "dp"),
            P("expert", "dp"),
            P("expert", "dp", None),
            P(),
        ),
        out_specs=P(("dp", "expert"), None),
        check_vma=False,
    )
```

profile of v0, /device:TPU:0, one launch (start us, length us, event | category | flops | bytes accessed | tf_op | source)
XLA Modules:
  0.0 216.1 jit_solution(15387900902896407806)
XLA Ops:
  6.5 0.7 and_select_fusion.1
  7.2 0.1 fusion.41
  7.3 0.2 reduce_window_sum.26
  7.5 0.2 select_reduce_fusion
  7.7 1.0 scatter_custom_fusion
  8.7 0.7 all_to_all.22
  9.3 6.3 %all-to-all-start = ((s32[4,32,1]{1,2,0:T(1,128)}), s32[4,32,1]{1,2,0:T(1,128)S(1)}, u32[]{:S(2)}, u32[]{:S(2)}) async-start(s32[4,32,1]{1,2,0:T(1,128)} %bitcast), calls=%async_computation | async-start | bytes 4096 | tf_op jit(solution)/shard_map/all_to_all | solution.py:49
  15.7 6.0 %scatter_custom_fusion.1 = bf16[128,8192]{1,0:T(8,128)(2,1)} fusion(s32[128]{0:T(128)S(1)} %compare_select_fusion.4, bf16[128,2048]{1,0:T(8,128)(2,1)} %param.17, bf16[]{:T(256)} %constant.112, bf16[128,2048]{1,0:T(8,128)(2,1)} %param.16, bf16[128,2048]{1,0:T(8,128)(2,1)} %param.15, bf16[128,2048]{1,0:T(8,128)(2,1)} %param.14, bf16[]{:T(256)} %constant.47.clone.1), kind=kCustom, calls=%fused_computation.12 | custom fusion | flops 8388608 | bytes 4194308 | tf_op jit(solution)/shard_map/scatter | solution.py:45
  21.7 5.2 %all-to-all-start.1 = ((bf16[4,32,8192]{2,1,0:T(8,128)(2,1)}), bf16[4,32,8192]{2,1,0:T(8,128)(2,1)S(1)}, u32[]{:S(2)}, u32[]{:S(2)}) async-start(bf16[4,32,8192]{2,1,0:T(8,128)(2,1)} %bitcast.2), calls=%async_computation.1 | async-start | bytes 4194304 | tf_op jit(solution)/shard_map/all_to_all | solution.py:48
  26.9 0.6 reduce-window.6
  27.5 0.2 slice_reduce_fusion
  27.8 0.1 fusion.42
  27.9 0.1 broadcast_compare_fusion
  28.0 0.5 broadcast.249
  28.5 0.7 reduce.5
  29.2 0.1 all_to_all.24
  29.3 45.3 %all-to-all-done.1 = bf16[4,32,8192]{2,1,0:T(8,128)(2,1)S(1)} async-done(((bf16[4,32,8192]{2,1,0:T(8,128)(2,1)}), bf16[4,32,8192]{2,1,0:T(8,128)(2,1)S(1)}, u32[]{:S(2)}, u32[]{:S(2)}) %all-to-all-start.1) | async-done | bytes 2097184 | tf_op jit(solution)/shard_map/all_to_all | solution.py:48
  74.5 1.3 copy-done.1
  75.9 5.2 %scatter_custom_fusion.2 = bf16[128,8192]{1,0:T(8,128)(2,1)S(1)} fusion(s32[128]{0:T(128)S(1)} %fusion.44, bf16[128,8192]{1,0:T(8,128)(2,1)} %bitcast.67, bf16[]{:T(256)} %constant.47.clone.1), kind=kCustom, calls=%fused_computation.35 | custom fusion | bytes 2097664 | tf_op jit(solution)/shard_map/scatter | solution.py:51
  81.1 0.9 fusion.51
  82.0 1.0 copy.28
  83.0 1.0 copy.27
  84.0 1.5 fusion.18
  85.6 0.2 fusion.53
  85.8 2.1 copy.26
  87.9 2.5 %fusion.34 = f32[16,128,128]{2,1,0:T(8,128)} fusion(bf16[128,16,128]{0,2,1:T(8,128)(2,1)} %bitcast.72, f32[16,128]{1,0:T(8,128)S(1)} %fusion.53, f32[16,128,128]{1,2,0:T(8,128)S(1)} %fusion.18), kind=kOutput, calls=%fused_computation.38 | convolution fusion | flops 67897472 | bytes 2629632 | tf_op jit(solution)/shard_map/while/body/eval_jaxpr/hqk,khd->qhd/dot_general | solution.py:78
  90.3 1.6 copy.32
  91.9 0.0 copy-start.2
  91.9 0.2 fusion.50
  92.1 0.3 multiply_reduce_fusion
  92.4 0.2 copy-done.2
  92.6 0.0 copy-done.3
  92.6 1.1 add_convert_fusion
  93.6 1.9 scatter_custom_fusion.3
  95.6 2.0 scatter_fusion
  97.5 10.6 %all_to_all.34 = bf16[8,8,2048]{2,1,0:T(8,128)(2,1)} all-to-all(bf16[8,8,2048]{2,1,0:T(8,128)(2,1)S(1)} %bitcast.66), channel_id=1, replica_groups=mesh['dp'=4,'expert'=8] {'expert'}, dimensions={0} | all-to-all | bytes 524288 | tf_op jit(solution)/shard_map/all_to_all | solution.py:114
  108.1 0.0 all-gather.2.cloned.1.call-update
  108.1 0.0 all-reduce.2.cloned.1.call-start
  108.2 25.3 %all-gather.2.cloned.1.call-done = bf16[256,2048]{1,0:T(8,128)(2,1)} async-done(((bf16[64,2048]{1,0:T(8,128)(2,1)}), bf16[256,2048]{1,0:T(8,128)(2,1)}) %all-gather.2.cloned.1.call-update) | async-done | bytes 1048592 | tf_op jit(solution)/shard_map/all_gather | solution.py:123
  133.5 7.2 %fusion.5 = bf16[256,2048]{1,0:T(8,128)(2,1)} fusion(bf16[1,1024,2048]{2,1,0:T(8,128)(2,1)} %param.26, bf16[256,2048]{1,0:T(8,128)(2,1)} %all-gather.2.cloned.1.call-done, bf16[1,2048,1024]{2,1,0:T(8,128)(2,1)} %param.24, f32[1024]{0:T(1024)S(1)} %bitcast.77), kind=kOutput, calls=%fused_computation.11 | convolution fusion | flops 2148794368 | bytes 10489856 | tf_op jit(solution)/shard_map/dot_general | solution.py:128
  140.6 0.0 all-reduce.2.cloned.1.call-update
  140.7 51.4 %all-reduce.2.cloned.1.call-done = bf16[256,2048]{1,0:T(8,128)(2,1)} async-done(((bf16[256,2048]{1,0:T(8,128)(2,1)}), bf16[256,2048]{1,0:T(8,128)(2,1)}) %all-reduce.2.cloned.1.call-update) | async-done | bytes 1048592 | tf_op jit(solution)/shard_map/psum | solution.py:131
  192.1 1.7 fusion.38
  193.8 3.7 %all-to-all-start.3 = ((bf16[8,8,2048]{2,1,0:T(8,128)(2,1)}), bf16[8,8,2048]{2,1,0:T(8,128)(2,1)S(1)}, u32[]{:S(2)}, u32[]{:S(2)}) async-start(bf16[8,8,2048]{2,1,0:T(8,128)(2,1)} %fusion.38), calls=%async_computation.3 | async-start | bytes 524288 | tf_op jit(solution)/shard_map/all_to_all | solution.py:135
  197.5 6.9 %all-to-all-done.3 = bf16[8,8,2048]{2,1,0:T(8,128)(2,1)S(1)} async-done(((bf16[8,8,2048]{2,1,0:T(8,128)(2,1)}), bf16[8,8,2048]{2,1,0:T(8,128)(2,1)S(1)}, u32[]{:S(2)}, u32[]{:S(2)}) %all-to-all-start.3) | async-done | bytes 262176 | tf_op jit(solution)/shard_map/all_to_all | solution.py:135
  204.4 2.3 %gather_fusion = bf16[256,2048]{1,0:T(8,128)(2,1)} fusion(bf16[64,2048]{1,0:T(8,128)(2,1)S(1)} %bitcast.65, s32[1024]{0:T(1024)S(1)} %pad_clamp_fusion), kind=kCustom, calls=%fused_computation | custom fusion | bytes 2098176 | tf_op jit(solution)/shard_map/gather | solution.py:147
  206.8 1.4 convert_multiply_fusion
  208.2 1.1 fusion.28
  (31 shorter events, 0.2 us)
Async XLA Ops:
  6.5 134.2 %copy-start = (f32[8,2048]{1,0:T(8,128)S(1)}, f32[8,2048]{1,0:T(8,128)}, u32[]{:S(2)}) copy-start(f32[8,2048]{1,0:T(8,128)} %param.27) | copy-start | bytes 196612
  9.3 12.3 %all-to-all-start = ((s32[4,32,1]{1,2,0:T(1,128)}), s32[4,32,1]{1,2,0:T(1,128)S(1)}, u32[]{:S(2)}, u32[]{:S(2)}) async-start(s32[4,32,1]{1,2,0:T(1,128)} %bitcast), calls=%async_computation | async-start | bytes 4096 | tf_op jit(solution)/shard_map/all_to_all | solution.py:49
  21.7 5.2 %copy-start.5 = (s32[128,2]{0,1:T(2,128)S(1)}, s32[128,2]{0,1:T(2,128)}, u32[]{:S(2)}) copy-start(s32[128,2]{0,1:T(2,128)} %param.20) | copy-start | bytes 3076
  21.7 6.2 %copy-start.4 = (s32[1,128]{1,0:T(1,128)S(1)}, s32[1,128]{1,0:T(1,128)}, u32[]{:S(2)}) copy-start(s32[1,128]{1,0:T(1,128)} %param.19) | copy-start | bytes 1540
  21.7 52.9 %all-to-all-start.1 = ((bf16[4,32,8192]{2,1,0:T(8,128)(2,1)}), bf16[4,32,8192]{2,1,0:T(8,128)(2,1)S(1)}, u32[]{:S(2)}, u32[]{:S(2)}) async-start(bf16[4,32,8192]{2,1,0:T(8,128)(2,1)} %bitcast.2), calls=%async_computation.1 | async-start | bytes 4194304 | tf_op jit(solution)/shard_map/all_to_all | solution.py:48
  26.9 106.5 %all-gather.2.cloned.1.call-start = ((), (), s32[]{:S(2)}) async-start(), calls=%async_computation.4 | async-start | bytes 1310720 | tf_op jit(solution)/shard_map/all_gather | solution.py:123
  74.5 1.4 copy-start.1
  91.9 0.7 copy-start.2
  91.9 0.7 copy-start.3
  95.5 37.9 %copy-start.7 = (f32[1,1024]{1,0:T(1,128)S(1)}, f32[1,1024]{1,0:T(1,128)}, u32[]{:S(2)}) copy-start(f32[1,1024]{1,0:T(1,128)} %param.25) | copy-start | bytes 12292
  108.1 84.0 %all-reduce.2.cloned.1.call-start = ((), (), s32[]{:S(2)}) async-start(), calls=%async_computation.5 | async-start | bytes 2097152 | tf_op jit(solution)/shard_map/psum | solution.py:131
  133.5 7.2 %copy-start.6 = (s32[128,2]{0,1:T(2,128)S(1)}, s32[128,2]{0,1:T(2,128)}, u32[]{:S(2)}) copy-start(s32[128,2]{0,1:T(2,128)} %param.21) | copy-start | bytes 3076
  193.8 10.6 %all-to-all-start.3 = ((bf16[8,8,2048]{2,1,0:T(8,128)(2,1)}), bf16[8,8,2048]{2,1,0:T(8,128)(2,1)S(1)}, u32[]{:S(2)}, u32[]{:S(2)}) async-start(bf16[8,8,2048]{2,1,0:T(8,128)(2,1)} %fusion.38), calls=%async_computation.3 | async-start | bytes 524288 | tf_op jit(solution)/shard_map/all_to_all | solution.py:135
Sparse Core Ops, SparseCore 0:
  108.3 25.1 all-gather.1
  140.8 51.3 all-reduce.1
where the time goes:
time: 217 us; the launch traced here: 216 us
  waiting for transfers between devices  129 us (59%)
  local copies, waits for them, and re-layouts  22 us (10%)
  starting transfers between devices  15.2 us (7%)
  other arithmetic  14.7 us (7%)
  between operations  13.6 us (6%)
  matrix products  11.2 us (5%)
  blocking collectives  10.6 us (5%)
    psum x1, waiting for transfers between devices, per_device(): summed = lax.psum(partial_value, 'dp').astype(jnp.float32)  51.4 us
    all_to_all x1, waiting for transfers between devices, per_device(): lax.all_to_all(send_rows, 'dp', split_axis=0, concat_axis=0, tiled=True)  45.3 us
    all_gather x1, waiting for transfers between devices, per_device(): lax.all_gather(arrived, 'dp', axis=0, tiled=True)  25.3 us
    all_to_all x1, blocking collectives, per_device(): lax.all_to_all(buffer.reshape(expert_count, capacity, model_width), 'expe...  10.6 us
    dot_general x1, matrix products, per_device(): jnp.dot(hidden, second_matrix, preferred_element_type=jnp.float32)  7.16 us
    all_to_all x1, waiting for transfers between devices, per_device(): lax.all_to_all(results.reshape(expert_count, capacity, model_width), 'exp...  6.91 us
    all_to_all x1, starting transfers between devices, per_device(): lax.all_to_all(send_offsets, 'dp', split_axis=0, concat_axis=0, tiled=True)  6.32 us
    scatter x1, other arithmetic, per_device(): send_rows = jnp.zeros_like(joined).at[send_index].set(joined)  6.02 us
  transfers between devices with their start and end apart: 5, of which 4 were waited for; matrix products, arithmetic and copies ran while one was open for 4% of the time, Pallas kernels for 0%

commit v1 on v0

v1 whole, which is shorter than its diff:
```python
import functools
import math

import jax
import jax.numpy as jnp
from jax import lax
from jax.experimental import pallas as pl
from jax.experimental.pallas import tpu as pltpu
from jax.sharding import PartitionSpec as P

HEAD_DIM = 128
ROUNDS = 4
LANES = 128

epsilon = 1e-05
mask_fill = -1e30

F32 = jnp.float32
BF16 = jnp.bfloat16

VMEM_BYTES = 32 * 1024 * 1024


def iota(shape, axis):
    return lax.broadcasted_iota(jnp.int32, shape, axis)


def one_hot(condition):
    return jnp.where(condition, 1.0, 0.0)


def across(row, rows):
    lanes = jnp.broadcast_to(row.astype(F32), (rows, row.shape[1]))
    return lanes, lanes.T


def call(body, out_shape, *operands, flops=0):
    moved = sum(x.size * x.dtype.itemsize for x in operands)
    moved += sum(x.size * x.dtype.itemsize for x in jax.tree.leaves(out_shape))
    return pl.pallas_call(
        body,
        out_shape=out_shape,
        compiler_params=pltpu.CompilerParams(vmem_limit_bytes=VMEM_BYTES),
        cost_estimate=pl.CostEstimate(flops=flops, bytes_accessed=moved, transcendentals=0),
    )(*operands)


def pack_kernel(pos_ref, *refs):
    x_refs, out_ref = refs[:-1], refs[-1]
    tok = pos_ref.shape[1]
    lanes, subl = across(pos_ref[...], tok)
    _, offset = across(lax.rem(pos_ref[...], tok), tok)
    rank = jnp.sum(one_hot(subl < lanes), axis=0, keepdims=True)
    order = one_hot(iota((tok, tok), 0).astype(F32) == rank).astype(BF16)
    at = 0
    for x in [r[...] for r in x_refs] + [offset.astype(BF16)]:
        out_ref[:, at : at + x.shape[1]] = jnp.dot(order, x, preferred_element_type=F32).astype(BF16)
        at += x.shape[1]


def slots_of(ids_ref, cap, experts):
    tok = ids_ref.shape[1]
    first, first_t = across(ids_ref[0:1, :], tok)
    second, second_t = across(ids_ref[1:2, :], tok)
    earlier = iota((tok, tok), 0) < iota((tok, tok), 1)
    rank_first = jnp.sum(one_hot((first_t == first) & earlier), axis=0, keepdims=True)
    rank_second = jnp.sum(one_hot(first_t == second), axis=0, keepdims=True)
    rank_second += jnp.sum(one_hot((second_t == second) & earlier), axis=0, keepdims=True)

    def slot(expert, rank):
        return jnp.where((expert < experts) & (rank < cap), expert * cap + rank, -1.0)

    return slot(first[0:1, :], rank_first), slot(second[0:1, :], rank_second)


def attend_kernel(cap, experts, copies, rows_ref, seg_ref, ids_ref, gain_ref, bias_ref, hidden_ref, send_ref):
    tok, width = hidden_ref.shape
    _, seg_q = across(seg_ref[...], tok)
    offset_of_key = rows_ref[:, 4 * width :].astype(F32).T
    place = offset_of_key == iota((tok, tok), 0).astype(F32)
    seg_k = jnp.sum(jnp.where(place, seg_q, 0.0), axis=0, keepdims=True)
    same = seg_q == seg_k
    place = one_hot(place).astype(BF16)
    scale = 1.0 / math.sqrt(HEAD_DIM)
    for h in range(width // HEAD_DIM):
        lo = h * HEAD_DIM
        q = rows_ref[:, width + lo : width + lo + HEAD_DIM]
        k = rows_ref[:, 2 * width + lo : 2 * width + lo + HEAD_DIM]
        v = rows_ref[:, 3 * width + lo : 3 * width + lo + HEAD_DIM]
        s = rows_ref[:, lo : lo + HEAD_DIM]
        q = jnp.dot(place, q, preferred_element_type=F32).astype(BF16)
        scores = lax.dot_general(q, k, (((1,), (1,)), ((), ())), preferred_element_type=F32) * scale
        scores = jnp.where(same, scores, mask_fill)
        terms = jnp.exp(scores - jnp.max(scores, axis=1, keepdims=True))
        probs = (terms / jnp.sum(terms, axis=1, keepdims=True)).astype(BF16)
        mixed = jnp.dot(probs, v, preferred_element_type=F32)
        hidden_ref[:, lo : lo + HEAD_DIM] = mixed + jnp.dot(place, s, preferred_element_type=F32)
    hidden = hidden_ref[...]
    centered = hidden - jnp.mean(hidden, axis=1, keepdims=True)
    variance = jnp.mean(centered * centered, axis=1, keepdims=True)
    normed = (centered * lax.rsqrt(variance + epsilon) * gain_ref[...] + bias_ref[...]).astype(BF16)
    slot_first, slot_second = slots_of(ids_ref, cap, experts)
    slot = iota((experts * cap, tok), 0).astype(F32)
    taken = one_hot((slot == slot_first) | (slot == slot_second)).astype(BF16)
    picked = jnp.dot(taken, normed, preferred_element_type=F32).astype(BF16)
    for n in range(copies):
        send_ref[n] = picked


def combine_kernel(cap, experts, parts_ref, hidden_ref, ids_ref, code_ref, bias_ref, out_ref):
    tok = out_ref.shape[0]
    total = parts_ref[0].astype(F32)
    for n in range(1, parts_ref.shape[0]):
        total += parts_ref[n].astype(F32)
    result = (total + bias_ref[...]).astype(BF16)
    slot_first, slot_second = slots_of(ids_ref, cap, experts)
    slot = iota((experts * cap, tok), 0).astype(F32)
    high = (code_ref[...] >> 8).astype(F32)
    low = (code_ref[...] & 255).astype(F32)

    def weights(code):
        return jnp.where(slot == slot_first, code[0:1, :], 0.0) + jnp.where(
            slot == slot_second, code[1:2, :], 0.0
        )

    both = jnp.concatenate([weights(high) / 256.0, weights(low) / 65536.0], axis=0)
    result = jnp.concatenate([result, result], axis=0)
    added = jnp.dot(both.T.astype(BF16), result, preferred_element_type=F32)
    out_ref[...] = (hidden_ref[...] + added).astype(BF16)


def per_device(
    pivot_states,
    queries,
    keys,
    values,
    pack_pos,
    segment_ids,
    expert_ids,
    gate_code,
    ln_gain,
    ln_bias,
    w_in,
    b_in,
    w_out,
    b_out,
):
    tok, width = pivot_states.shape
    dp = lax.axis_size("dp")
    experts = lax.axis_size("expert")
    cap = max(2, 2 * tok // (ROUNDS * experts))
    slots = experts * cap
    ids = expert_ids.T
    codes = gate_code.T
    wide = 4 * width + LANES
    rows = call(
        pack_kernel,
        jax.ShapeDtypeStruct((tok, wide), BF16),
        pack_pos.reshape(1, tok),
        pivot_states,
        queries,
        keys,
        values,
    )
    rows = lax.all_to_all(
        rows.reshape(dp, tok // dp, wide), "dp", split_axis=0, concat_axis=0, tiled=True
    ).reshape(tok, wide)
    hidden_state, send = call(
        functools.partial(attend_kernel, cap, experts, dp),
        (
            jax.ShapeDtypeStruct((tok, width), F32),
            jax.ShapeDtypeStruct((dp, slots, width), BF16),
        ),
        rows,
        segment_ids,
        ids,
        ln_gain.reshape(1, width),
        ln_bias.reshape(1, width),
    )
    arrived = lax.all_to_all(
        send.reshape(dp * experts, cap, width), ("dp", "expert"), split_axis=0, concat_axis=0, tiled=True
    ).reshape(dp * slots, width)
    inner = jnp.dot(arrived, w_in[0], preferred_element_type=F32)
    inner = jnp.maximum(inner + b_in[0], 0.0).astype(BF16)
    share = jnp.dot(inner, w_out[0], preferred_element_type=F32).astype(BF16)
    parts = lax.all_to_all(
        share.reshape(dp * experts, cap, width), ("dp", "expert"), split_axis=0, concat_axis=0, tiled=True
    ).reshape(dp, slots, width)
    return call(
        functools.partial(combine_kernel, cap, experts),
        jax.ShapeDtypeStruct((tok, width), BF16),
        parts,
        hidden_state,
        ids,
        codes,
        jnp.repeat(b_out, cap, axis=0),
    )


def solution(mesh):
    return jax.shard_map(
        per_device,
        mesh=mesh,
        in_specs=(
            P(("dp", "expert"), None),
            P(("dp", "expert"), None),
            P(("dp", "expert"), None),
            P(("dp", "expert"), None),
            P(("dp", "expert")),
            P(("dp", "expert"), None),
            P(("dp", "expert"), None),
            P(("dp", "expert"), None),
            P(),
            P(),
            P("expert", None, "dp"),
            P("expert", "dp"),
            P("expert", "dp", None),
            P(),
        ),
        out_specs=P(("dp", "expert"), None),
        check_vma=False,
    )
```

time: 217 us -> 135 us (0.62)
  waiting for transfers between devices: 129 us -> 26.2 us
  blocking collectives: 10.6 us -> 84.9 us
  local copies, waits for them, and re-layouts: 22 us -> 4.92 us
  other arithmetic: 14.7 us -> 0 us
  between operations: 13.6 us -> 0.07 us
  starting transfers between devices: 15.2 us -> 3.62 us
  Pallas kernels: 0 us -> 8 us
  matrix products: 11.2 us -> 6.84 us
    all_to_all x1 -> x2, blocking collectives: 10.6 us -> 84.9 us  [the longest x1 55 us: per_device(): lax.all_to_all(rows.reshape(dp, tok // dp, wide), 'dp', split_axis=0, con...]
    psum x1 -> x0, waiting for transfers between devices: 51.4 us -> none  [per_device(): summed = lax.psum(partial_value, 'dp').astype(jnp.float32)]
    all_to_all x3 -> x1, waiting for transfers between devices: 52.2 us -> 26.2 us  [per_device(): lax.all_to_all(share.reshape(dp * experts, cap, width), ('dp', 'expert'),...]
    all_gather x1 -> x0, waiting for transfers between devices: 25.3 us -> none  [per_device(): lax.all_gather(arrived, 'dp', axis=0, tiled=True)]
    all_to_all x3 -> x1, starting transfers between devices: 15.2 us -> 3.62 us  [per_device(): lax.all_to_all(share.reshape(dp * experts, cap, width), ('dp', 'expert'),...]
    scatter x4 -> x0, local copies, waits for them, and re-layouts: 10 us -> none  [the longest x1 5.18 us: per_device(): packed = jnp.zeros_like(recv_rows).at[recv_offsets].set(recv_rows)]
    pallas_call x0 -> x3, Pallas kernels: none -> 8 us  [call(): pl.pallas_call(body, out_shape=out_shape, compiler_params=pltpu.CompilerP...]
    scatter x1 -> x0, other arithmetic: 6.02 us -> none  [per_device(): send_rows = jnp.zeros_like(joined).at[send_index].set(joined)]
  transfers between devices with their start and end apart: 5 -> 1, of which waited for: 4 -> 1; matrix products, arithmetic and copies ran while one was open for 4% -> 0% of each run, Pallas kernels for 0% -> 0%
where the time goes in v1:
time: 135 us
  blocking collectives  84.9 us (63%)
  waiting for transfers between devices  26.2 us (19%)
  Pallas kernels  8 us (6%)
  matrix products  6.84 us (5%)
  local copies, waits for them, and re-layouts  4.92 us (4%)
  starting transfers between devices  3.62 us (3%)
    all_to_all x1, blocking collectives, per_device(): lax.all_to_all(rows.reshape(dp, tok // dp, wide), 'dp', split_axis=0, con...  55 us
    all_to_all x1, blocking collectives, per_device(): lax.all_to_all(send.reshape(dp * experts, cap, width), ('dp', 'expert'),...  29.9 us
    all_to_all x1, waiting for transfers between devices, per_device(): lax.all_to_all(share.reshape(dp * experts, cap, width), ('dp', 'expert'),...  26.2 us
    pallas_call x3, Pallas kernels, call(): pl.pallas_call(body, out_shape=out_shape, compiler_params=pltpu.CompilerP...  8 us
    dot_general x1, matrix products, per_device(): share = jnp.dot(inner, w_out[0], preferred_element_type=F32).astype(BF16)  6.84 us
    unnamed x24, local copies, waits for them, and re-layouts  4.88 us
    all_to_all x1, starting transfers between devices, per_device(): lax.all_to_all(share.reshape(dp * experts, cap, width), ('dp', 'expert'),...  3.62 us
  transfers between devices with their start and end apart: 1, of which 1 were waited for; matrix products, arithmetic and copies ran while one was open for 0% of the time, Pallas kernels for 0%

profile of v1, /device:TPU:0, one launch (start us, length us, event | category | flops | bytes accessed | tf_op | source)
XLA Modules:
  0.0 134.5 jit_solution(13698861568336347715)
XLA Ops:
  0.0 0.0 copy-start
  0.0 0.0 copy-start.1
  0.0 1.1 copy-done.1
  1.1 0.0 copy-start.2
  1.1 1.0 copy-done.2
  2.1 0.0 copy-start.3
  2.1 1.0 copy-done.3
  3.2 0.0 copy-start.4
  3.2 1.0 copy-done.4
  4.2 0.0 copy-start.9
  4.2 0.7 copy-done.9
  4.9 0.0 copy-start.5
  4.9 0.0 copy-start.6
  4.9 0.0 copy-start.7
  4.9 0.0 copy-start.10
  4.9 0.8 shard_map.136
  5.7 0.0 copy-start.11
  5.7 55.0 %all_to_all.15 = bf16[4,32,8320]{2,1,0:T(8,128)(2,1)S(1)} all-to-all(bf16[4,32,8320]{2,1,0:T(8,128)(2,1)S(1)} %bitcast.38), channel_id=1, replica_groups=mesh['dp'=4,'expert'=8] {'dp'}, dimensions={0} | all-to-all | bytes 4259840 | tf_op jit(solution)/shard_map/all_to_all | solution.py:165
  60.7 0.0 copy-done.5
  60.7 0.0 copy-done.6
  60.7 0.0 copy-done.7
  60.7 0.0 copy-done.10
  60.7 5.9 %shard_map.137 = (f32[128,2048]{1,0:T(8,128)S(1)}, bf16[4,64,2048]{2,1,0:T(8,128)(2,1)S(1)}) custom-call(bf16[128,8320]{1,0:T(8,128)(2,1)S(1)} %bitcast.37, s32[1,128]{1,0:T(1,128)S(1)} %copy-done.10, s32[2,128]{1,0:T(2,128)S(1)} %bitcast.43, f32[1,2048]{1,0:T(1,128)S(1)} %bitcast.41, f32[1,2048]{1,0:T(1,128)S(1)} %bitcast.42), custom_call_target="tpu_custom_call" | custom-call | bytes 4244992 | tf_op jit(solution)/shard_map/pallas_call | solution.py:40
  66.7 29.9 %all_to_all.16 = bf16[32,8,2048]{2,1,0:T(8,128)(2,1)S(1)} all-to-all(bf16[32,8,2048]{2,1,0:T(8,128)(2,1)S(1)} %bitcast.40), channel_id=1, replica_groups=mesh['dp'=4,'expert'=8] {'dp','expert'}, dimensions={0} | all-to-all | bytes 2097152 | tf_op jit(solution)/shard_map/all_to_all | solution.py:180
  96.5 0.0 copy-done.11
  96.5 0.0 copy-start.8
  96.5 6.8 %fusion.7 = bf16[32,8,2048]{2,1,0:T(8,128)(2,1)} fusion(bf16[1,1024,2048]{2,1,0:T(8,128)(2,1)} %param.26, bf16[1,2048,1024]{2,1,0:T(8,128)(2,1)} %param.24, bf16[32,8,2048]{2,1,0:T(8,128)(2,1)S(1)} %all_to_all.16, f32[1024]{0:T(1024)S(1)} %bitcast.47), kind=kOutput, calls=%fused_computation.5 | convolution fusion | flops 2148794368 | bytes 10489856 | tf_op jit(solution)/shard_map/dot_general | solution.py:185
  103.4 3.6 %all-to-all-start.2 = ((bf16[32,8,2048]{2,1,0:T(8,128)(2,1)}), bf16[32,8,2048]{2,1,0:T(8,128)(2,1)S(1)}, u32[]{:S(2)}, u32[]{:S(2)}) async-start(bf16[32,8,2048]{2,1,0:T(8,128)(2,1)} %fusion.7), calls=%async_computation.2 | async-start | bytes 2097152 | tf_op jit(solution)/shard_map/all_to_all | solution.py:186
  107.0 0.0 copy-done
  107.1 26.2 %all-to-all-done.2 = bf16[32,8,2048]{2,1,0:T(8,128)(2,1)S(1)} async-done(((bf16[32,8,2048]{2,1,0:T(8,128)(2,1)}), bf16[32,8,2048]{2,1,0:T(8,128)(2,1)S(1)}, u32[]{:S(2)}, u32[]{:S(2)}) %all-to-all-start.2) | async-done | bytes 1048608 | tf_op jit(solution)/shard_map/all_to_all | solution.py:186
  133.3 0.0 copy-done.8
  133.3 1.3 shard_map.138
  (1 shorter events, 0.0 us)
Async XLA Ops:
  0.0 107.0 %copy-start = (f32[8,2048]{1,0:T(8,128)S(1)}, f32[8,2048]{1,0:T(8,128)}, u32[]{:S(2)}) copy-start(f32[8,2048]{1,0:T(8,128)} %param.27) | copy-start | bytes 196612
  0.0 1.1 copy-start.1
  1.1 1.0 copy-start.2
  2.1 1.0 copy-start.3
  3.2 1.0 copy-start.4
  4.2 0.7 copy-start.9
  4.9 55.8 %copy-start.5 = (f32[2048]{0:T(1024)S(1)}, f32[2048]{0:T(1024)}, u32[]{:S(2)}) copy-start(f32[2048]{0:T(1024)} %param.22) | copy-start | bytes 24580
  4.9 55.8 %copy-start.6 = (f32[2048]{0:T(1024)S(1)}, f32[2048]{0:T(1024)}, u32[]{:S(2)}) copy-start(f32[2048]{0:T(1024)} %param.23) | copy-start | bytes 24580
  4.9 55.8 %copy-start.7 = (s32[128,2]{0,1:T(2,128)S(1)}, s32[128,2]{0,1:T(2,128)}, u32[]{:S(2)}) copy-start(s32[128,2]{0,1:T(2,128)} %param.20) | copy-start | bytes 3076
  4.9 55.8 %copy-start.10 = (s32[1,128]{1,0:T(1,128)S(1)}, s32[1,128]{1,0:T(1,128)}, u32[]{:S(2)}) copy-start(s32[1,128]{1,0:T(1,128)} %seg_ref.1) | copy-start | bytes 1540
  5.7 90.9 %copy-start.11 = (f32[1,1024]{1,0:T(1,128)S(1)}, f32[1,1024]{1,0:T(1,128)}, u32[]{:S(2)}) copy-start(f32[1,1024]{1,0:T(1,128)} %param.25) | copy-start | bytes 12292
  96.5 36.7 %copy-start.8 = (s32[128,2]{0,1:T(2,128)S(1)}, s32[128,2]{0,1:T(2,128)}, u32[]{:S(2)}) copy-start(s32[128,2]{0,1:T(2,128)} %param.21) | copy-start | bytes 3076
  103.4 29.9 %all-to-all-start.2 = ((bf16[32,8,2048]{2,1,0:T(8,128)(2,1)}), bf16[32,8,2048]{2,1,0:T(8,128)(2,1)S(1)}, u32[]{:S(2)}, u32[]{:S(2)}) async-start(bf16[32,8,2048]{2,1,0:T(8,128)(2,1)} %fusion.7), calls=%async_computation.2 | async-start | bytes 2097152 | tf_op jit(solution)/shard_map/all_to_all | solution.py:186

commit v2 on v1

v2 whole, which is shorter than its diff:
```python
import functools
import math

import jax
import jax.numpy as jnp
from jax import lax
from jax.experimental import pallas as pl
from jax.experimental.pallas import tpu as pltpu
from jax.sharding import PartitionSpec as P

HEAD_DIM = 128
ROUNDS = 4
LANES = 128

epsilon = 1e-05
mask_fill = -1e30

F32 = jnp.float32
BF16 = jnp.bfloat16

VMEM_BYTES = 32 * 1024 * 1024


def iota(shape, axis):
    return lax.broadcasted_iota(jnp.int32, shape, axis)


def one_hot(condition):
    return jnp.where(condition, 1.0, 0.0)


def across(row, rows):
    lanes = jnp.broadcast_to(row.astype(F32), (rows, row.shape[1]))
    return lanes, lanes.T


def call(body, out_shape, *operands, flops=0):
    moved = sum(x.size * x.dtype.itemsize for x in operands)
    moved += sum(x.size * x.dtype.itemsize for x in jax.tree.leaves(out_shape))
    return pl.pallas_call(
        body,
        out_shape=out_shape,
        compiler_params=pltpu.CompilerParams(vmem_limit_bytes=VMEM_BYTES),
        cost_estimate=pl.CostEstimate(flops=flops, bytes_accessed=moved, transcendentals=0),
    )(*operands)


def pack_kernel(offsets, pos_ref, x_ref, *out_refs):
    tok, width = x_ref.shape
    share = tok // len(out_refs)
    lanes, subl = across(pos_ref[...], tok)
    rank = jnp.sum(one_hot(subl < lanes), axis=0, keepdims=True)
    order = one_hot(iota((tok, tok), 0).astype(F32) == rank).astype(BF16)
    rows = jnp.dot(order, x_ref[...], preferred_element_type=F32).astype(BF16)
    for n, out_ref in enumerate(out_refs):
        out_ref[:, :width] = rows[n * share : (n + 1) * share]
    if offsets:
        _, offset = across(lax.rem(pos_ref[...], tok), tok)
        rows = jnp.dot(order, offset.astype(BF16), preferred_element_type=F32).astype(BF16)
        for n, out_ref in enumerate(out_refs):
            out_ref[:, width:] = rows[n * share : (n + 1) * share]


def joined(refs, columns=slice(None)):
    return jnp.concatenate([r[:, columns] for r in refs], axis=0)


def slots_of(ids_ref, cap, experts):
    tok = ids_ref.shape[1]
    first, first_t = across(ids_ref[0:1, :], tok)
    second, second_t = across(ids_ref[1:2, :], tok)
    earlier = iota((tok, tok), 0) < iota((tok, tok), 1)
    rank_first = jnp.sum(one_hot((first_t == first) & earlier), axis=0, keepdims=True)
    rank_second = jnp.sum(one_hot(first_t == second), axis=0, keepdims=True)
    rank_second += jnp.sum(one_hot((second_t == second) & earlier), axis=0, keepdims=True)

    def slot(expert, rank):
        return jnp.where((expert < experts) & (rank < cap), expert * cap + rank, -1.0)

    return slot(first[0:1, :], rank_first), slot(second[0:1, :], rank_second)


def route_kernel(cap, experts, width, seg_ref, ids_ref, code_ref, *refs):
    *key_refs, place_ref, outside_ref, taken_ref, give_ref = refs
    tok = seg_ref.shape[1]
    _, seg_q = across(seg_ref[...], tok)
    place = joined(key_refs, slice(width, width + LANES)).astype(F32).T == iota((tok, tok), 0).astype(F32)
    place_ref[...] = one_hot(place).astype(BF16)
    seg_k = jnp.sum(jnp.where(place, seg_q, 0.0), axis=0, keepdims=True)
    outside_ref[...] = one_hot(seg_q != seg_k)
    slot_first, slot_second = slots_of(ids_ref, cap, experts)
    slot = iota((experts * cap, tok), 0).astype(F32)
    taken_ref[...] = one_hot((slot == slot_first) | (slot == slot_second)).astype(BF16)
    high = (code_ref[...] >> 8).astype(F32)
    low = (code_ref[...] & 255).astype(F32)

    def weights(code):
        return jnp.where(slot == slot_first, code[0:1, :], 0.0) + jnp.where(
            slot == slot_second, code[1:2, :], 0.0
        )

    both = jnp.concatenate([weights(high) / 256.0, weights(low) / 65536.0], axis=0)
    give_ref[...] = both.T.astype(BF16)


def probs_kernel(place_ref, outside_ref, *refs):
    *row_refs, out_ref = refs
    key_refs, query_refs = row_refs[: len(row_refs) // 2], row_refs[len(row_refs) // 2 :]
    scale = 1.0 / math.sqrt(HEAD_DIM)
    outside = outside_ref[...] > 0.0
    for h in range(out_ref.shape[0]):
        columns = slice(h * HEAD_DIM, (h + 1) * HEAD_DIM)
        q = jnp.dot(place_ref[...], joined(query_refs, columns), preferred_element_type=F32).astype(BF16)
        scores = lax.dot_general(
            q, joined(key_refs, columns), (((1,), (1,)), ((), ())), preferred_element_type=F32
        )
        scores = jnp.where(outside, mask_fill, scores * scale)
        terms = jnp.exp(scores - jnp.max(scores, axis=1, keepdims=True))
        out_ref[h] = (terms / jnp.sum(terms, axis=1, keepdims=True)).astype(BF16)


def mix_kernel(probs_ref, *refs):
    *value_refs, out_ref = refs
    for h in range(probs_ref.shape[0]):
        columns = slice(h * HEAD_DIM, (h + 1) * HEAD_DIM)
        out_ref[:, columns] = jnp.dot(
            probs_ref[h], joined(value_refs, columns), preferred_element_type=F32
        )


def norm_kernel(copies, place_ref, taken_ref, gain_ref, bias_ref, mixed_ref, *refs):
    *state_refs, hidden_ref, send_ref = refs
    hidden = mixed_ref[...] + jnp.dot(place_ref[...], joined(state_refs), preferred_element_type=F32)
    hidden_ref[...] = hidden
    centered = hidden - jnp.mean(hidden, axis=1, keepdims=True)
    variance = jnp.mean(centered * centered, axis=1, keepdims=True)
    normed = (centered * lax.rsqrt(variance + epsilon) * gain_ref[...] + bias_ref[...]).astype(BF16)
    picked = jnp.dot(taken_ref[...], normed, preferred_element_type=F32).astype(BF16)
    for n in range(copies):
        send_ref[n] = picked


def expert_kernel(x_ref, bias_ref, w_in_ref, w_out_ref, out_ref):
    inner = jnp.dot(x_ref[...], w_in_ref[0], preferred_element_type=F32)
    inner = jnp.maximum(inner + bias_ref[...], 0.0).astype(BF16)
    out_ref[...] = jnp.dot(inner, w_out_ref[0], preferred_element_type=F32).astype(BF16)


def combine_kernel(cap, parts_ref, hidden_ref, give_ref, bias_ref, out_ref):
    total = parts_ref[0].astype(F32)
    for n in range(1, parts_ref.shape[0]):
        total += parts_ref[n].astype(F32)
    bias = jnp.concatenate(
        [jnp.broadcast_to(bias_ref[e : e + 1, :], (cap, bias_ref.shape[1])) for e in range(bias_ref.shape[0])],
        axis=0,
    )
    result = (total + bias).astype(BF16)
    result = jnp.concatenate([result, result], axis=0)
    added = jnp.dot(give_ref[...], result, preferred_element_type=F32)
    out_ref[...] = (hidden_ref[...] + added).astype(BF16)


def per_device(
    pivot_states,
    queries,
    keys,
    values,
    pack_pos,
    segment_ids,
    expert_ids,
    gate_code,
    ln_gain,
    ln_bias,
    w_in,
    b_in,
    w_out,
    b_out,
):
    tok, width = pivot_states.shape
    dp = lax.axis_size("dp")
    experts = lax.axis_size("expert")
    cap = max(2, 2 * tok // (ROUNDS * experts))
    slots = experts * cap
    heads = width // HEAD_DIM
    position = lax.rem(pack_pos + (dp - lax.axis_index("dp")) * tok, dp * tok).reshape(1, tok)

    def exchange(rows, offsets):
        wide = width + (LANES if offsets else 0)
        parts = call(
            functools.partial(pack_kernel, offsets),
            (jax.ShapeDtypeStruct((tok // dp, wide), BF16),) * dp,
            position,
            rows,
        )
        return [
            part if n == 0 else lax.ppermute(part, "dp", [(i, (i + n) % dp) for i in range(dp)])
            for n, part in enumerate(parts)
        ]

    key_rows = exchange(keys, True)
    query_rows = exchange(queries, False)
    value_rows = exchange(values, False)
    state_rows = exchange(pivot_states, False)
    place, outside, taken, give = call(
        functools.partial(route_kernel, cap, experts, width),
        (
            jax.ShapeDtypeStruct((tok, tok), BF16),
            jax.ShapeDtypeStruct((tok, tok), F32),
            jax.ShapeDtypeStruct((slots, tok), BF16),
            jax.ShapeDtypeStruct((tok, 2 * slots), BF16),
        ),
        segment_ids,
        expert_ids.T,
        gate_code.T,
        *key_rows,
    )
    probs = call(
        probs_kernel,
        jax.ShapeDtypeStruct((heads, tok, tok), BF16),
        place,
        outside,
        *key_rows,
        *query_rows,
    )
    mixed = call(mix_kernel, jax.ShapeDtypeStruct((tok, width), F32), probs, *value_rows)
    hidden_state, send = call(
        functools.partial(norm_kernel, dp),
        (
            jax.ShapeDtypeStruct((tok, width), F32),
            jax.ShapeDtypeStruct((dp, slots, width), BF16),
        ),
        place,
        taken,
        ln_gain.reshape(1, width),
        ln_bias.reshape(1, width),
        mixed,
        *state_rows,
    )

    def over_all(x):
        x = x.reshape(dp * experts, cap, width)
        return lax.all_to_all(x, ("dp", "expert"), split_axis=0, concat_axis=0, tiled=True)

    share = call(
        expert_kernel,
        jax.ShapeDtypeStruct((dp * slots, width), BF16),
        over_all(send).reshape(dp * slots, width),
        b_in,
        w_in,
        w_out,
    )
    return call(
        functools.partial(combine_kernel, cap),
        jax.ShapeDtypeStruct((tok, width), BF16),
        over_all(share).reshape(dp, slots, width),
        hidden_state,
        give,
        b_out,
    )


def solution(mesh):
    return jax.shard_map(
        per_device,
        mesh=mesh,
        in_specs=(
            P(("dp", "expert"), None),
            P(("dp", "expert"), None),
            P(("dp", "expert"), None),
            P(("dp", "expert"), None),
            P(("dp", "expert")),
            P(("dp", "expert"), None),
            P(("dp", "expert"), None),
            P(("dp", "expert"), None),
            P(),
            P(),
            P("expert", None, "dp"),
            P("expert", "dp"),
            P("expert", "dp", None),
            P(),
        ),
        out_specs=P(("dp", "expert"), None),
        check_vma=False,
    )
```

time: 135 us -> 123 us (0.911)
  starting transfers between devices: 3.62 us -> 25.6 us
  blocking collectives: 84.9 us -> 63.7 us
  waiting for transfers between devices: 26.2 us -> 18.4 us
  matrix products: 6.84 us -> 0 us
    all_to_all x1 -> x0, waiting for transfers between devices: 26.2 us -> none  [per_device(): lax.all_to_all(share.reshape(dp * experts, cap, width), ('dp', 'expert'),...]
    ppermute x0 -> x12, starting transfers between devices: none -> 25.6 us  [exchange(): lax.ppermute(part, 'dp', [(i, (i + n) % dp) for i in range(dp)])]
    all_to_all x2, blocking collectives: 84.9 us -> 63.7 us  [over_all(): lax.all_to_all(x, ('dp', 'expert'), split_axis=0, concat_axis=0, tiled=True)]
    ppermute x0 -> x12, waiting for transfers between devices: none -> 18.4 us  [exchange(): lax.ppermute(part, 'dp', [(i, (i + n) % dp) for i in range(dp)])]
    dot_general x1 -> x0, matrix products: 6.84 us -> none  [per_device(): share = jnp.dot(inner, w_out[0], preferred_element_type=F32).astype(BF16)]
    all_to_all x1 -> x0, starting transfers between devices: 3.62 us -> none  [per_device(): lax.all_to_all(share.reshape(dp * experts, cap, width), ('dp', 'expert'),...]
    unnamed x24 -> x26, local copies, waits for them, and re-layouts: 4.88 us -> 6.21 us
    pallas_call x3 -> x10, Pallas kernels: 8 us -> 7.8 us  [call(): pl.pallas_call(body, out_shape=out_shape, compiler_params=pltpu.CompilerP...]
  transfers between devices with their start and end apart: 1 -> 12, of which waited for: 1 -> 4; matrix products, arithmetic and copies ran while one was open for 0% -> 0% of each run, Pallas kernels for 0% -> 3%
where the time goes in v2:
time: 123 us
  blocking collectives  63.7 us (52%)
  starting transfers between devices  25.6 us (21%)
  waiting for transfers between devices  18.4 us (15%)
  Pallas kernels  7.8 us (6%)
  local copies, waits for them, and re-layouts  6.21 us (5%)
    all_to_all x2, blocking collectives, over_all(): lax.all_to_all(x, ('dp', 'expert'), split_axis=0, concat_axis=0, tiled=True)  63.7 us
    ppermute x12, starting transfers between devices, exchange(): lax.ppermute(part, 'dp', [(i, (i + n) % dp) for i in range(dp)])  25.6 us
    ppermute x12, waiting for transfers between devices, exchange(): lax.ppermute(part, 'dp', [(i, (i + n) % dp) for i in range(dp)])  18.4 us
    pallas_call x10, Pallas kernels, call(): pl.pallas_call(body, out_shape=out_shape, compiler_params=pltpu.CompilerP...  7.8 us
    unnamed x26, local copies, waits for them, and re-layouts  6.21 us
  transfers between devices with their start and end apart: 12, of which 4 were waited for; matrix products, arithmetic and copies ran while one was open for 0% of the time, Pallas kernels for 3%

profile of v2, /device:TPU:0, one launch (start us, length us, event | category | flops | bytes accessed | tf_op | source)
XLA Modules:
  0.0 122.5 jit_solution(15572060849934617239)
XLA Ops:
  0.0 0.7 fusion.1.pos_ref
  0.7 1.0 copy-done.2
  1.7 0.4 shard_map.138
  2.1 3.1 %collective-permute-start.3 = (bf16[32,2048]{1,0:T(8,128)(2,1)S(1)}, bf16[32,2048]{1,0:T(8,128)(2,1)S(1)}, u32[]{:S(2)}, u32[]{:S(2)}) collective-permute-start(bf16[32,2048]{1,0:T(8,128)(2,1)S(1)} %get-tuple-element.35), channel_id=1, source_target_pairs={{0,8},{8,16},{16,24},{24,0},{1,9},{9,17},{17,25},{25,1},{2,10},{10... | collective-permute-start | bytes 393224 | tf_op jit(solution)/shard_map/ppermute | solution.py:196
  5.2 2.6 %collective-permute-start.4 = (bf16[32,2048]{1,0:T(8,128)(2,1)S(1)}, bf16[32,2048]{1,0:T(8,128)(2,1)S(1)}, u32[]{:S(2)}, u32[]{:S(2)}) collective-permute-start(bf16[32,2048]{1,0:T(8,128)(2,1)S(1)} %get-tuple-element.36), channel_id=1, source_target_pairs={{0,16},{8,24},{16,0},{24,8},{1,17},{9,25},{17,1},{25,9},{2,18},{10... | collective-permute-start | bytes 393224 | tf_op jit(solution)/shard_map/ppermute | solution.py:196
  7.8 1.0 copy-done.3
  8.8 0.4 shard_map.136
  9.2 0.1 collective-permute-start
  9.3 1.8 %collective-permute-start.1 = (bf16[32,2176]{1,0:T(8,128)(2,1)S(1)}, bf16[32,2176]{1,0:T(8,128)(2,1)S(1)}, u32[]{:S(2)}, u32[]{:S(2)}) collective-permute-start(bf16[32,2176]{1,0:T(8,128)(2,1)S(1)} %get-tuple-element.29), channel_id=1, source_target_pairs={{0,16},{8,24},{16,0},{24,8},{1,17},{9,25},{17,1},{25,9},{2,18},{10... | collective-permute-start | bytes 417800 | tf_op jit(solution)/shard_map/ppermute | solution.py:196
  11.2 1.9 %collective-permute-start.2 = (bf16[32,2176]{1,0:T(8,128)(2,1)S(1)}, bf16[32,2176]{1,0:T(8,128)(2,1)S(1)}, u32[]{:S(2)}, u32[]{:S(2)}) collective-permute-start(bf16[32,2176]{1,0:T(8,128)(2,1)S(1)} %get-tuple-element.30), channel_id=1, source_target_pairs={{0,24},{8,0},{16,8},{24,16},{1,25},{9,1},{17,9},{25,17},{2,26},{10... | collective-permute-start | bytes 417800 | tf_op jit(solution)/shard_map/ppermute | solution.py:196
  13.1 1.0 copy-done.4
  14.1 0.4 shard_map.140
  14.5 0.0 collective-permute-done.3.refs_5_
  14.5 0.7 collective-permute-start.5
  15.2 7.3 %collective-permute-done.4.refs_6_ = bf16[32,2048]{1,0:T(8,128)(2,1)S(1)} collective-permute-done((bf16[32,2048]{1,0:T(8,128)(2,1)S(1)}, bf16[32,2048]{1,0:T(8,128)(2,1)S(1)}, u32[]{:S(2)}, u32[]{:S(2)}) %collective-permute-start.4) | collective-permute-done | bytes 131104 | tf_op jit(solution)/shard_map/ppermute | solution.py:196
  22.5 2.6 %collective-permute-start.6 = (bf16[32,2048]{1,0:T(8,128)(2,1)S(1)}, bf16[32,2048]{1,0:T(8,128)(2,1)S(1)}, u32[]{:S(2)}, u32[]{:S(2)}) collective-permute-start(bf16[32,2048]{1,0:T(8,128)(2,1)S(1)} %get-tuple-element.39), channel_id=1, source_target_pairs={{0,8},{8,16},{16,24},{24,0},{1,9},{9,17},{17,25},{25,1},{2,10},{10... | collective-permute-start | bytes 393224 | tf_op jit(solution)/shard_map/ppermute | solution.py:196
  25.1 1.0 copy-done.5
  26.1 0.4 shard_map.142
  26.5 0.0 copy-start
  26.5 0.0 copy-start.9
  26.5 2.5 %collective-permute-done.5.refs_7_ = bf16[32,2048]{1,0:T(8,128)(2,1)S(1)} collective-permute-done((bf16[32,2048]{1,0:T(8,128)(2,1)S(1)}, bf16[32,2048]{1,0:T(8,128)(2,1)S(1)}, u32[]{:S(2)}, u32[]{:S(2)}) %collective-permute-start.5) | collective-permute-done | bytes 131104 | tf_op jit(solution)/shard_map/ppermute | solution.py:196
  29.0 8.3 %collective-permute-start.9 = (bf16[32,2048]{1,0:T(8,128)(2,1)S(1)}, bf16[32,2048]{1,0:T(8,128)(2,1)S(1)}, u32[]{:S(2)}, u32[]{:S(2)}) collective-permute-start(bf16[32,2048]{1,0:T(8,128)(2,1)S(1)} %get-tuple-element.43), channel_id=1, source_target_pairs={{0,8},{8,16},{16,24},{24,0},{1,9},{9,17},{17,25},{25,1},{2,10},{10... | collective-permute-start | bytes 393224 | tf_op jit(solution)/shard_map/ppermute | solution.py:196
  37.3 0.0 collective-permute-done.6.refs_1_
  37.3 0.0 collective-permute-start.7
  37.3 0.0 collective-permute-done.refs_1_
  37.3 2.4 %collective-permute-start.8 = (bf16[32,2048]{1,0:T(8,128)(2,1)S(1)}, bf16[32,2048]{1,0:T(8,128)(2,1)S(1)}, u32[]{:S(2)}, u32[]{:S(2)}) collective-permute-start(bf16[32,2048]{1,0:T(8,128)(2,1)S(1)} %get-tuple-element.41), channel_id=1, source_target_pairs={{0,24},{8,0},{16,8},{24,16},{1,25},{9,1},{17,9},{25,17},{2,26},{10... | collective-permute-start | bytes 393224 | tf_op jit(solution)/shard_map/ppermute | solution.py:196
  39.7 0.0 collective-permute-done.1.refs_2_
  39.7 0.6 collective-permute-start.10
  40.3 0.0 collective-permute-done.2.refs_3_
  40.3 1.4 %collective-permute-start.11 = (bf16[32,2048]{1,0:T(8,128)(2,1)S(1)}, bf16[32,2048]{1,0:T(8,128)(2,1)S(1)}, u32[]{:S(2)}, u32[]{:S(2)}) collective-permute-start(bf16[32,2048]{1,0:T(8,128)(2,1)S(1)} %get-tuple-element.45), channel_id=1, source_target_pairs={{0,24},{8,0},{16,8},{24,16},{1,25},{9,1},{17,9},{25,17},{2,26},{10... | collective-permute-start | bytes 393224 | tf_op jit(solution)/shard_map/ppermute | solution.py:196
  41.8 0.7 copy-done.10
  42.5 0.7 copy-done.11
  43.2 0.7 copy-done.12
  43.8 0.2 shard_map.137
  44.0 1.5 %shard_map.139.probs_ref = bf16[16,128,128]{2,1,0:T(8,128)(2,1)S(1)} custom-call(bf16[128,128]{1,0:T(8,128)(2,1)S(1)} %get-tuple-element.31.place_ref, f32[128,128]{1,0:T(8,128)S(1)} %get-tuple-element.33.outside_ref, bf16[32,2176]{1,0:T(8,128)(2,1)S(1)} %get-tuple-element.27.refs_0_, bf16[32,2176]{1,0:T(8,128)(2,1)S(1)} %collective-permute-done.refs_1_, ...), custom_call_target="tpu_custom_call" | custom-call | bytes 1703936 | tf_op jit(solution)/shard_map/pallas_call | solution.py:40
  45.5 2.4 %collective-permute-done.7.refs_2_ = bf16[32,2048]{1,0:T(8,128)(2,1)S(1)} collective-permute-done((bf16[32,2048]{1,0:T(8,128)(2,1)S(1)}, bf16[32,2048]{1,0:T(8,128)(2,1)S(1)}, u32[]{:S(2)}, u32[]{:S(2)}) %collective-permute-start.7) | collective-permute-done | bytes 131104 | tf_op jit(solution)/shard_map/ppermute | solution.py:196
  48.0 0.0 collective-permute-done.8.refs_3_
  48.0 0.3 shard_map.141.mixed_ref
  48.3 0.0 collective-permute-done.9.refs_1_
  48.3 6.2 %collective-permute-done.10.refs_2_ = bf16[32,2048]{1,0:T(8,128)(2,1)S(1)} collective-permute-done((bf16[32,2048]{1,0:T(8,128)(2,1)S(1)}, bf16[32,2048]{1,0:T(8,128)(2,1)S(1)}, u32[]{:S(2)}, u32[]{:S(2)}) %collective-permute-start.10) | collective-permute-done | bytes 131104 | tf_op jit(solution)/shard_map/ppermute | solution.py:196
  54.4 0.0 collective-permute-done.11.refs_3_
  54.4 0.0 copy-done.8
  54.4 0.8 shard_map.143
  55.2 34.1 %all_to_all.10 = bf16[32,8,2048]{2,1,0:T(8,128)(2,1)S(1)} all-to-all(bf16[32,8,2048]{2,1,0:T(8,128)(2,1)S(1)} %bitcast.13), channel_id=1, replica_groups=mesh['dp'=4,'expert'=8] {'dp','expert'}, dimensions={0} | all-to-all | bytes 2097152 | tf_op jit(solution)/shard_map/all_to_all | solution.py:242
  89.3 0.0 copy-start.6
  89.3 2.4 %shard_map.144 = bf16[256,2048]{1,0:T(8,128)(2,1)S(1)} custom-call(bf16[256,2048]{1,0:T(8,128)(2,1)S(1)} %bitcast.10, f32[1,1024]{1,0:T(1,128)S(1)} %copy-done.9, bf16[1,2048,1024]{2,1,0:T(8,128)(2,1)S(1)} %copy-done, bf16[1,1024,2048]{2,1,0:T(8,128)(2,1)S(1)} %copy-done.1), custom_call_target="tpu_custom_call" | custom-call | bytes 10489856 | tf_op jit(solution)/shard_map/pallas_call | solution.py:40
  91.7 29.7 %all_to_all.11 = bf16[32,8,2048]{2,1,0:T(8,128)(2,1)S(1)} all-to-all(bf16[32,8,2048]{2,1,0:T(8,128)(2,1)S(1)} %bitcast.11), channel_id=1, replica_groups=mesh['dp'=4,'expert'=8] {'dp','expert'}, dimensions={0} | all-to-all | bytes 2097152 | tf_op jit(solution)/shard_map/all_to_all | solution.py:242
  121.4 1.2 shard_map.145
  (15 shorter events, 0.0 us)
Async XLA Ops:
  0.0 54.4 %copy-start.7 = (f32[2048]{0:T(1024)S(1)}, f32[2048]{0:T(1024)}, u32[]{:S(2)}) copy-start(f32[2048]{0:T(1024)} %param.22) | copy-start | bytes 24580
  0.7 1.0 copy-start.2
  1.7 52.7 %copy-start.8 = (f32[2048]{0:T(1024)S(1)}, f32[2048]{0:T(1024)}, u32[]{:S(2)}) copy-start(f32[2048]{0:T(1024)} %param.23) | copy-start | bytes 24580
  2.1 12.4 %collective-permute-start.3 = (bf16[32,2048]{1,0:T(8,128)(2,1)S(1)}, bf16[32,2048]{1,0:T(8,128)(2,1)S(1)}, u32[]{:S(2)}, u32[]{:S(2)}) collective-permute-start(bf16[32,2048]{1,0:T(8,128)(2,1)S(1)} %get-tuple-element.35), channel_id=1, source_target_pairs={{0,8},{8,16},{16,24},{24,0},{1,9},{9,17},{17,25},{25,1},{2,10},{10... | collective-permute-start | bytes 393224 | tf_op jit(solution)/shard_map/ppermute | solution.py:196
  5.2 17.3 %collective-permute-start.4 = (bf16[32,2048]{1,0:T(8,128)(2,1)S(1)}, bf16[32,2048]{1,0:T(8,128)(2,1)S(1)}, u32[]{:S(2)}, u32[]{:S(2)}) collective-permute-start(bf16[32,2048]{1,0:T(8,128)(2,1)S(1)} %get-tuple-element.36), channel_id=1, source_target_pairs={{0,16},{8,24},{16,0},{24,8},{1,17},{9,25},{17,1},{25,9},{2,18},{10... | collective-permute-start | bytes 393224 | tf_op jit(solution)/shard_map/ppermute | solution.py:196
  7.8 1.0 copy-start.3
  9.2 28.2 %collective-permute-start = (bf16[32,2176]{1,0:T(8,128)(2,1)S(1)}, bf16[32,2176]{1,0:T(8,128)(2,1)S(1)}, u32[]{:S(2)}, u32[]{:S(2)}) collective-permute-start(bf16[32,2176]{1,0:T(8,128)(2,1)S(1)} %get-tuple-element.28), channel_id=1, source_target_pairs={{0,8},{8,16},{16,24},{24,0},{1,9},{9,17},{17,25},{25,1},{2,10},{10... | collective-permute-start | bytes 417800 | tf_op jit(solution)/shard_map/ppermute | solution.py:196
  9.3 30.4 %collective-permute-start.1 = (bf16[32,2176]{1,0:T(8,128)(2,1)S(1)}, bf16[32,2176]{1,0:T(8,128)(2,1)S(1)}, u32[]{:S(2)}, u32[]{:S(2)}) collective-permute-start(bf16[32,2176]{1,0:T(8,128)(2,1)S(1)} %get-tuple-element.29), channel_id=1, source_target_pairs={{0,16},{8,24},{16,0},{24,8},{1,17},{9,25},{17,1},{25,9},{2,18},{10... | collective-permute-start | bytes 417800 | tf_op jit(solution)/shard_map/ppermute | solution.py:196
  11.2 29.2 %collective-permute-start.2 = (bf16[32,2176]{1,0:T(8,128)(2,1)S(1)}, bf16[32,2176]{1,0:T(8,128)(2,1)S(1)}, u32[]{:S(2)}, u32[]{:S(2)}) collective-permute-start(bf16[32,2176]{1,0:T(8,128)(2,1)S(1)} %get-tuple-element.30), channel_id=1, source_target_pairs={{0,24},{8,0},{16,8},{24,16},{1,25},{9,1},{17,9},{25,17},{2,26},{10... | collective-permute-start | bytes 417800 | tf_op jit(solution)/shard_map/ppermute | solution.py:196
  13.1 1.0 copy-start.4
  14.5 14.5 %collective-permute-start.5 = (bf16[32,2048]{1,0:T(8,128)(2,1)S(1)}, bf16[32,2048]{1,0:T(8,128)(2,1)S(1)}, u32[]{:S(2)}, u32[]{:S(2)}) collective-permute-start(bf16[32,2048]{1,0:T(8,128)(2,1)S(1)} %get-tuple-element.37), channel_id=1, source_target_pairs={{0,24},{8,0},{16,8},{24,16},{1,25},{9,1},{17,9},{25,17},{2,26},{10... | collective-permute-start | bytes 393224 | tf_op jit(solution)/shard_map/ppermute | solution.py:196
  22.5 14.8 %collective-permute-start.6 = (bf16[32,2048]{1,0:T(8,128)(2,1)S(1)}, bf16[32,2048]{1,0:T(8,128)(2,1)S(1)}, u32[]{:S(2)}, u32[]{:S(2)}) collective-permute-start(bf16[32,2048]{1,0:T(8,128)(2,1)S(1)} %get-tuple-element.39), channel_id=1, source_target_pairs={{0,8},{8,16},{16,24},{24,0},{1,9},{9,17},{17,25},{25,1},{2,10},{10... | collective-permute-start | bytes 393224 | tf_op jit(solution)/shard_map/ppermute | solution.py:196
  25.1 1.0 copy-start.5
  26.1 63.2 %copy-start.1 = (bf16[1,1024,2048]{2,1,0:T(8,128)(2,1)S(1)}, bf16[1,1024,2048]{2,1,0:T(8,128)(2,1)}, u32[]{:S(2)}) copy-start(bf16[1,1024,2048]{2,1,0:T(8,128)(2,1)} %w_out_ref.1) | copy-start | bytes 12582916
  26.5 62.8 %copy-start = (bf16[1,2048,1024]{2,1,0:T(8,128)(2,1)S(1)}, bf16[1,2048,1024]{2,1,0:T(8,128)(2,1)}, u32[]{:S(2)}) copy-start(bf16[1,2048,1024]{2,1,0:T(8,128)(2,1)} %w_in_ref.1) | copy-start | bytes 12582916
  26.5 62.8 %copy-start.9 = (f32[1,1024]{1,0:T(1,128)S(1)}, f32[1,1024]{1,0:T(1,128)}, u32[]{:S(2)}) copy-start(f32[1,1024]{1,0:T(1,128)} %bias_ref.2) | copy-start | bytes 12292
  29.0 19.3 %collective-permute-start.9 = (bf16[32,2048]{1,0:T(8,128)(2,1)S(1)}, bf16[32,2048]{1,0:T(8,128)(2,1)S(1)}, u32[]{:S(2)}, u32[]{:S(2)}) collective-permute-start(bf16[32,2048]{1,0:T(8,128)(2,1)S(1)} %get-tuple-element.43), channel_id=1, source_target_pairs={{0,8},{8,16},{16,24},{24,0},{1,9},{9,17},{17,25},{25,1},{2,10},{10... | collective-permute-start | bytes 393224 | tf_op jit(solution)/shard_map/ppermute | solution.py:196
  37.3 10.6 %collective-permute-start.7 = (bf16[32,2048]{1,0:T(8,128)(2,1)S(1)}, bf16[32,2048]{1,0:T(8,128)(2,1)S(1)}, u32[]{:S(2)}, u32[]{:S(2)}) collective-permute-start(bf16[32,2048]{1,0:T(8,128)(2,1)S(1)} %get-tuple-element.40), channel_id=1, source_target_pairs={{0,16},{8,24},{16,0},{24,8},{1,17},{9,25},{17,1},{25,9},{2,18},{10... | collective-permute-start | bytes 393224 | tf_op jit(solution)/shard_map/ppermute | solution.py:196
  37.3 10.6 %collective-permute-start.8 = (bf16[32,2048]{1,0:T(8,128)(2,1)S(1)}, bf16[32,2048]{1,0:T(8,128)(2,1)S(1)}, u32[]{:S(2)}, u32[]{:S(2)}) collective-permute-start(bf16[32,2048]{1,0:T(8,128)(2,1)S(1)} %get-tuple-element.41), channel_id=1, source_target_pairs={{0,24},{8,0},{16,8},{24,16},{1,25},{9,1},{17,9},{25,17},{2,26},{10... | collective-permute-start | bytes 393224 | tf_op jit(solution)/shard_map/ppermute | solution.py:196
  39.7 14.7 %collective-permute-start.10 = (bf16[32,2048]{1,0:T(8,128)(2,1)S(1)}, bf16[32,2048]{1,0:T(8,128)(2,1)S(1)}, u32[]{:S(2)}, u32[]{:S(2)}) collective-permute-start(bf16[32,2048]{1,0:T(8,128)(2,1)S(1)} %get-tuple-element.44), channel_id=1, source_target_pairs={{0,16},{8,24},{16,0},{24,8},{1,17},{9,25},{17,1},{25,9},{2,18},{10... | collective-permute-start | bytes 393224 | tf_op jit(solution)/shard_map/ppermute | solution.py:196
  40.3 14.1 %collective-permute-start.11 = (bf16[32,2048]{1,0:T(8,128)(2,1)S(1)}, bf16[32,2048]{1,0:T(8,128)(2,1)S(1)}, u32[]{:S(2)}, u32[]{:S(2)}) collective-permute-start(bf16[32,2048]{1,0:T(8,128)(2,1)S(1)} %get-tuple-element.45), channel_id=1, source_target_pairs={{0,24},{8,0},{16,8},{24,16},{1,25},{9,1},{17,9},{25,17},{2,26},{10... | collective-permute-start | bytes 393224 | tf_op jit(solution)/shard_map/ppermute | solution.py:196
  41.8 0.7 copy-start.10
  42.5 0.7 copy-start.11
  43.2 0.7 copy-start.12
  89.3 32.1 %copy-start.6 = (f32[8,2048]{1,0:T(8,128)S(1)}, f32[8,2048]{1,0:T(8,128)}, u32[]{:S(2)}) copy-start(f32[8,2048]{1,0:T(8,128)} %bias_ref.3) | copy-start | bytes 196612

commit v3 on v2

--- a/solution.py
+++ b/solution.py
@@ -45,20 +45,31 @@
     )(*operands)
 
 
-def pack_kernel(offsets, pos_ref, x_ref, *out_refs):
-    tok, width = x_ref.shape
-    share = tok // len(out_refs)
-    lanes, subl = across(pos_ref[...], tok)
-    rank = jnp.sum(one_hot(subl < lanes), axis=0, keepdims=True)
-    order = one_hot(iota((tok, tok), 0).astype(F32) == rank).astype(BF16)
-    rows = jnp.dot(order, x_ref[...], preferred_element_type=F32).astype(BF16)
-    for n, out_ref in enumerate(out_refs):
-        out_ref[:, :width] = rows[n * share : (n + 1) * share]
-    if offsets:
+def pack_kernel(keyed, pos_ref, *refs):
+    parts = lax.axis_size("dp")
+    *x_refs, order_ref = refs[: len(refs) - parts]
+    out_refs = refs[len(refs) - parts :]
+    tok = order_ref.shape[0]
+    share = tok // parts
+
+    def sort(x, at):
+        rows = jnp.dot(order, x, preferred_element_type=F32).astype(BF16)
+        for n, out_ref in enumerate(out_refs):
+            out_ref[:, at : at + x.shape[1]] = rows[n * share : (n + 1) * share]
+
+    if keyed:
+        lanes, subl = across(pos_ref[...], tok)
+        rank = jnp.sum(one_hot(subl < lanes), axis=0, keepdims=True)
+        order = one_hot(iota((tok, tok), 0).astype(F32) == rank).astype(BF16)
         _, offset = across(lax.rem(pos_ref[...], tok), tok)
-        rows = jnp.dot(order, offset.astype(BF16), preferred_element_type=F32).astype(BF16)
-        for n, out_ref in enumerate(out_refs):
-            out_ref[:, width:] = rows[n * share : (n + 1) * share]
+        sort(offset.astype(BF16), sum(x.shape[1] for x in x_refs))
+    else:
+        order = pos_ref[...]
+    order_ref[...] = order
+    at = 0
+    for x_ref in x_refs:
+        sort(x_ref[...], at)
+        at += x_ref.shape[1]
 
 
 def joined(refs, columns=slice(None)):
@@ -121,41 +132,50 @@
 
 def mix_kernel(probs_ref, *refs):
     *value_refs, out_ref = refs
+    width = out_ref.shape[1]
     for h in range(probs_ref.shape[0]):
-        columns = slice(h * HEAD_DIM, (h + 1) * HEAD_DIM)
-        out_ref[:, columns] = jnp.dot(
-            probs_ref[h], joined(value_refs, columns), preferred_element_type=F32
-        )
-
-
-def norm_kernel(copies, place_ref, taken_ref, gain_ref, bias_ref, mixed_ref, *refs):
+        lo = h * HEAD_DIM
+        values = joined(value_refs, slice(width + lo, width + lo + HEAD_DIM))
+        out_ref[:, lo : lo + HEAD_DIM] = jnp.dot(probs_ref[h], values, preferred_element_type=F32)
+
+
+def norm_kernel(place_ref, taken_ref, gain_ref, bias_ref, mixed_ref, *refs):
     *state_refs, hidden_ref, send_ref = refs
     hidden = mixed_ref[...] + jnp.dot(place_ref[...], joined(state_refs), preferred_element_type=F32)
     hidden_ref[...] = hidden
     centered = hidden - jnp.mean(hidden, axis=1, keepdims=True)
     variance = jnp.mean(centered * centered, axis=1, keepdims=True)
     normed = (centered * lax.rsqrt(variance + epsilon) * gain_ref[...] + bias_ref[...]).astype(BF16)
-    picked = jnp.dot(taken_ref[...], normed, preferred_element_type=F32).astype(BF16)
-    for n in range(copies):
-        send_ref[n] = picked
-
-
-def expert_kernel(x_ref, bias_ref, w_in_ref, w_out_ref, out_ref):
-    inner = jnp.dot(x_ref[...], w_in_ref[0], preferred_element_type=F32)
+    send_ref[...] = jnp.dot(taken_ref[...], normed, preferred_element_type=F32).astype(BF16)
+
+
+def expert_kernel(bias_ref, w_in_ref, w_out_ref, *refs):
+    x_refs, out_refs = refs[: len(refs) // 2], refs[len(refs) // 2 :]
+    inner = jnp.dot(joined(x_refs), w_in_ref[0], preferred_element_type=F32)
     inner = jnp.maximum(inner + bias_ref[...], 0.0).astype(BF16)
-    out_ref[...] = jnp.dot(inner, w_out_ref[0], preferred_element_type=F32).astype(BF16)
-
-
-def combine_kernel(cap, parts_ref, hidden_ref, give_ref, bias_ref, out_ref):
-    total = parts_ref[0].astype(F32)
-    for n in range(1, parts_ref.shape[0]):
-        total += parts_ref[n].astype(F32)
-    bias = jnp.concatenate(
-        [jnp.broadcast_to(bias_ref[e : e + 1, :], (cap, bias_ref.shape[1])) for e in range(bias_ref.shape[0])],
-        axis=0,
-    )
-    result = (total + bias).astype(BF16)
-    result = jnp.concatenate([result, result], axis=0)
+    share = jnp.dot(inner, w_out_ref[0], preferred_element_type=F32).astype(BF16)
+    at = 0
+    for out_ref in out_refs:
+        out_ref[...] = share[at : at + out_ref.shape[0]]
+        at += out_ref.shape[0]
+
+
+def add_kernel(first_ref, second_ref, out_ref):
+    out_ref[...] = (first_ref[...].astype(F32) + second_ref[...].astype(F32)).astype(BF16)
+
+
+def result_kernel(bias_ref, *refs):
+    *share_refs, out_ref = refs
+    total = share_refs[0][...].astype(F32)
+    for share_ref in share_refs[1:]:
+        total += share_ref[...].astype(F32)
+    row = lax.axis_index("expert") == iota(bias_ref.shape, 0)
+    bias = jnp.sum(jnp.where(row, bias_ref[...], 0.0), axis=0, keepdims=True)
+    out_ref[...] = (total + bias).astype(BF16)
+
+
+def combine_kernel(results_ref, hidden_ref, give_ref, out_ref):
+    result = jnp.concatenate([results_ref[...], results_ref[...]], axis=0)
     added = jnp.dot(give_ref[...], result, preferred_element_type=F32)
     out_ref[...] = (hidden_ref[...] + added).astype(BF16)
 
@@ -184,23 +204,22 @@
     heads = width // HEAD_DIM
     position = lax.rem(pack_pos + (dp - lax.axis_index("dp")) * tok, dp * tok).reshape(1, tok)
 
-    def exchange(rows, offsets):
-        wide = width + (LANES if offsets else 0)
-        parts = call(
-            functools.partial(pack_kernel, offsets),
-            (jax.ShapeDtypeStruct((tok // dp, wide), BF16),) * dp,
-            position,
-            rows,
-        )
-        return [
+    def exchange(guide, keyed, *arrays):
+        wide = width * len(arrays) + (LANES if keyed else 0)
+        order, *parts = call(
+            functools.partial(pack_kernel, keyed),
+            (jax.ShapeDtypeStruct((tok, tok), BF16),) + (jax.ShapeDtypeStruct((tok // dp, wide), BF16),) * dp,
+            guide,
+            *arrays,
+        )
+        return order, [
             part if n == 0 else lax.ppermute(part, "dp", [(i, (i + n) % dp) for i in range(dp)])
             for n, part in enumerate(parts)
         ]
 
-    key_rows = exchange(keys, True)
-    query_rows = exchange(queries, False)
-    value_rows = exchange(values, False)
-    state_rows = exchange(pivot_states, False)
+    order, key_rows = exchange(position, True, keys)
+    order, pair_rows = exchange(order, False, queries, values)
+    _, state_rows = exchange(order, False, pivot_states)
     place, outside, taken, give = call(
         functools.partial(route_kernel, cap, experts, width),
         (
@@ -220,14 +239,14 @@
         place,
         outside,
         *key_rows,
-        *query_rows,
-    )
-    mixed = call(mix_kernel, jax.ShapeDtypeStruct((tok, width), F32), probs, *value_rows)
+        *pair_rows,
+    )
+    mixed = call(mix_kernel, jax.ShapeDtypeStruct((tok, width), F32), probs, *pair_rows)
     hidden_state, send = call(
-        functools.partial(norm_kernel, dp),
+        norm_kernel,
         (
             jax.ShapeDtypeStruct((tok, width), F32),
-            jax.ShapeDtypeStruct((dp, slots, width), BF16),
+            jax.ShapeDtypeStruct((slots, width), BF16),
         ),
         place,
         taken,
@@ -237,25 +256,44 @@
         *state_rows,
     )
 
-    def over_all(x):
-        x = x.reshape(dp * experts, cap, width)
-        return lax.all_to_all(x, ("dp", "expert"), split_axis=0, concat_axis=0, tiled=True)
-
-    share = call(
-        expert_kernel,
-        jax.ShapeDtypeStruct((dp * slots, width), BF16),
-        over_all(send).reshape(dp * slots, width),
-        b_in,
-        w_in,
-        w_out,
-    )
+    def over_experts(x):
+        x = x.reshape(experts, cap, width)
+        return lax.all_to_all(x, "expert", split_axis=0, concat_axis=0, tiled=True).reshape(slots, width)
+
+    def apply(*rows):
+        shape = jax.ShapeDtypeStruct((slots, width), BF16)
+        return call(expert_kernel, (shape,) * len(rows), b_in, w_in, w_out, *rows)
+
+    def swap(x, distance):
+        return lax.ppermute(x, "dp", [(i, i ^ distance) for i in range(dp)])
+
+    own = over_experts(send)
+    if dp == 4:
+        far = swap(own, 2)
+        near = swap(own, 1)
+        corner = swap(far, 1)
+        own_share, near_share = apply(own, near)
+        corner_share, far_share = apply(corner, far)
+        corner_in = swap(corner_share, 1)
+        near_in = swap(near_share, 1)
+        pair = call(add_kernel, jax.ShapeDtypeStruct((slots, width), BF16), corner_in, far_share)
+        shares = [own_share, near_in, swap(pair, 2)]
+    else:
+        every = lax.all_gather(own, "dp", axis=0, tiled=True)
+        (share,) = call(
+            expert_kernel, (jax.ShapeDtypeStruct((dp * slots, width), BF16),), b_in, w_in, w_out, every
+        )
+        parts = lax.all_to_all(
+            share.reshape(dp, slots, width), "dp", split_axis=0, concat_axis=0, tiled=True
+        )
+        shares = [parts[n] for n in range(dp)]
+    results = call(result_kernel, jax.ShapeDtypeStruct((slots, width), BF16), b_out, *shares)
     return call(
-        functools.partial(combine_kernel, cap),
+        combine_kernel,
         jax.ShapeDtypeStruct((tok, width), BF16),
-        over_all(share).reshape(dp, slots, width),
+        over_experts(results),
         hidden_state,
         give,
-        b_out,
     )
 
 

time: 123 us -> 121 us (0.984)
  blocking collectives: 63.7 us -> 19.9 us
  waiting for transfers between devices: 18.4 us -> 55.3 us
  starting transfers between devices: 25.6 us -> 30.5 us
    all_to_all x2, blocking collectives: 63.7 us -> 19.9 us  [over_experts(): lax.all_to_all(x, 'expert', split_axis=0, concat_axis=0, tiled=True)]
    ppermute x0 -> x6, waiting for transfers between devices: none -> 37.8 us  [swap(): return lax.ppermute(x, 'dp', [(i, i ^ distance) for i in range(dp)])]
    ppermute x0 -> x6, starting transfers between devices: none -> 6.71 us  [swap(): return lax.ppermute(x, 'dp', [(i, i ^ distance) for i in range(dp)])]
    ppermute x12 -> x9, starting transfers between devices: 25.6 us -> 23.8 us  [exchange(): lax.ppermute(part, 'dp', [(i, (i + n) % dp) for i in range(dp)])]
    ppermute x12 -> x9, waiting for transfers between devices: 18.4 us -> 17.5 us  [exchange(): lax.ppermute(part, 'dp', [(i, (i + n) % dp) for i in range(dp)])]
    pallas_call x10 -> x12, Pallas kernels: 7.8 us -> 8.22 us  [call(): pl.pallas_call(body, out_shape=out_shape, compiler_params=pltpu.CompilerP...]
  transfers between devices with their start and end apart: 12 -> 15, of which waited for: 4 -> 8; matrix products, arithmetic and copies ran while one was open for 0% -> 0% of each run, Pallas kernels for 3% -> 5%
where the time goes in v3:
time: 121 us
  waiting for transfers between devices  55.3 us (46%)
  starting transfers between devices  30.5 us (25%)
  blocking collectives  19.9 us (16%)
  Pallas kernels  8.22 us (7%)
  local copies, waits for them, and re-layouts  6.2 us (5%)
    ppermute x6, waiting for transfers between devices, swap(): return lax.ppermute(x, 'dp', [(i, i ^ distance) for i in range(dp)])  37.8 us
    ppermute x9, starting transfers between devices, exchange(): lax.ppermute(part, 'dp', [(i, (i + n) % dp) for i in range(dp)])  23.8 us
    all_to_all x2, blocking collectives, over_experts(): lax.all_to_all(x, 'expert', split_axis=0, concat_axis=0, tiled=True)  19.9 us
    ppermute x9, waiting for transfers between devices, exchange(): lax.ppermute(part, 'dp', [(i, (i + n) % dp) for i in range(dp)])  17.5 us
    pallas_call x12, Pallas kernels, call(): pl.pallas_call(body, out_shape=out_shape, compiler_params=pltpu.CompilerP...  8.22 us
    ppermute x6, starting transfers between devices, swap(): return lax.ppermute(x, 'dp', [(i, i ^ distance) for i in range(dp)])  6.71 us
    unnamed x26, local copies, waits for them, and re-layouts  6.2 us
  transfers between devices with their start and end apart: 15, of which 8 were waited for; matrix products, arithmetic and copies ran while one was open for 0% of the time, Pallas kernels for 5%

profile of v3, /device:TPU:0, one launch (start us, length us, event | category | flops | bytes accessed | tf_op | source)
XLA Modules:
  0.0 120.9 jit_solution(458614133365971759)
XLA Ops:
  0.0 0.7 fusion.1.pos_ref
  0.7 1.0 copy-done.2
  1.7 0.4 shard_map.136
  2.1 3.1 %collective-permute-start = (bf16[32,2176]{1,0:T(8,128)(2,1)S(1)}, bf16[32,2176]{1,0:T(8,128)(2,1)S(1)}, u32[]{:S(2)}, u32[]{:S(2)}) collective-permute-start(bf16[32,2176]{1,0:T(8,128)(2,1)S(1)} %get-tuple-element.30), channel_id=1, source_target_pairs={{0,8},{8,16},{16,24},{24,0},{1,9},{9,17},{17,25},{25,1},{2,10},{10... | collective-permute-start | bytes 417800 | tf_op jit(solution)/shard_map/ppermute | solution.py:216
  5.2 1.0 copy-done.3
  6.2 1.0 copy-done.4
  7.3 0.4 shard_map.138
  7.7 0.0 copy-start
  7.7 1.6 %collective-permute-start.3 = (bf16[32,4096]{1,0:T(8,128)(2,1)S(1)}, bf16[32,4096]{1,0:T(8,128)(2,1)S(1)}, u32[]{:S(2)}, u32[]{:S(2)}) collective-permute-start(bf16[32,4096]{1,0:T(8,128)(2,1)S(1)} %get-tuple-element.38), channel_id=1, source_target_pairs={{0,8},{8,16},{16,24},{24,0},{1,9},{9,17},{17,25},{25,1},{2,10},{10... | collective-permute-start | bytes 786440 | tf_op jit(solution)/shard_map/ppermute | solution.py:216
  9.3 1.1 collective-permute-start.1
  10.4 2.8 %collective-permute-start.2 = (bf16[32,2176]{1,0:T(8,128)(2,1)S(1)}, bf16[32,2176]{1,0:T(8,128)(2,1)S(1)}, u32[]{:S(2)}, u32[]{:S(2)}) collective-permute-start(bf16[32,2176]{1,0:T(8,128)(2,1)S(1)} %get-tuple-element.32), channel_id=1, source_target_pairs={{0,24},{8,0},{16,8},{24,16},{1,25},{9,1},{17,9},{25,17},{2,26},{10... | collective-permute-start | bytes 417800 | tf_op jit(solution)/shard_map/ppermute | solution.py:216
  13.3 0.3 collective-permute-start.4
  13.6 0.0 collective-permute-done.refs_1_
  13.6 1.2 collective-permute-start.5
  14.8 1.0 copy-done.5
  15.9 0.7 shard_map.141
  16.6 11.1 %collective-permute-done.1.refs_2_ = bf16[32,2176]{1,0:T(8,128)(2,1)S(1)} collective-permute-done((bf16[32,2176]{1,0:T(8,128)(2,1)S(1)}, bf16[32,2176]{1,0:T(8,128)(2,1)S(1)}, u32[]{:S(2)}, u32[]{:S(2)}) %collective-permute-start.1) | collective-permute-done | bytes 139296 | tf_op jit(solution)/shard_map/ppermute | solution.py:216
  27.6 10.2 %collective-permute-start.6 = (bf16[32,2048]{1,0:T(8,128)(2,1)S(1)}, bf16[32,2048]{1,0:T(8,128)(2,1)S(1)}, u32[]{:S(2)}, u32[]{:S(2)}) collective-permute-start(bf16[32,2048]{1,0:T(8,128)(2,1)S(1)} %get-tuple-element.43), channel_id=1, source_target_pairs={{0,8},{8,16},{16,24},{24,0},{1,9},{9,17},{17,25},{25,1},{2,10},{10... | collective-permute-start | bytes 393224 | tf_op jit(solution)/shard_map/ppermute | solution.py:216
  37.9 0.0 collective-permute-done.2.refs_3_
  37.9 3.4 %collective-permute-start.7 = (bf16[32,2048]{1,0:T(8,128)(2,1)S(1)}, bf16[32,2048]{1,0:T(8,128)(2,1)S(1)}, u32[]{:S(2)}, u32[]{:S(2)}) collective-permute-start(bf16[32,2048]{1,0:T(8,128)(2,1)S(1)} %get-tuple-element.44), channel_id=1, source_target_pairs={{0,16},{8,24},{16,0},{24,8},{1,17},{9,25},{17,1},{25,9},{2,18},{10... | collective-permute-start | bytes 393224 | tf_op jit(solution)/shard_map/ppermute | solution.py:216
  41.3 0.7 copy-done.10
  42.0 0.7 copy-done.11
  42.6 0.7 copy-done.12
  43.3 0.2 shard_map.137
  43.5 1.5 %shard_map.139.probs_ref = bf16[16,128,128]{2,1,0:T(8,128)(2,1)S(1)} custom-call(bf16[128,128]{1,0:T(8,128)(2,1)S(1)} %get-tuple-element.33.place_ref, f32[128,128]{1,0:T(8,128)S(1)} %get-tuple-element.35.outside_ref, bf16[32,2176]{1,0:T(8,128)(2,1)S(1)} %get-tuple-element.29.refs_0_, bf16[32,2176]{1,0:T(8,128)(2,1)S(1)} %collective-permute-done.refs_1_, ...), custom_call_target="tpu_custom_call" | custom-call | bytes 2228224 | tf_op jit(solution)/shard_map/pallas_call | solution.py:40
  45.0 0.3 shard_map.140.mixed_ref
  45.3 6.4 %collective-permute-done.7.refs_2_ = bf16[32,2048]{1,0:T(8,128)(2,1)S(1)} collective-permute-done((bf16[32,2048]{1,0:T(8,128)(2,1)S(1)}, bf16[32,2048]{1,0:T(8,128)(2,1)S(1)}, u32[]{:S(2)}, u32[]{:S(2)}) %collective-permute-start.7) | collective-permute-done | bytes 131104 | tf_op jit(solution)/shard_map/ppermute | solution.py:216
  51.7 0.8 shard_map.142
  52.5 10.5 %all_to_all.10 = bf16[8,8,2048]{2,1,0:T(8,128)(2,1)S(1)} all-to-all(bf16[8,8,2048]{2,1,0:T(8,128)(2,1)S(1)} %bitcast.15), channel_id=1, replica_groups=mesh['dp'=4,'expert'=8] {'expert'}, dimensions={0} | all-to-all | bytes 524288 | tf_op jit(solution)/shard_map/all_to_all | solution.py:261
  63.0 2.2 %collective-permute-start.11 = (bf16[64,2048]{1,0:T(8,128)(2,1)S(1)}, bf16[64,2048]{1,0:T(8,128)(2,1)S(1)}, u32[]{:S(2)}, u32[]{:S(2)}) collective-permute-start(bf16[64,2048]{1,0:T(8,128)(2,1)S(1)} %bitcast.10), channel_id=1, source_target_pairs={{0,16},{8,24},{16,0},{24,8},{1,17},{9,25},{17,1},{25,9},{2,18},{10... | collective-permute-start | bytes 786440 | tf_op jit(solution)/shard_map/ppermute | solution.py:268
  65.2 11.7 %collective-permute-done.11.refs_1_ = bf16[64,2048]{1,0:T(8,128)(2,1)S(1)} collective-permute-done((bf16[64,2048]{1,0:T(8,128)(2,1)S(1)}, bf16[64,2048]{1,0:T(8,128)(2,1)S(1)}, u32[]{:S(2)}, u32[]{:S(2)}) %collective-permute-start.11) | collective-permute-done | bytes 262176 | tf_op jit(solution)/shard_map/ppermute | solution.py:268
  76.9 0.3 collective-permute-start.12
  77.2 1.7 %collective-permute-start.9 = (bf16[64,2048]{1,0:T(8,128)(2,1)S(1)}, bf16[64,2048]{1,0:T(8,128)(2,1)S(1)}, u32[]{:S(2)}, u32[]{:S(2)}) collective-permute-start(bf16[64,2048]{1,0:T(8,128)(2,1)S(1)} %bitcast.11), channel_id=1, source_target_pairs={{0,8},{8,0},{16,24},{24,16},{1,9},{9,1},{17,25},{25,17},{2,10},{10... | collective-permute-start | bytes 786440 | tf_op jit(solution)/shard_map/ppermute | solution.py:268
  78.9 7.2 %collective-permute-done.12.refs_0_ = bf16[64,2048]{1,0:T(8,128)(2,1)S(1)} collective-permute-done((bf16[64,2048]{1,0:T(8,128)(2,1)S(1)}, bf16[64,2048]{1,0:T(8,128)(2,1)S(1)}, u32[]{:S(2)}, u32[]{:S(2)}) %collective-permute-start.12) | collective-permute-done | bytes 262176 | tf_op jit(solution)/shard_map/ppermute | solution.py:268
  86.1 1.3 %shard_map.144 = (bf16[64,2048]{1,0:T(8,128)(2,1)S(1)}, bf16[64,2048]{1,0:T(8,128)(2,1)S(1)}) custom-call(f32[1,1024]{1,0:T(1,128)S(1)} %copy-done.7, bf16[1,2048,1024]{2,1,0:T(8,128)(2,1)S(1)} %copy-done, bf16[1,1024,2048]{2,1,0:T(8,128)(2,1)S(1)} %copy-done.1, bf16[64,2048]{1,0:T(8,128)(2,1)S(1)} %collective-permute-done.12.refs_0_, ...), custom_call_target="tpu_custom_call" | custom-call | bytes 9441280 | tf_op jit(solution)/shard_map/pallas_call | solution.py:40
  87.5 0.0 copy-start.6
  87.5 0.3 collective-permute-start.13
  87.8 3.9 %collective-permute-done.9.refs_1_ = bf16[64,2048]{1,0:T(8,128)(2,1)S(1)} collective-permute-done((bf16[64,2048]{1,0:T(8,128)(2,1)S(1)}, bf16[64,2048]{1,0:T(8,128)(2,1)S(1)}, u32[]{:S(2)}, u32[]{:S(2)}) %collective-permute-start.9) | collective-permute-done | bytes 262176 | tf_op jit(solution)/shard_map/ppermute | solution.py:268
  91.7 1.3 %shard_map.143 = (bf16[64,2048]{1,0:T(8,128)(2,1)S(1)}, bf16[64,2048]{1,0:T(8,128)(2,1)S(1)}) custom-call(f32[1,1024]{1,0:T(1,128)S(1)} %copy-done.7, bf16[1,2048,1024]{2,1,0:T(8,128)(2,1)S(1)} %copy-done, bf16[1,1024,2048]{2,1,0:T(8,128)(2,1)S(1)} %copy-done.1, bf16[64,2048]{1,0:T(8,128)(2,1)S(1)} %bitcast.12, ...), custom_call_target="tpu_custom_call" | custom-call | bytes 9441280 | tf_op jit(solution)/shard_map/pallas_call | solution.py:40
  93.0 0.4 collective-permute-start.10
  93.4 3.9 %collective-permute-done.13.first_ref = bf16[64,2048]{1,0:T(8,128)(2,1)S(1)} collective-permute-done((bf16[64,2048]{1,0:T(8,128)(2,1)S(1)}, bf16[64,2048]{1,0:T(8,128)(2,1)S(1)}, u32[]{:S(2)}, u32[]{:S(2)}) %collective-permute-start.13) | collective-permute-done | bytes 262176 | tf_op jit(solution)/shard_map/ppermute | solution.py:268
  97.3 0.1 shard_map.145
  97.3 1.7 %collective-permute-start.14 = (bf16[64,2048]{1,0:T(8,128)(2,1)S(1)}, bf16[64,2048]{1,0:T(8,128)(2,1)S(1)}, u32[]{:S(2)}, u32[]{:S(2)}) collective-permute-start(bf16[64,2048]{1,0:T(8,128)(2,1)S(1)} %shard_map.145), channel_id=1, source_target_pairs={{0,16},{8,24},{16,0},{24,8},{1,17},{9,25},{17,1},{25,9},{2,18},{10... | collective-permute-start | bytes 786440 | tf_op jit(solution)/shard_map/ppermute | solution.py:268
  99.1 5.9 %collective-permute-done.10.refs_1_ = bf16[64,2048]{1,0:T(8,128)(2,1)S(1)} collective-permute-done((bf16[64,2048]{1,0:T(8,128)(2,1)S(1)}, bf16[64,2048]{1,0:T(8,128)(2,1)S(1)}, u32[]{:S(2)}, u32[]{:S(2)}) %collective-permute-start.10) | collective-permute-done | bytes 262176 | tf_op jit(solution)/shard_map/ppermute | solution.py:268
  104.9 5.3 %collective-permute-done.14.refs_2_ = bf16[64,2048]{1,0:T(8,128)(2,1)S(1)} collective-permute-done((bf16[64,2048]{1,0:T(8,128)(2,1)S(1)}, bf16[64,2048]{1,0:T(8,128)(2,1)S(1)}, u32[]{:S(2)}, u32[]{:S(2)}) %collective-permute-start.14) | collective-permute-done | bytes 262176 | tf_op jit(solution)/shard_map/ppermute | solution.py:268
  110.3 0.1 shard_map.146
  110.4 9.4 %all_to_all.11 = bf16[8,8,2048]{2,1,0:T(8,128)(2,1)S(1)} all-to-all(bf16[8,8,2048]{2,1,0:T(8,128)(2,1)S(1)} %bitcast.14), channel_id=1, replica_groups=mesh['dp'=4,'expert'=8] {'expert'}, dimensions={0} | all-to-all | bytes 524288 | tf_op jit(solution)/shard_map/all_to_all | solution.py:261
  119.8 1.1 shard_map.147
  (23 shorter events, 0.0 us)
Async XLA Ops:
  0.0 51.7 %copy-start.8 = (f32[2048]{0:T(1024)S(1)}, f32[2048]{0:T(1024)}, u32[]{:S(2)}) copy-start(f32[2048]{0:T(1024)} %param.22) | copy-start | bytes 24580
  0.7 1.0 copy-start.2
  1.7 50.0 %copy-start.9 = (f32[2048]{0:T(1024)S(1)}, f32[2048]{0:T(1024)}, u32[]{:S(2)}) copy-start(f32[2048]{0:T(1024)} %param.23) | copy-start | bytes 24580
  1.7 84.4 %copy-start.7 = (f32[1,1024]{1,0:T(1,128)S(1)}, f32[1,1024]{1,0:T(1,128)}, u32[]{:S(2)}) copy-start(f32[1,1024]{1,0:T(1,128)} %bias_ref.4) | copy-start | bytes 12292
  2.1 11.5 %collective-permute-start = (bf16[32,2176]{1,0:T(8,128)(2,1)S(1)}, bf16[32,2176]{1,0:T(8,128)(2,1)S(1)}, u32[]{:S(2)}, u32[]{:S(2)}) collective-permute-start(bf16[32,2176]{1,0:T(8,128)(2,1)S(1)} %get-tuple-element.30), channel_id=1, source_target_pairs={{0,8},{8,16},{16,24},{24,0},{1,9},{9,17},{17,25},{25,1},{2,10},{10... | collective-permute-start | bytes 417800 | tf_op jit(solution)/shard_map/ppermute | solution.py:216
  5.2 1.0 copy-start.3
  6.2 1.0 copy-start.4
  7.3 78.8 %copy-start.1 = (bf16[1,1024,2048]{2,1,0:T(8,128)(2,1)S(1)}, bf16[1,1024,2048]{2,1,0:T(8,128)(2,1)}, u32[]{:S(2)}) copy-start(bf16[1,1024,2048]{2,1,0:T(8,128)(2,1)} %w_out_ref.3) | copy-start | bytes 12582916
  7.7 78.4 %copy-start = (bf16[1,2048,1024]{2,1,0:T(8,128)(2,1)S(1)}, bf16[1,2048,1024]{2,1,0:T(8,128)(2,1)}, u32[]{:S(2)}) copy-start(bf16[1,2048,1024]{2,1,0:T(8,128)(2,1)} %w_in_ref.3) | copy-start | bytes 12582916
  7.7 33.6 %collective-permute-start.3 = (bf16[32,4096]{1,0:T(8,128)(2,1)S(1)}, bf16[32,4096]{1,0:T(8,128)(2,1)S(1)}, u32[]{:S(2)}, u32[]{:S(2)}) collective-permute-start(bf16[32,4096]{1,0:T(8,128)(2,1)S(1)} %get-tuple-element.38), channel_id=1, source_target_pairs={{0,8},{8,16},{16,24},{24,0},{1,9},{9,17},{17,25},{25,1},{2,10},{10... | collective-permute-start | bytes 786440 | tf_op jit(solution)/shard_map/ppermute | solution.py:216
  9.3 18.3 %collective-permute-start.1 = (bf16[32,2176]{1,0:T(8,128)(2,1)S(1)}, bf16[32,2176]{1,0:T(8,128)(2,1)S(1)}, u32[]{:S(2)}, u32[]{:S(2)}) collective-permute-start(bf16[32,2176]{1,0:T(8,128)(2,1)S(1)} %get-tuple-element.31), channel_id=1, source_target_pairs={{0,16},{8,24},{16,0},{24,8},{1,17},{9,25},{17,1},{25,9},{2,18},{10... | collective-permute-start | bytes 417800 | tf_op jit(solution)/shard_map/ppermute | solution.py:216
  10.4 27.4 %collective-permute-start.2 = (bf16[32,2176]{1,0:T(8,128)(2,1)S(1)}, bf16[32,2176]{1,0:T(8,128)(2,1)S(1)}, u32[]{:S(2)}, u32[]{:S(2)}) collective-permute-start(bf16[32,2176]{1,0:T(8,128)(2,1)S(1)} %get-tuple-element.32), channel_id=1, source_target_pairs={{0,24},{8,0},{16,8},{24,16},{1,25},{9,1},{17,9},{25,17},{2,26},{10... | collective-permute-start | bytes 417800 | tf_op jit(solution)/shard_map/ppermute | solution.py:216
  13.3 30.2 %collective-permute-start.4 = (bf16[32,4096]{1,0:T(8,128)(2,1)S(1)}, bf16[32,4096]{1,0:T(8,128)(2,1)S(1)}, u32[]{:S(2)}, u32[]{:S(2)}) collective-permute-start(bf16[32,4096]{1,0:T(8,128)(2,1)S(1)} %get-tuple-element.39), channel_id=1, source_target_pairs={{0,16},{8,24},{16,0},{24,8},{1,17},{9,25},{17,1},{25,9},{2,18},{10... | collective-permute-start | bytes 786440 | tf_op jit(solution)/shard_map/ppermute | solution.py:216
  13.6 29.9 %collective-permute-start.5 = (bf16[32,4096]{1,0:T(8,128)(2,1)S(1)}, bf16[32,4096]{1,0:T(8,128)(2,1)S(1)}, u32[]{:S(2)}, u32[]{:S(2)}) collective-permute-start(bf16[32,4096]{1,0:T(8,128)(2,1)S(1)} %get-tuple-element.40), channel_id=1, source_target_pairs={{0,24},{8,0},{16,8},{24,16},{1,25},{9,1},{17,9},{25,17},{2,26},{10... | collective-permute-start | bytes 786440 | tf_op jit(solution)/shard_map/ppermute | solution.py:216
  14.8 1.0 copy-start.5
  27.6 17.7 %collective-permute-start.6 = (bf16[32,2048]{1,0:T(8,128)(2,1)S(1)}, bf16[32,2048]{1,0:T(8,128)(2,1)S(1)}, u32[]{:S(2)}, u32[]{:S(2)}) collective-permute-start(bf16[32,2048]{1,0:T(8,128)(2,1)S(1)} %get-tuple-element.43), channel_id=1, source_target_pairs={{0,8},{8,16},{16,24},{24,0},{1,9},{9,17},{17,25},{25,1},{2,10},{10... | collective-permute-start | bytes 393224 | tf_op jit(solution)/shard_map/ppermute | solution.py:216
  37.9 13.8 %collective-permute-start.7 = (bf16[32,2048]{1,0:T(8,128)(2,1)S(1)}, bf16[32,2048]{1,0:T(8,128)(2,1)S(1)}, u32[]{:S(2)}, u32[]{:S(2)}) collective-permute-start(bf16[32,2048]{1,0:T(8,128)(2,1)S(1)} %get-tuple-element.44), channel_id=1, source_target_pairs={{0,16},{8,24},{16,0},{24,8},{1,17},{9,25},{17,1},{25,9},{2,18},{10... | collective-permute-start | bytes 393224 | tf_op jit(solution)/shard_map/ppermute | solution.py:216
  41.3 10.4 %collective-permute-start.8 = (bf16[32,2048]{1,0:T(8,128)(2,1)S(1)}, bf16[32,2048]{1,0:T(8,128)(2,1)S(1)}, u32[]{:S(2)}, u32[]{:S(2)}) collective-permute-start(bf16[32,2048]{1,0:T(8,128)(2,1)S(1)} %get-tuple-element.45), channel_id=1, source_target_pairs={{0,24},{8,0},{16,8},{24,16},{1,25},{9,1},{17,9},{25,17},{2,26},{10... | collective-permute-start | bytes 393224 | tf_op jit(solution)/shard_map/ppermute | solution.py:216
  41.3 0.7 copy-start.10
  42.0 0.7 copy-start.11
  42.6 0.7 copy-start.12
  63.0 13.9 %collective-permute-start.11 = (bf16[64,2048]{1,0:T(8,128)(2,1)S(1)}, bf16[64,2048]{1,0:T(8,128)(2,1)S(1)}, u32[]{:S(2)}, u32[]{:S(2)}) collective-permute-start(bf16[64,2048]{1,0:T(8,128)(2,1)S(1)} %bitcast.10), channel_id=1, source_target_pairs={{0,16},{8,24},{16,0},{24,8},{1,17},{9,25},{17,1},{25,9},{2,18},{10... | collective-permute-start | bytes 786440 | tf_op jit(solution)/shard_map/ppermute | solution.py:268
  76.9 9.2 %collective-permute-start.12 = (bf16[64,2048]{1,0:T(8,128)(2,1)S(1)}, bf16[64,2048]{1,0:T(8,128)(2,1)S(1)}, u32[]{:S(2)}, u32[]{:S(2)}) collective-permute-start(bf16[64,2048]{1,0:T(8,128)(2,1)S(1)} %collective-permute-done.11.refs_1_), channel_id=1, source_target_pairs={{0,8},{8,0},{16,24},{24,16},{1,9},{9,1},{17,25},{25,17},{2,10},{10... | collective-permute-start | bytes 786440 | tf_op jit(solution)/shard_map/ppermute | solution.py:268
  77.2 14.5 %collective-permute-start.9 = (bf16[64,2048]{1,0:T(8,128)(2,1)S(1)}, bf16[64,2048]{1,0:T(8,128)(2,1)S(1)}, u32[]{:S(2)}, u32[]{:S(2)}) collective-permute-start(bf16[64,2048]{1,0:T(8,128)(2,1)S(1)} %bitcast.11), channel_id=1, source_target_pairs={{0,8},{8,0},{16,24},{24,16},{1,9},{9,1},{17,25},{25,17},{2,10},{10... | collective-permute-start | bytes 786440 | tf_op jit(solution)/shard_map/ppermute | solution.py:268
  87.5 22.8 %copy-start.6 = (f32[8,2048]{1,0:T(8,128)S(1)}, f32[8,2048]{1,0:T(8,128)}, u32[]{:S(2)}) copy-start(f32[8,2048]{1,0:T(8,128)} %bias_ref.5) | copy-start | bytes 196612
  87.5 9.8 %collective-permute-start.13 = (bf16[64,2048]{1,0:T(8,128)(2,1)S(1)}, bf16[64,2048]{1,0:T(8,128)(2,1)S(1)}, u32[]{:S(2)}, u32[]{:S(2)}) collective-permute-start(bf16[64,2048]{1,0:T(8,128)(2,1)S(1)} %get-tuple-element.49), channel_id=1, source_target_pairs={{0,8},{8,0},{16,24},{24,16},{1,9},{9,1},{17,25},{25,17},{2,10},{10... | collective-permute-start | bytes 786440 | tf_op jit(solution)/shard_map/ppermute | solution.py:268
  93.0 11.9 %collective-permute-start.10 = (bf16[64,2048]{1,0:T(8,128)(2,1)S(1)}, bf16[64,2048]{1,0:T(8,128)(2,1)S(1)}, u32[]{:S(2)}, u32[]{:S(2)}) collective-permute-start(bf16[64,2048]{1,0:T(8,128)(2,1)S(1)} %get-tuple-element.48), channel_id=1, source_target_pairs={{0,8},{8,0},{16,24},{24,16},{1,9},{9,1},{17,25},{25,17},{2,10},{10... | collective-permute-start | bytes 786440 | tf_op jit(solution)/shard_map/ppermute | solution.py:268
  97.3 13.0 %collective-permute-start.14 = (bf16[64,2048]{1,0:T(8,128)(2,1)S(1)}, bf16[64,2048]{1,0:T(8,128)(2,1)S(1)}, u32[]{:S(2)}, u32[]{:S(2)}) collective-permute-start(bf16[64,2048]{1,0:T(8,128)(2,1)S(1)} %shard_map.145), channel_id=1, source_target_pairs={{0,16},{8,24},{16,0},{24,8},{1,17},{9,25},{17,1},{25,9},{2,18},{10... | collective-permute-start | bytes 786440 | tf_op jit(solution)/shard_map/ppermute | solution.py:268

commit v4 on v3

v4 whole, which is shorter than its diff:
```python
import functools
import math

import jax
import jax.numpy as jnp
from jax import lax
from jax.experimental import pallas as pl
from jax.experimental.pallas import tpu as pltpu
from jax.sharding import PartitionSpec as P

HEAD_DIM = 128
ROUNDS = 4
LANES = 128

epsilon = 1e-05
mask_fill = -1e30

F32 = jnp.float32
BF16 = jnp.bfloat16

VMEM_BYTES = 32 * 1024 * 1024


def iota(shape, axis):
    return lax.broadcasted_iota(jnp.int32, shape, axis)


def one_hot(condition):
    return jnp.where(condition, 1.0, 0.0)


def across(row, rows):
    lanes = jnp.broadcast_to(row.astype(F32), (rows, row.shape[1]))
    return lanes, lanes.T


def call(body, out_shape, *operands, flops=0, vmem=VMEM_BYTES, **rest):
    moved = sum(x.size * x.dtype.itemsize for x in operands)
    moved += sum(x.size * x.dtype.itemsize for x in jax.tree.leaves(out_shape))
    return pl.pallas_call(
        body,
        out_shape=out_shape,
        compiler_params=pltpu.CompilerParams(vmem_limit_bytes=vmem),
        cost_estimate=pl.CostEstimate(flops=flops, bytes_accessed=moved, transcendentals=0),
        **rest,
    )(*operands)


def pack_kernel(pos_ref, *refs):
    parts = lax.axis_size("dp")
    count = len(refs) - parts
    x_refs, out_refs = refs[:count], refs[count:]
    tok = pos_ref.shape[1]
    share = tok // parts
    pos = lax.rem(pos_ref[...] + (parts - lax.axis_index("dp")) * tok, parts * tok)
    lanes, subl = across(pos, tok)
    rank = jnp.sum(one_hot(subl < lanes), axis=0, keepdims=True)
    order = one_hot(iota((tok, tok), 0).astype(F32) == rank).astype(BF16)

    def sort(x, at):
        rows = jnp.dot(order, x, preferred_element_type=F32).astype(BF16)
        for n, out_ref in enumerate(out_refs):
            out_ref[:, at : at + x.shape[1]] = rows[n * share : (n + 1) * share]

    at = 0
    for x_ref in x_refs:
        sort(x_ref[...], at)
        at += x_ref.shape[1]
    _, offset = across(lax.rem(pos, tok), tok)
    sort(offset.astype(BF16), at)


def joined(refs, columns=slice(None)):
    return jnp.concatenate([r[:, columns] for r in refs], axis=0)


def slots_of(ids_ref, cap, experts):
    tok = ids_ref.shape[1]
    first, first_t = across(ids_ref[0:1, :], tok)
    second, second_t = across(ids_ref[1:2, :], tok)
    earlier = iota((tok, tok), 0) < iota((tok, tok), 1)
    rank_first = jnp.sum(one_hot((first_t == first) & earlier), axis=0, keepdims=True)
    rank_second = jnp.sum(one_hot(first_t == second), axis=0, keepdims=True)
    rank_second += jnp.sum(one_hot((second_t == second) & earlier), axis=0, keepdims=True)

    def slot(expert, rank):
        return jnp.where((expert < experts) & (rank < cap), expert * cap + rank, -1.0)

    return slot(first[0:1, :], rank_first), slot(second[0:1, :], rank_second)


def slots_kernel(cap, experts, seg_ref, ids_ref, code_ref, own_ref, seg_q_ref, taken_ref, give_ref, kept_ref):
    kept_ref[...] = own_ref[...]
    tok = seg_ref.shape[1]
    _, seg_q_ref[...] = across(seg_ref[...], tok)
    slot_first, slot_second = slots_of(ids_ref, cap, experts)
    slot = iota((experts * cap, tok), 0).astype(F32)
    taken_ref[...] = one_hot((slot == slot_first) | (slot == slot_second)).astype(BF16)
    high = (code_ref[...] >> 8).astype(F32)
    low = (code_ref[...] & 255).astype(F32)

    def weights(code):
        return jnp.where(slot == slot_first, code[0:1, :], 0.0) + jnp.where(
            slot == slot_second, code[1:2, :], 0.0
        )

    both = jnp.concatenate([weights(high) / 256.0, weights(low) / 65536.0], axis=0)
    give_ref[...] = both.T.astype(BF16)


def place_kernel(first, seg_q_ref, *refs):
    *row_refs, place_ref, outside_ref = refs
    seg_q = seg_q_ref[...]
    offset = joined(row_refs, slice(first, first + LANES)).astype(F32).T
    place = offset == iota(offset.shape, 0).astype(F32)
    place_ref[...] = one_hot(place).astype(BF16)
    seg_k = jnp.sum(jnp.where(place, seg_q, 0.0), axis=0, keepdims=True)
    outside_ref[...] = one_hot(seg_q != seg_k)


def probs_kernel(place_ref, outside_ref, *refs):
    *row_refs, out_ref = refs
    width = out_ref.shape[0] * HEAD_DIM
    scale = 1.0 / math.sqrt(HEAD_DIM)
    outside = outside_ref[...] > 0.0
    for h in range(out_ref.shape[0]):
        lo = h * HEAD_DIM
        k = joined(row_refs, slice(lo, lo + HEAD_DIM))
        q = joined(row_refs, slice(width + lo, width + lo + HEAD_DIM))
        q = jnp.dot(place_ref[...], q, preferred_element_type=F32).astype(BF16)
        scores = lax.dot_general(q, k, (((1,), (1,)), ((), ())), preferred_element_type=F32)
        scores = jnp.where(outside, mask_fill, scores * scale)
        terms = jnp.exp(scores - jnp.max(scores, axis=1, keepdims=True))
        out_ref[h] = (terms / jnp.sum(terms, axis=1, keepdims=True)).astype(BF16)


def mix_kernel(probs_ref, *refs):
    *value_refs, out_ref = refs
    width = out_ref.shape[1]
    for h in range(probs_ref.shape[0]):
        lo = h * HEAD_DIM
        values = joined(value_refs, slice(2 * width + lo, 2 * width + lo + HEAD_DIM))
        out_ref[:, lo : lo + HEAD_DIM] = jnp.dot(probs_ref[h], values, preferred_element_type=F32)


def norm_kernel(place_ref, taken_ref, gain_ref, bias_ref, mixed_ref, *refs):
    *state_refs, hidden_ref, send_ref = refs
    hidden = mixed_ref[...] + jnp.dot(
        place_ref[...], joined(state_refs, slice(3 * mixed_ref.shape[1], 4 * mixed_ref.shape[1])), preferred_element_type=F32
    )
    hidden_ref[...] = hidden
    centered = hidden - jnp.mean(hidden, axis=1, keepdims=True)
    variance = jnp.mean(centered * centered, axis=1, keepdims=True)
    normed = (centered * lax.rsqrt(variance + epsilon) * gain_ref[...] + bias_ref[...]).astype(BF16)
    send_ref[...] = jnp.dot(taken_ref[...], normed, preferred_element_type=F32).astype(BF16)


def expert_kernel(count, bias_ref, w_in_ref, w_out_ref, *refs):
    x_refs, out_refs = refs[:count], refs[-count:]
    inner = jnp.dot(joined(x_refs), w_in_ref[0], preferred_element_type=F32)
    inner = jnp.maximum(inner + bias_ref[...], 0.0).astype(BF16)
    share = jnp.dot(inner, w_out_ref[0], preferred_element_type=F32).astype(BF16)
    at = 0
    for out_ref in out_refs:
        out_ref[...] = share[at : at + out_ref.shape[0]]
        at += out_ref.shape[0]


def add_kernel(first_ref, second_ref, out_ref):
    out_ref[...] = (first_ref[...].astype(F32) + second_ref[...].astype(F32)).astype(BF16)


def shares_of(refs, rows):
    shares, parts = [], []
    for ref in refs:
        parts.append(ref)
        if sum(p.shape[0] for p in parts) == rows:
            shares.append(joined(parts))
            parts = []
    return shares


def result_kernel(bias_ref, *refs):
    *share_refs, out_ref = refs
    total = 0.0
    for share in shares_of(share_refs, out_ref.shape[0]):
        total += share.astype(F32)
    row = lax.axis_index("expert") == iota(bias_ref.shape, 0)
    bias = jnp.sum(jnp.where(row, bias_ref[...], 0.0), axis=0, keepdims=True)
    out_ref[...] = (total + bias).astype(BF16)


def combine_kernel(results_ref, hidden_ref, give_ref, out_ref):
    result = jnp.concatenate([results_ref[...], results_ref[...]], axis=0)
    added = jnp.dot(give_ref[...], result, preferred_element_type=F32)
    out_ref[...] = (hidden_ref[...] + added).astype(BF16)


def per_device(
    pivot_states,
    queries,
    keys,
    values,
    pack_pos,
    segment_ids,
    expert_ids,
    gate_code,
    ln_gain,
    ln_bias,
    w_in,
    b_in,
    w_out,
    b_out,
):
    tok, width = pivot_states.shape
    dp = lax.axis_size("dp")
    experts = lax.axis_size("expert")
    cap = max(2, 2 * tok // (ROUNDS * experts))
    slots = experts * cap
    heads = width // HEAD_DIM
    packed = call(
        pack_kernel,
        (jax.ShapeDtypeStruct((tok // dp, 4 * width + LANES), BF16),) * dp,
        pack_pos.reshape(1, tok),
        keys,
        queries,
        values,
        pivot_states,
        vmem=62 * 1024 * 1024,
    )
    seg_q, taken, give, kept = call(
        functools.partial(slots_kernel, cap, experts),
        (
            jax.ShapeDtypeStruct((tok, tok), F32),
            jax.ShapeDtypeStruct((slots, tok), BF16),
            jax.ShapeDtypeStruct((tok, 2 * slots), BF16),
            jax.ShapeDtypeStruct(packed[0].shape, BF16),
        ),
        segment_ids,
        expert_ids.T,
        gate_code.T,
        packed[0],
    )
    rows = [kept]
    for n in range(1, dp):
        rows.append(lax.ppermute(packed[n], "dp", [(i, (i + n) % dp) for i in range(dp)]))
    place, outside = call(
        functools.partial(place_kernel, 4 * width),
        (jax.ShapeDtypeStruct((tok, tok), BF16), jax.ShapeDtypeStruct((tok, tok), F32)),
        seg_q,
        *rows,
    )
    probs = call(
        probs_kernel,
        jax.ShapeDtypeStruct((heads, tok, tok), BF16),
        place,
        outside,
        *rows,
    )
    mixed = call(mix_kernel, jax.ShapeDtypeStruct((tok, width), F32), probs, *rows)
    hidden_state, send = call(
        norm_kernel,
        (
            jax.ShapeDtypeStruct((tok, width), F32),
            jax.ShapeDtypeStruct((slots, width), BF16),
        ),
        place,
        taken,
        ln_gain.reshape(1, width),
        ln_bias.reshape(1, width),
        mixed,
        *rows,
    )

    def over_experts(x):
        x = x.reshape(experts, cap, width)
        return lax.all_to_all(x, "expert", split_axis=0, concat_axis=0, tiled=True).reshape(slots, width)

    def apply(rows, after=()):
        count = sum(x.shape[0] for x in rows)
        return call(
            functools.partial(expert_kernel, len(rows)),
            tuple(jax.ShapeDtypeStruct(x.shape, BF16) for x in rows),
            b_in,
            w_in,
            w_out,
            *rows,
            *after,
            flops=4 * count * width * w_in.shape[2],
        )

    def swap(x, distance):
        return lax.ppermute(x, "dp", [(i, i ^ distance) for i in range(dp)])

    own = over_experts(send)
    if dp == 4:
        half = slots // 2
        far = [swap(own[:half], 2), swap(own[half:], 2)]
        own_share, near_share = apply([own, swap(own, 1)])
        *corner_share, far_first, far_second = apply([swap(x, 1) for x in far] + far, after=[own_share])
        shares = [own_share, swap(near_share, 1)]
        for x, y in zip(corner_share, (far_first, far_second)):
            pair = call(add_kernel, jax.ShapeDtypeStruct((half, width), BF16), swap(x, 1), y)
            shares.append(swap(pair, 2))
    else:
        every = lax.all_gather(own, "dp", axis=0, tiled=True)
        (share,) = apply([every])
        parts = lax.all_to_all(
            share.reshape(dp, slots, width), "dp", split_axis=0, concat_axis=0, tiled=True
        )
        shares = [parts[n] for n in range(dp)]
    results = call(result_kernel, jax.ShapeDtypeStruct((slots, width), BF16), b_out, *shares)
    return call(
        combine_kernel,
        jax.ShapeDtypeStruct((tok, width), BF16),
        over_experts(results),
        hidden_state,
        give,
    )


def solution(mesh):
    return jax.shard_map(
        per_device,
        mesh=mesh,
        in_specs=(
            P(("dp", "expert"), None),
            P(("dp", "expert"), None),
            P(("dp", "expert"), None),
            P(("dp", "expert"), None),
            P(("dp", "expert")),
            P(("dp", "expert"), None),
            P(("dp", "expert"), None),
            P(("dp", "expert"), None),
            P(),
            P(),
            P("expert", None, "dp"),
            P("expert", "dp"),
            P("expert", "dp", None),
            P(),
        ),
        out_specs=P(("dp", "expert"), None),
        check_vma=False,
    )
```

time: 121 us -> 121 us (level)
  local copies, waits for them, and re-layouts: 6.2 us -> 3.1 us
  starting transfers between devices: 30.5 us -> 28 us
  waiting for transfers between devices: 55.3 us -> 57.7 us
  Pallas kernels: 8.22 us -> 10.6 us
    ppermute x9 -> x3, starting transfers between devices: 23.8 us -> 6.96 us  [per_device(): lax.ppermute(packed[n], 'dp', [(i, (i + n) % dp) for i in range(dp)])]
    ppermute x6 -> x10, starting transfers between devices: 6.71 us -> 21.1 us  [swap(): return lax.ppermute(x, 'dp', [(i, i ^ distance) for i in range(dp)])]
    ppermute x9 -> x3, waiting for transfers between devices: 17.5 us -> 30.1 us  [per_device(): lax.ppermute(packed[n], 'dp', [(i, (i + n) % dp) for i in range(dp)])]
    ppermute x6 -> x10, waiting for transfers between devices: 37.8 us -> 27.7 us  [swap(): return lax.ppermute(x, 'dp', [(i, i ^ distance) for i in range(dp)])]
    unnamed x26 -> x20, local copies, waits for them, and re-layouts: 6.2 us -> 3.09 us
    pallas_call x12, Pallas kernels: 8.22 us -> 10.6 us  [call(): pl.pallas_call(body, out_shape=out_shape, compiler_params=pltpu.CompilerP...]
  transfers between devices with their start and end apart: 15 -> 13, of which waited for: 8 -> 10; matrix products, arithmetic and copies ran while one was open for 0% -> 0% of each run, Pallas kernels for 5% -> 1%
where the time goes in v4:
time: 121 us
  waiting for transfers between devices  57.7 us (48%)
  starting transfers between devices  28 us (23%)
  blocking collectives  20.9 us (17%)
  Pallas kernels  10.6 us (9%)
  local copies, waits for them, and re-layouts  3.1 us (3%)
    ppermute x3, waiting for transfers between devices, per_device(): lax.ppermute(packed[n], 'dp', [(i, (i + n) % dp) for i in range(dp)])  30.1 us
    ppermute x10, waiting for transfers between devices, swap(): return lax.ppermute(x, 'dp', [(i, i ^ distance) for i in range(dp)])  27.7 us
    ppermute x10, starting transfers between devices, swap(): return lax.ppermute(x, 'dp', [(i, i ^ distance) for i in range(dp)])  21.1 us
    all_to_all x2, blocking collectives, over_experts(): lax.all_to_all(x, 'expert', split_axis=0, concat_axis=0, tiled=True)  20.9 us
    pallas_call x12, Pallas kernels, call(): pl.pallas_call(body, out_shape=out_shape, compiler_params=pltpu.CompilerP...  10.6 us
    ppermute x3, starting transfers between devices, per_device(): lax.ppermute(packed[n], 'dp', [(i, (i + n) % dp) for i in range(dp)])  6.96 us
    unnamed x20, local copies, waits for them, and re-layouts  3.09 us
  transfers between devices with their start and end apart: 13, of which 10 were waited for; matrix products, arithmetic and copies ran while one was open for 0% of the time, Pallas kernels for 1%

profile of v4, /device:TPU:0, one launch (start us, length us, event | category | flops | bytes accessed | tf_op | source)
XLA Modules:
  0.0 120.5 jit_solution(8953922859068924771)
XLA Ops:
  0.0 3.7 %shard_map.136 = (bf16[32,8320]{1,0:T(8,128)(2,1)}, bf16[32,8320]{1,0:T(8,128)(2,1)}, bf16[32,8320]{1,0:T(8,128)(2,1)}, bf16[32,8320]{1,0:T(8,128)(2,1)}) custom-call(s32[1,128]{1,0:T(1,128)} %bitcast.22, bf16[128,2048]{1,0:T(8,128)(2,1)} %refs_0_.1, bf16[128,2048]{1,0:T(8,128)(2,1)} %refs_1_.1, bf16[128,2048]{1,0:T(8,128)(2,1)} %refs_2_.1, ...), custom_call_target="tpu_custom_call" | custom-call | bytes 4227584 | tf_op jit(solution)/shard_map/pallas_call | solution.py:40
  3.7 3.0 %collective-permute-start = (bf16[32,8320]{1,0:T(8,128)(2,1)}, bf16[32,8320]{1,0:T(8,128)(2,1)S(1)}, u32[]{:S(2)}, u32[]{:S(2)}) collective-permute-start(bf16[32,8320]{1,0:T(8,128)(2,1)} %get-tuple-element.26), channel_id=1, source_target_pairs={{0,8},{8,16},{16,24},{24,0},{1,9},{9,17},{17,25},{25,1},{2,10},{10... | collective-permute-start | bytes 1597448 | tf_op jit(solution)/shard_map/ppermute | solution.py:246
  6.7 2.6 %collective-permute-start.1 = (bf16[32,8320]{1,0:T(8,128)(2,1)}, bf16[32,8320]{1,0:T(8,128)(2,1)S(1)}, u32[]{:S(2)}, u32[]{:S(2)}) collective-permute-start(bf16[32,8320]{1,0:T(8,128)(2,1)} %get-tuple-element.27), channel_id=1, source_target_pairs={{0,16},{8,24},{16,0},{24,8},{1,17},{9,25},{17,1},{25,9},{2,18},{10... | collective-permute-start | bytes 1597448 | tf_op jit(solution)/shard_map/ppermute | solution.py:246
  9.3 1.3 %collective-permute-start.2 = (bf16[32,8320]{1,0:T(8,128)(2,1)}, bf16[32,8320]{1,0:T(8,128)(2,1)S(1)}, u32[]{:S(2)}, u32[]{:S(2)}) collective-permute-start(bf16[32,8320]{1,0:T(8,128)(2,1)} %get-tuple-element.28), channel_id=1, source_target_pairs={{0,24},{8,0},{16,8},{24,16},{1,25},{9,1},{17,9},{25,17},{2,26},{10... | collective-permute-start | bytes 1597448 | tf_op jit(solution)/shard_map/ppermute | solution.py:246
  10.7 1.0 copy-done.2
  11.7 0.7 copy-done.7
  12.4 0.7 copy-done.8
  13.1 0.7 copy-done.9
  13.7 0.2 shard_map.137
  13.9 8.1 %collective-permute-done.refs_1_ = bf16[32,8320]{1,0:T(8,128)(2,1)S(1)} collective-permute-done((bf16[32,8320]{1,0:T(8,128)(2,1)}, bf16[32,8320]{1,0:T(8,128)(2,1)S(1)}, u32[]{:S(2)}, u32[]{:S(2)}) %collective-permute-start) | collective-permute-done | bytes 532512 | tf_op jit(solution)/shard_map/ppermute | solution.py:246
  22.0 22.0 %collective-permute-done.1.refs_2_ = bf16[32,8320]{1,0:T(8,128)(2,1)S(1)} collective-permute-done((bf16[32,8320]{1,0:T(8,128)(2,1)}, bf16[32,8320]{1,0:T(8,128)(2,1)S(1)}, u32[]{:S(2)}, u32[]{:S(2)}) %collective-permute-start.1) | collective-permute-done | bytes 532512 | tf_op jit(solution)/shard_map/ppermute | solution.py:246
  44.0 0.0 collective-permute-done.2.refs_3_
  44.0 0.1 shard_map.138
  44.1 0.0 copy-start.1
  44.2 1.5 %shard_map.139.probs_ref = bf16[16,128,128]{2,1,0:T(8,128)(2,1)S(1)} custom-call(bf16[128,128]{1,0:T(8,128)(2,1)S(1)} %get-tuple-element.29.place_ref, f32[128,128]{1,0:T(8,128)S(1)} %get-tuple-element.31.outside_ref, bf16[32,8320]{1,0:T(8,128)(2,1)S(1)} %get-tuple-element.25.refs_0_, bf16[32,8320]{1,0:T(8,128)(2,1)S(1)} %collective-permute-done.refs_1_, ...), custom_call_target="tpu_custom_call" | custom-call | bytes 2752512 | tf_op jit(solution)/shard_map/pallas_call | solution.py:40
  45.7 0.0 copy-start
  45.7 0.0 copy-start.4
  45.7 0.3 shard_map.140.mixed_ref
  46.0 0.0 copy-done.5
  46.0 0.0 copy-done.6
  46.0 0.8 shard_map.141
  46.8 10.6 %all_to_all.10 = bf16[8,8,2048]{2,1,0:T(8,128)(2,1)S(1)} all-to-all(bf16[8,8,2048]{2,1,0:T(8,128)(2,1)S(1)} %bitcast.17), channel_id=1, replica_groups=mesh['dp'=4,'expert'=8] {'expert'}, dimensions={0} | all-to-all | bytes 524288 | tf_op jit(solution)/shard_map/all_to_all | solution.py:277
  57.4 11.9 %collective-permute-start.3 = (bf16[64,2048]{1,0:T(8,128)(2,1)S(1)}, bf16[64,2048]{1,0:T(8,128)(2,1)S(1)}, u32[]{:S(2)}, u32[]{:S(2)}) collective-permute-start(bf16[64,2048]{1,0:T(8,128)(2,1)S(1)} %bitcast.13), channel_id=1, source_target_pairs={{0,8},{8,0},{16,24},{24,16},{1,9},{9,1},{17,25},{25,17},{2,10},{10... | collective-permute-start | bytes 786440 | tf_op jit(solution)/shard_map/ppermute | solution.py:293
  69.3 1.7 %collective-permute-start.7 = (bf16[32,2048]{1,0:T(8,128)(2,1)S(1)}, bf16[32,2048]{1,0:T(8,128)(2,1)S(1)}, u32[]{:S(2)}, u32[]{:S(2)}) collective-permute-start(bf16[32,2048]{1,0:T(8,128)(2,1)S(1)} %get-tuple-element.41), channel_id=1, source_target_pairs={{0,16},{8,24},{16,0},{24,8},{1,17},{9,25},{17,1},{25,9},{2,18},{10... | collective-permute-start | bytes 393224 | tf_op jit(solution)/shard_map/ppermute | solution.py:293
  71.0 1.3 %collective-permute-start.5 = (bf16[32,2048]{1,0:T(8,128)(2,1)S(1)}, bf16[32,2048]{1,0:T(8,128)(2,1)S(1)}, u32[]{:S(2)}, u32[]{:S(2)}) collective-permute-start(bf16[32,2048]{1,0:T(8,128)(2,1)S(1)} %get-tuple-element.42), channel_id=1, source_target_pairs={{0,16},{8,24},{16,0},{24,8},{1,17},{9,25},{17,1},{25,9},{2,18},{10... | collective-permute-start | bytes 393224 | tf_op jit(solution)/shard_map/ppermute | solution.py:293
  72.3 6.6 %collective-permute-done.7.refs_3_ = bf16[32,2048]{1,0:T(8,128)(2,1)S(1)} collective-permute-done((bf16[32,2048]{1,0:T(8,128)(2,1)S(1)}, bf16[32,2048]{1,0:T(8,128)(2,1)S(1)}, u32[]{:S(2)}, u32[]{:S(2)}) %collective-permute-start.7) | collective-permute-done | bytes 131104 | tf_op jit(solution)/shard_map/ppermute | solution.py:293
  78.9 1.9 %collective-permute-start.8 = (bf16[32,2048]{1,0:T(8,128)(2,1)S(1)}, bf16[32,2048]{1,0:T(8,128)(2,1)S(1)}, u32[]{:S(2)}, u32[]{:S(2)}) collective-permute-start(bf16[32,2048]{1,0:T(8,128)(2,1)S(1)} %collective-permute-done.7.refs_3_), channel_id=1, source_target_pairs={{0,8},{8,0},{16,24},{24,16},{1,9},{9,1},{17,25},{25,17},{2,10},{10... | collective-permute-start | bytes 393224 | tf_op jit(solution)/shard_map/ppermute | solution.py:293
  80.8 2.3 %collective-permute-done.5.refs_2_ = bf16[32,2048]{1,0:T(8,128)(2,1)S(1)} collective-permute-done((bf16[32,2048]{1,0:T(8,128)(2,1)S(1)}, bf16[32,2048]{1,0:T(8,128)(2,1)S(1)}, u32[]{:S(2)}, u32[]{:S(2)}) %collective-permute-start.5) | collective-permute-done | bytes 131104 | tf_op jit(solution)/shard_map/ppermute | solution.py:293
  83.1 0.2 collective-permute-start.6
  83.4 0.0 collective-permute-done.3.refs_1_
  83.4 0.0 copy-done.1
  83.4 1.3 %shard_map.142 = (bf16[64,2048]{1,0:T(8,128)(2,1)S(1)}, bf16[64,2048]{1,0:T(8,128)(2,1)S(1)}) custom-call(f32[1,1024]{1,0:T(1,128)S(1)} %copy-done.4, bf16[1,2048,1024]{2,1,0:T(8,128)(2,1)S(1)} %copy-done, bf16[1,1024,2048]{2,1,0:T(8,128)(2,1)S(1)} %copy-done.1, bf16[64,2048]{1,0:T(8,128)(2,1)S(1)} %bitcast.14, ...), custom_call_target="tpu_custom_call" | custom-call | flops 1073741824 | bytes 9441280 | tf_op jit(solution)/shard_map/pallas_call | solution.py:40
  84.7 0.5 collective-permute-done.8.refs_1_
  85.2 2.9 %collective-permute-done.6.refs_0_ = bf16[32,2048]{1,0:T(8,128)(2,1)S(1)} collective-permute-done((bf16[32,2048]{1,0:T(8,128)(2,1)S(1)}, bf16[32,2048]{1,0:T(8,128)(2,1)S(1)}, u32[]{:S(2)}, u32[]{:S(2)}) %collective-permute-start.6) | collective-permute-done | bytes 131104 | tf_op jit(solution)/shard_map/ppermute | solution.py:293
  88.1 1.4 %shard_map.143 = (bf16[32,2048]{1,0:T(8,128)(2,1)S(1)}, bf16[32,2048]{1,0:T(8,128)(2,1)S(1)}, bf16[32,2048]{1,0:T(8,128)(2,1)S(1)}, bf16[32,2048]{1,0:T(8,128)(2,1)S(1)}) custom-call(f32[1,1024]{1,0:T(1,128)S(1)} %copy-done.4, bf16[1,2048,1024]{2,1,0:T(8,128)(2,1)S(1)} %copy-done, bf16[1,1024,2048]{2,1,0:T(8,128)(2,1)S(1)} %copy-done.1, ...), custom_call_target="tpu_custom_call" | custom-call | flops 1073741824 | bytes 9703424 | tf_op jit(solution)/shard_map/pallas_call | solution.py:40
  89.5 0.3 collective-permute-start.9
  89.8 1.8 %collective-permute-start.11 = (bf16[32,2048]{1,0:T(8,128)(2,1)S(1)}, bf16[32,2048]{1,0:T(8,128)(2,1)S(1)}, u32[]{:S(2)}, u32[]{:S(2)}) collective-permute-start(bf16[32,2048]{1,0:T(8,128)(2,1)S(1)} %get-tuple-element.37), channel_id=1, source_target_pairs={{0,8},{8,0},{16,24},{24,16},{1,9},{9,1},{17,25},{25,17},{2,10},{10... | collective-permute-start | bytes 393224 | tf_op jit(solution)/shard_map/ppermute | solution.py:293
  91.6 0.2 collective-permute-start.4
  91.8 7.0 %collective-permute-done.9.first_ref = bf16[32,2048]{1,0:T(8,128)(2,1)S(1)} collective-permute-done((bf16[32,2048]{1,0:T(8,128)(2,1)S(1)}, bf16[32,2048]{1,0:T(8,128)(2,1)S(1)}, u32[]{:S(2)}, u32[]{:S(2)}) %collective-permute-start.9) | collective-permute-done | bytes 131104 | tf_op jit(solution)/shard_map/ppermute | solution.py:293
  98.8 0.1 collective-permute-start.10
  98.9 1.3 %collective-permute-done.11.first_ref = bf16[32,2048]{1,0:T(8,128)(2,1)S(1)} collective-permute-done((bf16[32,2048]{1,0:T(8,128)(2,1)S(1)}, bf16[32,2048]{1,0:T(8,128)(2,1)S(1)}, u32[]{:S(2)}, u32[]{:S(2)}) %collective-permute-start.11) | collective-permute-done | bytes 131104 | tf_op jit(solution)/shard_map/ppermute | solution.py:293
  100.2 1.7 %collective-permute-start.12 = (bf16[32,2048]{1,0:T(8,128)(2,1)S(1)}, bf16[32,2048]{1,0:T(8,128)(2,1)S(1)}, u32[]{:S(2)}, u32[]{:S(2)}) collective-permute-start(bf16[32,2048]{1,0:T(8,128)(2,1)S(1)} %shard_map.145), channel_id=1, source_target_pairs={{0,16},{8,24},{16,0},{24,8},{1,17},{9,25},{17,1},{25,9},{2,18},{10... | collective-permute-start | bytes 393224 | tf_op jit(solution)/shard_map/ppermute | solution.py:293
  101.9 5.6 %collective-permute-done.10.refs_2_ = bf16[32,2048]{1,0:T(8,128)(2,1)S(1)} collective-permute-done((bf16[32,2048]{1,0:T(8,128)(2,1)S(1)}, bf16[32,2048]{1,0:T(8,128)(2,1)S(1)}, u32[]{:S(2)}, u32[]{:S(2)}) %collective-permute-start.10) | collective-permute-done | bytes 131104 | tf_op jit(solution)/shard_map/ppermute | solution.py:293
  107.6 1.4 %collective-permute-done.12.refs_3_ = bf16[32,2048]{1,0:T(8,128)(2,1)S(1)} collective-permute-done((bf16[32,2048]{1,0:T(8,128)(2,1)S(1)}, bf16[32,2048]{1,0:T(8,128)(2,1)S(1)}, u32[]{:S(2)}, u32[]{:S(2)}) %collective-permute-start.12) | collective-permute-done | bytes 131104 | tf_op jit(solution)/shard_map/ppermute | solution.py:293
  109.0 0.0 collective-permute-done.4.refs_1_
  109.0 0.1 shard_map.146
  109.1 10.3 %all_to_all.11 = bf16[8,8,2048]{2,1,0:T(8,128)(2,1)S(1)} all-to-all(bf16[8,8,2048]{2,1,0:T(8,128)(2,1)S(1)} %bitcast.16), channel_id=1, replica_groups=mesh['dp'=4,'expert'=8] {'expert'}, dimensions={0} | all-to-all | bytes 524288 | tf_op jit(solution)/shard_map/all_to_all | solution.py:277
  119.4 1.1 shard_map.147
  (13 shorter events, 0.1 us)
Async XLA Ops:
  3.7 18.3 %collective-permute-start = (bf16[32,8320]{1,0:T(8,128)(2,1)}, bf16[32,8320]{1,0:T(8,128)(2,1)S(1)}, u32[]{:S(2)}, u32[]{:S(2)}) collective-permute-start(bf16[32,8320]{1,0:T(8,128)(2,1)} %get-tuple-element.26), channel_id=1, source_target_pairs={{0,8},{8,16},{16,24},{24,0},{1,9},{9,17},{17,25},{25,1},{2,10},{10... | collective-permute-start | bytes 1597448 | tf_op jit(solution)/shard_map/ppermute | solution.py:246
  6.7 37.3 %collective-permute-start.1 = (bf16[32,8320]{1,0:T(8,128)(2,1)}, bf16[32,8320]{1,0:T(8,128)(2,1)S(1)}, u32[]{:S(2)}, u32[]{:S(2)}) collective-permute-start(bf16[32,8320]{1,0:T(8,128)(2,1)} %get-tuple-element.27), channel_id=1, source_target_pairs={{0,16},{8,24},{16,0},{24,8},{1,17},{9,25},{17,1},{25,9},{2,18},{10... | collective-permute-start | bytes 1597448 | tf_op jit(solution)/shard_map/ppermute | solution.py:246
  9.3 34.7 %collective-permute-start.2 = (bf16[32,8320]{1,0:T(8,128)(2,1)}, bf16[32,8320]{1,0:T(8,128)(2,1)S(1)}, u32[]{:S(2)}, u32[]{:S(2)}) collective-permute-start(bf16[32,8320]{1,0:T(8,128)(2,1)} %get-tuple-element.28), channel_id=1, source_target_pairs={{0,24},{8,0},{16,8},{24,16},{1,25},{9,1},{17,9},{25,17},{2,26},{10... | collective-permute-start | bytes 1597448 | tf_op jit(solution)/shard_map/ppermute | solution.py:246
  10.7 1.0 copy-start.2
  11.7 0.7 copy-start.7
  12.4 0.7 copy-start.8
  13.1 0.7 copy-start.9
  44.0 2.0 %copy-start.5 = (f32[2048]{0:T(1024)S(1)}, f32[2048]{0:T(1024)}, u32[]{:S(2)}) copy-start(f32[2048]{0:T(1024)} %param.22) | copy-start | bytes 24580
  44.0 2.0 %copy-start.6 = (f32[2048]{0:T(1024)S(1)}, f32[2048]{0:T(1024)}, u32[]{:S(2)}) copy-start(f32[2048]{0:T(1024)} %param.23) | copy-start | bytes 24580
  44.1 39.2 %copy-start.1 = (bf16[1,1024,2048]{2,1,0:T(8,128)(2,1)S(1)}, bf16[1,1024,2048]{2,1,0:T(8,128)(2,1)}, u32[]{:S(2)}) copy-start(bf16[1,1024,2048]{2,1,0:T(8,128)(2,1)} %w_out_ref.3) | copy-start | bytes 12582916
  45.7 37.7 %copy-start = (bf16[1,2048,1024]{2,1,0:T(8,128)(2,1)S(1)}, bf16[1,2048,1024]{2,1,0:T(8,128)(2,1)}, u32[]{:S(2)}) copy-start(bf16[1,2048,1024]{2,1,0:T(8,128)(2,1)} %w_in_ref.3) | copy-start | bytes 12582916
  45.7 37.7 %copy-start.4 = (f32[1,1024]{1,0:T(1,128)S(1)}, f32[1,1024]{1,0:T(1,128)}, u32[]{:S(2)}) copy-start(f32[1,1024]{1,0:T(1,128)} %bias_ref.4) | copy-start | bytes 12292
  57.4 26.0 %collective-permute-start.3 = (bf16[64,2048]{1,0:T(8,128)(2,1)S(1)}, bf16[64,2048]{1,0:T(8,128)(2,1)S(1)}, u32[]{:S(2)}, u32[]{:S(2)}) collective-permute-start(bf16[64,2048]{1,0:T(8,128)(2,1)S(1)} %bitcast.13), channel_id=1, source_target_pairs={{0,8},{8,0},{16,24},{24,16},{1,9},{9,1},{17,25},{25,17},{2,10},{10... | collective-permute-start | bytes 786440 | tf_op jit(solution)/shard_map/ppermute | solution.py:293
  69.3 9.6 %collective-permute-start.7 = (bf16[32,2048]{1,0:T(8,128)(2,1)S(1)}, bf16[32,2048]{1,0:T(8,128)(2,1)S(1)}, u32[]{:S(2)}, u32[]{:S(2)}) collective-permute-start(bf16[32,2048]{1,0:T(8,128)(2,1)S(1)} %get-tuple-element.41), channel_id=1, source_target_pairs={{0,16},{8,24},{16,0},{24,8},{1,17},{9,25},{17,1},{25,9},{2,18},{10... | collective-permute-start | bytes 393224 | tf_op jit(solution)/shard_map/ppermute | solution.py:293
  71.0 12.2 %collective-permute-start.5 = (bf16[32,2048]{1,0:T(8,128)(2,1)S(1)}, bf16[32,2048]{1,0:T(8,128)(2,1)S(1)}, u32[]{:S(2)}, u32[]{:S(2)}) collective-permute-start(bf16[32,2048]{1,0:T(8,128)(2,1)S(1)} %get-tuple-element.42), channel_id=1, source_target_pairs={{0,16},{8,24},{16,0},{24,8},{1,17},{9,25},{17,1},{25,9},{2,18},{10... | collective-permute-start | bytes 393224 | tf_op jit(solution)/shard_map/ppermute | solution.py:293
  78.9 6.3 %collective-permute-start.8 = (bf16[32,2048]{1,0:T(8,128)(2,1)S(1)}, bf16[32,2048]{1,0:T(8,128)(2,1)S(1)}, u32[]{:S(2)}, u32[]{:S(2)}) collective-permute-start(bf16[32,2048]{1,0:T(8,128)(2,1)S(1)} %collective-permute-done.7.refs_3_), channel_id=1, source_target_pairs={{0,8},{8,0},{16,24},{24,16},{1,9},{9,1},{17,25},{25,17},{2,10},{10... | collective-permute-start | bytes 393224 | tf_op jit(solution)/shard_map/ppermute | solution.py:293
  83.1 5.0 %collective-permute-start.6 = (bf16[32,2048]{1,0:T(8,128)(2,1)S(1)}, bf16[32,2048]{1,0:T(8,128)(2,1)S(1)}, u32[]{:S(2)}, u32[]{:S(2)}) collective-permute-start(bf16[32,2048]{1,0:T(8,128)(2,1)S(1)} %collective-permute-done.5.refs_2_), channel_id=1, source_target_pairs={{0,8},{8,0},{16,24},{24,16},{1,9},{9,1},{17,25},{25,17},{2,10},{10... | collective-permute-start | bytes 393224 | tf_op jit(solution)/shard_map/ppermute | solution.py:293
  88.1 20.9 %copy-start.3 = (f32[8,2048]{1,0:T(8,128)S(1)}, f32[8,2048]{1,0:T(8,128)}, u32[]{:S(2)}) copy-start(f32[8,2048]{1,0:T(8,128)} %bias_ref.5) | copy-start | bytes 196612
  89.5 9.3 %collective-permute-start.9 = (bf16[32,2048]{1,0:T(8,128)(2,1)S(1)}, bf16[32,2048]{1,0:T(8,128)(2,1)S(1)}, u32[]{:S(2)}, u32[]{:S(2)}) collective-permute-start(bf16[32,2048]{1,0:T(8,128)(2,1)S(1)} %get-tuple-element.35), channel_id=1, source_target_pairs={{0,8},{8,0},{16,24},{24,16},{1,9},{9,1},{17,25},{25,17},{2,10},{10... | collective-permute-start | bytes 393224 | tf_op jit(solution)/shard_map/ppermute | solution.py:293
  89.8 10.4 %collective-permute-start.11 = (bf16[32,2048]{1,0:T(8,128)(2,1)S(1)}, bf16[32,2048]{1,0:T(8,128)(2,1)S(1)}, u32[]{:S(2)}, u32[]{:S(2)}) collective-permute-start(bf16[32,2048]{1,0:T(8,128)(2,1)S(1)} %get-tuple-element.37), channel_id=1, source_target_pairs={{0,8},{8,0},{16,24},{24,16},{1,9},{9,1},{17,25},{25,17},{2,10},{10... | collective-permute-start | bytes 393224 | tf_op jit(solution)/shard_map/ppermute | solution.py:293
  91.6 17.4 %collective-permute-start.4 = (bf16[64,2048]{1,0:T(8,128)(2,1)S(1)}, bf16[64,2048]{1,0:T(8,128)(2,1)S(1)}, u32[]{:S(2)}, u32[]{:S(2)}) collective-permute-start(bf16[64,2048]{1,0:T(8,128)(2,1)S(1)} %get-tuple-element.34), channel_id=1, source_target_pairs={{0,8},{8,0},{16,24},{24,16},{1,9},{9,1},{17,25},{25,17},{2,10},{10... | collective-permute-start | bytes 786440 | tf_op jit(solution)/shard_map/ppermute | solution.py:293
  98.8 8.7 %collective-permute-start.10 = (bf16[32,2048]{1,0:T(8,128)(2,1)S(1)}, bf16[32,2048]{1,0:T(8,128)(2,1)S(1)}, u32[]{:S(2)}, u32[]{:S(2)}) collective-permute-start(bf16[32,2048]{1,0:T(8,128)(2,1)S(1)} %shard_map.144), channel_id=1, source_target_pairs={{0,16},{8,24},{16,0},{24,8},{1,17},{9,25},{17,1},{25,9},{2,18},{10... | collective-permute-start | bytes 393224 | tf_op jit(solution)/shard_map/ppermute | solution.py:293
  100.2 8.7 %collective-permute-start.12 = (bf16[32,2048]{1,0:T(8,128)(2,1)S(1)}, bf16[32,2048]{1,0:T(8,128)(2,1)S(1)}, u32[]{:S(2)}, u32[]{:S(2)}) collective-permute-start(bf16[32,2048]{1,0:T(8,128)(2,1)S(1)} %shard_map.145), channel_id=1, source_target_pairs={{0,16},{8,24},{16,0},{24,8},{1,17},{9,25},{17,1},{25,9},{2,18},{10... | collective-permute-start | bytes 393224 | tf_op jit(solution)/shard_map/ppermute | solution.py:293

commit v5 on v4

--- a/solution.py
+++ b/solution.py
@@ -19,6 +19,7 @@
 BF16 = jnp.bfloat16
 
 VMEM_BYTES = 32 * 1024 * 1024
+PACK_BYTES = 62 * 1024 * 1024
 
 
 def iota(shape, axis):
@@ -46,28 +47,44 @@
     )(*operands)
 
 
-def pack_kernel(pos_ref, *refs):
-    parts = lax.axis_size("dp")
-    count = len(refs) - parts
-    x_refs, out_refs = refs[:count], refs[count:]
-    tok = pos_ref.shape[1]
-    share = tok // parts
-    pos = lax.rem(pos_ref[...] + (parts - lax.axis_index("dp")) * tok, parts * tok)
-    lanes, subl = across(pos, tok)
-    rank = jnp.sum(one_hot(subl < lanes), axis=0, keepdims=True)
-    order = one_hot(iota((tok, tok), 0).astype(F32) == rank).astype(BF16)
-
-    def sort(x, at):
+def pack_kernel(count, pos_ref, *refs):
+    keyed = pos_ref.dtype == jnp.int32
+    x_refs, order_ref, out_refs = refs[:count], refs[count], refs[count + 1 : -4]
+    in_buf, out_buf, in_sem, out_sem = refs[-4:]
+    parts, share, _ = out_buf.shape
+    tok, width = parts * share, in_buf.shape[2]
+    loads = [pltpu.make_async_copy(x, in_buf.at[i], in_sem.at[i]) for i, x in enumerate(x_refs)]
+    for load in loads:
+        load.start()
+    stores = []
+
+    def sort(x, i):
+        columns = slice(i * width, i * width + x.shape[1])
         rows = jnp.dot(order, x, preferred_element_type=F32).astype(BF16)
-        for n, out_ref in enumerate(out_refs):
-            out_ref[:, at : at + x.shape[1]] = rows[n * share : (n + 1) * share]
-
-    at = 0
-    for x_ref in x_refs:
-        sort(x_ref[...], at)
-        at += x_ref.shape[1]
-    _, offset = across(lax.rem(pos, tok), tok)
-    sort(offset.astype(BF16), at)
+        for n in range(parts):
+            out_buf[n, :, columns] = rows[n * share : (n + 1) * share]
+        for n in range(parts):
+            store = pltpu.make_async_copy(
+                out_buf.at[n, :, columns], out_refs[n].at[:, columns], out_sem.at[i, n]
+            )
+            store.start()
+            stores.append(store)
+
+    if keyed:
+        pos = lax.rem(pos_ref[...] + (parts - lax.axis_index("dp")) * tok, parts * tok)
+        lanes, subl = across(pos, tok)
+        rank = jnp.sum(one_hot(subl < lanes), axis=0, keepdims=True)
+        order = one_hot(iota((tok, tok), 0).astype(F32) == rank).astype(BF16)
+        _, offset = across(lax.rem(pos, tok), tok)
+        sort(offset.astype(BF16), count)
+    else:
+        order = pos_ref[...]
+    order_ref[...] = order
+    for i, load in enumerate(loads):
+        load.wait()
+        sort(in_buf[i], i)
+    for store in stores:
+        store.wait()
 
 
 def joined(refs, columns=slice(None)):
@@ -89,8 +106,10 @@
     return slot(first[0:1, :], rank_first), slot(second[0:1, :], rank_second)
 
 
-def slots_kernel(cap, experts, seg_ref, ids_ref, code_ref, own_ref, seg_q_ref, taken_ref, give_ref, kept_ref):
+def slots_kernel(cap, experts, seg_ref, ids_ref, code_ref, own_ref, own_states_ref, *refs):
+    seg_q_ref, taken_ref, give_ref, kept_ref, kept_states_ref = refs
     kept_ref[...] = own_ref[...]
+    kept_states_ref[...] = own_states_ref[...]
     tok = seg_ref.shape[1]
     _, seg_q_ref[...] = across(seg_ref[...], tok)
     slot_first, slot_second = slots_of(ids_ref, cap, experts)
@@ -146,7 +165,7 @@
 def norm_kernel(place_ref, taken_ref, gain_ref, bias_ref, mixed_ref, *refs):
     *state_refs, hidden_ref, send_ref = refs
     hidden = mixed_ref[...] + jnp.dot(
-        place_ref[...], joined(state_refs, slice(3 * mixed_ref.shape[1], 4 * mixed_ref.shape[1])), preferred_element_type=F32
+        place_ref[...], joined(state_refs), preferred_element_type=F32
     )
     hidden_ref[...] = hidden
     centered = hidden - jnp.mean(hidden, axis=1, keepdims=True)
@@ -218,34 +237,52 @@
     cap = max(2, 2 * tok // (ROUNDS * experts))
     slots = experts * cap
     heads = width // HEAD_DIM
-    packed = call(
-        pack_kernel,
-        (jax.ShapeDtypeStruct((tok // dp, 4 * width + LANES), BF16),) * dp,
-        pack_pos.reshape(1, tok),
-        keys,
-        queries,
-        values,
-        pivot_states,
-        vmem=62 * 1024 * 1024,
-    )
-    seg_q, taken, give, kept = call(
+    def pack(guide, *arrays):
+        wide = len(arrays) * width + (LANES if guide.dtype == jnp.int32 else 0)
+        vmem, hbm = pl.BlockSpec(memory_space=pltpu.VMEM), pl.BlockSpec(memory_space=pl.ANY)
+        return call(
+            functools.partial(pack_kernel, len(arrays)),
+            (jax.ShapeDtypeStruct((tok, tok), BF16),) + (jax.ShapeDtypeStruct((tok // dp, wide), BF16),) * dp,
+            guide,
+            *arrays,
+            vmem=PACK_BYTES,
+            in_specs=[vmem] + [hbm] * len(arrays),
+            out_specs=(vmem,) + (hbm,) * dp,
+            scratch_shapes=[
+                pltpu.VMEM((len(arrays), tok, width), BF16),
+                pltpu.VMEM((dp, tok // dp, wide), BF16),
+                pltpu.SemaphoreType.DMA((len(arrays),)),
+                pltpu.SemaphoreType.DMA((len(arrays) + 1, dp)),
+            ],
+        )
+
+    def spread(parts):
+        return [
+            lax.ppermute(part, "dp", [(i, (i + n) % dp) for i in range(dp)]) if n else part
+            for n, part in enumerate(parts)
+        ]
+
+    order, *packed = pack(pack_pos.reshape(1, tok), keys, queries, values)
+    _, *packed_states = pack(order, pivot_states)
+    seg_q, taken, give, kept, kept_states = call(
         functools.partial(slots_kernel, cap, experts),
         (
             jax.ShapeDtypeStruct((tok, tok), F32),
             jax.ShapeDtypeStruct((slots, tok), BF16),
             jax.ShapeDtypeStruct((tok, 2 * slots), BF16),
             jax.ShapeDtypeStruct(packed[0].shape, BF16),
+            jax.ShapeDtypeStruct(packed_states[0].shape, BF16),
         ),
         segment_ids,
         expert_ids.T,
         gate_code.T,
         packed[0],
-    )
-    rows = [kept]
-    for n in range(1, dp):
-        rows.append(lax.ppermute(packed[n], "dp", [(i, (i + n) % dp) for i in range(dp)]))
+        packed_states[0],
+    )
+    rows = [kept] + spread(packed)[1:]
+    states = [kept_states] + spread(packed_states)[1:]
     place, outside = call(
-        functools.partial(place_kernel, 4 * width),
+        functools.partial(place_kernel, 3 * width),
         (jax.ShapeDtypeStruct((tok, tok), BF16), jax.ShapeDtypeStruct((tok, tok), F32)),
         seg_q,
         *rows,
@@ -269,7 +306,7 @@
         ln_gain.reshape(1, width),
         ln_bias.reshape(1, width),
         mixed,
-        *rows,
+        *states,
     )
 
     def over_experts(x):

time: 121 us -> 119 us (0.983)
  starting transfers between devices: 28 us -> 21.5 us
  Pallas kernels: 10.6 us -> 14.5 us
    ppermute x10, starting transfers between devices: 21.1 us -> 11 us  [swap(): return lax.ppermute(x, 'dp', [(i, i ^ distance) for i in range(dp)])]
    pallas_call x12 -> x13, Pallas kernels: 10.6 us -> 14.5 us  [call(): pl.pallas_call(body, out_shape=out_shape, compiler_params=pltpu.CompilerP...]
    ppermute x3 -> x6, starting transfers between devices: 6.96 us -> 10.6 us  [spread(): lax.ppermute(part, 'dp', [(i, (i + n) % dp) for i in range(dp)])]
    ppermute x3 -> x6, waiting for transfers between devices: 30.1 us -> 28.8 us  [spread(): lax.ppermute(part, 'dp', [(i, (i + n) % dp) for i in range(dp)])]
    unnamed x20 -> x22, local copies, waits for them, and re-layouts: 3.09 us -> 3.95 us
  transfers between devices with their start and end apart: 13 -> 16, of which waited for: 10 -> 12; matrix products, arithmetic and copies ran while one was open for 0% -> 0% of each run, Pallas kernels for 1% -> 6%
where the time goes in v5:
time: 119 us
  waiting for transfers between devices  57.3 us (48%)
  starting transfers between devices  21.5 us (18%)
  blocking collectives  21.4 us (18%)
  Pallas kernels  14.5 us (12%)
  local copies, waits for them, and re-layouts  3.96 us (3%)
    ppermute x6, waiting for transfers between devices, spread(): lax.ppermute(part, 'dp', [(i, (i + n) % dp) for i in range(dp)])  28.8 us
    ppermute x10, waiting for transfers between devices, swap(): return lax.ppermute(x, 'dp', [(i, i ^ distance) for i in range(dp)])  28.5 us
    all_to_all x2, blocking collectives, over_experts(): lax.all_to_all(x, 'expert', split_axis=0, concat_axis=0, tiled=True)  21.4 us
    pallas_call x13, Pallas kernels, call(): pl.pallas_call(body, out_shape=out_shape, compiler_params=pltpu.CompilerP...  14.5 us
    ppermute x10, starting transfers between devices, swap(): return lax.ppermute(x, 'dp', [(i, i ^ distance) for i in range(dp)])  11 us
    ppermute x6, starting transfers between devices, spread(): lax.ppermute(part, 'dp', [(i, (i + n) % dp) for i in range(dp)])  10.6 us
    unnamed x22, local copies, waits for them, and re-layouts  3.95 us
  transfers between devices with their start and end apart: 16, of which 12 were waited for; matrix products, arithmetic and copies ran while one was open for 0% of the time, Pallas kernels for 6%

profile of v5, /device:TPU:0, one launch (start us, length us, event | category | flops | bytes accessed | tf_op | source)
XLA Modules:
  0.0 118.9 jit_solution(3862695140923390979)
XLA Ops:
  0.0 4.1 %shard_map.136 = (bf16[128,128]{1,0:T(8,128)(2,1)}, bf16[32,6272]{1,0:T(8,128)(2,1)}, bf16[32,6272]{1,0:T(8,128)(2,1)}, bf16[32,6272]{1,0:T(8,128)(2,1)}, bf16[32,6272]{1,0:T(8,128)(2,1)}) custom-call(s32[1,128]{1,0:T(1,128)} %bitcast.22, bf16[128,2048]{1,0:T(8,128)(2,1)} %refs_0_.2, bf16[128,2048]{1,0:T(8,128)(2,1)} %refs_1_.1, bf16[128,2048]{1,0:T(8,128)(2,1)} %refs_2_.1), custom_call_target="tpu_custom_call" | custom-call | bytes 3211776 | tf_op jit(solution)/shard_map/pallas_call | solution.py:41
  4.1 0.0 copy-start.6
  4.1 0.0 copy-start.7
  4.1 3.1 %collective-permute-start = (bf16[32,6272]{1,0:T(8,128)(2,1)}, bf16[32,6272]{1,0:T(8,128)(2,1)S(1)}, u32[]{:S(2)}, u32[]{:S(2)}) collective-permute-start(bf16[32,6272]{1,0:T(8,128)(2,1)} %get-tuple-element.34), channel_id=1, source_target_pairs={{0,8},{8,16},{16,24},{24,0},{1,9},{9,17},{17,25},{25,1},{2,10},{10... | collective-permute-start | bytes 1204232 | tf_op jit(solution)/shard_map/ppermute | solution.py:261
  7.2 2.6 %collective-permute-start.1 = (bf16[32,6272]{1,0:T(8,128)(2,1)}, bf16[32,6272]{1,0:T(8,128)(2,1)S(1)}, u32[]{:S(2)}, u32[]{:S(2)}) collective-permute-start(bf16[32,6272]{1,0:T(8,128)(2,1)} %get-tuple-element.35), channel_id=1, source_target_pairs={{0,16},{8,24},{16,0},{24,8},{1,17},{9,25},{17,1},{25,9},{2,18},{10... | collective-permute-start | bytes 1204232 | tf_op jit(solution)/shard_map/ppermute | solution.py:261
  9.8 1.3 %collective-permute-start.2 = (bf16[32,6272]{1,0:T(8,128)(2,1)}, bf16[32,6272]{1,0:T(8,128)(2,1)S(1)}, u32[]{:S(2)}, u32[]{:S(2)}) collective-permute-start(bf16[32,6272]{1,0:T(8,128)(2,1)} %get-tuple-element.36), channel_id=1, source_target_pairs={{0,24},{8,0},{16,8},{24,16},{1,25},{9,1},{17,9},{25,17},{2,26},{10... | collective-permute-start | bytes 1204232 | tf_op jit(solution)/shard_map/ppermute | solution.py:261
  11.2 3.5 %shard_map.137 = (bf16[128,128]{1,0:T(8,128)(2,1)}, bf16[32,2048]{1,0:T(8,128)(2,1)}, bf16[32,2048]{1,0:T(8,128)(2,1)}, bf16[32,2048]{1,0:T(8,128)(2,1)}, bf16[32,2048]{1,0:T(8,128)(2,1)}) custom-call(bf16[128,128]{1,0:T(8,128)(2,1)} %get-tuple-element.30.pos_ref, bf16[128,2048]{1,0:T(8,128)(2,1)} %refs_0_.3), custom_call_target="tpu_custom_call" | custom-call | bytes 1114112 | tf_op jit(solution)/shard_map/pallas_call | solution.py:41
  14.7 0.7 collective-permute-start.3
  15.4 0.3 collective-permute-start.4
  15.8 3.9 %collective-permute-done.refs_1_ = bf16[32,6272]{1,0:T(8,128)(2,1)S(1)} collective-permute-done((bf16[32,6272]{1,0:T(8,128)(2,1)}, bf16[32,6272]{1,0:T(8,128)(2,1)S(1)}, u32[]{:S(2)}, u32[]{:S(2)}) %collective-permute-start) | collective-permute-done | bytes 401440 | tf_op jit(solution)/shard_map/ppermute | solution.py:261
  19.7 2.5 %collective-permute-start.5 = (bf16[32,2048]{1,0:T(8,128)(2,1)}, bf16[32,2048]{1,0:T(8,128)(2,1)S(1)}, u32[]{:S(2)}, u32[]{:S(2)}) collective-permute-start(bf16[32,2048]{1,0:T(8,128)(2,1)} %get-tuple-element.43), channel_id=1, source_target_pairs={{0,24},{8,0},{16,8},{24,16},{1,25},{9,1},{17,9},{25,17},{2,26},{10... | collective-permute-start | bytes 393224 | tf_op jit(solution)/shard_map/ppermute | solution.py:261
  22.2 1.0 copy-done.2
  23.2 0.9 copy-done.3
  24.1 0.7 copy-done.8
  24.8 0.7 copy-done.9
  25.5 0.7 copy-done.10
  26.1 0.2 shard_map.138
  26.3 10.6 %collective-permute-done.1.refs_2_ = bf16[32,6272]{1,0:T(8,128)(2,1)S(1)} collective-permute-done((bf16[32,6272]{1,0:T(8,128)(2,1)}, bf16[32,6272]{1,0:T(8,128)(2,1)S(1)}, u32[]{:S(2)}, u32[]{:S(2)}) %collective-permute-start.1) | collective-permute-done | bytes 401440 | tf_op jit(solution)/shard_map/ppermute | solution.py:261
  37.0 0.1 shard_map.139
  37.1 1.5 %shard_map.140.probs_ref = bf16[16,128,128]{2,1,0:T(8,128)(2,1)S(1)} custom-call(bf16[128,128]{1,0:T(8,128)(2,1)S(1)} %get-tuple-element.37.place_ref, f32[128,128]{1,0:T(8,128)S(1)} %get-tuple-element.39.outside_ref, bf16[32,6272]{1,0:T(8,128)(2,1)S(1)} %get-tuple-element.33.refs_0_, bf16[32,6272]{1,0:T(8,128)(2,1)S(1)} %collective-permute-done.refs_1_, ...), custom_call_target="tpu_custom_call" | custom-call | bytes 2228224 | tf_op jit(solution)/shard_map/pallas_call | solution.py:41
  38.6 0.3 shard_map.141.mixed_ref
  38.9 0.8 collective-permute-done.3.refs_1_
  39.8 13.4 %collective-permute-done.4.refs_2_ = bf16[32,2048]{1,0:T(8,128)(2,1)S(1)} collective-permute-done((bf16[32,2048]{1,0:T(8,128)(2,1)}, bf16[32,2048]{1,0:T(8,128)(2,1)S(1)}, u32[]{:S(2)}, u32[]{:S(2)}) %collective-permute-start.4) | collective-permute-done | bytes 131104 | tf_op jit(solution)/shard_map/ppermute | solution.py:261
  53.2 0.8 shard_map.142
  54.0 10.4 %all_to_all.10 = bf16[8,8,2048]{2,1,0:T(8,128)(2,1)S(1)} all-to-all(bf16[8,8,2048]{2,1,0:T(8,128)(2,1)S(1)} %bitcast.17), channel_id=1, replica_groups=mesh['dp'=4,'expert'=8] {'expert'}, dimensions={0} | all-to-all | bytes 524288 | tf_op jit(solution)/shard_map/all_to_all | solution.py:314
  64.4 3.3 %collective-permute-start.6 = (bf16[64,2048]{1,0:T(8,128)(2,1)S(1)}, bf16[64,2048]{1,0:T(8,128)(2,1)S(1)}, u32[]{:S(2)}, u32[]{:S(2)}) collective-permute-start(bf16[64,2048]{1,0:T(8,128)(2,1)S(1)} %bitcast.13), channel_id=1, source_target_pairs={{0,8},{8,0},{16,24},{24,16},{1,9},{9,1},{17,25},{25,17},{2,10},{10... | collective-permute-start | bytes 786440 | tf_op jit(solution)/shard_map/ppermute | solution.py:330
  67.7 1.6 %collective-permute-start.10 = (bf16[32,2048]{1,0:T(8,128)(2,1)S(1)}, bf16[32,2048]{1,0:T(8,128)(2,1)S(1)}, u32[]{:S(2)}, u32[]{:S(2)}) collective-permute-start(bf16[32,2048]{1,0:T(8,128)(2,1)S(1)} %get-tuple-element.53), channel_id=1, source_target_pairs={{0,16},{8,24},{16,0},{24,8},{1,17},{9,25},{17,1},{25,9},{2,18},{10... | collective-permute-start | bytes 393224 | tf_op jit(solution)/shard_map/ppermute | solution.py:330
  69.3 1.4 %collective-permute-start.8 = (bf16[32,2048]{1,0:T(8,128)(2,1)S(1)}, bf16[32,2048]{1,0:T(8,128)(2,1)S(1)}, u32[]{:S(2)}, u32[]{:S(2)}) collective-permute-start(bf16[32,2048]{1,0:T(8,128)(2,1)S(1)} %get-tuple-element.54), channel_id=1, source_target_pairs={{0,16},{8,24},{16,0},{24,8},{1,17},{9,25},{17,1},{25,9},{2,18},{10... | collective-permute-start | bytes 393224 | tf_op jit(solution)/shard_map/ppermute | solution.py:330
  70.7 8.3 %collective-permute-done.10.refs_3_ = bf16[32,2048]{1,0:T(8,128)(2,1)S(1)} collective-permute-done((bf16[32,2048]{1,0:T(8,128)(2,1)S(1)}, bf16[32,2048]{1,0:T(8,128)(2,1)S(1)}, u32[]{:S(2)}, u32[]{:S(2)}) %collective-permute-start.10) | collective-permute-done | bytes 131104 | tf_op jit(solution)/shard_map/ppermute | solution.py:330
  79.0 0.2 collective-permute-start.11
  79.2 2.4 %collective-permute-done.8.refs_2_ = bf16[32,2048]{1,0:T(8,128)(2,1)S(1)} collective-permute-done((bf16[32,2048]{1,0:T(8,128)(2,1)S(1)}, bf16[32,2048]{1,0:T(8,128)(2,1)S(1)}, u32[]{:S(2)}, u32[]{:S(2)}) %collective-permute-start.8) | collective-permute-done | bytes 131104 | tf_op jit(solution)/shard_map/ppermute | solution.py:330
  81.5 0.1 collective-permute-start.9
  81.7 1.4 %shard_map.143 = (bf16[64,2048]{1,0:T(8,128)(2,1)S(1)}, bf16[64,2048]{1,0:T(8,128)(2,1)S(1)}) custom-call(f32[1,1024]{1,0:T(1,128)S(1)} %copy-done.5, bf16[1,2048,1024]{2,1,0:T(8,128)(2,1)S(1)} %copy-done, bf16[1,1024,2048]{2,1,0:T(8,128)(2,1)S(1)} %copy-done.1, bf16[64,2048]{1,0:T(8,128)(2,1)S(1)} %bitcast.14, ...), custom_call_target="tpu_custom_call" | custom-call | flops 1073741824 | bytes 9441280 | tf_op jit(solution)/shard_map/pallas_call | solution.py:41
  83.0 0.9 collective-permute-done.11.refs_1_
  83.9 2.6 %collective-permute-done.9.refs_0_ = bf16[32,2048]{1,0:T(8,128)(2,1)S(1)} collective-permute-done((bf16[32,2048]{1,0:T(8,128)(2,1)S(1)}, bf16[32,2048]{1,0:T(8,128)(2,1)S(1)}, u32[]{:S(2)}, u32[]{:S(2)}) %collective-permute-start.9) | collective-permute-done | bytes 131104 | tf_op jit(solution)/shard_map/ppermute | solution.py:330
  86.5 1.3 %shard_map.144 = (bf16[32,2048]{1,0:T(8,128)(2,1)S(1)}, bf16[32,2048]{1,0:T(8,128)(2,1)S(1)}, bf16[32,2048]{1,0:T(8,128)(2,1)S(1)}, bf16[32,2048]{1,0:T(8,128)(2,1)S(1)}) custom-call(f32[1,1024]{1,0:T(1,128)S(1)} %copy-done.5, bf16[1,2048,1024]{2,1,0:T(8,128)(2,1)S(1)} %copy-done, bf16[1,1024,2048]{2,1,0:T(8,128)(2,1)S(1)} %copy-done.1, ...), custom_call_target="tpu_custom_call" | custom-call | flops 1073741824 | bytes 9703424 | tf_op jit(solution)/shard_map/pallas_call | solution.py:41
  87.9 0.2 collective-permute-start.12
  88.0 1.9 %collective-permute-start.14 = (bf16[32,2048]{1,0:T(8,128)(2,1)S(1)}, bf16[32,2048]{1,0:T(8,128)(2,1)S(1)}, u32[]{:S(2)}, u32[]{:S(2)}) collective-permute-start(bf16[32,2048]{1,0:T(8,128)(2,1)S(1)} %get-tuple-element.49), channel_id=1, source_target_pairs={{0,8},{8,0},{16,24},{24,16},{1,9},{9,1},{17,25},{25,17},{2,10},{10... | collective-permute-start | bytes 393224 | tf_op jit(solution)/shard_map/ppermute | solution.py:330
  89.9 0.1 collective-permute-start.7
  90.1 6.5 %collective-permute-done.12.first_ref = bf16[32,2048]{1,0:T(8,128)(2,1)S(1)} collective-permute-done((bf16[32,2048]{1,0:T(8,128)(2,1)S(1)}, bf16[32,2048]{1,0:T(8,128)(2,1)S(1)}, u32[]{:S(2)}, u32[]{:S(2)}) %collective-permute-start.12) | collective-permute-done | bytes 131104 | tf_op jit(solution)/shard_map/ppermute | solution.py:330
  96.6 0.4 collective-permute-start.13
  97.0 0.9 collective-permute-done.14.first_ref
  98.0 1.7 %collective-permute-start.15 = (bf16[32,2048]{1,0:T(8,128)(2,1)S(1)}, bf16[32,2048]{1,0:T(8,128)(2,1)S(1)}, u32[]{:S(2)}, u32[]{:S(2)}) collective-permute-start(bf16[32,2048]{1,0:T(8,128)(2,1)S(1)} %shard_map.146), channel_id=1, source_target_pairs={{0,16},{8,24},{16,0},{24,8},{1,17},{9,25},{17,1},{25,9},{2,18},{10... | collective-permute-start | bytes 393224 | tf_op jit(solution)/shard_map/ppermute | solution.py:330
  99.7 5.6 %collective-permute-done.13.refs_2_ = bf16[32,2048]{1,0:T(8,128)(2,1)S(1)} collective-permute-done((bf16[32,2048]{1,0:T(8,128)(2,1)S(1)}, bf16[32,2048]{1,0:T(8,128)(2,1)S(1)}, u32[]{:S(2)}, u32[]{:S(2)}) %collective-permute-start.13) | collective-permute-done | bytes 131104 | tf_op jit(solution)/shard_map/ppermute | solution.py:330
  105.3 1.4 %collective-permute-done.15.refs_3_ = bf16[32,2048]{1,0:T(8,128)(2,1)S(1)} collective-permute-done((bf16[32,2048]{1,0:T(8,128)(2,1)S(1)}, bf16[32,2048]{1,0:T(8,128)(2,1)S(1)}, u32[]{:S(2)}, u32[]{:S(2)}) %collective-permute-start.15) | collective-permute-done | bytes 131104 | tf_op jit(solution)/shard_map/ppermute | solution.py:330
  106.7 0.1 shard_map.147
  106.8 10.9 %all_to_all.11 = bf16[8,8,2048]{2,1,0:T(8,128)(2,1)S(1)} all-to-all(bf16[8,8,2048]{2,1,0:T(8,128)(2,1)S(1)} %bitcast.16), channel_id=1, replica_groups=mesh['dp'=4,'expert'=8] {'expert'}, dimensions={0} | all-to-all | bytes 524288 | tf_op jit(solution)/shard_map/all_to_all | solution.py:314
  117.8 1.1 shard_map.148
  (22 shorter events, 0.1 us)
Async XLA Ops:
  4.1 49.0 %copy-start.6 = (f32[2048]{0:T(1024)S(1)}, f32[2048]{0:T(1024)}, u32[]{:S(2)}) copy-start(f32[2048]{0:T(1024)} %param.22) | copy-start | bytes 24580
  4.1 49.0 %copy-start.7 = (f32[2048]{0:T(1024)S(1)}, f32[2048]{0:T(1024)}, u32[]{:S(2)}) copy-start(f32[2048]{0:T(1024)} %param.23) | copy-start | bytes 24580
  4.1 15.6 %collective-permute-start = (bf16[32,6272]{1,0:T(8,128)(2,1)}, bf16[32,6272]{1,0:T(8,128)(2,1)S(1)}, u32[]{:S(2)}, u32[]{:S(2)}) collective-permute-start(bf16[32,6272]{1,0:T(8,128)(2,1)} %get-tuple-element.34), channel_id=1, source_target_pairs={{0,8},{8,16},{16,24},{24,0},{1,9},{9,17},{17,25},{25,1},{2,10},{10... | collective-permute-start | bytes 1204232 | tf_op jit(solution)/shard_map/ppermute | solution.py:261
  7.2 29.8 %collective-permute-start.1 = (bf16[32,6272]{1,0:T(8,128)(2,1)}, bf16[32,6272]{1,0:T(8,128)(2,1)S(1)}, u32[]{:S(2)}, u32[]{:S(2)}) collective-permute-start(bf16[32,6272]{1,0:T(8,128)(2,1)} %get-tuple-element.35), channel_id=1, source_target_pairs={{0,16},{8,24},{16,0},{24,8},{1,17},{9,25},{17,1},{25,9},{2,18},{10... | collective-permute-start | bytes 1204232 | tf_op jit(solution)/shard_map/ppermute | solution.py:261
  9.8 27.2 %collective-permute-start.2 = (bf16[32,6272]{1,0:T(8,128)(2,1)}, bf16[32,6272]{1,0:T(8,128)(2,1)S(1)}, u32[]{:S(2)}, u32[]{:S(2)}) collective-permute-start(bf16[32,6272]{1,0:T(8,128)(2,1)} %get-tuple-element.36), channel_id=1, source_target_pairs={{0,24},{8,0},{16,8},{24,16},{1,25},{9,1},{17,9},{25,17},{2,26},{10... | collective-permute-start | bytes 1204232 | tf_op jit(solution)/shard_map/ppermute | solution.py:261
  14.7 25.1 %collective-permute-start.3 = (bf16[32,2048]{1,0:T(8,128)(2,1)}, bf16[32,2048]{1,0:T(8,128)(2,1)S(1)}, u32[]{:S(2)}, u32[]{:S(2)}) collective-permute-start(bf16[32,2048]{1,0:T(8,128)(2,1)} %get-tuple-element.41), channel_id=1, source_target_pairs={{0,8},{8,16},{16,24},{24,0},{1,9},{9,17},{17,25},{25,1},{2,10},{10... | collective-permute-start | bytes 393224 | tf_op jit(solution)/shard_map/ppermute | solution.py:261
  15.4 37.7 %collective-permute-start.4 = (bf16[32,2048]{1,0:T(8,128)(2,1)}, bf16[32,2048]{1,0:T(8,128)(2,1)S(1)}, u32[]{:S(2)}, u32[]{:S(2)}) collective-permute-start(bf16[32,2048]{1,0:T(8,128)(2,1)} %get-tuple-element.42), channel_id=1, source_target_pairs={{0,16},{8,24},{16,0},{24,8},{1,17},{9,25},{17,1},{25,9},{2,18},{10... | collective-permute-start | bytes 393224 | tf_op jit(solution)/shard_map/ppermute | solution.py:261
  19.7 33.5 %collective-permute-start.5 = (bf16[32,2048]{1,0:T(8,128)(2,1)}, bf16[32,2048]{1,0:T(8,128)(2,1)S(1)}, u32[]{:S(2)}, u32[]{:S(2)}) collective-permute-start(bf16[32,2048]{1,0:T(8,128)(2,1)} %get-tuple-element.43), channel_id=1, source_target_pairs={{0,24},{8,0},{16,8},{24,16},{1,25},{9,1},{17,9},{25,17},{2,26},{10... | collective-permute-start | bytes 393224 | tf_op jit(solution)/shard_map/ppermute | solution.py:261
  22.2 1.0 copy-start.2
  23.2 0.9 copy-start.3
  24.1 0.7 copy-start.8
  24.8 0.7 copy-start.9
  25.5 0.7 copy-start.10
  37.0 44.7 %copy-start.1 = (bf16[1,1024,2048]{2,1,0:T(8,128)(2,1)S(1)}, bf16[1,1024,2048]{2,1,0:T(8,128)(2,1)}, u32[]{:S(2)}) copy-start(bf16[1,1024,2048]{2,1,0:T(8,128)(2,1)} %w_out_ref.3) | copy-start | bytes 12582916
  37.1 44.6 %copy-start = (bf16[1,2048,1024]{2,1,0:T(8,128)(2,1)S(1)}, bf16[1,2048,1024]{2,1,0:T(8,128)(2,1)}, u32[]{:S(2)}) copy-start(bf16[1,2048,1024]{2,1,0:T(8,128)(2,1)} %w_in_ref.3) | copy-start | bytes 12582916
  37.1 44.6 %copy-start.5 = (f32[1,1024]{1,0:T(1,128)S(1)}, f32[1,1024]{1,0:T(1,128)}, u32[]{:S(2)}) copy-start(f32[1,1024]{1,0:T(1,128)} %bias_ref.4) | copy-start | bytes 12292
  64.4 17.3 %collective-permute-start.6 = (bf16[64,2048]{1,0:T(8,128)(2,1)S(1)}, bf16[64,2048]{1,0:T(8,128)(2,1)S(1)}, u32[]{:S(2)}, u32[]{:S(2)}) collective-permute-start(bf16[64,2048]{1,0:T(8,128)(2,1)S(1)} %bitcast.13), channel_id=1, source_target_pairs={{0,8},{8,0},{16,24},{24,16},{1,9},{9,1},{17,25},{25,17},{2,10},{10... | collective-permute-start | bytes 786440 | tf_op jit(solution)/shard_map/ppermute | solution.py:330
  67.7 11.3 %collective-permute-start.10 = (bf16[32,2048]{1,0:T(8,128)(2,1)S(1)}, bf16[32,2048]{1,0:T(8,128)(2,1)S(1)}, u32[]{:S(2)}, u32[]{:S(2)}) collective-permute-start(bf16[32,2048]{1,0:T(8,128)(2,1)S(1)} %get-tuple-element.53), channel_id=1, source_target_pairs={{0,16},{8,24},{16,0},{24,8},{1,17},{9,25},{17,1},{25,9},{2,18},{10... | collective-permute-start | bytes 393224 | tf_op jit(solution)/shard_map/ppermute | solution.py:330
  69.3 12.2 %collective-permute-start.8 = (bf16[32,2048]{1,0:T(8,128)(2,1)S(1)}, bf16[32,2048]{1,0:T(8,128)(2,1)S(1)}, u32[]{:S(2)}, u32[]{:S(2)}) collective-permute-start(bf16[32,2048]{1,0:T(8,128)(2,1)S(1)} %get-tuple-element.54), channel_id=1, source_target_pairs={{0,16},{8,24},{16,0},{24,8},{1,17},{9,25},{17,1},{25,9},{2,18},{10... | collective-permute-start | bytes 393224 | tf_op jit(solution)/shard_map/ppermute | solution.py:330
  79.0 5.0 %collective-permute-start.11 = (bf16[32,2048]{1,0:T(8,128)(2,1)S(1)}, bf16[32,2048]{1,0:T(8,128)(2,1)S(1)}, u32[]{:S(2)}, u32[]{:S(2)}) collective-permute-start(bf16[32,2048]{1,0:T(8,128)(2,1)S(1)} %collective-permute-done.10.refs_3_), channel_id=1, source_target_pairs={{0,8},{8,0},{16,24},{24,16},{1,9},{9,1},{17,25},{25,17},{2,10},{10... | collective-permute-start | bytes 393224 | tf_op jit(solution)/shard_map/ppermute | solution.py:330
  81.5 5.0 %collective-permute-start.9 = (bf16[32,2048]{1,0:T(8,128)(2,1)S(1)}, bf16[32,2048]{1,0:T(8,128)(2,1)S(1)}, u32[]{:S(2)}, u32[]{:S(2)}) collective-permute-start(bf16[32,2048]{1,0:T(8,128)(2,1)S(1)} %collective-permute-done.8.refs_2_), channel_id=1, source_target_pairs={{0,8},{8,0},{16,24},{24,16},{1,9},{9,1},{17,25},{25,17},{2,10},{10... | collective-permute-start | bytes 393224 | tf_op jit(solution)/shard_map/ppermute | solution.py:330
  86.5 20.2 %copy-start.4 = (f32[8,2048]{1,0:T(8,128)S(1)}, f32[8,2048]{1,0:T(8,128)}, u32[]{:S(2)}) copy-start(f32[8,2048]{1,0:T(8,128)} %bias_ref.5) | copy-start | bytes 196612
  87.9 8.7 %collective-permute-start.12 = (bf16[32,2048]{1,0:T(8,128)(2,1)S(1)}, bf16[32,2048]{1,0:T(8,128)(2,1)S(1)}, u32[]{:S(2)}, u32[]{:S(2)}) collective-permute-start(bf16[32,2048]{1,0:T(8,128)(2,1)S(1)} %get-tuple-element.47), channel_id=1, source_target_pairs={{0,8},{8,0},{16,24},{24,16},{1,9},{9,1},{17,25},{25,17},{2,10},{10... | collective-permute-start | bytes 393224 | tf_op jit(solution)/shard_map/ppermute | solution.py:330
  88.0 9.9 %collective-permute-start.14 = (bf16[32,2048]{1,0:T(8,128)(2,1)S(1)}, bf16[32,2048]{1,0:T(8,128)(2,1)S(1)}, u32[]{:S(2)}, u32[]{:S(2)}) collective-permute-start(bf16[32,2048]{1,0:T(8,128)(2,1)S(1)} %get-tuple-element.49), channel_id=1, source_target_pairs={{0,8},{8,0},{16,24},{24,16},{1,9},{9,1},{17,25},{25,17},{2,10},{10... | collective-permute-start | bytes 393224 | tf_op jit(solution)/shard_map/ppermute | solution.py:330
  89.9 16.8 %collective-permute-start.7 = (bf16[64,2048]{1,0:T(8,128)(2,1)S(1)}, bf16[64,2048]{1,0:T(8,128)(2,1)S(1)}, u32[]{:S(2)}, u32[]{:S(2)}) collective-permute-start(bf16[64,2048]{1,0:T(8,128)(2,1)S(1)} %get-tuple-element.46), channel_id=1, source_target_pairs={{0,8},{8,0},{16,24},{24,16},{1,9},{9,1},{17,25},{25,17},{2,10},{10... | collective-permute-start | bytes 786440 | tf_op jit(solution)/shard_map/ppermute | solution.py:330
  96.6 8.7 %collective-permute-start.13 = (bf16[32,2048]{1,0:T(8,128)(2,1)S(1)}, bf16[32,2048]{1,0:T(8,128)(2,1)S(1)}, u32[]{:S(2)}, u32[]{:S(2)}) collective-permute-start(bf16[32,2048]{1,0:T(8,128)(2,1)S(1)} %shard_map.145), channel_id=1, source_target_pairs={{0,16},{8,24},{16,0},{24,8},{1,17},{9,25},{17,1},{25,9},{2,18},{10... | collective-permute-start | bytes 393224 | tf_op jit(solution)/shard_map/ppermute | solution.py:330
  98.0 8.7 %collective-permute-start.15 = (bf16[32,2048]{1,0:T(8,128)(2,1)S(1)}, bf16[32,2048]{1,0:T(8,128)(2,1)S(1)}, u32[]{:S(2)}, u32[]{:S(2)}) collective-permute-start(bf16[32,2048]{1,0:T(8,128)(2,1)S(1)} %shard_map.146), channel_id=1, source_target_pairs={{0,16},{8,24},{16,0},{24,8},{1,17},{9,25},{17,1},{25,9},{2,18},{10... | collective-permute-start | bytes 393224 | tf_op jit(solution)/shard_map/ppermute | solution.py:330

commit v6 on v4

--- a/solution.py
+++ b/solution.py
@@ -19,6 +19,7 @@
 BF16 = jnp.bfloat16
 
 VMEM_BYTES = 32 * 1024 * 1024
+PACK_BYTES = 62 * 1024 * 1024
 
 
 def iota(shape, axis):
@@ -34,7 +35,7 @@
     return lanes, lanes.T
 
 
-def call(body, out_shape, *operands, flops=0, vmem=VMEM_BYTES, **rest):
+def call(body, out_shape, *operands, flops=0, vmem=VMEM_BYTES):
     moved = sum(x.size * x.dtype.itemsize for x in operands)
     moved += sum(x.size * x.dtype.itemsize for x in jax.tree.leaves(out_shape))
     return pl.pallas_call(
@@ -42,32 +43,35 @@
         out_shape=out_shape,
         compiler_params=pltpu.CompilerParams(vmem_limit_bytes=vmem),
         cost_estimate=pl.CostEstimate(flops=flops, bytes_accessed=moved, transcendentals=0),
-        **rest,
     )(*operands)
 
 
 def pack_kernel(pos_ref, *refs):
     parts = lax.axis_size("dp")
-    count = len(refs) - parts
-    x_refs, out_refs = refs[:count], refs[count:]
-    tok = pos_ref.shape[1]
+    *x_refs, order_ref = refs[: len(refs) - parts]
+    out_refs = refs[len(refs) - parts :]
+    tok = order_ref.shape[0]
     share = tok // parts
-    pos = lax.rem(pos_ref[...] + (parts - lax.axis_index("dp")) * tok, parts * tok)
-    lanes, subl = across(pos, tok)
-    rank = jnp.sum(one_hot(subl < lanes), axis=0, keepdims=True)
-    order = one_hot(iota((tok, tok), 0).astype(F32) == rank).astype(BF16)
 
     def sort(x, at):
         rows = jnp.dot(order, x, preferred_element_type=F32).astype(BF16)
         for n, out_ref in enumerate(out_refs):
             out_ref[:, at : at + x.shape[1]] = rows[n * share : (n + 1) * share]
 
+    if pos_ref.dtype == jnp.int32:
+        pos = lax.rem(pos_ref[...] + (parts - lax.axis_index("dp")) * tok, parts * tok)
+        lanes, subl = across(pos, tok)
+        rank = jnp.sum(one_hot(subl < lanes), axis=0, keepdims=True)
+        order = one_hot(iota((tok, tok), 0).astype(F32) == rank).astype(BF16)
+        _, offset = across(lax.rem(pos, tok), tok)
+        sort(offset.astype(BF16), sum(x.shape[1] for x in x_refs))
+    else:
+        order = pos_ref[...]
+    order_ref[...] = order
     at = 0
     for x_ref in x_refs:
         sort(x_ref[...], at)
         at += x_ref.shape[1]
-    _, offset = across(lax.rem(pos, tok), tok)
-    sort(offset.astype(BF16), at)
 
 
 def joined(refs, columns=slice(None)):
@@ -89,8 +93,10 @@
     return slot(first[0:1, :], rank_first), slot(second[0:1, :], rank_second)
 
 
-def slots_kernel(cap, experts, seg_ref, ids_ref, code_ref, own_ref, seg_q_ref, taken_ref, give_ref, kept_ref):
+def slots_kernel(cap, experts, seg_ref, ids_ref, code_ref, own_ref, own_later_ref, *refs):
+    seg_q_ref, taken_ref, give_ref, kept_ref, kept_later_ref = refs
     kept_ref[...] = own_ref[...]
+    kept_later_ref[...] = own_later_ref[...]
     tok = seg_ref.shape[1]
     _, seg_q_ref[...] = across(seg_ref[...], tok)
     slot_first, slot_second = slots_of(ids_ref, cap, experts)
@@ -139,14 +145,14 @@
     width = out_ref.shape[1]
     for h in range(probs_ref.shape[0]):
         lo = h * HEAD_DIM
-        values = joined(value_refs, slice(2 * width + lo, 2 * width + lo + HEAD_DIM))
+        values = joined(value_refs, slice(lo, lo + HEAD_DIM))
         out_ref[:, lo : lo + HEAD_DIM] = jnp.dot(probs_ref[h], values, preferred_element_type=F32)
 
 
 def norm_kernel(place_ref, taken_ref, gain_ref, bias_ref, mixed_ref, *refs):
     *state_refs, hidden_ref, send_ref = refs
     hidden = mixed_ref[...] + jnp.dot(
-        place_ref[...], joined(state_refs, slice(3 * mixed_ref.shape[1], 4 * mixed_ref.shape[1])), preferred_element_type=F32
+        place_ref[...], joined(state_refs, slice(mixed_ref.shape[1], None)), preferred_element_type=F32
     )
     hidden_ref[...] = hidden
     centered = hidden - jnp.mean(hidden, axis=1, keepdims=True)
@@ -218,34 +224,43 @@
     cap = max(2, 2 * tok // (ROUNDS * experts))
     slots = experts * cap
     heads = width // HEAD_DIM
-    packed = call(
-        pack_kernel,
-        (jax.ShapeDtypeStruct((tok // dp, 4 * width + LANES), BF16),) * dp,
-        pack_pos.reshape(1, tok),
-        keys,
-        queries,
-        values,
-        pivot_states,
-        vmem=62 * 1024 * 1024,
-    )
-    seg_q, taken, give, kept = call(
+    def pack(guide, *arrays):
+        wide = len(arrays) * width + (LANES if guide.dtype == jnp.int32 else 0)
+        return call(
+            pack_kernel,
+            (jax.ShapeDtypeStruct((tok, tok), BF16),) + (jax.ShapeDtypeStruct((tok // dp, wide), BF16),) * dp,
+            guide,
+            *arrays,
+            vmem=PACK_BYTES,
+        )
+
+    def spread(parts):
+        return [
+            lax.ppermute(part, "dp", [(i, (i + n) % dp) for i in range(dp)]) if n else part
+            for n, part in enumerate(parts)
+        ]
+
+    order, *packed = pack(pack_pos.reshape(1, tok), keys, queries)
+    _, *packed_later = pack(order, values, pivot_states)
+    seg_q, taken, give, kept, kept_later = call(
         functools.partial(slots_kernel, cap, experts),
         (
             jax.ShapeDtypeStruct((tok, tok), F32),
             jax.ShapeDtypeStruct((slots, tok), BF16),
             jax.ShapeDtypeStruct((tok, 2 * slots), BF16),
             jax.ShapeDtypeStruct(packed[0].shape, BF16),
+            jax.ShapeDtypeStruct(packed_later[0].shape, BF16),
         ),
         segment_ids,
         expert_ids.T,
         gate_code.T,
         packed[0],
-    )
-    rows = [kept]
-    for n in range(1, dp):
-        rows.append(lax.ppermute(packed[n], "dp", [(i, (i + n) % dp) for i in range(dp)]))
+        packed_later[0],
+    )
+    rows = [kept] + spread(packed)[1:]
+    later = [kept_later] + spread(packed_later)[1:]
     place, outside = call(
-        functools.partial(place_kernel, 4 * width),
+        functools.partial(place_kernel, 2 * width),
         (jax.ShapeDtypeStruct((tok, tok), BF16), jax.ShapeDtypeStruct((tok, tok), F32)),
         seg_q,
         *rows,
@@ -257,7 +272,7 @@
         outside,
         *rows,
     )
-    mixed = call(mix_kernel, jax.ShapeDtypeStruct((tok, width), F32), probs, *rows)
+    mixed = call(mix_kernel, jax.ShapeDtypeStruct((tok, width), F32), probs, *later)
     hidden_state, send = call(
         norm_kernel,
         (
@@ -269,7 +284,7 @@
         ln_gain.reshape(1, width),
         ln_bias.reshape(1, width),
         mixed,
-        *rows,
+        *later,
     )
 
     def over_experts(x):

time: 121 us -> 118 us (0.975)
  waiting for transfers between devices: 57.7 us -> 55 us
  starting transfers between devices: 28 us -> 25.7 us
  Pallas kernels: 10.6 us -> 12.2 us
    ppermute x10, starting transfers between devices: 21.1 us -> 15.3 us  [swap(): return lax.ppermute(x, 'dp', [(i, i ^ distance) for i in range(dp)])]
    ppermute x3 -> x6, starting transfers between devices: 6.96 us -> 10.5 us  [spread(): lax.ppermute(part, 'dp', [(i, (i + n) % dp) for i in range(dp)])]
    ppermute x3 -> x6, waiting for transfers between devices: 30.1 us -> 27.3 us  [spread(): lax.ppermute(part, 'dp', [(i, (i + n) % dp) for i in range(dp)])]
    pallas_call x12 -> x13, Pallas kernels: 10.6 us -> 12.2 us  [call(): pl.pallas_call(body, out_shape=out_shape, compiler_params=pltpu.CompilerP...]
    unnamed x20 -> x22, local copies, waits for them, and re-layouts: 3.09 us -> 3.94 us
  transfers between devices with their start and end apart: 13 -> 16, of which waited for: 10 -> 12; matrix products, arithmetic and copies ran while one was open for 0% -> 0% of each run, Pallas kernels for 1% -> 5%
where the time goes in v6:
time: 118 us
  waiting for transfers between devices  55 us (47%)
  starting transfers between devices  25.7 us (22%)
  blocking collectives  20.8 us (18%)
  Pallas kernels  12.2 us (10%)
  local copies, waits for them, and re-layouts  3.95 us (3%)
    ppermute x10, waiting for transfers between devices, swap(): return lax.ppermute(x, 'dp', [(i, i ^ distance) for i in range(dp)])  27.6 us
    ppermute x6, waiting for transfers between devices, spread(): lax.ppermute(part, 'dp', [(i, (i + n) % dp) for i in range(dp)])  27.3 us
    all_to_all x2, blocking collectives, over_experts(): lax.all_to_all(x, 'expert', split_axis=0, concat_axis=0, tiled=True)  20.8 us
    ppermute x10, starting transfers between devices, swap(): return lax.ppermute(x, 'dp', [(i, i ^ distance) for i in range(dp)])  15.3 us
    pallas_call x13, Pallas kernels, call(): pl.pallas_call(body, out_shape=out_shape, compiler_params=pltpu.CompilerP...  12.2 us
    ppermute x6, starting transfers between devices, spread(): lax.ppermute(part, 'dp', [(i, (i + n) % dp) for i in range(dp)])  10.5 us
    unnamed x22, local copies, waits for them, and re-layouts  3.94 us
  transfers between devices with their start and end apart: 16, of which 12 were waited for; matrix products, arithmetic and copies ran while one was open for 0% of the time, Pallas kernels for 5%

profile of v6, /device:TPU:0, one launch (start us, length us, event | category | flops | bytes accessed | tf_op | source)
XLA Modules:
  0.0 117.8 jit_solution(3874338491448141613)
XLA Ops:
  0.0 2.7 %shard_map.136 = (bf16[128,128]{1,0:T(8,128)(2,1)}, bf16[32,4224]{1,0:T(8,128)(2,1)}, bf16[32,4224]{1,0:T(8,128)(2,1)}, bf16[32,4224]{1,0:T(8,128)(2,1)}, bf16[32,4224]{1,0:T(8,128)(2,1)}) custom-call(s32[1,128]{1,0:T(1,128)} %bitcast.22, bf16[128,2048]{1,0:T(8,128)(2,1)} %refs_0_.2, bf16[128,2048]{1,0:T(8,128)(2,1)} %refs_1_.2), custom_call_target="tpu_custom_call" | custom-call | bytes 2163200 | tf_op jit(solution)/shard_map/pallas_call | solution.py:41
  2.8 3.0 %collective-permute-start = (bf16[32,4224]{1,0:T(8,128)(2,1)}, bf16[32,4224]{1,0:T(8,128)(2,1)S(1)}, u32[]{:S(2)}, u32[]{:S(2)}) collective-permute-start(bf16[32,4224]{1,0:T(8,128)(2,1)} %get-tuple-element.34), channel_id=1, source_target_pairs={{0,8},{8,16},{16,24},{24,0},{1,9},{9,17},{17,25},{25,1},{2,10},{10... | collective-permute-start | bytes 811016 | tf_op jit(solution)/shard_map/ppermute | solution.py:239
  5.8 2.6 %collective-permute-start.1 = (bf16[32,4224]{1,0:T(8,128)(2,1)}, bf16[32,4224]{1,0:T(8,128)(2,1)S(1)}, u32[]{:S(2)}, u32[]{:S(2)}) collective-permute-start(bf16[32,4224]{1,0:T(8,128)(2,1)} %get-tuple-element.35), channel_id=1, source_target_pairs={{0,16},{8,24},{16,0},{24,8},{1,17},{9,25},{17,1},{25,9},{2,18},{10... | collective-permute-start | bytes 811016 | tf_op jit(solution)/shard_map/ppermute | solution.py:239
  8.4 1.3 %collective-permute-start.2 = (bf16[32,4224]{1,0:T(8,128)(2,1)}, bf16[32,4224]{1,0:T(8,128)(2,1)S(1)}, u32[]{:S(2)}, u32[]{:S(2)}) collective-permute-start(bf16[32,4224]{1,0:T(8,128)(2,1)} %get-tuple-element.36), channel_id=1, source_target_pairs={{0,24},{8,0},{16,8},{24,16},{1,25},{9,1},{17,9},{25,17},{2,26},{10... | collective-permute-start | bytes 811016 | tf_op jit(solution)/shard_map/ppermute | solution.py:239
  9.7 2.6 %shard_map.137 = (bf16[128,128]{1,0:T(8,128)(2,1)}, bf16[32,4096]{1,0:T(8,128)(2,1)}, bf16[32,4096]{1,0:T(8,128)(2,1)}, bf16[32,4096]{1,0:T(8,128)(2,1)}, bf16[32,4096]{1,0:T(8,128)(2,1)}) custom-call(bf16[128,128]{1,0:T(8,128)(2,1)} %get-tuple-element.30.pos_ref, bf16[128,2048]{1,0:T(8,128)(2,1)} %refs_0_.3, bf16[128,2048]{1,0:T(8,128)(2,1)} %refs_1_.3), custom_call_target="tpu_custom_call" | custom-call | bytes 2162688 | tf_op jit(solution)/shard_map/pallas_call | solution.py:41
  12.3 0.7 collective-permute-start.3
  13.0 0.3 collective-permute-start.4
  13.3 2.1 %collective-permute-done.refs_1_ = bf16[32,4224]{1,0:T(8,128)(2,1)S(1)} collective-permute-done((bf16[32,4224]{1,0:T(8,128)(2,1)}, bf16[32,4224]{1,0:T(8,128)(2,1)S(1)}, u32[]{:S(2)}, u32[]{:S(2)}) %collective-permute-start) | collective-permute-done | bytes 270368 | tf_op jit(solution)/shard_map/ppermute | solution.py:239
  15.5 2.5 %collective-permute-start.5 = (bf16[32,4096]{1,0:T(8,128)(2,1)}, bf16[32,4096]{1,0:T(8,128)(2,1)S(1)}, u32[]{:S(2)}, u32[]{:S(2)}) collective-permute-start(bf16[32,4096]{1,0:T(8,128)(2,1)} %get-tuple-element.43), channel_id=1, source_target_pairs={{0,24},{8,0},{16,8},{24,16},{1,25},{9,1},{17,9},{25,17},{2,26},{10... | collective-permute-start | bytes 786440 | tf_op jit(solution)/shard_map/ppermute | solution.py:239
  17.9 1.0 copy-done.2
  18.9 0.9 copy-done.3
  19.9 0.7 copy-done.8
  20.5 0.7 copy-done.9
  21.2 0.7 copy-done.10
  21.9 0.2 shard_map.138
  22.1 5.0 %collective-permute-done.1.refs_2_ = bf16[32,4224]{1,0:T(8,128)(2,1)S(1)} collective-permute-done((bf16[32,4224]{1,0:T(8,128)(2,1)}, bf16[32,4224]{1,0:T(8,128)(2,1)S(1)}, u32[]{:S(2)}, u32[]{:S(2)}) %collective-permute-start.1) | collective-permute-done | bytes 270368 | tf_op jit(solution)/shard_map/ppermute | solution.py:239
  27.1 0.0 collective-permute-done.2.refs_3_
  27.1 0.1 shard_map.139
  27.2 1.5 %shard_map.140.probs_ref = bf16[16,128,128]{2,1,0:T(8,128)(2,1)S(1)} custom-call(bf16[128,128]{1,0:T(8,128)(2,1)S(1)} %get-tuple-element.37.place_ref, f32[128,128]{1,0:T(8,128)S(1)} %get-tuple-element.39.outside_ref, bf16[32,4224]{1,0:T(8,128)(2,1)S(1)} %get-tuple-element.33.refs_0_, bf16[32,4224]{1,0:T(8,128)(2,1)S(1)} %collective-permute-done.refs_1_, ...), custom_call_target="tpu_custom_call" | custom-call | bytes 1703936 | tf_op jit(solution)/shard_map/pallas_call | solution.py:41
  28.7 4.0 %collective-permute-done.3.refs_1_ = bf16[32,4096]{1,0:T(8,128)(2,1)S(1)} collective-permute-done((bf16[32,4096]{1,0:T(8,128)(2,1)}, bf16[32,4096]{1,0:T(8,128)(2,1)S(1)}, u32[]{:S(2)}, u32[]{:S(2)}) %collective-permute-start.3) | collective-permute-done | bytes 262176 | tf_op jit(solution)/shard_map/ppermute | solution.py:239
  32.7 16.2 %collective-permute-done.4.refs_2_ = bf16[32,4096]{1,0:T(8,128)(2,1)S(1)} collective-permute-done((bf16[32,4096]{1,0:T(8,128)(2,1)}, bf16[32,4096]{1,0:T(8,128)(2,1)S(1)}, u32[]{:S(2)}, u32[]{:S(2)}) %collective-permute-start.4) | collective-permute-done | bytes 262176 | tf_op jit(solution)/shard_map/ppermute | solution.py:239
  48.9 0.0 collective-permute-done.5.refs_3_
  48.9 0.3 shard_map.141.mixed_ref
  49.2 0.8 shard_map.142
  50.0 10.5 %all_to_all.10 = bf16[8,8,2048]{2,1,0:T(8,128)(2,1)S(1)} all-to-all(bf16[8,8,2048]{2,1,0:T(8,128)(2,1)S(1)} %bitcast.17), channel_id=1, replica_groups=mesh['dp'=4,'expert'=8] {'expert'}, dimensions={0} | all-to-all | bytes 524288 | tf_op jit(solution)/shard_map/all_to_all | solution.py:292
  60.5 6.1 %collective-permute-start.6 = (bf16[64,2048]{1,0:T(8,128)(2,1)S(1)}, bf16[64,2048]{1,0:T(8,128)(2,1)S(1)}, u32[]{:S(2)}, u32[]{:S(2)}) collective-permute-start(bf16[64,2048]{1,0:T(8,128)(2,1)S(1)} %bitcast.13), channel_id=1, source_target_pairs={{0,8},{8,0},{16,24},{24,16},{1,9},{9,1},{17,25},{25,17},{2,10},{10... | collective-permute-start | bytes 786440 | tf_op jit(solution)/shard_map/ppermute | solution.py:308
  66.6 1.7 %collective-permute-start.10 = (bf16[32,2048]{1,0:T(8,128)(2,1)S(1)}, bf16[32,2048]{1,0:T(8,128)(2,1)S(1)}, u32[]{:S(2)}, u32[]{:S(2)}) collective-permute-start(bf16[32,2048]{1,0:T(8,128)(2,1)S(1)} %get-tuple-element.53), channel_id=1, source_target_pairs={{0,16},{8,24},{16,0},{24,8},{1,17},{9,25},{17,1},{25,9},{2,18},{10... | collective-permute-start | bytes 393224 | tf_op jit(solution)/shard_map/ppermute | solution.py:308
  68.2 1.3 %collective-permute-start.8 = (bf16[32,2048]{1,0:T(8,128)(2,1)S(1)}, bf16[32,2048]{1,0:T(8,128)(2,1)S(1)}, u32[]{:S(2)}, u32[]{:S(2)}) collective-permute-start(bf16[32,2048]{1,0:T(8,128)(2,1)S(1)} %get-tuple-element.54), channel_id=1, source_target_pairs={{0,16},{8,24},{16,0},{24,8},{1,17},{9,25},{17,1},{25,9},{2,18},{10... | collective-permute-start | bytes 393224 | tf_op jit(solution)/shard_map/ppermute | solution.py:308
  69.6 6.6 %collective-permute-done.10.refs_3_ = bf16[32,2048]{1,0:T(8,128)(2,1)S(1)} collective-permute-done((bf16[32,2048]{1,0:T(8,128)(2,1)S(1)}, bf16[32,2048]{1,0:T(8,128)(2,1)S(1)}, u32[]{:S(2)}, u32[]{:S(2)}) %collective-permute-start.10) | collective-permute-done | bytes 131104 | tf_op jit(solution)/shard_map/ppermute | solution.py:308
  76.2 1.9 %collective-permute-start.11 = (bf16[32,2048]{1,0:T(8,128)(2,1)S(1)}, bf16[32,2048]{1,0:T(8,128)(2,1)S(1)}, u32[]{:S(2)}, u32[]{:S(2)}) collective-permute-start(bf16[32,2048]{1,0:T(8,128)(2,1)S(1)} %collective-permute-done.10.refs_3_), channel_id=1, source_target_pairs={{0,8},{8,0},{16,24},{24,16},{1,9},{9,1},{17,25},{25,17},{2,10},{10... | collective-permute-start | bytes 393224 | tf_op jit(solution)/shard_map/ppermute | solution.py:308
  78.1 2.3 %collective-permute-done.8.refs_2_ = bf16[32,2048]{1,0:T(8,128)(2,1)S(1)} collective-permute-done((bf16[32,2048]{1,0:T(8,128)(2,1)S(1)}, bf16[32,2048]{1,0:T(8,128)(2,1)S(1)}, u32[]{:S(2)}, u32[]{:S(2)}) %collective-permute-start.8) | collective-permute-done | bytes 131104 | tf_op jit(solution)/shard_map/ppermute | solution.py:308
  80.4 0.2 collective-permute-start.9
  80.6 1.3 %shard_map.143 = (bf16[64,2048]{1,0:T(8,128)(2,1)S(1)}, bf16[64,2048]{1,0:T(8,128)(2,1)S(1)}) custom-call(f32[1,1024]{1,0:T(1,128)S(1)} %copy-done.5, bf16[1,2048,1024]{2,1,0:T(8,128)(2,1)S(1)} %copy-done, bf16[1,1024,2048]{2,1,0:T(8,128)(2,1)S(1)} %copy-done.1, bf16[64,2048]{1,0:T(8,128)(2,1)S(1)} %bitcast.14, ...), custom_call_target="tpu_custom_call" | custom-call | flops 1073741824 | bytes 9441280 | tf_op jit(solution)/shard_map/pallas_call | solution.py:41
  82.0 0.5 collective-permute-done.11.refs_1_
  82.5 2.9 %collective-permute-done.9.refs_0_ = bf16[32,2048]{1,0:T(8,128)(2,1)S(1)} collective-permute-done((bf16[32,2048]{1,0:T(8,128)(2,1)S(1)}, bf16[32,2048]{1,0:T(8,128)(2,1)S(1)}, u32[]{:S(2)}, u32[]{:S(2)}) %collective-permute-start.9) | collective-permute-done | bytes 131104 | tf_op jit(solution)/shard_map/ppermute | solution.py:308
  85.4 1.4 %shard_map.144 = (bf16[32,2048]{1,0:T(8,128)(2,1)S(1)}, bf16[32,2048]{1,0:T(8,128)(2,1)S(1)}, bf16[32,2048]{1,0:T(8,128)(2,1)S(1)}, bf16[32,2048]{1,0:T(8,128)(2,1)S(1)}) custom-call(f32[1,1024]{1,0:T(1,128)S(1)} %copy-done.5, bf16[1,2048,1024]{2,1,0:T(8,128)(2,1)S(1)} %copy-done, bf16[1,1024,2048]{2,1,0:T(8,128)(2,1)S(1)} %copy-done.1, ...), custom_call_target="tpu_custom_call" | custom-call | flops 1073741824 | bytes 9703424 | tf_op jit(solution)/shard_map/pallas_call | solution.py:41
  86.7 0.3 collective-permute-start.12
  87.0 1.8 %collective-permute-start.14 = (bf16[32,2048]{1,0:T(8,128)(2,1)S(1)}, bf16[32,2048]{1,0:T(8,128)(2,1)S(1)}, u32[]{:S(2)}, u32[]{:S(2)}) collective-permute-start(bf16[32,2048]{1,0:T(8,128)(2,1)S(1)} %get-tuple-element.49), channel_id=1, source_target_pairs={{0,8},{8,0},{16,24},{24,16},{1,9},{9,1},{17,25},{25,17},{2,10},{10... | collective-permute-start | bytes 393224 | tf_op jit(solution)/shard_map/ppermute | solution.py:308
  88.8 0.2 collective-permute-start.7
  89.0 7.0 %collective-permute-done.12.first_ref = bf16[32,2048]{1,0:T(8,128)(2,1)S(1)} collective-permute-done((bf16[32,2048]{1,0:T(8,128)(2,1)S(1)}, bf16[32,2048]{1,0:T(8,128)(2,1)S(1)}, u32[]{:S(2)}, u32[]{:S(2)}) %collective-permute-start.12) | collective-permute-done | bytes 131104 | tf_op jit(solution)/shard_map/ppermute | solution.py:308
  96.1 0.1 collective-permute-start.13
  96.2 1.3 %collective-permute-done.14.first_ref = bf16[32,2048]{1,0:T(8,128)(2,1)S(1)} collective-permute-done((bf16[32,2048]{1,0:T(8,128)(2,1)S(1)}, bf16[32,2048]{1,0:T(8,128)(2,1)S(1)}, u32[]{:S(2)}, u32[]{:S(2)}) %collective-permute-start.14) | collective-permute-done | bytes 131104 | tf_op jit(solution)/shard_map/ppermute | solution.py:308
  97.5 1.7 %collective-permute-start.15 = (bf16[32,2048]{1,0:T(8,128)(2,1)S(1)}, bf16[32,2048]{1,0:T(8,128)(2,1)S(1)}, u32[]{:S(2)}, u32[]{:S(2)}) collective-permute-start(bf16[32,2048]{1,0:T(8,128)(2,1)S(1)} %shard_map.146), channel_id=1, source_target_pairs={{0,16},{8,24},{16,0},{24,8},{1,17},{9,25},{17,1},{25,9},{2,18},{10... | collective-permute-start | bytes 393224 | tf_op jit(solution)/shard_map/ppermute | solution.py:308
  99.2 5.6 %collective-permute-done.13.refs_2_ = bf16[32,2048]{1,0:T(8,128)(2,1)S(1)} collective-permute-done((bf16[32,2048]{1,0:T(8,128)(2,1)S(1)}, bf16[32,2048]{1,0:T(8,128)(2,1)S(1)}, u32[]{:S(2)}, u32[]{:S(2)}) %collective-permute-start.13) | collective-permute-done | bytes 131104 | tf_op jit(solution)/shard_map/ppermute | solution.py:308
  104.8 1.4 %collective-permute-done.15.refs_3_ = bf16[32,2048]{1,0:T(8,128)(2,1)S(1)} collective-permute-done((bf16[32,2048]{1,0:T(8,128)(2,1)S(1)}, bf16[32,2048]{1,0:T(8,128)(2,1)S(1)}, u32[]{:S(2)}, u32[]{:S(2)}) %collective-permute-start.15) | collective-permute-done | bytes 131104 | tf_op jit(solution)/shard_map/ppermute | solution.py:308
  106.2 0.1 shard_map.147
  106.4 10.3 %all_to_all.11 = bf16[8,8,2048]{2,1,0:T(8,128)(2,1)S(1)} all-to-all(bf16[8,8,2048]{2,1,0:T(8,128)(2,1)S(1)} %bitcast.16), channel_id=1, replica_groups=mesh['dp'=4,'expert'=8] {'expert'}, dimensions={0} | all-to-all | bytes 524288 | tf_op jit(solution)/shard_map/all_to_all | solution.py:292
  116.7 1.1 shard_map.148
  (22 shorter events, 0.1 us)
Async XLA Ops:
  0.0 49.2 %copy-start.7 = (f32[2048]{0:T(1024)S(1)}, f32[2048]{0:T(1024)}, u32[]{:S(2)}) copy-start(f32[2048]{0:T(1024)} %param.23) | copy-start | bytes 24580
  0.0 49.2 %copy-start.6 = (f32[2048]{0:T(1024)S(1)}, f32[2048]{0:T(1024)}, u32[]{:S(2)}) copy-start(f32[2048]{0:T(1024)} %param.22) | copy-start | bytes 24580
  2.8 12.7 %collective-permute-start = (bf16[32,4224]{1,0:T(8,128)(2,1)}, bf16[32,4224]{1,0:T(8,128)(2,1)S(1)}, u32[]{:S(2)}, u32[]{:S(2)}) collective-permute-start(bf16[32,4224]{1,0:T(8,128)(2,1)} %get-tuple-element.34), channel_id=1, source_target_pairs={{0,8},{8,16},{16,24},{24,0},{1,9},{9,17},{17,25},{25,1},{2,10},{10... | collective-permute-start | bytes 811016 | tf_op jit(solution)/shard_map/ppermute | solution.py:239
  5.8 21.3 %collective-permute-start.1 = (bf16[32,4224]{1,0:T(8,128)(2,1)}, bf16[32,4224]{1,0:T(8,128)(2,1)S(1)}, u32[]{:S(2)}, u32[]{:S(2)}) collective-permute-start(bf16[32,4224]{1,0:T(8,128)(2,1)} %get-tuple-element.35), channel_id=1, source_target_pairs={{0,16},{8,24},{16,0},{24,8},{1,17},{9,25},{17,1},{25,9},{2,18},{10... | collective-permute-start | bytes 811016 | tf_op jit(solution)/shard_map/ppermute | solution.py:239
  8.4 18.7 %collective-permute-start.2 = (bf16[32,4224]{1,0:T(8,128)(2,1)}, bf16[32,4224]{1,0:T(8,128)(2,1)S(1)}, u32[]{:S(2)}, u32[]{:S(2)}) collective-permute-start(bf16[32,4224]{1,0:T(8,128)(2,1)} %get-tuple-element.36), channel_id=1, source_target_pairs={{0,24},{8,0},{16,8},{24,16},{1,25},{9,1},{17,9},{25,17},{2,26},{10... | collective-permute-start | bytes 811016 | tf_op jit(solution)/shard_map/ppermute | solution.py:239
  12.3 20.4 %collective-permute-start.3 = (bf16[32,4096]{1,0:T(8,128)(2,1)}, bf16[32,4096]{1,0:T(8,128)(2,1)S(1)}, u32[]{:S(2)}, u32[]{:S(2)}) collective-permute-start(bf16[32,4096]{1,0:T(8,128)(2,1)} %get-tuple-element.41), channel_id=1, source_target_pairs={{0,8},{8,16},{16,24},{24,0},{1,9},{9,17},{17,25},{25,1},{2,10},{10... | collective-permute-start | bytes 786440 | tf_op jit(solution)/shard_map/ppermute | solution.py:239
  13.0 35.9 %collective-permute-start.4 = (bf16[32,4096]{1,0:T(8,128)(2,1)}, bf16[32,4096]{1,0:T(8,128)(2,1)S(1)}, u32[]{:S(2)}, u32[]{:S(2)}) collective-permute-start(bf16[32,4096]{1,0:T(8,128)(2,1)} %get-tuple-element.42), channel_id=1, source_target_pairs={{0,16},{8,24},{16,0},{24,8},{1,17},{9,25},{17,1},{25,9},{2,18},{10... | collective-permute-start | bytes 786440 | tf_op jit(solution)/shard_map/ppermute | solution.py:239
  15.5 33.4 %collective-permute-start.5 = (bf16[32,4096]{1,0:T(8,128)(2,1)}, bf16[32,4096]{1,0:T(8,128)(2,1)S(1)}, u32[]{:S(2)}, u32[]{:S(2)}) collective-permute-start(bf16[32,4096]{1,0:T(8,128)(2,1)} %get-tuple-element.43), channel_id=1, source_target_pairs={{0,24},{8,0},{16,8},{24,16},{1,25},{9,1},{17,9},{25,17},{2,26},{10... | collective-permute-start | bytes 786440 | tf_op jit(solution)/shard_map/ppermute | solution.py:239
  17.9 1.0 copy-start.2
  18.9 0.9 copy-start.3
  19.8 0.7 copy-start.8
  20.5 0.7 copy-start.9
  21.2 0.7 copy-start.10
  27.1 53.5 %copy-start = (bf16[1,2048,1024]{2,1,0:T(8,128)(2,1)S(1)}, bf16[1,2048,1024]{2,1,0:T(8,128)(2,1)}, u32[]{:S(2)}) copy-start(bf16[1,2048,1024]{2,1,0:T(8,128)(2,1)} %w_in_ref.3) | copy-start | bytes 12582916
  27.1 53.5 %copy-start.1 = (bf16[1,1024,2048]{2,1,0:T(8,128)(2,1)S(1)}, bf16[1,1024,2048]{2,1,0:T(8,128)(2,1)}, u32[]{:S(2)}) copy-start(bf16[1,1024,2048]{2,1,0:T(8,128)(2,1)} %w_out_ref.3) | copy-start | bytes 12582916
  27.1 53.5 %copy-start.5 = (f32[1,1024]{1,0:T(1,128)S(1)}, f32[1,1024]{1,0:T(1,128)}, u32[]{:S(2)}) copy-start(f32[1,1024]{1,0:T(1,128)} %bias_ref.4) | copy-start | bytes 12292
  60.5 20.2 %collective-permute-start.6 = (bf16[64,2048]{1,0:T(8,128)(2,1)S(1)}, bf16[64,2048]{1,0:T(8,128)(2,1)S(1)}, u32[]{:S(2)}, u32[]{:S(2)}) collective-permute-start(bf16[64,2048]{1,0:T(8,128)(2,1)S(1)} %bitcast.13), channel_id=1, source_target_pairs={{0,8},{8,0},{16,24},{24,16},{1,9},{9,1},{17,25},{25,17},{2,10},{10... | collective-permute-start | bytes 786440 | tf_op jit(solution)/shard_map/ppermute | solution.py:308
  66.6 9.6 %collective-permute-start.10 = (bf16[32,2048]{1,0:T(8,128)(2,1)S(1)}, bf16[32,2048]{1,0:T(8,128)(2,1)S(1)}, u32[]{:S(2)}, u32[]{:S(2)}) collective-permute-start(bf16[32,2048]{1,0:T(8,128)(2,1)S(1)} %get-tuple-element.53), channel_id=1, source_target_pairs={{0,16},{8,24},{16,0},{24,8},{1,17},{9,25},{17,1},{25,9},{2,18},{10... | collective-permute-start | bytes 393224 | tf_op jit(solution)/shard_map/ppermute | solution.py:308
  68.2 12.2 %collective-permute-start.8 = (bf16[32,2048]{1,0:T(8,128)(2,1)S(1)}, bf16[32,2048]{1,0:T(8,128)(2,1)S(1)}, u32[]{:S(2)}, u32[]{:S(2)}) collective-permute-start(bf16[32,2048]{1,0:T(8,128)(2,1)S(1)} %get-tuple-element.54), channel_id=1, source_target_pairs={{0,16},{8,24},{16,0},{24,8},{1,17},{9,25},{17,1},{25,9},{2,18},{10... | collective-permute-start | bytes 393224 | tf_op jit(solution)/shard_map/ppermute | solution.py:308
  76.2 6.3 %collective-permute-start.11 = (bf16[32,2048]{1,0:T(8,128)(2,1)S(1)}, bf16[32,2048]{1,0:T(8,128)(2,1)S(1)}, u32[]{:S(2)}, u32[]{:S(2)}) collective-permute-start(bf16[32,2048]{1,0:T(8,128)(2,1)S(1)} %collective-permute-done.10.refs_3_), channel_id=1, source_target_pairs={{0,8},{8,0},{16,24},{24,16},{1,9},{9,1},{17,25},{25,17},{2,10},{10... | collective-permute-start | bytes 393224 | tf_op jit(solution)/shard_map/ppermute | solution.py:308
  80.4 5.0 %collective-permute-start.9 = (bf16[32,2048]{1,0:T(8,128)(2,1)S(1)}, bf16[32,2048]{1,0:T(8,128)(2,1)S(1)}, u32[]{:S(2)}, u32[]{:S(2)}) collective-permute-start(bf16[32,2048]{1,0:T(8,128)(2,1)S(1)} %collective-permute-done.8.refs_2_), channel_id=1, source_target_pairs={{0,8},{8,0},{16,24},{24,16},{1,9},{9,1},{17,25},{25,17},{2,10},{10... | collective-permute-start | bytes 393224 | tf_op jit(solution)/shard_map/ppermute | solution.py:308
  85.4 20.8 %copy-start.4 = (f32[8,2048]{1,0:T(8,128)S(1)}, f32[8,2048]{1,0:T(8,128)}, u32[]{:S(2)}) copy-start(f32[8,2048]{1,0:T(8,128)} %bias_ref.5) | copy-start | bytes 196612
  86.7 9.3 %collective-permute-start.12 = (bf16[32,2048]{1,0:T(8,128)(2,1)S(1)}, bf16[32,2048]{1,0:T(8,128)(2,1)S(1)}, u32[]{:S(2)}, u32[]{:S(2)}) collective-permute-start(bf16[32,2048]{1,0:T(8,128)(2,1)S(1)} %get-tuple-element.47), channel_id=1, source_target_pairs={{0,8},{8,0},{16,24},{24,16},{1,9},{9,1},{17,25},{25,17},{2,10},{10... | collective-permute-start | bytes 393224 | tf_op jit(solution)/shard_map/ppermute | solution.py:308
  87.0 10.4 %collective-permute-start.14 = (bf16[32,2048]{1,0:T(8,128)(2,1)S(1)}, bf16[32,2048]{1,0:T(8,128)(2,1)S(1)}, u32[]{:S(2)}, u32[]{:S(2)}) collective-permute-start(bf16[32,2048]{1,0:T(8,128)(2,1)S(1)} %get-tuple-element.49), channel_id=1, source_target_pairs={{0,8},{8,0},{16,24},{24,16},{1,9},{9,1},{17,25},{25,17},{2,10},{10... | collective-permute-start | bytes 393224 | tf_op jit(solution)/shard_map/ppermute | solution.py:308
  88.8 17.4 %collective-permute-start.7 = (bf16[64,2048]{1,0:T(8,128)(2,1)S(1)}, bf16[64,2048]{1,0:T(8,128)(2,1)S(1)}, u32[]{:S(2)}, u32[]{:S(2)}) collective-permute-start(bf16[64,2048]{1,0:T(8,128)(2,1)S(1)} %get-tuple-element.46), channel_id=1, source_target_pairs={{0,8},{8,0},{16,24},{24,16},{1,9},{9,1},{17,25},{25,17},{2,10},{10... | collective-permute-start | bytes 786440 | tf_op jit(solution)/shard_map/ppermute | solution.py:308
  96.1 8.7 %collective-permute-start.13 = (bf16[32,2048]{1,0:T(8,128)(2,1)S(1)}, bf16[32,2048]{1,0:T(8,128)(2,1)S(1)}, u32[]{:S(2)}, u32[]{:S(2)}) collective-permute-start(bf16[32,2048]{1,0:T(8,128)(2,1)S(1)} %shard_map.145), channel_id=1, source_target_pairs={{0,16},{8,24},{16,0},{24,8},{1,17},{9,25},{17,1},{25,9},{2,18},{10... | collective-permute-start | bytes 393224 | tf_op jit(solution)/shard_map/ppermute | solution.py:308
  97.5 8.7 %collective-permute-start.15 = (bf16[32,2048]{1,0:T(8,128)(2,1)S(1)}, bf16[32,2048]{1,0:T(8,128)(2,1)S(1)}, u32[]{:S(2)}, u32[]{:S(2)}) collective-permute-start(bf16[32,2048]{1,0:T(8,128)(2,1)S(1)} %shard_map.146), channel_id=1, source_target_pairs={{0,16},{8,24},{16,0},{24,8},{1,17},{9,25},{17,1},{25,9},{2,18},{10... | collective-permute-start | bytes 393224 | tf_op jit(solution)/shard_map/ppermute | solution.py:308

commit v7 on v6

--- a/solution.py
+++ b/solution.py
@@ -78,10 +78,10 @@
     return jnp.concatenate([r[:, columns] for r in refs], axis=0)
 
 
-def slots_of(ids_ref, cap, experts):
-    tok = ids_ref.shape[1]
-    first, first_t = across(ids_ref[0:1, :], tok)
-    second, second_t = across(ids_ref[1:2, :], tok)
+def slots_of(ids, cap, experts):
+    tok = ids.shape[1]
+    first, first_t = across(ids[0:1, :], tok)
+    second, second_t = across(ids[1:2, :], tok)
     earlier = iota((tok, tok), 0) < iota((tok, tok), 1)
     rank_first = jnp.sum(one_hot((first_t == first) & earlier), axis=0, keepdims=True)
     rank_second = jnp.sum(one_hot(first_t == second), axis=0, keepdims=True)
@@ -93,13 +93,17 @@
     return slot(first[0:1, :], rank_first), slot(second[0:1, :], rank_second)
 
 
-def slots_kernel(cap, experts, seg_ref, ids_ref, code_ref, own_ref, own_later_ref, *refs):
+def slots_kernel(cap, experts, relative, seg_ref, ids_ref, code_ref, own_ref, own_later_ref, *refs):
     seg_q_ref, taken_ref, give_ref, kept_ref, kept_later_ref = refs
     kept_ref[...] = own_ref[...]
     kept_later_ref[...] = own_later_ref[...]
     tok = seg_ref.shape[1]
     _, seg_q_ref[...] = across(seg_ref[...], tok)
-    slot_first, slot_second = slots_of(ids_ref, cap, experts)
+    ids = ids_ref[...]
+    if relative:
+        other = ids ^ lax.axis_index("expert")
+        ids = jnp.where(ids < experts, (other & 1) * (experts // 2) + (other >> 1), ids)
+    slot_first, slot_second = slots_of(ids, cap, experts)
     slot = iota((experts * cap, tok), 0).astype(F32)
     taken_ref[...] = one_hot((slot == slot_first) | (slot == slot_second)).astype(BF16)
     high = (code_ref[...] >> 8).astype(F32)
@@ -149,8 +153,8 @@
         out_ref[:, lo : lo + HEAD_DIM] = jnp.dot(probs_ref[h], values, preferred_element_type=F32)
 
 
-def norm_kernel(place_ref, taken_ref, gain_ref, bias_ref, mixed_ref, *refs):
-    *state_refs, hidden_ref, send_ref = refs
+def norm_kernel(parts, place_ref, taken_ref, gain_ref, bias_ref, mixed_ref, *refs):
+    state_refs, hidden_ref, send_refs = refs[: -parts - 1], refs[-parts - 1], refs[-parts:]
     hidden = mixed_ref[...] + jnp.dot(
         place_ref[...], joined(state_refs, slice(mixed_ref.shape[1], None)), preferred_element_type=F32
     )
@@ -158,7 +162,11 @@
     centered = hidden - jnp.mean(hidden, axis=1, keepdims=True)
     variance = jnp.mean(centered * centered, axis=1, keepdims=True)
     normed = (centered * lax.rsqrt(variance + epsilon) * gain_ref[...] + bias_ref[...]).astype(BF16)
-    send_ref[...] = jnp.dot(taken_ref[...], normed, preferred_element_type=F32).astype(BF16)
+    picked = jnp.dot(taken_ref[...], normed, preferred_element_type=F32).astype(BF16)
+    at = 0
+    for send_ref in send_refs:
+        send_ref[...] = picked[at : at + send_ref.shape[0]]
+        at += send_ref.shape[0]
 
 
 def expert_kernel(count, bias_ref, w_in_ref, w_out_ref, *refs):
@@ -176,28 +184,42 @@
     out_ref[...] = (first_ref[...].astype(F32) + second_ref[...].astype(F32)).astype(BF16)
 
 
-def shares_of(refs, rows):
-    shares, parts = [], []
-    for ref in refs:
-        parts.append(ref)
-        if sum(p.shape[0] for p in parts) == rows:
-            shares.append(joined(parts))
-            parts = []
-    return shares
-
-
-def result_kernel(bias_ref, *refs):
-    *share_refs, out_ref = refs
-    total = 0.0
-    for share in shares_of(share_refs, out_ref.shape[0]):
-        total += share.astype(F32)
+def result_kernel(lower, bias_ref, near_ref, *refs):
+    count = refs[0].shape[0]
+    outs = next(n for n in range(1, len(refs)) if sum(r.shape[0] for r in refs[-n:]) == count)
+    total = near_ref[lower : lower + count].astype(F32)
+    for share_ref in refs[:-outs]:
+        total += share_ref[...].astype(F32)
     row = lax.axis_index("expert") == iota(bias_ref.shape, 0)
     bias = jnp.sum(jnp.where(row, bias_ref[...], 0.0), axis=0, keepdims=True)
-    out_ref[...] = (total + bias).astype(BF16)
-
-
-def combine_kernel(results_ref, hidden_ref, give_ref, out_ref):
-    result = jnp.concatenate([results_ref[...], results_ref[...]], axis=0)
+    result = (total + bias).astype(BF16)
+    at = 0
+    for out_ref in refs[-outs:]:
+        out_ref[...] = result[at : at + out_ref.shape[0]]
+        at += out_ref.shape[0]
+
+
+def join_kernel(*refs):
+    refs[-1][...] = joined(refs[:-1])
+
+
+def pair_kernel(cap, mine_ref, other_ref, *piece_refs):
+    mine, other = mine_ref[...].astype(F32), other_ref[...].astype(F32)
+    for n, piece_ref in enumerate(piece_refs):
+        rows = slice(n * cap, (n + 1) * cap)
+        piece_ref[...] = jnp.concatenate([mine[rows], other[rows]], axis=0).astype(BF16)
+
+
+def part_kernel(cap, *refs):
+    *piece_refs, mine_ref, other_ref = refs
+    pieces = [piece_ref[...].astype(F32) for piece_ref in piece_refs]
+    mine_ref[...] = jnp.concatenate([piece[:cap] for piece in pieces], axis=0).astype(BF16)
+    other_ref[...] = jnp.concatenate([piece[cap:] for piece in pieces], axis=0).astype(BF16)
+
+
+def combine_kernel(hidden_ref, give_ref, *refs):
+    *result_refs, out_ref = refs
+    result = joined(list(result_refs) * 2)
     added = jnp.dot(give_ref[...], result, preferred_element_type=F32)
     out_ref[...] = (hidden_ref[...] + added).astype(BF16)
 
@@ -223,6 +245,7 @@
     experts = lax.axis_size("expert")
     cap = max(2, 2 * tok // (ROUNDS * experts))
     slots = experts * cap
+    relative = dp == 4 and experts == 8
     heads = width // HEAD_DIM
     def pack(guide, *arrays):
         wide = len(arrays) * width + (LANES if guide.dtype == jnp.int32 else 0)
@@ -243,7 +266,7 @@
     order, *packed = pack(pack_pos.reshape(1, tok), keys, queries)
     _, *packed_later = pack(order, values, pivot_states)
     seg_q, taken, give, kept, kept_later = call(
-        functools.partial(slots_kernel, cap, experts),
+        functools.partial(slots_kernel, cap, experts, relative),
         (
             jax.ShapeDtypeStruct((tok, tok), F32),
             jax.ShapeDtypeStruct((slots, tok), BF16),
@@ -273,12 +296,11 @@
         *rows,
     )
     mixed = call(mix_kernel, jax.ShapeDtypeStruct((tok, width), F32), probs, *later)
-    hidden_state, send = call(
-        norm_kernel,
-        (
-            jax.ShapeDtypeStruct((tok, width), F32),
-            jax.ShapeDtypeStruct((slots, width), BF16),
-        ),
+    parts = 2 if relative else 1
+    hidden_state, *send = call(
+        functools.partial(norm_kernel, parts),
+        (jax.ShapeDtypeStruct((tok, width), F32),)
+        + (jax.ShapeDtypeStruct((slots // parts, width), BF16),) * parts,
         place,
         taken,
         ln_gain.reshape(1, width),
@@ -291,11 +313,14 @@
         x = x.reshape(experts, cap, width)
         return lax.all_to_all(x, "expert", split_axis=0, concat_axis=0, tiled=True).reshape(slots, width)
 
+    def bf16(rows):
+        return jax.ShapeDtypeStruct((rows, width), BF16)
+
     def apply(rows, after=()):
         count = sum(x.shape[0] for x in rows)
         return call(
             functools.partial(expert_kernel, len(rows)),
-            tuple(jax.ShapeDtypeStruct(x.shape, BF16) for x in rows),
+            tuple(bf16(x.shape[0]) for x in rows),
             b_in,
             w_in,
             w_out,
@@ -304,33 +329,50 @@
             flops=4 * count * width * w_in.shape[2],
         )
 
-    def swap(x, distance):
-        return lax.ppermute(x, "dp", [(i, i ^ distance) for i in range(dp)])
-
-    own = over_experts(send)
-    if dp == 4:
+    def swap(x, distance, axis="dp"):
+        return lax.ppermute(x, axis, [(i, i ^ distance) for i in range(lax.axis_size(axis))])
+
+    if relative:
         half = slots // 2
-        far = [swap(own[:half], 2), swap(own[half:], 2)]
-        own_share, near_share = apply([own, swap(own, 1)])
-        *corner_share, far_first, far_second = apply([swap(x, 1) for x in far] + far, after=[own_share])
-        shares = [own_share, swap(near_share, 1)]
-        for x, y in zip(corner_share, (far_first, far_second)):
-            pair = call(add_kernel, jax.ShapeDtypeStruct((half, width), BF16), swap(x, 1), y)
-            shares.append(swap(pair, 2))
+        pieces = call(
+            functools.partial(pair_kernel, cap), (bf16(2 * cap),) * 4, send[0], swap(send[1], 1, "expert")
+        )
+        pieces = [swap(x, 2 * n, "expert") if n else x for n, x in enumerate(pieces)]
+        own = [call(join_kernel, bf16(half), *pieces[n : n + 2]) for n in (2, 0)]
+        far = [swap(x, 2) for x in own]
+        near = [swap(x, 1) for x in own]
+        *own_share, near_first, near_second = apply(own + near)
+        *corner_share, far_first, far_second = apply([swap(x, 1) for x in far] + far, after=own_share[:1])
+        near_shares = [swap(near_first, 1), swap(near_second, 1)]
+        far_shares = [far_first, far_second]
+        pieces = ()
+        for n in (1, 0):
+            pair = swap(call(add_kernel, bf16(half), swap(corner_share[n], 1), far_shares[n]), 2)
+            pieces += tuple(
+                call(
+                    functools.partial(result_kernel, 0),
+                    (bf16(2 * cap),) * 2,
+                    b_out,
+                    near_shares[n],
+                    own_share[n],
+                    pair,
+                )
+            )
+        pieces = [swap(x, 2 * n, "expert") if n else x for n, x in enumerate(pieces)]
+        mine, other = call(functools.partial(part_kernel, cap), (bf16(half),) * 2, *pieces)
+        returned = [mine, swap(other, 1, "expert")]
     else:
-        every = lax.all_gather(own, "dp", axis=0, tiled=True)
+        every = lax.all_gather(over_experts(send[0]), "dp", axis=0, tiled=True)
         (share,) = apply([every])
-        parts = lax.all_to_all(
+        shares = lax.all_to_all(
             share.reshape(dp, slots, width), "dp", split_axis=0, concat_axis=0, tiled=True
         )
-        shares = [parts[n] for n in range(dp)]
-    results = call(result_kernel, jax.ShapeDtypeStruct((slots, width), BF16), b_out, *shares)
+        (results,) = call(
+            functools.partial(result_kernel, 0), (bf16(slots),), b_out, *[shares[n] for n in range(dp)]
+        )
+        returned = [over_experts(results)]
     return call(
-        combine_kernel,
-        jax.ShapeDtypeStruct((tok, width), BF16),
-        over_experts(results),
-        hidden_state,
-        give,
+        combine_kernel, jax.ShapeDtypeStruct((tok, width), BF16), hidden_state, give, *returned
     )
 
 

time: 118 us -> 110 us (0.932)
  blocking collectives: 20.8 us -> 0 us
  starting transfers between devices: 25.7 us -> 42.9 us
  waiting for transfers between devices: 55 us -> 50.3 us
    all_to_all x2 -> x0, blocking collectives: 20.8 us -> none  [over_experts(): lax.all_to_all(x, 'expert', split_axis=0, concat_axis=0, tiled=True)]
    ppermute x10 -> x20, starting transfers between devices: 15.3 us -> 32.4 us  [swap(): lax.ppermute(x, axis, [(i, i ^ distance) for i in range(lax.axis_size(axi...]
    ppermute x10 -> x20, waiting for transfers between devices: 27.6 us -> 23 us  [swap(): lax.ppermute(x, axis, [(i, i ^ distance) for i in range(lax.axis_size(axi...]
    pallas_call x13 -> x18, Pallas kernels: 12.2 us -> 12.3 us  [call(): pl.pallas_call(body, out_shape=out_shape, compiler_params=pltpu.CompilerP...]
  transfers between devices with their start and end apart: 16 -> 26, of which waited for: 12 -> 18; matrix products, arithmetic and copies ran while one was open for 0% -> 0% of each run, Pallas kernels for 5% -> 5%
where the time goes in v7:
time: 110 us
  waiting for transfers between devices  50.3 us (46%)
  starting transfers between devices  42.9 us (39%)
  Pallas kernels  12.3 us (11%)
  local copies, waits for them, and re-layouts  3.94 us (4%)
    ppermute x20, starting transfers between devices, swap(): lax.ppermute(x, axis, [(i, i ^ distance) for i in range(lax.axis_size(axi...  32.4 us
    ppermute x6, waiting for transfers between devices, spread(): lax.ppermute(part, 'dp', [(i, (i + n) % dp) for i in range(dp)])  27.3 us
    ppermute x20, waiting for transfers between devices, swap(): lax.ppermute(x, axis, [(i, i ^ distance) for i in range(lax.axis_size(axi...  23 us
    pallas_call x18, Pallas kernels, call(): pl.pallas_call(body, out_shape=out_shape, compiler_params=pltpu.CompilerP...  12.3 us
    ppermute x6, starting transfers between devices, spread(): lax.ppermute(part, 'dp', [(i, (i + n) % dp) for i in range(dp)])  10.5 us
    unnamed x22, local copies, waits for them, and re-layouts  3.94 us
  transfers between devices with their start and end apart: 26, of which 18 were waited for; matrix products, arithmetic and copies ran while one was open for 0% of the time, Pallas kernels for 5%

profile of v7, /device:TPU:0, one launch (start us, length us, event | category | flops | bytes accessed | tf_op | source)
XLA Modules:
  0.0 109.6 jit_solution(12306720870505969475)
XLA Ops:
  0.0 2.8 %shard_map.136 = (bf16[128,128]{1,0:T(8,128)(2,1)}, bf16[32,4224]{1,0:T(8,128)(2,1)}, bf16[32,4224]{1,0:T(8,128)(2,1)}, bf16[32,4224]{1,0:T(8,128)(2,1)}, bf16[32,4224]{1,0:T(8,128)(2,1)}) custom-call(s32[1,128]{1,0:T(1,128)} %bitcast.9, bf16[128,2048]{1,0:T(8,128)(2,1)} %refs_0_.2, bf16[128,2048]{1,0:T(8,128)(2,1)} %refs_1_.2), custom_call_target="tpu_custom_call" | custom-call | bytes 2163200 | tf_op jit(solution)/shard_map/pallas_call | solution.py:41
  2.8 3.0 %collective-permute-start = (bf16[32,4224]{1,0:T(8,128)(2,1)}, bf16[32,4224]{1,0:T(8,128)(2,1)S(1)}, u32[]{:S(2)}, u32[]{:S(2)}) collective-permute-start(bf16[32,4224]{1,0:T(8,128)(2,1)} %get-tuple-element.47), channel_id=1, source_target_pairs={{0,8},{8,16},{16,24},{24,0},{1,9},{9,17},{17,25},{25,1},{2,10},{10... | collective-permute-start | bytes 811016 | tf_op jit(solution)/shard_map/ppermute | solution.py:262
  5.8 2.6 %collective-permute-start.1 = (bf16[32,4224]{1,0:T(8,128)(2,1)}, bf16[32,4224]{1,0:T(8,128)(2,1)S(1)}, u32[]{:S(2)}, u32[]{:S(2)}) collective-permute-start(bf16[32,4224]{1,0:T(8,128)(2,1)} %get-tuple-element.48), channel_id=1, source_target_pairs={{0,16},{8,24},{16,0},{24,8},{1,17},{9,25},{17,1},{25,9},{2,18},{10... | collective-permute-start | bytes 811016 | tf_op jit(solution)/shard_map/ppermute | solution.py:262
  8.4 1.3 %collective-permute-start.2 = (bf16[32,4224]{1,0:T(8,128)(2,1)}, bf16[32,4224]{1,0:T(8,128)(2,1)S(1)}, u32[]{:S(2)}, u32[]{:S(2)}) collective-permute-start(bf16[32,4224]{1,0:T(8,128)(2,1)} %get-tuple-element.49), channel_id=1, source_target_pairs={{0,24},{8,0},{16,8},{24,16},{1,25},{9,1},{17,9},{25,17},{2,26},{10... | collective-permute-start | bytes 811016 | tf_op jit(solution)/shard_map/ppermute | solution.py:262
  9.7 2.6 %shard_map.137 = (bf16[128,128]{1,0:T(8,128)(2,1)}, bf16[32,4096]{1,0:T(8,128)(2,1)}, bf16[32,4096]{1,0:T(8,128)(2,1)}, bf16[32,4096]{1,0:T(8,128)(2,1)}, bf16[32,4096]{1,0:T(8,128)(2,1)}) custom-call(bf16[128,128]{1,0:T(8,128)(2,1)} %get-tuple-element.43.pos_ref, bf16[128,2048]{1,0:T(8,128)(2,1)} %refs_0_.3, bf16[128,2048]{1,0:T(8,128)(2,1)} %refs_1_.3), custom_call_target="tpu_custom_call" | custom-call | bytes 2162688 | tf_op jit(solution)/shard_map/pallas_call | solution.py:41
  12.3 0.7 collective-permute-start.3
  13.3 2.1 %collective-permute-done.refs_1_ = bf16[32,4224]{1,0:T(8,128)(2,1)S(1)} collective-permute-done((bf16[32,4224]{1,0:T(8,128)(2,1)}, bf16[32,4224]{1,0:T(8,128)(2,1)S(1)}, u32[]{:S(2)}, u32[]{:S(2)}) %collective-permute-start) | collective-permute-done | bytes 270368 | tf_op jit(solution)/shard_map/ppermute | solution.py:262
  15.5 2.5 %collective-permute-start.5 = (bf16[32,4096]{1,0:T(8,128)(2,1)}, bf16[32,4096]{1,0:T(8,128)(2,1)S(1)}, u32[]{:S(2)}, u32[]{:S(2)}) collective-permute-start(bf16[32,4096]{1,0:T(8,128)(2,1)} %get-tuple-element.56), channel_id=1, source_target_pairs={{0,24},{8,0},{16,8},{24,16},{1,25},{9,1},{17,9},{25,17},{2,26},{10... | collective-permute-start | bytes 786440 | tf_op jit(solution)/shard_map/ppermute | solution.py:262
  18.0 1.0 copy-done.2
  18.9 0.9 copy-done.4
  19.9 0.7 copy-done.8
  20.5 0.7 copy-done.9
  21.2 0.7 copy-done.10
  22.1 5.0 %collective-permute-done.1.refs_2_ = bf16[32,4224]{1,0:T(8,128)(2,1)S(1)} collective-permute-done((bf16[32,4224]{1,0:T(8,128)(2,1)}, bf16[32,4224]{1,0:T(8,128)(2,1)S(1)}, u32[]{:S(2)}, u32[]{:S(2)}) %collective-permute-start.1) | collective-permute-done | bytes 270368 | tf_op jit(solution)/shard_map/ppermute | solution.py:262
  27.2 1.5 %shard_map.140.probs_ref = bf16[16,128,128]{2,1,0:T(8,128)(2,1)S(1)} custom-call(bf16[128,128]{1,0:T(8,128)(2,1)S(1)} %get-tuple-element.50.place_ref, f32[128,128]{1,0:T(8,128)S(1)} %get-tuple-element.52.outside_ref, bf16[32,4224]{1,0:T(8,128)(2,1)S(1)} %get-tuple-element.46.refs_0_, bf16[32,4224]{1,0:T(8,128)(2,1)S(1)} %collective-permute-done.refs_1_, ...), custom_call_target="tpu_custom_call" | custom-call | bytes 1703936 | tf_op jit(solution)/shard_map/pallas_call | solution.py:41
  28.8 4.0 %collective-permute-done.3.refs_1_ = bf16[32,4096]{1,0:T(8,128)(2,1)S(1)} collective-permute-done((bf16[32,4096]{1,0:T(8,128)(2,1)}, bf16[32,4096]{1,0:T(8,128)(2,1)S(1)}, u32[]{:S(2)}, u32[]{:S(2)}) %collective-permute-start.3) | collective-permute-done | bytes 262176 | tf_op jit(solution)/shard_map/ppermute | solution.py:262
  32.7 16.2 %collective-permute-done.4.refs_2_ = bf16[32,4096]{1,0:T(8,128)(2,1)S(1)} collective-permute-done((bf16[32,4096]{1,0:T(8,128)(2,1)}, bf16[32,4096]{1,0:T(8,128)(2,1)S(1)}, u32[]{:S(2)}, u32[]{:S(2)}) %collective-permute-start.4) | collective-permute-done | bytes 262176 | tf_op jit(solution)/shard_map/ppermute | solution.py:262
  49.2 0.8 shard_map.142
  50.1 1.3 %collective-permute-done.6.other_ref = bf16[32,2048]{1,0:T(8,128)(2,1)S(1)} collective-permute-done((bf16[32,2048]{1,0:T(8,128)(2,1)S(1)}, bf16[32,2048]{1,0:T(8,128)(2,1)S(1)}, u32[]{:S(2)}, u32[]{:S(2)}) %collective-permute-start.6) | collective-permute-done | bytes 131104 | tf_op jit(solution)/shard_map/ppermute | solution.py:333
  51.5 1.6 %collective-permute-start.9 = (bf16[16,2048]{1,0:T(8,128)(2,1)S(1)}, bf16[16,2048]{1,0:T(8,128)(2,1)S(1)}, u32[]{:S(2)}, u32[]{:S(2)}) collective-permute-start(bf16[16,2048]{1,0:T(8,128)(2,1)S(1)} %get-tuple-element.64), channel_id=1, source_target_pairs={{0,2},{1,3},{2,0},{3,1},{4,6},{5,7},{6,4},{7,5},{8,10},{9,11},{10,... | collective-permute-start | bytes 196616 | tf_op jit(solution)/shard_map/ppermute | solution.py:333
  53.0 1.5 %collective-permute-start.7 = (bf16[16,2048]{1,0:T(8,128)(2,1)S(1)}, bf16[16,2048]{1,0:T(8,128)(2,1)S(1)}, u32[]{:S(2)}, u32[]{:S(2)}) collective-permute-start(bf16[16,2048]{1,0:T(8,128)(2,1)S(1)} %get-tuple-element.61), channel_id=1, source_target_pairs={{0,4},{1,5},{2,6},{3,7},{4,0},{5,1},{6,2},{7,3},{8,12},{9,13},{10,... | collective-permute-start | bytes 196616 | tf_op jit(solution)/shard_map/ppermute | solution.py:333
  55.0 0.8 collective-permute-done.9.refs_1_
  55.8 5.2 %collective-permute-start.15 = (bf16[32,2048]{1,0:T(8,128)(2,1)S(1)}, bf16[32,2048]{1,0:T(8,128)(2,1)S(1)}, u32[]{:S(2)}, u32[]{:S(2)}) collective-permute-start(bf16[32,2048]{1,0:T(8,128)(2,1)S(1)} %shard_map.145.refs_1_), channel_id=1, source_target_pairs={{0,16},{8,24},{16,0},{24,8},{1,17},{9,25},{17,1},{25,9},{2,18},{10... | collective-permute-start | bytes 393224 | tf_op jit(solution)/shard_map/ppermute | solution.py:333
  61.1 3.9 %collective-permute-start.13 = (bf16[32,2048]{1,0:T(8,128)(2,1)S(1)}, bf16[32,2048]{1,0:T(8,128)(2,1)S(1)}, u32[]{:S(2)}, u32[]{:S(2)}) collective-permute-start(bf16[32,2048]{1,0:T(8,128)(2,1)S(1)} %shard_map.144.refs_0_), channel_id=1, source_target_pairs={{0,16},{8,24},{16,0},{24,8},{1,17},{9,25},{17,1},{25,9},{2,18},{10... | collective-permute-start | bytes 393224 | tf_op jit(solution)/shard_map/ppermute | solution.py:333
  64.9 2.5 %collective-permute-start.11 = (bf16[32,2048]{1,0:T(8,128)(2,1)S(1)}, bf16[32,2048]{1,0:T(8,128)(2,1)S(1)}, u32[]{:S(2)}, u32[]{:S(2)}) collective-permute-start(bf16[32,2048]{1,0:T(8,128)(2,1)S(1)} %shard_map.145.refs_1_), channel_id=1, source_target_pairs={{0,8},{8,0},{16,24},{24,16},{1,9},{9,1},{17,25},{25,17},{2,10},{10... | collective-permute-start | bytes 393224 | tf_op jit(solution)/shard_map/ppermute | solution.py:333
  67.5 3.2 %collective-permute-start.16 = (bf16[32,2048]{1,0:T(8,128)(2,1)S(1)}, bf16[32,2048]{1,0:T(8,128)(2,1)S(1)}, u32[]{:S(2)}, u32[]{:S(2)}) collective-permute-start(bf16[32,2048]{1,0:T(8,128)(2,1)S(1)} %collective-permute-done.15.refs_3_), channel_id=1, source_target_pairs={{0,8},{8,0},{16,24},{24,16},{1,9},{9,1},{17,25},{25,17},{2,10},{10... | collective-permute-start | bytes 393224 | tf_op jit(solution)/shard_map/ppermute | solution.py:333
  70.7 1.6 %collective-permute-done.13.refs_2_ = bf16[32,2048]{1,0:T(8,128)(2,1)S(1)} collective-permute-done((bf16[32,2048]{1,0:T(8,128)(2,1)S(1)}, bf16[32,2048]{1,0:T(8,128)(2,1)S(1)}, u32[]{:S(2)}, u32[]{:S(2)}) %collective-permute-start.13) | collective-permute-done | bytes 131104 | tf_op jit(solution)/shard_map/ppermute | solution.py:333
  72.3 0.9 collective-permute-start.14
  73.2 0.7 collective-permute-done.11.refs_3_
  73.9 2.8 %collective-permute-done.10.refs_2_ = bf16[32,2048]{1,0:T(8,128)(2,1)S(1)} collective-permute-done((bf16[32,2048]{1,0:T(8,128)(2,1)S(1)}, bf16[32,2048]{1,0:T(8,128)(2,1)S(1)}, u32[]{:S(2)}, u32[]{:S(2)}) %collective-permute-start.10) | collective-permute-done | bytes 131104 | tf_op jit(solution)/shard_map/ppermute | solution.py:333
  76.7 1.3 %shard_map.146 = (bf16[32,2048]{1,0:T(8,128)(2,1)S(1)}, bf16[32,2048]{1,0:T(8,128)(2,1)S(1)}, bf16[32,2048]{1,0:T(8,128)(2,1)S(1)}, bf16[32,2048]{1,0:T(8,128)(2,1)S(1)}) custom-call(f32[1,1024]{1,0:T(1,128)S(1)} %copy-done.5, bf16[1,2048,1024]{2,1,0:T(8,128)(2,1)S(1)} %copy-done, bf16[1,1024,2048]{2,1,0:T(8,128)(2,1)S(1)} %copy-done.1, ...), custom_call_target="tpu_custom_call" | custom-call | flops 1073741824 | bytes 9441280 | tf_op jit(solution)/shard_map/pallas_call | solution.py:41
  78.1 0.5 collective-permute-done.16.refs_1_
  78.6 1.4 %collective-permute-done.14.refs_0_ = bf16[32,2048]{1,0:T(8,128)(2,1)S(1)} collective-permute-done((bf16[32,2048]{1,0:T(8,128)(2,1)S(1)}, bf16[32,2048]{1,0:T(8,128)(2,1)S(1)}, u32[]{:S(2)}, u32[]{:S(2)}) %collective-permute-start.14) | collective-permute-done | bytes 131104 | tf_op jit(solution)/shard_map/ppermute | solution.py:333
  80.0 1.3 %shard_map.147 = (bf16[32,2048]{1,0:T(8,128)(2,1)S(1)}, bf16[32,2048]{1,0:T(8,128)(2,1)S(1)}, bf16[32,2048]{1,0:T(8,128)(2,1)S(1)}, bf16[32,2048]{1,0:T(8,128)(2,1)S(1)}) custom-call(f32[1,1024]{1,0:T(1,128)S(1)} %copy-done.5, bf16[1,2048,1024]{2,1,0:T(8,128)(2,1)S(1)} %copy-done, bf16[1,1024,2048]{2,1,0:T(8,128)(2,1)S(1)} %copy-done.1, ...), custom_call_target="tpu_custom_call" | custom-call | flops 1073741824 | bytes 9572352 | tf_op jit(solution)/shard_map/pallas_call | solution.py:41
  81.3 0.9 collective-permute-start.17
  82.2 1.2 %collective-permute-start.21 = (bf16[32,2048]{1,0:T(8,128)(2,1)S(1)}, bf16[32,2048]{1,0:T(8,128)(2,1)S(1)}, u32[]{:S(2)}, u32[]{:S(2)}) collective-permute-start(bf16[32,2048]{1,0:T(8,128)(2,1)S(1)} %get-tuple-element.73), channel_id=1, source_target_pairs={{0,8},{8,0},{16,24},{24,16},{1,9},{9,1},{17,25},{25,17},{2,10},{10... | collective-permute-start | bytes 393224 | tf_op jit(solution)/shard_map/ppermute | solution.py:333
  83.4 0.8 collective-permute-start.12
  84.3 3.1 %collective-permute-done.17.first_ref = bf16[32,2048]{1,0:T(8,128)(2,1)S(1)} collective-permute-done((bf16[32,2048]{1,0:T(8,128)(2,1)S(1)}, bf16[32,2048]{1,0:T(8,128)(2,1)S(1)}, u32[]{:S(2)}, u32[]{:S(2)}) %collective-permute-start.17) | collective-permute-done | bytes 131104 | tf_op jit(solution)/shard_map/ppermute | solution.py:333
  87.4 4.2 %collective-permute-start.18 = (bf16[32,2048]{1,0:T(8,128)(2,1)S(1)}, bf16[32,2048]{1,0:T(8,128)(2,1)S(1)}, u32[]{:S(2)}, u32[]{:S(2)}) collective-permute-start(bf16[32,2048]{1,0:T(8,128)(2,1)S(1)} %shard_map.148), channel_id=1, source_target_pairs={{0,16},{8,24},{16,0},{24,8},{1,17},{9,25},{17,1},{25,9},{2,18},{10... | collective-permute-start | bytes 393224 | tf_op jit(solution)/shard_map/ppermute | solution.py:333
  91.6 2.2 %collective-permute-start.20 = (bf16[32,2048]{1,0:T(8,128)(2,1)S(1)}, bf16[32,2048]{1,0:T(8,128)(2,1)S(1)}, u32[]{:S(2)}, u32[]{:S(2)}) collective-permute-start(bf16[32,2048]{1,0:T(8,128)(2,1)S(1)} %get-tuple-element.72), channel_id=1, source_target_pairs={{0,8},{8,0},{16,24},{24,16},{1,9},{9,1},{17,25},{25,17},{2,10},{10... | collective-permute-start | bytes 393224 | tf_op jit(solution)/shard_map/ppermute | solution.py:333
  93.8 2.3 %collective-permute-start.22 = (bf16[32,2048]{1,0:T(8,128)(2,1)S(1)}, bf16[32,2048]{1,0:T(8,128)(2,1)S(1)}, u32[]{:S(2)}, u32[]{:S(2)}) collective-permute-start(bf16[32,2048]{1,0:T(8,128)(2,1)S(1)} %shard_map.150), channel_id=1, source_target_pairs={{0,16},{8,24},{16,0},{24,8},{1,17},{9,25},{17,1},{25,9},{2,18},{10... | collective-permute-start | bytes 393224 | tf_op jit(solution)/shard_map/ppermute | solution.py:333
  96.1 1.8 %collective-permute-done.18.refs_1_ = bf16[32,2048]{1,0:T(8,128)(2,1)S(1)} collective-permute-done((bf16[32,2048]{1,0:T(8,128)(2,1)S(1)}, bf16[32,2048]{1,0:T(8,128)(2,1)S(1)}, u32[]{:S(2)}, u32[]{:S(2)}) %collective-permute-start.18) | collective-permute-done | bytes 131104 | tf_op jit(solution)/shard_map/ppermute | solution.py:333
  98.3 3.3 %collective-permute-done.22.refs_1_ = bf16[32,2048]{1,0:T(8,128)(2,1)S(1)} collective-permute-done((bf16[32,2048]{1,0:T(8,128)(2,1)S(1)}, bf16[32,2048]{1,0:T(8,128)(2,1)S(1)}, u32[]{:S(2)}, u32[]{:S(2)}) %collective-permute-start.22) | collective-permute-done | bytes 131104 | tf_op jit(solution)/shard_map/ppermute | solution.py:333
  101.8 1.2 %collective-permute-start.24 = (bf16[16,2048]{1,0:T(8,128)(2,1)S(1)}, bf16[16,2048]{1,0:T(8,128)(2,1)S(1)}, u32[]{:S(2)}, u32[]{:S(2)}) collective-permute-start(bf16[16,2048]{1,0:T(8,128)(2,1)S(1)} %get-tuple-element.76), channel_id=1, source_target_pairs={{0,6},{1,7},{2,4},{3,5},{4,2},{5,3},{6,0},{7,1},{8,14},{9,15},{10,... | collective-permute-start | bytes 196616 | tf_op jit(solution)/shard_map/ppermute | solution.py:333
  103.0 3.0 %collective-permute-done.23.refs_2_ = bf16[16,2048]{1,0:T(8,128)(2,1)S(1)} collective-permute-done((bf16[16,2048]{1,0:T(8,128)(2,1)S(1)}, bf16[16,2048]{1,0:T(8,128)(2,1)S(1)}, u32[]{:S(2)}, u32[]{:S(2)}) %collective-permute-start.23) | collective-permute-done | bytes 65568 | tf_op jit(solution)/shard_map/ppermute | solution.py:333
  106.1 1.0 collective-permute-done.24.refs_3_
  107.1 1.3 %collective-permute-done.25.refs_1_ = bf16[32,2048]{1,0:T(8,128)(2,1)S(1)} collective-permute-done((bf16[32,2048]{1,0:T(8,128)(2,1)S(1)}, bf16[32,2048]{1,0:T(8,128)(2,1)S(1)}, u32[]{:S(2)}, u32[]{:S(2)}) %collective-permute-start.25) | collective-permute-done | bytes 131104 | tf_op jit(solution)/shard_map/ppermute | solution.py:333
  108.5 1.1 shard_map.153
  (44 shorter events, 2.3 us)
Async XLA Ops:
  0.0 49.2 %copy-start.7 = (f32[2048]{0:T(1024)S(1)}, f32[2048]{0:T(1024)}, u32[]{:S(2)}) copy-start(f32[2048]{0:T(1024)} %param.23) | copy-start | bytes 24580
  0.0 49.2 %copy-start.6 = (f32[2048]{0:T(1024)S(1)}, f32[2048]{0:T(1024)}, u32[]{:S(2)}) copy-start(f32[2048]{0:T(1024)} %param.22) | copy-start | bytes 24580
  2.8 12.7 %collective-permute-start = (bf16[32,4224]{1,0:T(8,128)(2,1)}, bf16[32,4224]{1,0:T(8,128)(2,1)S(1)}, u32[]{:S(2)}, u32[]{:S(2)}) collective-permute-start(bf16[32,4224]{1,0:T(8,128)(2,1)} %get-tuple-element.47), channel_id=1, source_target_pairs={{0,8},{8,16},{16,24},{24,0},{1,9},{9,17},{17,25},{25,1},{2,10},{10... | collective-permute-start | bytes 811016 | tf_op jit(solution)/shard_map/ppermute | solution.py:262
  5.8 21.3 %collective-permute-start.1 = (bf16[32,4224]{1,0:T(8,128)(2,1)}, bf16[32,4224]{1,0:T(8,128)(2,1)S(1)}, u32[]{:S(2)}, u32[]{:S(2)}) collective-permute-start(bf16[32,4224]{1,0:T(8,128)(2,1)} %get-tuple-element.48), channel_id=1, source_target_pairs={{0,16},{8,24},{16,0},{24,8},{1,17},{9,25},{17,1},{25,9},{2,18},{10... | collective-permute-start | bytes 811016 | tf_op jit(solution)/shard_map/ppermute | solution.py:262
  8.4 18.7 %collective-permute-start.2 = (bf16[32,4224]{1,0:T(8,128)(2,1)}, bf16[32,4224]{1,0:T(8,128)(2,1)S(1)}, u32[]{:S(2)}, u32[]{:S(2)}) collective-permute-start(bf16[32,4224]{1,0:T(8,128)(2,1)} %get-tuple-element.49), channel_id=1, source_target_pairs={{0,24},{8,0},{16,8},{24,16},{1,25},{9,1},{17,9},{25,17},{2,26},{10... | collective-permute-start | bytes 811016 | tf_op jit(solution)/shard_map/ppermute | solution.py:262
  12.3 20.4 %collective-permute-start.3 = (bf16[32,4096]{1,0:T(8,128)(2,1)}, bf16[32,4096]{1,0:T(8,128)(2,1)S(1)}, u32[]{:S(2)}, u32[]{:S(2)}) collective-permute-start(bf16[32,4096]{1,0:T(8,128)(2,1)} %get-tuple-element.54), channel_id=1, source_target_pairs={{0,8},{8,16},{16,24},{24,0},{1,9},{9,17},{17,25},{25,1},{2,10},{10... | collective-permute-start | bytes 786440 | tf_op jit(solution)/shard_map/ppermute | solution.py:262
  13.0 35.9 %collective-permute-start.4 = (bf16[32,4096]{1,0:T(8,128)(2,1)}, bf16[32,4096]{1,0:T(8,128)(2,1)S(1)}, u32[]{:S(2)}, u32[]{:S(2)}) collective-permute-start(bf16[32,4096]{1,0:T(8,128)(2,1)} %get-tuple-element.55), channel_id=1, source_target_pairs={{0,16},{8,24},{16,0},{24,8},{1,17},{9,25},{17,1},{25,9},{2,18},{10... | collective-permute-start | bytes 786440 | tf_op jit(solution)/shard_map/ppermute | solution.py:262
  15.5 33.4 %collective-permute-start.5 = (bf16[32,4096]{1,0:T(8,128)(2,1)}, bf16[32,4096]{1,0:T(8,128)(2,1)S(1)}, u32[]{:S(2)}, u32[]{:S(2)}) collective-permute-start(bf16[32,4096]{1,0:T(8,128)(2,1)} %get-tuple-element.56), channel_id=1, source_target_pairs={{0,24},{8,0},{16,8},{24,16},{1,25},{9,1},{17,9},{25,17},{2,26},{10... | collective-permute-start | bytes 786440 | tf_op jit(solution)/shard_map/ppermute | solution.py:262
  18.0 1.0 copy-start.2
  18.9 0.9 copy-start.4
  19.9 0.7 copy-start.8
  20.5 0.7 copy-start.9
  21.2 0.7 copy-start.10
  27.1 49.6 %copy-start = (bf16[1,2048,1024]{2,1,0:T(8,128)(2,1)S(1)}, bf16[1,2048,1024]{2,1,0:T(8,128)(2,1)}, u32[]{:S(2)}) copy-start(bf16[1,2048,1024]{2,1,0:T(8,128)(2,1)} %w_in_ref.3) | copy-start | bytes 12582916
  27.1 49.6 %copy-start.1 = (bf16[1,1024,2048]{2,1,0:T(8,128)(2,1)S(1)}, bf16[1,1024,2048]{2,1,0:T(8,128)(2,1)}, u32[]{:S(2)}) copy-start(bf16[1,1024,2048]{2,1,0:T(8,128)(2,1)} %w_out_ref.3) | copy-start | bytes 12582916
  27.1 49.6 %copy-start.5 = (f32[1,1024]{1,0:T(1,128)S(1)}, f32[1,1024]{1,0:T(1,128)}, u32[]{:S(2)}) copy-start(f32[1,1024]{1,0:T(1,128)} %bias_ref.5) | copy-start | bytes 12292
  50.0 1.4 %collective-permute-start.6 = (bf16[32,2048]{1,0:T(8,128)(2,1)S(1)}, bf16[32,2048]{1,0:T(8,128)(2,1)S(1)}, u32[]{:S(2)}, u32[]{:S(2)}) collective-permute-start(bf16[32,2048]{1,0:T(8,128)(2,1)S(1)} %get-tuple-element.60), channel_id=1, source_target_pairs={{0,1},{1,0},{2,3},{3,2},{4,5},{5,4},{6,7},{7,6},{8,9},{9,8},{10,11... | collective-permute-start | bytes 393224 | tf_op jit(solution)/shard_map/ppermute | solution.py:333
  51.5 4.3 %collective-permute-start.9 = (bf16[16,2048]{1,0:T(8,128)(2,1)S(1)}, bf16[16,2048]{1,0:T(8,128)(2,1)S(1)}, u32[]{:S(2)}, u32[]{:S(2)}) collective-permute-start(bf16[16,2048]{1,0:T(8,128)(2,1)S(1)} %get-tuple-element.64), channel_id=1, source_target_pairs={{0,2},{1,3},{2,0},{3,1},{4,6},{5,7},{6,4},{7,5},{8,10},{9,11},{10,... | collective-permute-start | bytes 196616 | tf_op jit(solution)/shard_map/ppermute | solution.py:333
  53.0 8.0 %collective-permute-start.7 = (bf16[16,2048]{1,0:T(8,128)(2,1)S(1)}, bf16[16,2048]{1,0:T(8,128)(2,1)S(1)}, u32[]{:S(2)}, u32[]{:S(2)}) collective-permute-start(bf16[16,2048]{1,0:T(8,128)(2,1)S(1)} %get-tuple-element.61), channel_id=1, source_target_pairs={{0,4},{1,5},{2,6},{3,7},{4,0},{5,1},{6,2},{7,3},{8,12},{9,13},{10,... | collective-permute-start | bytes 196616 | tf_op jit(solution)/shard_map/ppermute | solution.py:333
  54.5 6.5 %collective-permute-start.8 = (bf16[16,2048]{1,0:T(8,128)(2,1)S(1)}, bf16[16,2048]{1,0:T(8,128)(2,1)S(1)}, u32[]{:S(2)}, u32[]{:S(2)}) collective-permute-start(bf16[16,2048]{1,0:T(8,128)(2,1)S(1)} %get-tuple-element.62), channel_id=1, source_target_pairs={{0,6},{1,7},{2,4},{3,5},{4,2},{5,3},{6,0},{7,1},{8,14},{9,15},{10,... | collective-permute-start | bytes 196616 | tf_op jit(solution)/shard_map/ppermute | solution.py:333
  55.8 11.7 %collective-permute-start.15 = (bf16[32,2048]{1,0:T(8,128)(2,1)S(1)}, bf16[32,2048]{1,0:T(8,128)(2,1)S(1)}, u32[]{:S(2)}, u32[]{:S(2)}) collective-permute-start(bf16[32,2048]{1,0:T(8,128)(2,1)S(1)} %shard_map.145.refs_1_), channel_id=1, source_target_pairs={{0,16},{8,24},{16,0},{24,8},{1,17},{9,25},{17,1},{25,9},{2,18},{10... | collective-permute-start | bytes 393224 | tf_op jit(solution)/shard_map/ppermute | solution.py:333
  61.1 11.2 %collective-permute-start.13 = (bf16[32,2048]{1,0:T(8,128)(2,1)S(1)}, bf16[32,2048]{1,0:T(8,128)(2,1)S(1)}, u32[]{:S(2)}, u32[]{:S(2)}) collective-permute-start(bf16[32,2048]{1,0:T(8,128)(2,1)S(1)} %shard_map.144.refs_0_), channel_id=1, source_target_pairs={{0,16},{8,24},{16,0},{24,8},{1,17},{9,25},{17,1},{25,9},{2,18},{10... | collective-permute-start | bytes 393224 | tf_op jit(solution)/shard_map/ppermute | solution.py:333
  64.9 9.0 %collective-permute-start.11 = (bf16[32,2048]{1,0:T(8,128)(2,1)S(1)}, bf16[32,2048]{1,0:T(8,128)(2,1)S(1)}, u32[]{:S(2)}, u32[]{:S(2)}) collective-permute-start(bf16[32,2048]{1,0:T(8,128)(2,1)S(1)} %shard_map.145.refs_1_), channel_id=1, source_target_pairs={{0,8},{8,0},{16,24},{24,16},{1,9},{9,1},{17,25},{25,17},{2,10},{10... | collective-permute-start | bytes 393224 | tf_op jit(solution)/shard_map/ppermute | solution.py:333
  67.4 9.3 %collective-permute-start.10 = (bf16[32,2048]{1,0:T(8,128)(2,1)S(1)}, bf16[32,2048]{1,0:T(8,128)(2,1)S(1)}, u32[]{:S(2)}, u32[]{:S(2)}) collective-permute-start(bf16[32,2048]{1,0:T(8,128)(2,1)S(1)} %shard_map.144.refs_0_), channel_id=1, source_target_pairs={{0,8},{8,0},{16,24},{24,16},{1,9},{9,1},{17,25},{25,17},{2,10},{10... | collective-permute-start | bytes 393224 | tf_op jit(solution)/shard_map/ppermute | solution.py:333
  67.5 11.1 %collective-permute-start.16 = (bf16[32,2048]{1,0:T(8,128)(2,1)S(1)}, bf16[32,2048]{1,0:T(8,128)(2,1)S(1)}, u32[]{:S(2)}, u32[]{:S(2)}) collective-permute-start(bf16[32,2048]{1,0:T(8,128)(2,1)S(1)} %collective-permute-done.15.refs_3_), channel_id=1, source_target_pairs={{0,8},{8,0},{16,24},{24,16},{1,9},{9,1},{17,25},{25,17},{2,10},{10... | collective-permute-start | bytes 393224 | tf_op jit(solution)/shard_map/ppermute | solution.py:333
  72.3 7.7 %collective-permute-start.14 = (bf16[32,2048]{1,0:T(8,128)(2,1)S(1)}, bf16[32,2048]{1,0:T(8,128)(2,1)S(1)}, u32[]{:S(2)}, u32[]{:S(2)}) collective-permute-start(bf16[32,2048]{1,0:T(8,128)(2,1)S(1)} %collective-permute-done.13.refs_2_), channel_id=1, source_target_pairs={{0,8},{8,0},{16,24},{24,16},{1,9},{9,1},{17,25},{25,17},{2,10},{10... | collective-permute-start | bytes 393224 | tf_op jit(solution)/shard_map/ppermute | solution.py:333
  80.0 17.9 %copy-start.3 = (f32[8,2048]{1,0:T(8,128)S(1)}, f32[8,2048]{1,0:T(8,128)}, u32[]{:S(2)}) copy-start(f32[8,2048]{1,0:T(8,128)} %bias_ref.7) | copy-start | bytes 196612
  81.3 6.0 %collective-permute-start.17 = (bf16[32,2048]{1,0:T(8,128)(2,1)S(1)}, bf16[32,2048]{1,0:T(8,128)(2,1)S(1)}, u32[]{:S(2)}, u32[]{:S(2)}) collective-permute-start(bf16[32,2048]{1,0:T(8,128)(2,1)S(1)} %get-tuple-element.68), channel_id=1, source_target_pairs={{0,8},{8,0},{16,24},{24,16},{1,9},{9,1},{17,25},{25,17},{2,10},{10... | collective-permute-start | bytes 393224 | tf_op jit(solution)/shard_map/ppermute | solution.py:333
  82.2 11.5 %collective-permute-start.21 = (bf16[32,2048]{1,0:T(8,128)(2,1)S(1)}, bf16[32,2048]{1,0:T(8,128)(2,1)S(1)}, u32[]{:S(2)}, u32[]{:S(2)}) collective-permute-start(bf16[32,2048]{1,0:T(8,128)(2,1)S(1)} %get-tuple-element.73), channel_id=1, source_target_pairs={{0,8},{8,0},{16,24},{24,16},{1,9},{9,1},{17,25},{25,17},{2,10},{10... | collective-permute-start | bytes 393224 | tf_op jit(solution)/shard_map/ppermute | solution.py:333
  83.4 12.7 %collective-permute-start.12 = (bf16[32,2048]{1,0:T(8,128)(2,1)S(1)}, bf16[32,2048]{1,0:T(8,128)(2,1)S(1)}, u32[]{:S(2)}, u32[]{:S(2)}) collective-permute-start(bf16[32,2048]{1,0:T(8,128)(2,1)S(1)} %get-tuple-element.65), channel_id=1, source_target_pairs={{0,8},{8,0},{16,24},{24,16},{1,9},{9,1},{17,25},{25,17},{2,10},{10... | collective-permute-start | bytes 393224 | tf_op jit(solution)/shard_map/ppermute | solution.py:333
  87.4 10.5 %collective-permute-start.18 = (bf16[32,2048]{1,0:T(8,128)(2,1)S(1)}, bf16[32,2048]{1,0:T(8,128)(2,1)S(1)}, u32[]{:S(2)}, u32[]{:S(2)}) collective-permute-start(bf16[32,2048]{1,0:T(8,128)(2,1)S(1)} %shard_map.148), channel_id=1, source_target_pairs={{0,16},{8,24},{16,0},{24,8},{1,17},{9,25},{17,1},{25,9},{2,18},{10... | collective-permute-start | bytes 393224 | tf_op jit(solution)/shard_map/ppermute | solution.py:333
  91.6 6.7 %collective-permute-start.20 = (bf16[32,2048]{1,0:T(8,128)(2,1)S(1)}, bf16[32,2048]{1,0:T(8,128)(2,1)S(1)}, u32[]{:S(2)}, u32[]{:S(2)}) collective-permute-start(bf16[32,2048]{1,0:T(8,128)(2,1)S(1)} %get-tuple-element.72), channel_id=1, source_target_pairs={{0,8},{8,0},{16,24},{24,16},{1,9},{9,1},{17,25},{25,17},{2,10},{10... | collective-permute-start | bytes 393224 | tf_op jit(solution)/shard_map/ppermute | solution.py:333
  93.8 7.8 %collective-permute-start.22 = (bf16[32,2048]{1,0:T(8,128)(2,1)S(1)}, bf16[32,2048]{1,0:T(8,128)(2,1)S(1)}, u32[]{:S(2)}, u32[]{:S(2)}) collective-permute-start(bf16[32,2048]{1,0:T(8,128)(2,1)S(1)} %shard_map.150), channel_id=1, source_target_pairs={{0,16},{8,24},{16,0},{24,8},{1,17},{9,25},{17,1},{25,9},{2,18},{10... | collective-permute-start | bytes 393224 | tf_op jit(solution)/shard_map/ppermute | solution.py:333
  98.0 5.0 %collective-permute-start.19 = (bf16[16,2048]{1,0:T(8,128)(2,1)S(1)}, bf16[16,2048]{1,0:T(8,128)(2,1)S(1)}, u32[]{:S(2)}, u32[]{:S(2)}) collective-permute-start(bf16[16,2048]{1,0:T(8,128)(2,1)S(1)} %get-tuple-element.71), channel_id=1, source_target_pairs={{0,2},{1,3},{2,0},{3,1},{4,6},{5,7},{6,4},{7,5},{8,10},{9,11},{10,... | collective-permute-start | bytes 196616 | tf_op jit(solution)/shard_map/ppermute | solution.py:333
  101.7 4.3 %collective-permute-start.23 = (bf16[16,2048]{1,0:T(8,128)(2,1)S(1)}, bf16[16,2048]{1,0:T(8,128)(2,1)S(1)}, u32[]{:S(2)}, u32[]{:S(2)}) collective-permute-start(bf16[16,2048]{1,0:T(8,128)(2,1)S(1)} %get-tuple-element.75), channel_id=1, source_target_pairs={{0,4},{1,5},{2,6},{3,7},{4,0},{5,1},{6,2},{7,3},{8,12},{9,13},{10,... | collective-permute-start | bytes 196616 | tf_op jit(solution)/shard_map/ppermute | solution.py:333
  101.8 5.2 %collective-permute-start.24 = (bf16[16,2048]{1,0:T(8,128)(2,1)S(1)}, bf16[16,2048]{1,0:T(8,128)(2,1)S(1)}, u32[]{:S(2)}, u32[]{:S(2)}) collective-permute-start(bf16[16,2048]{1,0:T(8,128)(2,1)S(1)} %get-tuple-element.76), channel_id=1, source_target_pairs={{0,6},{1,7},{2,4},{3,5},{4,2},{5,3},{6,0},{7,1},{8,14},{9,15},{10,... | collective-permute-start | bytes 196616 | tf_op jit(solution)/shard_map/ppermute | solution.py:333
  107.1 1.4 %collective-permute-start.25 = (bf16[32,2048]{1,0:T(8,128)(2,1)S(1)}, bf16[32,2048]{1,0:T(8,128)(2,1)S(1)}, u32[]{:S(2)}, u32[]{:S(2)}) collective-permute-start(bf16[32,2048]{1,0:T(8,128)(2,1)S(1)} %get-tuple-element.78), channel_id=1, source_target_pairs={{0,1},{1,0},{2,3},{3,2},{4,5},{5,4},{6,7},{7,6},{8,9},{9,8},{10,11... | collective-permute-start | bytes 393224 | tf_op jit(solution)/shard_map/ppermute | solution.py:333

commit v8 on v7

--- a/solution.py
+++ b/solution.py
@@ -341,8 +341,11 @@
         own = [call(join_kernel, bf16(half), *pieces[n : n + 2]) for n in (2, 0)]
         far = [swap(x, 2) for x in own]
         near = [swap(x, 1) for x in own]
-        *own_share, near_first, near_second = apply(own + near)
-        *corner_share, far_first, far_second = apply([swap(x, 1) for x in far] + far, after=own_share[:1])
+        early_share, near_second = apply([own[1], near[1]])
+        late_share, near_first = apply([own[0], near[0]], after=[early_share])
+        own_share = [late_share, early_share]
+        far_first, far_second = apply(far, after=[late_share])
+        corner_share = apply([swap(x, 1) for x in far], after=[far_first])
         near_shares = [swap(near_first, 1), swap(near_second, 1)]
         far_shares = [far_first, far_second]
         pieces = ()

time: 110 us -> 109 us (level)
  starting transfers between devices: 42.9 us -> 38 us
  Pallas kernels: 12.3 us -> 16 us
    ppermute x20, starting transfers between devices: 32.4 us -> 27.5 us  [swap(): lax.ppermute(x, axis, [(i, i ^ distance) for i in range(lax.axis_size(axi...]
    pallas_call x18 -> x20, Pallas kernels: 12.3 us -> 16 us  [call(): pl.pallas_call(body, out_shape=out_shape, compiler_params=pltpu.CompilerP...]
  transfers between devices with their start and end apart: 26 -> 26, of which waited for: 18 -> 16; matrix products, arithmetic and copies ran while one was open for 0% -> 0% of each run, Pallas kernels for 5% -> 9%
where the time goes in v8:
time: 109 us
  waiting for transfers between devices  50.7 us (47%)
  starting transfers between devices  38 us (35%)
  Pallas kernels  16 us (15%)
  local copies, waits for them, and re-layouts  3.94 us (4%)
    ppermute x20, starting transfers between devices, swap(): lax.ppermute(x, axis, [(i, i ^ distance) for i in range(lax.axis_size(axi...  27.5 us
    ppermute x6, waiting for transfers between devices, spread(): lax.ppermute(part, 'dp', [(i, (i + n) % dp) for i in range(dp)])  27.3 us
    ppermute x20, waiting for transfers between devices, swap(): lax.ppermute(x, axis, [(i, i ^ distance) for i in range(lax.axis_size(axi...  23.4 us
    pallas_call x20, Pallas kernels, call(): pl.pallas_call(body, out_shape=out_shape, compiler_params=pltpu.CompilerP...  16 us
    ppermute x6, starting transfers between devices, spread(): lax.ppermute(part, 'dp', [(i, (i + n) % dp) for i in range(dp)])  10.5 us
    unnamed x22, local copies, waits for them, and re-layouts  3.94 us
  transfers between devices with their start and end apart: 26, of which 16 were waited for; matrix products, arithmetic and copies ran while one was open for 0% of the time, Pallas kernels for 9%

profile of v8, /device:TPU:0, one launch (start us, length us, event | category | flops | bytes accessed | tf_op | source)
XLA Modules:
  0.0 108.8 jit_solution(1098975548291227730)
XLA Ops:
  0.0 2.7 %shard_map.136 = (bf16[128,128]{1,0:T(8,128)(2,1)}, bf16[32,4224]{1,0:T(8,128)(2,1)}, bf16[32,4224]{1,0:T(8,128)(2,1)}, bf16[32,4224]{1,0:T(8,128)(2,1)}, bf16[32,4224]{1,0:T(8,128)(2,1)}) custom-call(s32[1,128]{1,0:T(1,128)} %bitcast.9, bf16[128,2048]{1,0:T(8,128)(2,1)} %refs_0_.2, bf16[128,2048]{1,0:T(8,128)(2,1)} %refs_1_.2), custom_call_target="tpu_custom_call" | custom-call | bytes 2163200 | tf_op jit(solution)/shard_map/pallas_call | solution.py:41
  2.8 3.0 %collective-permute-start = (bf16[32,4224]{1,0:T(8,128)(2,1)}, bf16[32,4224]{1,0:T(8,128)(2,1)S(1)}, u32[]{:S(2)}, u32[]{:S(2)}) collective-permute-start(bf16[32,4224]{1,0:T(8,128)(2,1)} %get-tuple-element.47), channel_id=1, source_target_pairs={{0,8},{8,16},{16,24},{24,0},{1,9},{9,17},{17,25},{25,1},{2,10},{10... | collective-permute-start | bytes 811016 | tf_op jit(solution)/shard_map/ppermute | solution.py:262
  5.8 2.6 %collective-permute-start.1 = (bf16[32,4224]{1,0:T(8,128)(2,1)}, bf16[32,4224]{1,0:T(8,128)(2,1)S(1)}, u32[]{:S(2)}, u32[]{:S(2)}) collective-permute-start(bf16[32,4224]{1,0:T(8,128)(2,1)} %get-tuple-element.48), channel_id=1, source_target_pairs={{0,16},{8,24},{16,0},{24,8},{1,17},{9,25},{17,1},{25,9},{2,18},{10... | collective-permute-start | bytes 811016 | tf_op jit(solution)/shard_map/ppermute | solution.py:262
  8.4 1.3 %collective-permute-start.2 = (bf16[32,4224]{1,0:T(8,128)(2,1)}, bf16[32,4224]{1,0:T(8,128)(2,1)S(1)}, u32[]{:S(2)}, u32[]{:S(2)}) collective-permute-start(bf16[32,4224]{1,0:T(8,128)(2,1)} %get-tuple-element.49), channel_id=1, source_target_pairs={{0,24},{8,0},{16,8},{24,16},{1,25},{9,1},{17,9},{25,17},{2,26},{10... | collective-permute-start | bytes 811016 | tf_op jit(solution)/shard_map/ppermute | solution.py:262
  9.7 2.6 %shard_map.137 = (bf16[128,128]{1,0:T(8,128)(2,1)}, bf16[32,4096]{1,0:T(8,128)(2,1)}, bf16[32,4096]{1,0:T(8,128)(2,1)}, bf16[32,4096]{1,0:T(8,128)(2,1)}, bf16[32,4096]{1,0:T(8,128)(2,1)}) custom-call(bf16[128,128]{1,0:T(8,128)(2,1)} %get-tuple-element.43.pos_ref, bf16[128,2048]{1,0:T(8,128)(2,1)} %refs_0_.3, bf16[128,2048]{1,0:T(8,128)(2,1)} %refs_1_.3), custom_call_target="tpu_custom_call" | custom-call | bytes 2162688 | tf_op jit(solution)/shard_map/pallas_call | solution.py:41
  12.3 0.7 collective-permute-start.3
  13.3 2.1 %collective-permute-done.refs_1_ = bf16[32,4224]{1,0:T(8,128)(2,1)S(1)} collective-permute-done((bf16[32,4224]{1,0:T(8,128)(2,1)}, bf16[32,4224]{1,0:T(8,128)(2,1)S(1)}, u32[]{:S(2)}, u32[]{:S(2)}) %collective-permute-start) | collective-permute-done | bytes 270368 | tf_op jit(solution)/shard_map/ppermute | solution.py:262
  15.5 2.5 %collective-permute-start.5 = (bf16[32,4096]{1,0:T(8,128)(2,1)}, bf16[32,4096]{1,0:T(8,128)(2,1)S(1)}, u32[]{:S(2)}, u32[]{:S(2)}) collective-permute-start(bf16[32,4096]{1,0:T(8,128)(2,1)} %get-tuple-element.56), channel_id=1, source_target_pairs={{0,24},{8,0},{16,8},{24,16},{1,25},{9,1},{17,9},{25,17},{2,26},{10... | collective-permute-start | bytes 786440 | tf_op jit(solution)/shard_map/ppermute | solution.py:262
  17.9 1.0 copy-done.2
  18.9 0.9 copy-done.4
  19.9 0.7 copy-done.8
  20.5 0.7 copy-done.9
  21.2 0.7 copy-done.10
  22.1 5.0 %collective-permute-done.1.refs_2_ = bf16[32,4224]{1,0:T(8,128)(2,1)S(1)} collective-permute-done((bf16[32,4224]{1,0:T(8,128)(2,1)}, bf16[32,4224]{1,0:T(8,128)(2,1)S(1)}, u32[]{:S(2)}, u32[]{:S(2)}) %collective-permute-start.1) | collective-permute-done | bytes 270368 | tf_op jit(solution)/shard_map/ppermute | solution.py:262
  27.2 1.5 %shard_map.140.probs_ref = bf16[16,128,128]{2,1,0:T(8,128)(2,1)S(1)} custom-call(bf16[128,128]{1,0:T(8,128)(2,1)S(1)} %get-tuple-element.50.place_ref, f32[128,128]{1,0:T(8,128)S(1)} %get-tuple-element.52.outside_ref, bf16[32,4224]{1,0:T(8,128)(2,1)S(1)} %get-tuple-element.46.refs_0_, bf16[32,4224]{1,0:T(8,128)(2,1)S(1)} %collective-permute-done.refs_1_, ...), custom_call_target="tpu_custom_call" | custom-call | bytes 1703936 | tf_op jit(solution)/shard_map/pallas_call | solution.py:41
  28.7 4.0 %collective-permute-done.3.refs_1_ = bf16[32,4096]{1,0:T(8,128)(2,1)S(1)} collective-permute-done((bf16[32,4096]{1,0:T(8,128)(2,1)}, bf16[32,4096]{1,0:T(8,128)(2,1)S(1)}, u32[]{:S(2)}, u32[]{:S(2)}) %collective-permute-start.3) | collective-permute-done | bytes 262176 | tf_op jit(solution)/shard_map/ppermute | solution.py:262
  32.7 16.2 %collective-permute-done.4.refs_2_ = bf16[32,4096]{1,0:T(8,128)(2,1)S(1)} collective-permute-done((bf16[32,4096]{1,0:T(8,128)(2,1)}, bf16[32,4096]{1,0:T(8,128)(2,1)S(1)}, u32[]{:S(2)}, u32[]{:S(2)}) %collective-permute-start.4) | collective-permute-done | bytes 262176 | tf_op jit(solution)/shard_map/ppermute | solution.py:262
  49.2 0.8 shard_map.142
  50.1 1.3 %collective-permute-done.6.other_ref = bf16[32,2048]{1,0:T(8,128)(2,1)S(1)} collective-permute-done((bf16[32,2048]{1,0:T(8,128)(2,1)S(1)}, bf16[32,2048]{1,0:T(8,128)(2,1)S(1)}, u32[]{:S(2)}, u32[]{:S(2)}) %collective-permute-start.6) | collective-permute-done | bytes 131104 | tf_op jit(solution)/shard_map/ppermute | solution.py:333
  51.4 1.6 %collective-permute-start.10 = (bf16[16,2048]{1,0:T(8,128)(2,1)S(1)}, bf16[16,2048]{1,0:T(8,128)(2,1)S(1)}, u32[]{:S(2)}, u32[]{:S(2)}) collective-permute-start(bf16[16,2048]{1,0:T(8,128)(2,1)S(1)} %get-tuple-element.65), channel_id=1, source_target_pairs={{0,4},{1,5},{2,6},{3,7},{4,0},{5,1},{6,2},{7,3},{8,12},{9,13},{10,... | collective-permute-start | bytes 196616 | tf_op jit(solution)/shard_map/ppermute | solution.py:333
  53.0 1.4 %collective-permute-start.11 = (bf16[16,2048]{1,0:T(8,128)(2,1)S(1)}, bf16[16,2048]{1,0:T(8,128)(2,1)S(1)}, u32[]{:S(2)}, u32[]{:S(2)}) collective-permute-start(bf16[16,2048]{1,0:T(8,128)(2,1)S(1)} %get-tuple-element.66), channel_id=1, source_target_pairs={{0,6},{1,7},{2,4},{3,5},{4,2},{5,3},{6,0},{7,1},{8,14},{9,15},{10,... | collective-permute-start | bytes 196616 | tf_op jit(solution)/shard_map/ppermute | solution.py:333
  54.5 0.5 collective-permute-start.7
  55.0 0.8 collective-permute-done.10.refs_0_
  55.8 3.0 %collective-permute-done.11.refs_1_ = bf16[16,2048]{1,0:T(8,128)(2,1)S(1)} collective-permute-done((bf16[16,2048]{1,0:T(8,128)(2,1)S(1)}, bf16[16,2048]{1,0:T(8,128)(2,1)S(1)}, u32[]{:S(2)}, u32[]{:S(2)}) %collective-permute-start.11) | collective-permute-done | bytes 65568 | tf_op jit(solution)/shard_map/ppermute | solution.py:333
  58.8 5.2 %collective-permute-start.12 = (bf16[32,2048]{1,0:T(8,128)(2,1)S(1)}, bf16[32,2048]{1,0:T(8,128)(2,1)S(1)}, u32[]{:S(2)}, u32[]{:S(2)}) collective-permute-start(bf16[32,2048]{1,0:T(8,128)(2,1)S(1)} %shard_map.146.refs_0_), channel_id=1, source_target_pairs={{0,16},{8,24},{16,0},{24,8},{1,17},{9,25},{17,1},{25,9},{2,18},{10... | collective-permute-start | bytes 393224 | tf_op jit(solution)/shard_map/ppermute | solution.py:333
  64.1 3.8 %collective-permute-start.8 = (bf16[32,2048]{1,0:T(8,128)(2,1)S(1)}, bf16[32,2048]{1,0:T(8,128)(2,1)S(1)}, u32[]{:S(2)}, u32[]{:S(2)}) collective-permute-start(bf16[32,2048]{1,0:T(8,128)(2,1)S(1)} %shard_map.144.refs_0_), channel_id=1, source_target_pairs={{0,8},{8,0},{16,24},{24,16},{1,9},{9,1},{17,25},{25,17},{2,10},{10... | collective-permute-start | bytes 393224 | tf_op jit(solution)/shard_map/ppermute | solution.py:333
  68.0 5.3 %collective-permute-done.12.refs_0_ = bf16[32,2048]{1,0:T(8,128)(2,1)S(1)} collective-permute-done((bf16[32,2048]{1,0:T(8,128)(2,1)S(1)}, bf16[32,2048]{1,0:T(8,128)(2,1)S(1)}, u32[]{:S(2)}, u32[]{:S(2)}) %collective-permute-start.12) | collective-permute-done | bytes 131104 | tf_op jit(solution)/shard_map/ppermute | solution.py:333
  73.2 2.2 %collective-permute-done.14.refs_1_ = bf16[32,2048]{1,0:T(8,128)(2,1)S(1)} collective-permute-done((bf16[32,2048]{1,0:T(8,128)(2,1)S(1)}, bf16[32,2048]{1,0:T(8,128)(2,1)S(1)}, u32[]{:S(2)}, u32[]{:S(2)}) %collective-permute-start.14) | collective-permute-done | bytes 131104 | tf_op jit(solution)/shard_map/ppermute | solution.py:333
  75.4 1.6 %shard_map.145 = (bf16[32,2048]{1,0:T(8,128)(2,1)S(1)}, bf16[32,2048]{1,0:T(8,128)(2,1)S(1)}) custom-call(f32[1,1024]{1,0:T(1,128)S(1)} %copy-done.5, bf16[1,2048,1024]{2,1,0:T(8,128)(2,1)S(1)} %copy-done, bf16[1,1024,2048]{2,1,0:T(8,128)(2,1)S(1)} %copy-done.1, bf16[32,2048]{1,0:T(8,128)(2,1)S(1)} %shard_map.144.refs_0_, ...), custom_call_target="tpu_custom_call" | custom-call | flops 536870912 | bytes 8916992 | tf_op jit(solution)/shard_map/pallas_call | solution.py:41
  77.0 1.6 %shard_map.147 = (bf16[32,2048]{1,0:T(8,128)(2,1)S(1)}, bf16[32,2048]{1,0:T(8,128)(2,1)S(1)}) custom-call(f32[1,1024]{1,0:T(1,128)S(1)} %copy-done.5, bf16[1,2048,1024]{2,1,0:T(8,128)(2,1)S(1)} %copy-done, bf16[1,1024,2048]{2,1,0:T(8,128)(2,1)S(1)} %copy-done.1, bf16[32,2048]{1,0:T(8,128)(2,1)S(1)} %shard_map.146.refs_0_, ...), custom_call_target="tpu_custom_call" | custom-call | flops 536870912 | bytes 9048064 | tf_op jit(solution)/shard_map/pallas_call | solution.py:41
  78.6 1.6 %shard_map.148 = (bf16[32,2048]{1,0:T(8,128)(2,1)S(1)}, bf16[32,2048]{1,0:T(8,128)(2,1)S(1)}) custom-call(f32[1,1024]{1,0:T(1,128)S(1)} %copy-done.5, bf16[1,2048,1024]{2,1,0:T(8,128)(2,1)S(1)} %copy-done, bf16[1,1024,2048]{2,1,0:T(8,128)(2,1)S(1)} %copy-done.1, bf16[32,2048]{1,0:T(8,128)(2,1)S(1)} %collective-permute-done.12.refs_0_, ...), custom_call_target="tpu_custom_call" | custom-call | flops 536870912 | bytes 9048064 | tf_op jit(solution)/shard_map/pallas_call | solution.py:41
  80.2 1.0 collective-permute-done.15.refs_1_
  81.2 1.6 %shard_map.149 = (bf16[32,2048]{1,0:T(8,128)(2,1)S(1)}, bf16[32,2048]{1,0:T(8,128)(2,1)S(1)}) custom-call(f32[1,1024]{1,0:T(1,128)S(1)} %copy-done.5, bf16[1,2048,1024]{2,1,0:T(8,128)(2,1)S(1)} %copy-done, bf16[1,1024,2048]{2,1,0:T(8,128)(2,1)S(1)} %copy-done.1, bf16[32,2048]{1,0:T(8,128)(2,1)S(1)} %collective-permute-done.13.refs_0_, ...), custom_call_target="tpu_custom_call" | custom-call | flops 536870912 | bytes 9048064 | tf_op jit(solution)/shard_map/pallas_call | solution.py:41
  82.8 1.1 %collective-permute-start.21 = (bf16[32,2048]{1,0:T(8,128)(2,1)S(1)}, bf16[32,2048]{1,0:T(8,128)(2,1)S(1)}, u32[]{:S(2)}, u32[]{:S(2)}) collective-permute-start(bf16[32,2048]{1,0:T(8,128)(2,1)S(1)} %get-tuple-element.74), channel_id=1, source_target_pairs={{0,8},{8,0},{16,24},{24,16},{1,9},{9,1},{17,25},{25,17},{2,10},{10... | collective-permute-start | bytes 393224 | tf_op jit(solution)/shard_map/ppermute | solution.py:333
  83.9 1.0 collective-permute-start.17
  84.9 1.0 collective-permute-start.20
  86.0 4.8 %collective-permute-done.21.first_ref = bf16[32,2048]{1,0:T(8,128)(2,1)S(1)} collective-permute-done((bf16[32,2048]{1,0:T(8,128)(2,1)S(1)}, bf16[32,2048]{1,0:T(8,128)(2,1)S(1)}, u32[]{:S(2)}, u32[]{:S(2)}) %collective-permute-start.21) | collective-permute-done | bytes 131104 | tf_op jit(solution)/shard_map/ppermute | solution.py:333
  90.8 2.0 %collective-permute-start.22 = (bf16[32,2048]{1,0:T(8,128)(2,1)S(1)}, bf16[32,2048]{1,0:T(8,128)(2,1)S(1)}, u32[]{:S(2)}, u32[]{:S(2)}) collective-permute-start(bf16[32,2048]{1,0:T(8,128)(2,1)S(1)} %shard_map.152), channel_id=1, source_target_pairs={{0,16},{8,24},{16,0},{24,8},{1,17},{9,25},{17,1},{25,9},{2,18},{10... | collective-permute-start | bytes 393224 | tf_op jit(solution)/shard_map/ppermute | solution.py:333
  92.8 3.0 %collective-permute-start.9 = (bf16[32,2048]{1,0:T(8,128)(2,1)S(1)}, bf16[32,2048]{1,0:T(8,128)(2,1)S(1)}, u32[]{:S(2)}, u32[]{:S(2)}) collective-permute-start(bf16[32,2048]{1,0:T(8,128)(2,1)S(1)} %get-tuple-element.63), channel_id=1, source_target_pairs={{0,8},{8,0},{16,24},{24,16},{1,9},{9,1},{17,25},{25,17},{2,10},{10... | collective-permute-start | bytes 393224 | tf_op jit(solution)/shard_map/ppermute | solution.py:333
  95.8 1.7 %collective-permute-start.18 = (bf16[32,2048]{1,0:T(8,128)(2,1)S(1)}, bf16[32,2048]{1,0:T(8,128)(2,1)S(1)}, u32[]{:S(2)}, u32[]{:S(2)}) collective-permute-start(bf16[32,2048]{1,0:T(8,128)(2,1)S(1)} %shard_map.150), channel_id=1, source_target_pairs={{0,16},{8,24},{16,0},{24,8},{1,17},{9,25},{17,1},{25,9},{2,18},{10... | collective-permute-start | bytes 393224 | tf_op jit(solution)/shard_map/ppermute | solution.py:333
  97.5 0.8 collective-permute-done.20.near_ref
  98.4 0.8 collective-permute-start.23
  99.2 2.4 %collective-permute-start.24 = (bf16[16,2048]{1,0:T(8,128)(2,1)S(1)}, bf16[16,2048]{1,0:T(8,128)(2,1)S(1)}, u32[]{:S(2)}, u32[]{:S(2)}) collective-permute-start(bf16[16,2048]{1,0:T(8,128)(2,1)S(1)} %get-tuple-element.76), channel_id=1, source_target_pairs={{0,6},{1,7},{2,4},{3,5},{4,2},{5,3},{6,0},{7,1},{8,14},{9,15},{10,... | collective-permute-start | bytes 196616 | tf_op jit(solution)/shard_map/ppermute | solution.py:333
  102.0 1.7 %collective-permute-start.19 = (bf16[16,2048]{1,0:T(8,128)(2,1)S(1)}, bf16[16,2048]{1,0:T(8,128)(2,1)S(1)}, u32[]{:S(2)}, u32[]{:S(2)}) collective-permute-start(bf16[16,2048]{1,0:T(8,128)(2,1)S(1)} %get-tuple-element.72), channel_id=1, source_target_pairs={{0,2},{1,3},{2,0},{3,1},{4,6},{5,7},{6,4},{7,5},{8,10},{9,11},{10,... | collective-permute-start | bytes 196616 | tf_op jit(solution)/shard_map/ppermute | solution.py:333
  103.7 0.6 collective-permute-done.24.refs_3_
  104.3 2.0 %collective-permute-done.19.refs_1_ = bf16[16,2048]{1,0:T(8,128)(2,1)S(1)} collective-permute-done((bf16[16,2048]{1,0:T(8,128)(2,1)S(1)}, bf16[16,2048]{1,0:T(8,128)(2,1)S(1)}, u32[]{:S(2)}, u32[]{:S(2)}) %collective-permute-start.19) | collective-permute-done | bytes 65568 | tf_op jit(solution)/shard_map/ppermute | solution.py:333
  106.4 1.3 %collective-permute-done.25.refs_1_ = bf16[32,2048]{1,0:T(8,128)(2,1)S(1)} collective-permute-done((bf16[32,2048]{1,0:T(8,128)(2,1)S(1)}, bf16[32,2048]{1,0:T(8,128)(2,1)S(1)}, u32[]{:S(2)}, u32[]{:S(2)}) %collective-permute-start.25) | collective-permute-done | bytes 131104 | tf_op jit(solution)/shard_map/ppermute | solution.py:333
  107.7 1.1 shard_map.155
  (46 shorter events, 1.9 us)
Async XLA Ops:
  0.0 49.2 %copy-start.7 = (f32[2048]{0:T(1024)S(1)}, f32[2048]{0:T(1024)}, u32[]{:S(2)}) copy-start(f32[2048]{0:T(1024)} %param.23) | copy-start | bytes 24580
  0.0 49.2 %copy-start.6 = (f32[2048]{0:T(1024)S(1)}, f32[2048]{0:T(1024)}, u32[]{:S(2)}) copy-start(f32[2048]{0:T(1024)} %param.22) | copy-start | bytes 24580
  2.8 12.7 %collective-permute-start = (bf16[32,4224]{1,0:T(8,128)(2,1)}, bf16[32,4224]{1,0:T(8,128)(2,1)S(1)}, u32[]{:S(2)}, u32[]{:S(2)}) collective-permute-start(bf16[32,4224]{1,0:T(8,128)(2,1)} %get-tuple-element.47), channel_id=1, source_target_pairs={{0,8},{8,16},{16,24},{24,0},{1,9},{9,17},{17,25},{25,1},{2,10},{10... | collective-permute-start | bytes 811016 | tf_op jit(solution)/shard_map/ppermute | solution.py:262
  5.8 21.3 %collective-permute-start.1 = (bf16[32,4224]{1,0:T(8,128)(2,1)}, bf16[32,4224]{1,0:T(8,128)(2,1)S(1)}, u32[]{:S(2)}, u32[]{:S(2)}) collective-permute-start(bf16[32,4224]{1,0:T(8,128)(2,1)} %get-tuple-element.48), channel_id=1, source_target_pairs={{0,16},{8,24},{16,0},{24,8},{1,17},{9,25},{17,1},{25,9},{2,18},{10... | collective-permute-start | bytes 811016 | tf_op jit(solution)/shard_map/ppermute | solution.py:262
  8.4 18.7 %collective-permute-start.2 = (bf16[32,4224]{1,0:T(8,128)(2,1)}, bf16[32,4224]{1,0:T(8,128)(2,1)S(1)}, u32[]{:S(2)}, u32[]{:S(2)}) collective-permute-start(bf16[32,4224]{1,0:T(8,128)(2,1)} %get-tuple-element.49), channel_id=1, source_target_pairs={{0,24},{8,0},{16,8},{24,16},{1,25},{9,1},{17,9},{25,17},{2,26},{10... | collective-permute-start | bytes 811016 | tf_op jit(solution)/shard_map/ppermute | solution.py:262
  12.3 20.4 %collective-permute-start.3 = (bf16[32,4096]{1,0:T(8,128)(2,1)}, bf16[32,4096]{1,0:T(8,128)(2,1)S(1)}, u32[]{:S(2)}, u32[]{:S(2)}) collective-permute-start(bf16[32,4096]{1,0:T(8,128)(2,1)} %get-tuple-element.54), channel_id=1, source_target_pairs={{0,8},{8,16},{16,24},{24,0},{1,9},{9,17},{17,25},{25,1},{2,10},{10... | collective-permute-start | bytes 786440 | tf_op jit(solution)/shard_map/ppermute | solution.py:262
  13.0 35.9 %collective-permute-start.4 = (bf16[32,4096]{1,0:T(8,128)(2,1)}, bf16[32,4096]{1,0:T(8,128)(2,1)S(1)}, u32[]{:S(2)}, u32[]{:S(2)}) collective-permute-start(bf16[32,4096]{1,0:T(8,128)(2,1)} %get-tuple-element.55), channel_id=1, source_target_pairs={{0,16},{8,24},{16,0},{24,8},{1,17},{9,25},{17,1},{25,9},{2,18},{10... | collective-permute-start | bytes 786440 | tf_op jit(solution)/shard_map/ppermute | solution.py:262
  15.5 33.4 %collective-permute-start.5 = (bf16[32,4096]{1,0:T(8,128)(2,1)}, bf16[32,4096]{1,0:T(8,128)(2,1)S(1)}, u32[]{:S(2)}, u32[]{:S(2)}) collective-permute-start(bf16[32,4096]{1,0:T(8,128)(2,1)} %get-tuple-element.56), channel_id=1, source_target_pairs={{0,24},{8,0},{16,8},{24,16},{1,25},{9,1},{17,9},{25,17},{2,26},{10... | collective-permute-start | bytes 786440 | tf_op jit(solution)/shard_map/ppermute | solution.py:262
  17.9 1.0 copy-start.2
  18.9 0.9 copy-start.4
  19.9 0.7 copy-start.8
  20.5 0.7 copy-start.9
  21.2 0.7 copy-start.10
  27.1 48.3 %copy-start = (bf16[1,2048,1024]{2,1,0:T(8,128)(2,1)S(1)}, bf16[1,2048,1024]{2,1,0:T(8,128)(2,1)}, u32[]{:S(2)}) copy-start(bf16[1,2048,1024]{2,1,0:T(8,128)(2,1)} %w_in_ref.7) | copy-start | bytes 12582916
  27.1 48.3 %copy-start.1 = (bf16[1,1024,2048]{2,1,0:T(8,128)(2,1)S(1)}, bf16[1,1024,2048]{2,1,0:T(8,128)(2,1)}, u32[]{:S(2)}) copy-start(bf16[1,1024,2048]{2,1,0:T(8,128)(2,1)} %w_out_ref.7) | copy-start | bytes 12582916
  27.1 48.3 %copy-start.5 = (f32[1,1024]{1,0:T(1,128)S(1)}, f32[1,1024]{1,0:T(1,128)}, u32[]{:S(2)}) copy-start(f32[1,1024]{1,0:T(1,128)} %bias_ref.9) | copy-start | bytes 12292
  50.0 1.4 %collective-permute-start.6 = (bf16[32,2048]{1,0:T(8,128)(2,1)S(1)}, bf16[32,2048]{1,0:T(8,128)(2,1)S(1)}, u32[]{:S(2)}, u32[]{:S(2)}) collective-permute-start(bf16[32,2048]{1,0:T(8,128)(2,1)S(1)} %get-tuple-element.60), channel_id=1, source_target_pairs={{0,1},{1,0},{2,3},{3,2},{4,5},{5,4},{6,7},{7,6},{8,9},{9,8},{10,11... | collective-permute-start | bytes 393224 | tf_op jit(solution)/shard_map/ppermute | solution.py:333
  51.4 4.3 %collective-permute-start.10 = (bf16[16,2048]{1,0:T(8,128)(2,1)S(1)}, bf16[16,2048]{1,0:T(8,128)(2,1)S(1)}, u32[]{:S(2)}, u32[]{:S(2)}) collective-permute-start(bf16[16,2048]{1,0:T(8,128)(2,1)S(1)} %get-tuple-element.65), channel_id=1, source_target_pairs={{0,4},{1,5},{2,6},{3,7},{4,0},{5,1},{6,2},{7,3},{8,12},{9,13},{10,... | collective-permute-start | bytes 196616 | tf_op jit(solution)/shard_map/ppermute | solution.py:333
  53.0 5.8 %collective-permute-start.11 = (bf16[16,2048]{1,0:T(8,128)(2,1)S(1)}, bf16[16,2048]{1,0:T(8,128)(2,1)S(1)}, u32[]{:S(2)}, u32[]{:S(2)}) collective-permute-start(bf16[16,2048]{1,0:T(8,128)(2,1)S(1)} %get-tuple-element.66), channel_id=1, source_target_pairs={{0,6},{1,7},{2,4},{3,5},{4,2},{5,3},{6,0},{7,1},{8,14},{9,15},{10,... | collective-permute-start | bytes 196616 | tf_op jit(solution)/shard_map/ppermute | solution.py:333
  54.5 9.6 %collective-permute-start.7 = (bf16[16,2048]{1,0:T(8,128)(2,1)S(1)}, bf16[16,2048]{1,0:T(8,128)(2,1)S(1)}, u32[]{:S(2)}, u32[]{:S(2)}) collective-permute-start(bf16[16,2048]{1,0:T(8,128)(2,1)S(1)} %get-tuple-element.62), channel_id=1, source_target_pairs={{0,2},{1,3},{2,0},{3,1},{4,6},{5,7},{6,4},{7,5},{8,10},{9,11},{10,... | collective-permute-start | bytes 196616 | tf_op jit(solution)/shard_map/ppermute | solution.py:333
  58.8 14.4 %collective-permute-start.12 = (bf16[32,2048]{1,0:T(8,128)(2,1)S(1)}, bf16[32,2048]{1,0:T(8,128)(2,1)S(1)}, u32[]{:S(2)}, u32[]{:S(2)}) collective-permute-start(bf16[32,2048]{1,0:T(8,128)(2,1)S(1)} %shard_map.146.refs_0_), channel_id=1, source_target_pairs={{0,16},{8,24},{16,0},{24,8},{1,17},{9,25},{17,1},{25,9},{2,18},{10... | collective-permute-start | bytes 393224 | tf_op jit(solution)/shard_map/ppermute | solution.py:333
  64.0 11.3 %collective-permute-start.14 = (bf16[32,2048]{1,0:T(8,128)(2,1)S(1)}, bf16[32,2048]{1,0:T(8,128)(2,1)S(1)}, u32[]{:S(2)}, u32[]{:S(2)}) collective-permute-start(bf16[32,2048]{1,0:T(8,128)(2,1)S(1)} %shard_map.144.refs_0_), channel_id=1, source_target_pairs={{0,16},{8,24},{16,0},{24,8},{1,17},{9,25},{17,1},{25,9},{2,18},{10... | collective-permute-start | bytes 393224 | tf_op jit(solution)/shard_map/ppermute | solution.py:333
  64.1 11.3 %collective-permute-start.8 = (bf16[32,2048]{1,0:T(8,128)(2,1)S(1)}, bf16[32,2048]{1,0:T(8,128)(2,1)S(1)}, u32[]{:S(2)}, u32[]{:S(2)}) collective-permute-start(bf16[32,2048]{1,0:T(8,128)(2,1)S(1)} %shard_map.144.refs_0_), channel_id=1, source_target_pairs={{0,8},{8,0},{16,24},{24,16},{1,9},{9,1},{17,25},{25,17},{2,10},{10... | collective-permute-start | bytes 393224 | tf_op jit(solution)/shard_map/ppermute | solution.py:333
  67.9 9.1 %collective-permute-start.16 = (bf16[32,2048]{1,0:T(8,128)(2,1)S(1)}, bf16[32,2048]{1,0:T(8,128)(2,1)S(1)}, u32[]{:S(2)}, u32[]{:S(2)}) collective-permute-start(bf16[32,2048]{1,0:T(8,128)(2,1)S(1)} %shard_map.146.refs_0_), channel_id=1, source_target_pairs={{0,8},{8,0},{16,24},{24,16},{1,9},{9,1},{17,25},{25,17},{2,10},{10... | collective-permute-start | bytes 393224 | tf_op jit(solution)/shard_map/ppermute | solution.py:333
  73.2 7.0 %collective-permute-start.13 = (bf16[32,2048]{1,0:T(8,128)(2,1)S(1)}, bf16[32,2048]{1,0:T(8,128)(2,1)S(1)}, u32[]{:S(2)}, u32[]{:S(2)}) collective-permute-start(bf16[32,2048]{1,0:T(8,128)(2,1)S(1)} %collective-permute-done.12.refs_0_), channel_id=1, source_target_pairs={{0,8},{8,0},{16,24},{24,16},{1,9},{9,1},{17,25},{25,17},{2,10},{10... | collective-permute-start | bytes 393224 | tf_op jit(solution)/shard_map/ppermute | solution.py:333
  75.4 5.9 %collective-permute-start.15 = (bf16[32,2048]{1,0:T(8,128)(2,1)S(1)}, bf16[32,2048]{1,0:T(8,128)(2,1)S(1)}, u32[]{:S(2)}, u32[]{:S(2)}) collective-permute-start(bf16[32,2048]{1,0:T(8,128)(2,1)S(1)} %collective-permute-done.14.refs_1_), channel_id=1, source_target_pairs={{0,8},{8,0},{16,24},{24,16},{1,9},{9,1},{17,25},{25,17},{2,10},{10... | collective-permute-start | bytes 393224 | tf_op jit(solution)/shard_map/ppermute | solution.py:333
  81.2 17.1 %copy-start.3 = (f32[8,2048]{1,0:T(8,128)S(1)}, f32[8,2048]{1,0:T(8,128)}, u32[]{:S(2)}) copy-start(f32[8,2048]{1,0:T(8,128)} %bias_ref.11) | copy-start | bytes 196612
  82.8 7.9 %collective-permute-start.21 = (bf16[32,2048]{1,0:T(8,128)(2,1)S(1)}, bf16[32,2048]{1,0:T(8,128)(2,1)S(1)}, u32[]{:S(2)}, u32[]{:S(2)}) collective-permute-start(bf16[32,2048]{1,0:T(8,128)(2,1)S(1)} %get-tuple-element.74), channel_id=1, source_target_pairs={{0,8},{8,0},{16,24},{24,16},{1,9},{9,1},{17,25},{25,17},{2,10},{10... | collective-permute-start | bytes 393224 | tf_op jit(solution)/shard_map/ppermute | solution.py:333
  83.9 11.8 %collective-permute-start.17 = (bf16[32,2048]{1,0:T(8,128)(2,1)S(1)}, bf16[32,2048]{1,0:T(8,128)(2,1)S(1)}, u32[]{:S(2)}, u32[]{:S(2)}) collective-permute-start(bf16[32,2048]{1,0:T(8,128)(2,1)S(1)} %get-tuple-element.69), channel_id=1, source_target_pairs={{0,8},{8,0},{16,24},{24,16},{1,9},{9,1},{17,25},{25,17},{2,10},{10... | collective-permute-start | bytes 393224 | tf_op jit(solution)/shard_map/ppermute | solution.py:333
  84.9 13.4 %collective-permute-start.20 = (bf16[32,2048]{1,0:T(8,128)(2,1)S(1)}, bf16[32,2048]{1,0:T(8,128)(2,1)S(1)}, u32[]{:S(2)}, u32[]{:S(2)}) collective-permute-start(bf16[32,2048]{1,0:T(8,128)(2,1)S(1)} %get-tuple-element.73), channel_id=1, source_target_pairs={{0,8},{8,0},{16,24},{24,16},{1,9},{9,1},{17,25},{25,17},{2,10},{10... | collective-permute-start | bytes 393224 | tf_op jit(solution)/shard_map/ppermute | solution.py:333
  90.8 7.5 %collective-permute-start.22 = (bf16[32,2048]{1,0:T(8,128)(2,1)S(1)}, bf16[32,2048]{1,0:T(8,128)(2,1)S(1)}, u32[]{:S(2)}, u32[]{:S(2)}) collective-permute-start(bf16[32,2048]{1,0:T(8,128)(2,1)S(1)} %shard_map.152), channel_id=1, source_target_pairs={{0,16},{8,24},{16,0},{24,8},{1,17},{9,25},{17,1},{25,9},{2,18},{10... | collective-permute-start | bytes 393224 | tf_op jit(solution)/shard_map/ppermute | solution.py:333
  92.8 8.8 %collective-permute-start.9 = (bf16[32,2048]{1,0:T(8,128)(2,1)S(1)}, bf16[32,2048]{1,0:T(8,128)(2,1)S(1)}, u32[]{:S(2)}, u32[]{:S(2)}) collective-permute-start(bf16[32,2048]{1,0:T(8,128)(2,1)S(1)} %get-tuple-element.63), channel_id=1, source_target_pairs={{0,8},{8,0},{16,24},{24,16},{1,9},{9,1},{17,25},{25,17},{2,10},{10... | collective-permute-start | bytes 393224 | tf_op jit(solution)/shard_map/ppermute | solution.py:333
  95.8 6.1 %collective-permute-start.18 = (bf16[32,2048]{1,0:T(8,128)(2,1)S(1)}, bf16[32,2048]{1,0:T(8,128)(2,1)S(1)}, u32[]{:S(2)}, u32[]{:S(2)}) collective-permute-start(bf16[32,2048]{1,0:T(8,128)(2,1)S(1)} %shard_map.150), channel_id=1, source_target_pairs={{0,16},{8,24},{16,0},{24,8},{1,17},{9,25},{17,1},{25,9},{2,18},{10... | collective-permute-start | bytes 393224 | tf_op jit(solution)/shard_map/ppermute | solution.py:333
  98.4 5.3 %collective-permute-start.23 = (bf16[16,2048]{1,0:T(8,128)(2,1)S(1)}, bf16[16,2048]{1,0:T(8,128)(2,1)S(1)}, u32[]{:S(2)}, u32[]{:S(2)}) collective-permute-start(bf16[16,2048]{1,0:T(8,128)(2,1)S(1)} %get-tuple-element.75), channel_id=1, source_target_pairs={{0,4},{1,5},{2,6},{3,7},{4,0},{5,1},{6,2},{7,3},{8,12},{9,13},{10,... | collective-permute-start | bytes 196616 | tf_op jit(solution)/shard_map/ppermute | solution.py:333
  99.2 5.2 %collective-permute-start.24 = (bf16[16,2048]{1,0:T(8,128)(2,1)S(1)}, bf16[16,2048]{1,0:T(8,128)(2,1)S(1)}, u32[]{:S(2)}, u32[]{:S(2)}) collective-permute-start(bf16[16,2048]{1,0:T(8,128)(2,1)S(1)} %get-tuple-element.76), channel_id=1, source_target_pairs={{0,6},{1,7},{2,4},{3,5},{4,2},{5,3},{6,0},{7,1},{8,14},{9,15},{10,... | collective-permute-start | bytes 196616 | tf_op jit(solution)/shard_map/ppermute | solution.py:333
  102.0 4.3 %collective-permute-start.19 = (bf16[16,2048]{1,0:T(8,128)(2,1)S(1)}, bf16[16,2048]{1,0:T(8,128)(2,1)S(1)}, u32[]{:S(2)}, u32[]{:S(2)}) collective-permute-start(bf16[16,2048]{1,0:T(8,128)(2,1)S(1)} %get-tuple-element.72), channel_id=1, source_target_pairs={{0,2},{1,3},{2,0},{3,1},{4,6},{5,7},{6,4},{7,5},{8,10},{9,11},{10,... | collective-permute-start | bytes 196616 | tf_op jit(solution)/shard_map/ppermute | solution.py:333
  106.3 1.4 %collective-permute-start.25 = (bf16[32,2048]{1,0:T(8,128)(2,1)S(1)}, bf16[32,2048]{1,0:T(8,128)(2,1)S(1)}, u32[]{:S(2)}, u32[]{:S(2)}) collective-permute-start(bf16[32,2048]{1,0:T(8,128)(2,1)S(1)} %get-tuple-element.78), channel_id=1, source_target_pairs={{0,1},{1,0},{2,3},{3,2},{4,5},{5,4},{6,7},{7,6},{8,9},{9,8},{10,11... | collective-permute-start | bytes 393224 | tf_op jit(solution)/shard_map/ppermute | solution.py:333

commit v9 on v7

--- a/solution.py
+++ b/solution.py
@@ -169,8 +169,8 @@
         at += send_ref.shape[0]
 
 
-def expert_kernel(count, bias_ref, w_in_ref, w_out_ref, *refs):
-    x_refs, out_refs = refs[:count], refs[-count:]
+def expert_kernel(count, outs, bias_ref, w_in_ref, w_out_ref, *refs):
+    x_refs, out_refs = refs[:count], refs[-outs:]
     inner = jnp.dot(joined(x_refs), w_in_ref[0], preferred_element_type=F32)
     inner = jnp.maximum(inner + bias_ref[...], 0.0).astype(BF16)
     share = jnp.dot(inner, w_out_ref[0], preferred_element_type=F32).astype(BF16)
@@ -316,11 +316,11 @@
     def bf16(rows):
         return jax.ShapeDtypeStruct((rows, width), BF16)
 
-    def apply(rows, after=()):
+    def apply(rows, outs, after=()):
         count = sum(x.shape[0] for x in rows)
         return call(
-            functools.partial(expert_kernel, len(rows)),
-            tuple(bf16(x.shape[0]) for x in rows),
+            functools.partial(expert_kernel, len(rows), len(outs)),
+            tuple(bf16(n) for n in outs),
             b_in,
             w_in,
             w_out,
@@ -341,29 +341,30 @@
         own = [call(join_kernel, bf16(half), *pieces[n : n + 2]) for n in (2, 0)]
         far = [swap(x, 2) for x in own]
         near = [swap(x, 1) for x in own]
-        *own_share, near_first, near_second = apply(own + near)
-        *corner_share, far_first, far_second = apply([swap(x, 1) for x in far] + far, after=own_share[:1])
-        near_shares = [swap(near_first, 1), swap(near_second, 1)]
-        far_shares = [far_first, far_second]
-        pieces = ()
-        for n in (1, 0):
-            pair = swap(call(add_kernel, bf16(half), swap(corner_share[n], 1), far_shares[n]), 2)
-            pieces += tuple(
-                call(
-                    functools.partial(result_kernel, 0),
-                    (bf16(2 * cap),) * 2,
-                    b_out,
-                    near_shares[n],
-                    own_share[n],
-                    pair,
-                )
+        *own_share, near_share = apply(own + near, [half, half, slots])
+        *corner_share, far_first, far_second = apply(
+            [swap(x, 1) for x in far] + far, [half] * 4, after=own_share[:1]
+        )
+        far_share = [far_first, far_second]
+        near_share = swap(near_share, 1)
+        back = [None, None]
+        for n in (0, 1):
+            pair = swap(call(add_kernel, bf16(half), swap(corner_share[n], 1), far_share[n]), 2)
+            back[n] = call(
+                functools.partial(result_kernel, n * half),
+                (bf16(2 * cap),) * 2,
+                b_out,
+                near_share,
+                own_share[n],
+                pair,
             )
+        pieces = [x for n in (1, 0) for x in back[n]]
         pieces = [swap(x, 2 * n, "expert") if n else x for n, x in enumerate(pieces)]
         mine, other = call(functools.partial(part_kernel, cap), (bf16(half),) * 2, *pieces)
         returned = [mine, swap(other, 1, "expert")]
     else:
         every = lax.all_gather(over_experts(send[0]), "dp", axis=0, tiled=True)
-        (share,) = apply([every])
+        (share,) = apply([every], [dp * slots])
         shares = lax.all_to_all(
             share.reshape(dp, slots, width), "dp", split_axis=0, concat_axis=0, tiled=True
         )

time: 110 us -> 113 us (1.027)
  waiting for transfers between devices: 50.3 us -> 54.1 us
    ppermute x20 -> x19, waiting for transfers between devices: 23 us -> 26.8 us  [swap(): lax.ppermute(x, axis, [(i, i ^ distance) for i in range(lax.axis_size(axi...]
    ppermute x20 -> x19, starting transfers between devices: 32.4 us -> 31.3 us  [swap(): lax.ppermute(x, axis, [(i, i ^ distance) for i in range(lax.axis_size(axi...]
  transfers between devices with their start and end apart: 26 -> 25, of which waited for: 18 -> 17; matrix products, arithmetic and copies ran while one was open for 0% -> 0% of each run, Pallas kernels for 5% -> 5%
where the time goes in v9:
time: 113 us; the launch traced here: 112 us
  waiting for transfers between devices  54.1 us (48%)
  starting transfers between devices  41.8 us (37%)
  Pallas kernels  12.3 us (11%)
  local copies, waits for them, and re-layouts  3.94 us (3%)
    ppermute x19, starting transfers between devices, swap(): lax.ppermute(x, axis, [(i, i ^ distance) for i in range(lax.axis_size(axi...  31.3 us
    ppermute x6, waiting for transfers between devices, spread(): lax.ppermute(part, 'dp', [(i, (i + n) % dp) for i in range(dp)])  27.3 us
    ppermute x19, waiting for transfers between devices, swap(): lax.ppermute(x, axis, [(i, i ^ distance) for i in range(lax.axis_size(axi...  26.8 us
    pallas_call x18, Pallas kernels, call(): pl.pallas_call(body, out_shape=out_shape, compiler_params=pltpu.CompilerP...  12.3 us
    ppermute x6, starting transfers between devices, spread(): lax.ppermute(part, 'dp', [(i, (i + n) % dp) for i in range(dp)])  10.5 us
    unnamed x22, local copies, waits for them, and re-layouts  3.94 us
  transfers between devices with their start and end apart: 25, of which 17 were waited for; matrix products, arithmetic and copies ran while one was open for 0% of the time, Pallas kernels for 5%

profile of v9, /device:TPU:0, one launch (start us, length us, event | category | flops | bytes accessed | tf_op | source)
XLA Modules:
  0.0 112.3 jit_solution(468430250977665777)
XLA Ops:
  0.0 2.8 %shard_map.136 = (bf16[128,128]{1,0:T(8,128)(2,1)}, bf16[32,4224]{1,0:T(8,128)(2,1)}, bf16[32,4224]{1,0:T(8,128)(2,1)}, bf16[32,4224]{1,0:T(8,128)(2,1)}, bf16[32,4224]{1,0:T(8,128)(2,1)}) custom-call(s32[1,128]{1,0:T(1,128)} %bitcast.9, bf16[128,2048]{1,0:T(8,128)(2,1)} %refs_0_.2, bf16[128,2048]{1,0:T(8,128)(2,1)} %refs_1_.2), custom_call_target="tpu_custom_call" | custom-call | bytes 2163200 | tf_op jit(solution)/shard_map/pallas_call | solution.py:41
  2.8 3.0 %collective-permute-start = (bf16[32,4224]{1,0:T(8,128)(2,1)}, bf16[32,4224]{1,0:T(8,128)(2,1)S(1)}, u32[]{:S(2)}, u32[]{:S(2)}) collective-permute-start(bf16[32,4224]{1,0:T(8,128)(2,1)} %get-tuple-element.46), channel_id=1, source_target_pairs={{0,8},{8,16},{16,24},{24,0},{1,9},{9,17},{17,25},{25,1},{2,10},{10... | collective-permute-start | bytes 811016 | tf_op jit(solution)/shard_map/ppermute | solution.py:262
  5.8 2.6 %collective-permute-start.1 = (bf16[32,4224]{1,0:T(8,128)(2,1)}, bf16[32,4224]{1,0:T(8,128)(2,1)S(1)}, u32[]{:S(2)}, u32[]{:S(2)}) collective-permute-start(bf16[32,4224]{1,0:T(8,128)(2,1)} %get-tuple-element.47), channel_id=1, source_target_pairs={{0,16},{8,24},{16,0},{24,8},{1,17},{9,25},{17,1},{25,9},{2,18},{10... | collective-permute-start | bytes 811016 | tf_op jit(solution)/shard_map/ppermute | solution.py:262
  8.4 1.3 %collective-permute-start.2 = (bf16[32,4224]{1,0:T(8,128)(2,1)}, bf16[32,4224]{1,0:T(8,128)(2,1)S(1)}, u32[]{:S(2)}, u32[]{:S(2)}) collective-permute-start(bf16[32,4224]{1,0:T(8,128)(2,1)} %get-tuple-element.48), channel_id=1, source_target_pairs={{0,24},{8,0},{16,8},{24,16},{1,25},{9,1},{17,9},{25,17},{2,26},{10... | collective-permute-start | bytes 811016 | tf_op jit(solution)/shard_map/ppermute | solution.py:262
  9.7 2.6 %shard_map.137 = (bf16[128,128]{1,0:T(8,128)(2,1)}, bf16[32,4096]{1,0:T(8,128)(2,1)}, bf16[32,4096]{1,0:T(8,128)(2,1)}, bf16[32,4096]{1,0:T(8,128)(2,1)}, bf16[32,4096]{1,0:T(8,128)(2,1)}) custom-call(bf16[128,128]{1,0:T(8,128)(2,1)} %get-tuple-element.42.pos_ref, bf16[128,2048]{1,0:T(8,128)(2,1)} %refs_0_.3, bf16[128,2048]{1,0:T(8,128)(2,1)} %refs_1_.3), custom_call_target="tpu_custom_call" | custom-call | bytes 2162688 | tf_op jit(solution)/shard_map/pallas_call | solution.py:41
  12.3 0.7 collective-permute-start.3
  13.0 0.3 collective-permute-start.4
  13.3 2.1 %collective-permute-done.refs_1_ = bf16[32,4224]{1,0:T(8,128)(2,1)S(1)} collective-permute-done((bf16[32,4224]{1,0:T(8,128)(2,1)}, bf16[32,4224]{1,0:T(8,128)(2,1)S(1)}, u32[]{:S(2)}, u32[]{:S(2)}) %collective-permute-start) | collective-permute-done | bytes 270368 | tf_op jit(solution)/shard_map/ppermute | solution.py:262
  15.5 2.5 %collective-permute-start.5 = (bf16[32,4096]{1,0:T(8,128)(2,1)}, bf16[32,4096]{1,0:T(8,128)(2,1)S(1)}, u32[]{:S(2)}, u32[]{:S(2)}) collective-permute-start(bf16[32,4096]{1,0:T(8,128)(2,1)} %get-tuple-element.55), channel_id=1, source_target_pairs={{0,24},{8,0},{16,8},{24,16},{1,25},{9,1},{17,9},{25,17},{2,26},{10... | collective-permute-start | bytes 786440 | tf_op jit(solution)/shard_map/ppermute | solution.py:262
  18.0 1.0 copy-done.2
  18.9 0.9 copy-done.4
  19.9 0.7 copy-done.8
  20.5 0.7 copy-done.9
  21.2 0.7 copy-done.10
  22.1 5.0 %collective-permute-done.1.refs_2_ = bf16[32,4224]{1,0:T(8,128)(2,1)S(1)} collective-permute-done((bf16[32,4224]{1,0:T(8,128)(2,1)}, bf16[32,4224]{1,0:T(8,128)(2,1)S(1)}, u32[]{:S(2)}, u32[]{:S(2)}) %collective-permute-start.1) | collective-permute-done | bytes 270368 | tf_op jit(solution)/shard_map/ppermute | solution.py:262
  27.2 1.5 %shard_map.140.probs_ref = bf16[16,128,128]{2,1,0:T(8,128)(2,1)S(1)} custom-call(bf16[128,128]{1,0:T(8,128)(2,1)S(1)} %get-tuple-element.49.place_ref, f32[128,128]{1,0:T(8,128)S(1)} %get-tuple-element.51.outside_ref, bf16[32,4224]{1,0:T(8,128)(2,1)S(1)} %get-tuple-element.45.refs_0_, bf16[32,4224]{1,0:T(8,128)(2,1)S(1)} %collective-permute-done.refs_1_, ...), custom_call_target="tpu_custom_call" | custom-call | bytes 1703936 | tf_op jit(solution)/shard_map/pallas_call | solution.py:41
  28.7 4.0 %collective-permute-done.3.refs_1_ = bf16[32,4096]{1,0:T(8,128)(2,1)S(1)} collective-permute-done((bf16[32,4096]{1,0:T(8,128)(2,1)}, bf16[32,4096]{1,0:T(8,128)(2,1)S(1)}, u32[]{:S(2)}, u32[]{:S(2)}) %collective-permute-start.3) | collective-permute-done | bytes 262176 | tf_op jit(solution)/shard_map/ppermute | solution.py:262
  32.7 16.2 %collective-permute-done.4.refs_2_ = bf16[32,4096]{1,0:T(8,128)(2,1)S(1)} collective-permute-done((bf16[32,4096]{1,0:T(8,128)(2,1)}, bf16[32,4096]{1,0:T(8,128)(2,1)S(1)}, u32[]{:S(2)}, u32[]{:S(2)}) %collective-permute-start.4) | collective-permute-done | bytes 262176 | tf_op jit(solution)/shard_map/ppermute | solution.py:262
  49.2 0.8 shard_map.142
  50.1 1.3 %collective-permute-done.6.other_ref = bf16[32,2048]{1,0:T(8,128)(2,1)S(1)} collective-permute-done((bf16[32,2048]{1,0:T(8,128)(2,1)S(1)}, bf16[32,2048]{1,0:T(8,128)(2,1)S(1)}, u32[]{:S(2)}, u32[]{:S(2)}) %collective-permute-start.6) | collective-permute-done | bytes 131104 | tf_op jit(solution)/shard_map/ppermute | solution.py:333
  51.5 1.6 %collective-permute-start.9 = (bf16[16,2048]{1,0:T(8,128)(2,1)S(1)}, bf16[16,2048]{1,0:T(8,128)(2,1)S(1)}, u32[]{:S(2)}, u32[]{:S(2)}) collective-permute-start(bf16[16,2048]{1,0:T(8,128)(2,1)S(1)} %get-tuple-element.63), channel_id=1, source_target_pairs={{0,2},{1,3},{2,0},{3,1},{4,6},{5,7},{6,4},{7,5},{8,10},{9,11},{10,... | collective-permute-start | bytes 196616 | tf_op jit(solution)/shard_map/ppermute | solution.py:333
  53.0 1.5 %collective-permute-start.7 = (bf16[16,2048]{1,0:T(8,128)(2,1)S(1)}, bf16[16,2048]{1,0:T(8,128)(2,1)S(1)}, u32[]{:S(2)}, u32[]{:S(2)}) collective-permute-start(bf16[16,2048]{1,0:T(8,128)(2,1)S(1)} %get-tuple-element.60), channel_id=1, source_target_pairs={{0,4},{1,5},{2,6},{3,7},{4,0},{5,1},{6,2},{7,3},{8,12},{9,13},{10,... | collective-permute-start | bytes 196616 | tf_op jit(solution)/shard_map/ppermute | solution.py:333
  54.5 0.5 collective-permute-start.8
  55.0 0.8 collective-permute-done.9.refs_1_
  55.8 5.2 %collective-permute-start.15 = (bf16[32,2048]{1,0:T(8,128)(2,1)S(1)}, bf16[32,2048]{1,0:T(8,128)(2,1)S(1)}, u32[]{:S(2)}, u32[]{:S(2)}) collective-permute-start(bf16[32,2048]{1,0:T(8,128)(2,1)S(1)} %shard_map.145.refs_1_), channel_id=1, source_target_pairs={{0,16},{8,24},{16,0},{24,8},{1,17},{9,25},{17,1},{25,9},{2,18},{10... | collective-permute-start | bytes 393224 | tf_op jit(solution)/shard_map/ppermute | solution.py:333
  61.0 3.9 %collective-permute-start.13 = (bf16[32,2048]{1,0:T(8,128)(2,1)S(1)}, bf16[32,2048]{1,0:T(8,128)(2,1)S(1)}, u32[]{:S(2)}, u32[]{:S(2)}) collective-permute-start(bf16[32,2048]{1,0:T(8,128)(2,1)S(1)} %shard_map.144.refs_0_), channel_id=1, source_target_pairs={{0,16},{8,24},{16,0},{24,8},{1,17},{9,25},{17,1},{25,9},{2,18},{10... | collective-permute-start | bytes 393224 | tf_op jit(solution)/shard_map/ppermute | solution.py:333
  64.9 2.5 %collective-permute-start.11 = (bf16[32,2048]{1,0:T(8,128)(2,1)S(1)}, bf16[32,2048]{1,0:T(8,128)(2,1)S(1)}, u32[]{:S(2)}, u32[]{:S(2)}) collective-permute-start(bf16[32,2048]{1,0:T(8,128)(2,1)S(1)} %shard_map.145.refs_1_), channel_id=1, source_target_pairs={{0,8},{8,0},{16,24},{24,16},{1,9},{9,1},{17,25},{25,17},{2,10},{10... | collective-permute-start | bytes 393224 | tf_op jit(solution)/shard_map/ppermute | solution.py:333
  67.5 3.2 %collective-permute-start.16 = (bf16[32,2048]{1,0:T(8,128)(2,1)S(1)}, bf16[32,2048]{1,0:T(8,128)(2,1)S(1)}, u32[]{:S(2)}, u32[]{:S(2)}) collective-permute-start(bf16[32,2048]{1,0:T(8,128)(2,1)S(1)} %collective-permute-done.15.refs_3_), channel_id=1, source_target_pairs={{0,8},{8,0},{16,24},{24,16},{1,9},{9,1},{17,25},{25,17},{2,10},{10... | collective-permute-start | bytes 393224 | tf_op jit(solution)/shard_map/ppermute | solution.py:333
  70.7 1.6 %collective-permute-done.13.refs_2_ = bf16[32,2048]{1,0:T(8,128)(2,1)S(1)} collective-permute-done((bf16[32,2048]{1,0:T(8,128)(2,1)S(1)}, bf16[32,2048]{1,0:T(8,128)(2,1)S(1)}, u32[]{:S(2)}, u32[]{:S(2)}) %collective-permute-start.13) | collective-permute-done | bytes 131104 | tf_op jit(solution)/shard_map/ppermute | solution.py:333
  72.3 0.9 collective-permute-start.14
  73.2 0.7 collective-permute-done.11.refs_3_
  73.9 2.8 %collective-permute-done.10.refs_2_ = bf16[32,2048]{1,0:T(8,128)(2,1)S(1)} collective-permute-done((bf16[32,2048]{1,0:T(8,128)(2,1)S(1)}, bf16[32,2048]{1,0:T(8,128)(2,1)S(1)}, u32[]{:S(2)}, u32[]{:S(2)}) %collective-permute-start.10) | collective-permute-done | bytes 131104 | tf_op jit(solution)/shard_map/ppermute | solution.py:333
  76.7 1.3 %shard_map.146 = (bf16[32,2048]{1,0:T(8,128)(2,1)S(1)}, bf16[32,2048]{1,0:T(8,128)(2,1)S(1)}, bf16[64,2048]{1,0:T(8,128)(2,1)S(1)}) custom-call(f32[1,1024]{1,0:T(1,128)S(1)} %copy-done.5, bf16[1,2048,1024]{2,1,0:T(8,128)(2,1)S(1)} %copy-done, bf16[1,1024,2048]{2,1,0:T(8,128)(2,1)S(1)} %copy-done.1, bf16[32,2048]{1,0:T(8,128)(2,1)S(1)} %shard_map.144.refs_0_, ...), custom_call_target="tpu_custom_call" | custom-call | flops 1073741824 | bytes 9441280 | tf_op jit(solution)/shard_map/pallas_call | solution.py:41
  78.1 0.5 collective-permute-done.16.refs_1_
  78.6 1.4 %collective-permute-done.14.refs_0_ = bf16[32,2048]{1,0:T(8,128)(2,1)S(1)} collective-permute-done((bf16[32,2048]{1,0:T(8,128)(2,1)S(1)}, bf16[32,2048]{1,0:T(8,128)(2,1)S(1)}, u32[]{:S(2)}, u32[]{:S(2)}) %collective-permute-start.14) | collective-permute-done | bytes 131104 | tf_op jit(solution)/shard_map/ppermute | solution.py:333
  80.0 1.3 %shard_map.147 = (bf16[32,2048]{1,0:T(8,128)(2,1)S(1)}, bf16[32,2048]{1,0:T(8,128)(2,1)S(1)}, bf16[32,2048]{1,0:T(8,128)(2,1)S(1)}, bf16[32,2048]{1,0:T(8,128)(2,1)S(1)}) custom-call(f32[1,1024]{1,0:T(1,128)S(1)} %copy-done.5, bf16[1,2048,1024]{2,1,0:T(8,128)(2,1)S(1)} %copy-done, bf16[1,1024,2048]{2,1,0:T(8,128)(2,1)S(1)} %copy-done.1, ...), custom_call_target="tpu_custom_call" | custom-call | flops 1073741824 | bytes 9572352 | tf_op jit(solution)/shard_map/pallas_call | solution.py:41
  81.3 0.9 collective-permute-start.20
  82.2 1.2 %collective-permute-start.12 = (bf16[64,2048]{1,0:T(8,128)(2,1)S(1)}, bf16[64,2048]{1,0:T(8,128)(2,1)S(1)}, u32[]{:S(2)}, u32[]{:S(2)}) collective-permute-start(bf16[64,2048]{1,0:T(8,128)(2,1)S(1)} %get-tuple-element.64), channel_id=1, source_target_pairs={{0,8},{8,0},{16,24},{24,16},{1,9},{9,1},{17,25},{25,17},{2,10},{10... | collective-permute-start | bytes 786440 | tf_op jit(solution)/shard_map/ppermute | solution.py:333
  83.4 0.8 collective-permute-start.17
  84.3 3.6 %collective-permute-done.20.first_ref = bf16[32,2048]{1,0:T(8,128)(2,1)S(1)} collective-permute-done((bf16[32,2048]{1,0:T(8,128)(2,1)S(1)}, bf16[32,2048]{1,0:T(8,128)(2,1)S(1)}, u32[]{:S(2)}, u32[]{:S(2)}) %collective-permute-start.20) | collective-permute-done | bytes 131104 | tf_op jit(solution)/shard_map/ppermute | solution.py:333
  87.9 3.7 %collective-permute-start.21 = (bf16[32,2048]{1,0:T(8,128)(2,1)S(1)}, bf16[32,2048]{1,0:T(8,128)(2,1)S(1)}, u32[]{:S(2)}, u32[]{:S(2)}) collective-permute-start(bf16[32,2048]{1,0:T(8,128)(2,1)S(1)} %shard_map.150), channel_id=1, source_target_pairs={{0,16},{8,24},{16,0},{24,8},{1,17},{9,25},{17,1},{25,9},{2,18},{10... | collective-permute-start | bytes 393224 | tf_op jit(solution)/shard_map/ppermute | solution.py:333
  91.6 4.2 %collective-permute-done.17.first_ref = bf16[32,2048]{1,0:T(8,128)(2,1)S(1)} collective-permute-done((bf16[32,2048]{1,0:T(8,128)(2,1)S(1)}, bf16[32,2048]{1,0:T(8,128)(2,1)S(1)}, u32[]{:S(2)}, u32[]{:S(2)}) %collective-permute-start.17) | collective-permute-done | bytes 131104 | tf_op jit(solution)/shard_map/ppermute | solution.py:333
  95.9 4.5 %collective-permute-start.18 = (bf16[32,2048]{1,0:T(8,128)(2,1)S(1)}, bf16[32,2048]{1,0:T(8,128)(2,1)S(1)}, u32[]{:S(2)}, u32[]{:S(2)}) collective-permute-start(bf16[32,2048]{1,0:T(8,128)(2,1)S(1)} %shard_map.148), channel_id=1, source_target_pairs={{0,16},{8,24},{16,0},{24,8},{1,17},{9,25},{17,1},{25,9},{2,18},{10... | collective-permute-start | bytes 393224 | tf_op jit(solution)/shard_map/ppermute | solution.py:333
  100.5 0.6 collective-permute-start.23
  101.1 4.3 %collective-permute-done.18.refs_1_ = bf16[32,2048]{1,0:T(8,128)(2,1)S(1)} collective-permute-done((bf16[32,2048]{1,0:T(8,128)(2,1)S(1)}, bf16[32,2048]{1,0:T(8,128)(2,1)S(1)}, u32[]{:S(2)}, u32[]{:S(2)}) %collective-permute-start.18) | collective-permute-done | bytes 131104 | tf_op jit(solution)/shard_map/ppermute | solution.py:333
  105.7 4.1 %collective-permute-done.19.refs_1_ = bf16[16,2048]{1,0:T(8,128)(2,1)S(1)} collective-permute-done((bf16[16,2048]{1,0:T(8,128)(2,1)S(1)}, bf16[16,2048]{1,0:T(8,128)(2,1)S(1)}, u32[]{:S(2)}, u32[]{:S(2)}) %collective-permute-start.19) | collective-permute-done | bytes 65568 | tf_op jit(solution)/shard_map/ppermute | solution.py:333
  109.9 1.3 %collective-permute-done.24.refs_1_ = bf16[32,2048]{1,0:T(8,128)(2,1)S(1)} collective-permute-done((bf16[32,2048]{1,0:T(8,128)(2,1)S(1)}, bf16[32,2048]{1,0:T(8,128)(2,1)S(1)}, u32[]{:S(2)}, u32[]{:S(2)}) %collective-permute-start.24) | collective-permute-done | bytes 131104 | tf_op jit(solution)/shard_map/ppermute | solution.py:333
  111.2 1.1 shard_map.153
  (42 shorter events, 1.5 us)
Async XLA Ops:
  0.0 49.2 %copy-start.7 = (f32[2048]{0:T(1024)S(1)}, f32[2048]{0:T(1024)}, u32[]{:S(2)}) copy-start(f32[2048]{0:T(1024)} %param.23) | copy-start | bytes 24580
  0.0 49.2 %copy-start.6 = (f32[2048]{0:T(1024)S(1)}, f32[2048]{0:T(1024)}, u32[]{:S(2)}) copy-start(f32[2048]{0:T(1024)} %param.22) | copy-start | bytes 24580
  2.8 12.7 %collective-permute-start = (bf16[32,4224]{1,0:T(8,128)(2,1)}, bf16[32,4224]{1,0:T(8,128)(2,1)S(1)}, u32[]{:S(2)}, u32[]{:S(2)}) collective-permute-start(bf16[32,4224]{1,0:T(8,128)(2,1)} %get-tuple-element.46), channel_id=1, source_target_pairs={{0,8},{8,16},{16,24},{24,0},{1,9},{9,17},{17,25},{25,1},{2,10},{10... | collective-permute-start | bytes 811016 | tf_op jit(solution)/shard_map/ppermute | solution.py:262
  5.8 21.3 %collective-permute-start.1 = (bf16[32,4224]{1,0:T(8,128)(2,1)}, bf16[32,4224]{1,0:T(8,128)(2,1)S(1)}, u32[]{:S(2)}, u32[]{:S(2)}) collective-permute-start(bf16[32,4224]{1,0:T(8,128)(2,1)} %get-tuple-element.47), channel_id=1, source_target_pairs={{0,16},{8,24},{16,0},{24,8},{1,17},{9,25},{17,1},{25,9},{2,18},{10... | collective-permute-start | bytes 811016 | tf_op jit(solution)/shard_map/ppermute | solution.py:262
  8.4 18.7 %collective-permute-start.2 = (bf16[32,4224]{1,0:T(8,128)(2,1)}, bf16[32,4224]{1,0:T(8,128)(2,1)S(1)}, u32[]{:S(2)}, u32[]{:S(2)}) collective-permute-start(bf16[32,4224]{1,0:T(8,128)(2,1)} %get-tuple-element.48), channel_id=1, source_target_pairs={{0,24},{8,0},{16,8},{24,16},{1,25},{9,1},{17,9},{25,17},{2,26},{10... | collective-permute-start | bytes 811016 | tf_op jit(solution)/shard_map/ppermute | solution.py:262
  12.3 20.4 %collective-permute-start.3 = (bf16[32,4096]{1,0:T(8,128)(2,1)}, bf16[32,4096]{1,0:T(8,128)(2,1)S(1)}, u32[]{:S(2)}, u32[]{:S(2)}) collective-permute-start(bf16[32,4096]{1,0:T(8,128)(2,1)} %get-tuple-element.53), channel_id=1, source_target_pairs={{0,8},{8,16},{16,24},{24,0},{1,9},{9,17},{17,25},{25,1},{2,10},{10... | collective-permute-start | bytes 786440 | tf_op jit(solution)/shard_map/ppermute | solution.py:262
  13.0 35.9 %collective-permute-start.4 = (bf16[32,4096]{1,0:T(8,128)(2,1)}, bf16[32,4096]{1,0:T(8,128)(2,1)S(1)}, u32[]{:S(2)}, u32[]{:S(2)}) collective-permute-start(bf16[32,4096]{1,0:T(8,128)(2,1)} %get-tuple-element.54), channel_id=1, source_target_pairs={{0,16},{8,24},{16,0},{24,8},{1,17},{9,25},{17,1},{25,9},{2,18},{10... | collective-permute-start | bytes 786440 | tf_op jit(solution)/shard_map/ppermute | solution.py:262
  15.5 33.4 %collective-permute-start.5 = (bf16[32,4096]{1,0:T(8,128)(2,1)}, bf16[32,4096]{1,0:T(8,128)(2,1)S(1)}, u32[]{:S(2)}, u32[]{:S(2)}) collective-permute-start(bf16[32,4096]{1,0:T(8,128)(2,1)} %get-tuple-element.55), channel_id=1, source_target_pairs={{0,24},{8,0},{16,8},{24,16},{1,25},{9,1},{17,9},{25,17},{2,26},{10... | collective-permute-start | bytes 786440 | tf_op jit(solution)/shard_map/ppermute | solution.py:262
  18.0 1.0 copy-start.2
  18.9 0.9 copy-start.4
  19.9 0.7 copy-start.8
  20.5 0.7 copy-start.9
  21.2 0.7 copy-start.10
  27.1 49.6 %copy-start = (bf16[1,2048,1024]{2,1,0:T(8,128)(2,1)S(1)}, bf16[1,2048,1024]{2,1,0:T(8,128)(2,1)}, u32[]{:S(2)}) copy-start(bf16[1,2048,1024]{2,1,0:T(8,128)(2,1)} %w_in_ref.3) | copy-start | bytes 12582916
  27.1 49.6 %copy-start.1 = (bf16[1,1024,2048]{2,1,0:T(8,128)(2,1)S(1)}, bf16[1,1024,2048]{2,1,0:T(8,128)(2,1)}, u32[]{:S(2)}) copy-start(bf16[1,1024,2048]{2,1,0:T(8,128)(2,1)} %w_out_ref.3) | copy-start | bytes 12582916
  27.1 49.6 %copy-start.5 = (f32[1,1024]{1,0:T(1,128)S(1)}, f32[1,1024]{1,0:T(1,128)}, u32[]{:S(2)}) copy-start(f32[1,1024]{1,0:T(1,128)} %bias_ref.5) | copy-start | bytes 12292
  50.0 1.4 %collective-permute-start.6 = (bf16[32,2048]{1,0:T(8,128)(2,1)S(1)}, bf16[32,2048]{1,0:T(8,128)(2,1)S(1)}, u32[]{:S(2)}, u32[]{:S(2)}) collective-permute-start(bf16[32,2048]{1,0:T(8,128)(2,1)S(1)} %get-tuple-element.59), channel_id=1, source_target_pairs={{0,1},{1,0},{2,3},{3,2},{4,5},{5,4},{6,7},{7,6},{8,9},{9,8},{10,11... | collective-permute-start | bytes 393224 | tf_op jit(solution)/shard_map/ppermute | solution.py:333
  51.5 4.3 %collective-permute-start.9 = (bf16[16,2048]{1,0:T(8,128)(2,1)S(1)}, bf16[16,2048]{1,0:T(8,128)(2,1)S(1)}, u32[]{:S(2)}, u32[]{:S(2)}) collective-permute-start(bf16[16,2048]{1,0:T(8,128)(2,1)S(1)} %get-tuple-element.63), channel_id=1, source_target_pairs={{0,2},{1,3},{2,0},{3,1},{4,6},{5,7},{6,4},{7,5},{8,10},{9,11},{10,... | collective-permute-start | bytes 196616 | tf_op jit(solution)/shard_map/ppermute | solution.py:333
  53.0 8.0 %collective-permute-start.7 = (bf16[16,2048]{1,0:T(8,128)(2,1)S(1)}, bf16[16,2048]{1,0:T(8,128)(2,1)S(1)}, u32[]{:S(2)}, u32[]{:S(2)}) collective-permute-start(bf16[16,2048]{1,0:T(8,128)(2,1)S(1)} %get-tuple-element.60), channel_id=1, source_target_pairs={{0,4},{1,5},{2,6},{3,7},{4,0},{5,1},{6,2},{7,3},{8,12},{9,13},{10,... | collective-permute-start | bytes 196616 | tf_op jit(solution)/shard_map/ppermute | solution.py:333
  54.5 6.5 %collective-permute-start.8 = (bf16[16,2048]{1,0:T(8,128)(2,1)S(1)}, bf16[16,2048]{1,0:T(8,128)(2,1)S(1)}, u32[]{:S(2)}, u32[]{:S(2)}) collective-permute-start(bf16[16,2048]{1,0:T(8,128)(2,1)S(1)} %get-tuple-element.61), channel_id=1, source_target_pairs={{0,6},{1,7},{2,4},{3,5},{4,2},{5,3},{6,0},{7,1},{8,14},{9,15},{10,... | collective-permute-start | bytes 196616 | tf_op jit(solution)/shard_map/ppermute | solution.py:333
  55.8 11.7 %collective-permute-start.15 = (bf16[32,2048]{1,0:T(8,128)(2,1)S(1)}, bf16[32,2048]{1,0:T(8,128)(2,1)S(1)}, u32[]{:S(2)}, u32[]{:S(2)}) collective-permute-start(bf16[32,2048]{1,0:T(8,128)(2,1)S(1)} %shard_map.145.refs_1_), channel_id=1, source_target_pairs={{0,16},{8,24},{16,0},{24,8},{1,17},{9,25},{17,1},{25,9},{2,18},{10... | collective-permute-start | bytes 393224 | tf_op jit(solution)/shard_map/ppermute | solution.py:333
  61.0 11.2 %collective-permute-start.13 = (bf16[32,2048]{1,0:T(8,128)(2,1)S(1)}, bf16[32,2048]{1,0:T(8,128)(2,1)S(1)}, u32[]{:S(2)}, u32[]{:S(2)}) collective-permute-start(bf16[32,2048]{1,0:T(8,128)(2,1)S(1)} %shard_map.144.refs_0_), channel_id=1, source_target_pairs={{0,16},{8,24},{16,0},{24,8},{1,17},{9,25},{17,1},{25,9},{2,18},{10... | collective-permute-start | bytes 393224 | tf_op jit(solution)/shard_map/ppermute | solution.py:333
  64.9 9.0 %collective-permute-start.11 = (bf16[32,2048]{1,0:T(8,128)(2,1)S(1)}, bf16[32,2048]{1,0:T(8,128)(2,1)S(1)}, u32[]{:S(2)}, u32[]{:S(2)}) collective-permute-start(bf16[32,2048]{1,0:T(8,128)(2,1)S(1)} %shard_map.145.refs_1_), channel_id=1, source_target_pairs={{0,8},{8,0},{16,24},{24,16},{1,9},{9,1},{17,25},{25,17},{2,10},{10... | collective-permute-start | bytes 393224 | tf_op jit(solution)/shard_map/ppermute | solution.py:333
  67.4 9.3 %collective-permute-start.10 = (bf16[32,2048]{1,0:T(8,128)(2,1)S(1)}, bf16[32,2048]{1,0:T(8,128)(2,1)S(1)}, u32[]{:S(2)}, u32[]{:S(2)}) collective-permute-start(bf16[32,2048]{1,0:T(8,128)(2,1)S(1)} %shard_map.144.refs_0_), channel_id=1, source_target_pairs={{0,8},{8,0},{16,24},{24,16},{1,9},{9,1},{17,25},{25,17},{2,10},{10... | collective-permute-start | bytes 393224 | tf_op jit(solution)/shard_map/ppermute | solution.py:333
  67.5 11.1 %collective-permute-start.16 = (bf16[32,2048]{1,0:T(8,128)(2,1)S(1)}, bf16[32,2048]{1,0:T(8,128)(2,1)S(1)}, u32[]{:S(2)}, u32[]{:S(2)}) collective-permute-start(bf16[32,2048]{1,0:T(8,128)(2,1)S(1)} %collective-permute-done.15.refs_3_), channel_id=1, source_target_pairs={{0,8},{8,0},{16,24},{24,16},{1,9},{9,1},{17,25},{25,17},{2,10},{10... | collective-permute-start | bytes 393224 | tf_op jit(solution)/shard_map/ppermute | solution.py:333
  72.3 7.7 %collective-permute-start.14 = (bf16[32,2048]{1,0:T(8,128)(2,1)S(1)}, bf16[32,2048]{1,0:T(8,128)(2,1)S(1)}, u32[]{:S(2)}, u32[]{:S(2)}) collective-permute-start(bf16[32,2048]{1,0:T(8,128)(2,1)S(1)} %collective-permute-done.13.refs_2_), channel_id=1, source_target_pairs={{0,8},{8,0},{16,24},{24,16},{1,9},{9,1},{17,25},{25,17},{2,10},{10... | collective-permute-start | bytes 393224 | tf_op jit(solution)/shard_map/ppermute | solution.py:333
  80.0 20.3 %copy-start.3 = (f32[8,2048]{1,0:T(8,128)S(1)}, f32[8,2048]{1,0:T(8,128)}, u32[]{:S(2)}) copy-start(f32[8,2048]{1,0:T(8,128)} %bias_ref.7) | copy-start | bytes 196612
  81.3 6.5 %collective-permute-start.20 = (bf16[32,2048]{1,0:T(8,128)(2,1)S(1)}, bf16[32,2048]{1,0:T(8,128)(2,1)S(1)}, u32[]{:S(2)}, u32[]{:S(2)}) collective-permute-start(bf16[32,2048]{1,0:T(8,128)(2,1)S(1)} %get-tuple-element.71), channel_id=1, source_target_pairs={{0,8},{8,0},{16,24},{24,16},{1,9},{9,1},{17,25},{25,17},{2,10},{10... | collective-permute-start | bytes 393224 | tf_op jit(solution)/shard_map/ppermute | solution.py:333
  82.2 18.1 %collective-permute-start.12 = (bf16[64,2048]{1,0:T(8,128)(2,1)S(1)}, bf16[64,2048]{1,0:T(8,128)(2,1)S(1)}, u32[]{:S(2)}, u32[]{:S(2)}) collective-permute-start(bf16[64,2048]{1,0:T(8,128)(2,1)S(1)} %get-tuple-element.64), channel_id=1, source_target_pairs={{0,8},{8,0},{16,24},{24,16},{1,9},{9,1},{17,25},{25,17},{2,10},{10... | collective-permute-start | bytes 786440 | tf_op jit(solution)/shard_map/ppermute | solution.py:333
  83.4 12.4 %collective-permute-start.17 = (bf16[32,2048]{1,0:T(8,128)(2,1)S(1)}, bf16[32,2048]{1,0:T(8,128)(2,1)S(1)}, u32[]{:S(2)}, u32[]{:S(2)}) collective-permute-start(bf16[32,2048]{1,0:T(8,128)(2,1)S(1)} %get-tuple-element.67), channel_id=1, source_target_pairs={{0,8},{8,0},{16,24},{24,16},{1,9},{9,1},{17,25},{25,17},{2,10},{10... | collective-permute-start | bytes 393224 | tf_op jit(solution)/shard_map/ppermute | solution.py:333
  87.9 12.4 %collective-permute-start.21 = (bf16[32,2048]{1,0:T(8,128)(2,1)S(1)}, bf16[32,2048]{1,0:T(8,128)(2,1)S(1)}, u32[]{:S(2)}, u32[]{:S(2)}) collective-permute-start(bf16[32,2048]{1,0:T(8,128)(2,1)S(1)} %shard_map.150), channel_id=1, source_target_pairs={{0,16},{8,24},{16,0},{24,8},{1,17},{9,25},{17,1},{25,9},{2,18},{10... | collective-permute-start | bytes 393224 | tf_op jit(solution)/shard_map/ppermute | solution.py:333
  95.9 9.5 %collective-permute-start.18 = (bf16[32,2048]{1,0:T(8,128)(2,1)S(1)}, bf16[32,2048]{1,0:T(8,128)(2,1)S(1)}, u32[]{:S(2)}, u32[]{:S(2)}) collective-permute-start(bf16[32,2048]{1,0:T(8,128)(2,1)S(1)} %shard_map.148), channel_id=1, source_target_pairs={{0,16},{8,24},{16,0},{24,8},{1,17},{9,25},{17,1},{25,9},{2,18},{10... | collective-permute-start | bytes 393224 | tf_op jit(solution)/shard_map/ppermute | solution.py:333
  100.4 5.1 %collective-permute-start.22 = (bf16[16,2048]{1,0:T(8,128)(2,1)S(1)}, bf16[16,2048]{1,0:T(8,128)(2,1)S(1)}, u32[]{:S(2)}, u32[]{:S(2)}) collective-permute-start(bf16[16,2048]{1,0:T(8,128)(2,1)S(1)} %get-tuple-element.73), channel_id=1, source_target_pairs={{0,4},{1,5},{2,6},{3,7},{4,0},{5,1},{6,2},{7,3},{8,12},{9,13},{10,... | collective-permute-start | bytes 196616 | tf_op jit(solution)/shard_map/ppermute | solution.py:333
  100.5 5.2 %collective-permute-start.23 = (bf16[16,2048]{1,0:T(8,128)(2,1)S(1)}, bf16[16,2048]{1,0:T(8,128)(2,1)S(1)}, u32[]{:S(2)}, u32[]{:S(2)}) collective-permute-start(bf16[16,2048]{1,0:T(8,128)(2,1)S(1)} %get-tuple-element.74), channel_id=1, source_target_pairs={{0,6},{1,7},{2,4},{3,5},{4,2},{5,3},{6,0},{7,1},{8,14},{9,15},{10,... | collective-permute-start | bytes 196616 | tf_op jit(solution)/shard_map/ppermute | solution.py:333
  105.5 4.3 %collective-permute-start.19 = (bf16[16,2048]{1,0:T(8,128)(2,1)S(1)}, bf16[16,2048]{1,0:T(8,128)(2,1)S(1)}, u32[]{:S(2)}, u32[]{:S(2)}) collective-permute-start(bf16[16,2048]{1,0:T(8,128)(2,1)S(1)} %get-tuple-element.70), channel_id=1, source_target_pairs={{0,2},{1,3},{2,0},{3,1},{4,6},{5,7},{6,4},{7,5},{8,10},{9,11},{10,... | collective-permute-start | bytes 196616 | tf_op jit(solution)/shard_map/ppermute | solution.py:333
  109.8 1.4 %collective-permute-start.24 = (bf16[32,2048]{1,0:T(8,128)(2,1)S(1)}, bf16[32,2048]{1,0:T(8,128)(2,1)S(1)}, u32[]{:S(2)}, u32[]{:S(2)}) collective-permute-start(bf16[32,2048]{1,0:T(8,128)(2,1)S(1)} %get-tuple-element.76), channel_id=1, source_target_pairs={{0,1},{1,0},{2,3},{3,2},{4,5},{5,4},{6,7},{7,6},{8,9},{9,8},{10,11... | collective-permute-start | bytes 393224 | tf_op jit(solution)/shard_map/ppermute | solution.py:333

commit v10 on v7

--- a/solution.py
+++ b/solution.py
@@ -341,23 +341,26 @@
         own = [call(join_kernel, bf16(half), *pieces[n : n + 2]) for n in (2, 0)]
         far = [swap(x, 2) for x in own]
         near = [swap(x, 1) for x in own]
-        *own_share, near_first, near_second = apply(own + near)
-        *corner_share, far_first, far_second = apply([swap(x, 1) for x in far] + far, after=own_share[:1])
-        near_shares = [swap(near_first, 1), swap(near_second, 1)]
+        own_share, near_shares, last = [None, None], [None, None], ()
+        for n in (1, 0):
+            own_share[n], near_shares[n] = apply([own[n], near[n]], after=last)
+            last = own_share[n : n + 1]
+        last = last[0]
+        *corner_share, far_first, far_second = apply([swap(x, 1) for x in far] + far, after=[last])
         far_shares = [far_first, far_second]
-        pieces = ()
+        near_shares = [swap(x, 1) for x in near_shares]
+        backs = [None, None]
         for n in (1, 0):
             pair = swap(call(add_kernel, bf16(half), swap(corner_share[n], 1), far_shares[n]), 2)
-            pieces += tuple(
-                call(
-                    functools.partial(result_kernel, 0),
-                    (bf16(2 * cap),) * 2,
-                    b_out,
-                    near_shares[n],
-                    own_share[n],
-                    pair,
-                )
+            backs[n] = call(
+                functools.partial(result_kernel, 0),
+                (bf16(2 * cap),) * 2,
+                b_out,
+                near_shares[n],
+                own_share[n],
+                pair,
             )
+        pieces = [x for n in (1, 0) for x in backs[n]]
         pieces = [swap(x, 2 * n, "expert") if n else x for n, x in enumerate(pieces)]
         mine, other = call(functools.partial(part_kernel, cap), (bf16(half),) * 2, *pieces)
         returned = [mine, swap(other, 1, "expert")]

time: 110 us -> 109 us (level)
  starting transfers between devices: 42.9 us -> 37.4 us
  waiting for transfers between devices: 50.3 us -> 52.9 us
  Pallas kernels: 12.3 us -> 14.2 us
    ppermute x20, starting transfers between devices: 32.4 us -> 26.9 us  [swap(): lax.ppermute(x, axis, [(i, i ^ distance) for i in range(lax.axis_size(axi...]
    ppermute x20, waiting for transfers between devices: 23 us -> 25.6 us  [swap(): lax.ppermute(x, axis, [(i, i ^ distance) for i in range(lax.axis_size(axi...]
    pallas_call x18 -> x19, Pallas kernels: 12.3 us -> 14.2 us  [call(): pl.pallas_call(body, out_shape=out_shape, compiler_params=pltpu.CompilerP...]
  transfers between devices with their start and end apart: 26 -> 26, of which waited for: 18 -> 17; matrix products, arithmetic and copies ran while one was open for 0% -> 0% of each run, Pallas kernels for 5% -> 7%
where the time goes in v10:
time: 109 us
  waiting for transfers between devices  52.9 us (49%)
  starting transfers between devices  37.4 us (34%)
  Pallas kernels  14.2 us (13%)
  local copies, waits for them, and re-layouts  3.94 us (4%)
    ppermute x6, waiting for transfers between devices, spread(): lax.ppermute(part, 'dp', [(i, (i + n) % dp) for i in range(dp)])  27.3 us
    ppermute x20, starting transfers between devices, swap(): lax.ppermute(x, axis, [(i, i ^ distance) for i in range(lax.axis_size(axi...  26.9 us
    ppermute x20, waiting for transfers between devices, swap(): lax.ppermute(x, axis, [(i, i ^ distance) for i in range(lax.axis_size(axi...  25.6 us
    pallas_call x19, Pallas kernels, call(): pl.pallas_call(body, out_shape=out_shape, compiler_params=pltpu.CompilerP...  14.2 us
    ppermute x6, starting transfers between devices, spread(): lax.ppermute(part, 'dp', [(i, (i + n) % dp) for i in range(dp)])  10.5 us
    unnamed x22, local copies, waits for them, and re-layouts  3.94 us
  transfers between devices with their start and end apart: 26, of which 17 were waited for; matrix products, arithmetic and copies ran while one was open for 0% of the time, Pallas kernels for 7%

profile of v10, /device:TPU:0, one launch (start us, length us, event | category | flops | bytes accessed | tf_op | source)
XLA Modules:
  0.0 108.6 jit_solution(17671113360823470998)
XLA Ops:
  0.0 2.8 %shard_map.136 = (bf16[128,128]{1,0:T(8,128)(2,1)}, bf16[32,4224]{1,0:T(8,128)(2,1)}, bf16[32,4224]{1,0:T(8,128)(2,1)}, bf16[32,4224]{1,0:T(8,128)(2,1)}, bf16[32,4224]{1,0:T(8,128)(2,1)}) custom-call(s32[1,128]{1,0:T(1,128)} %bitcast.9, bf16[128,2048]{1,0:T(8,128)(2,1)} %refs_0_.2, bf16[128,2048]{1,0:T(8,128)(2,1)} %refs_1_.2), custom_call_target="tpu_custom_call" | custom-call | bytes 2163200 | tf_op jit(solution)/shard_map/pallas_call | solution.py:41
  2.8 3.0 %collective-permute-start = (bf16[32,4224]{1,0:T(8,128)(2,1)}, bf16[32,4224]{1,0:T(8,128)(2,1)S(1)}, u32[]{:S(2)}, u32[]{:S(2)}) collective-permute-start(bf16[32,4224]{1,0:T(8,128)(2,1)} %get-tuple-element.47), channel_id=1, source_target_pairs={{0,8},{8,16},{16,24},{24,0},{1,9},{9,17},{17,25},{25,1},{2,10},{10... | collective-permute-start | bytes 811016 | tf_op jit(solution)/shard_map/ppermute | solution.py:262
  5.8 2.6 %collective-permute-start.1 = (bf16[32,4224]{1,0:T(8,128)(2,1)}, bf16[32,4224]{1,0:T(8,128)(2,1)S(1)}, u32[]{:S(2)}, u32[]{:S(2)}) collective-permute-start(bf16[32,4224]{1,0:T(8,128)(2,1)} %get-tuple-element.48), channel_id=1, source_target_pairs={{0,16},{8,24},{16,0},{24,8},{1,17},{9,25},{17,1},{25,9},{2,18},{10... | collective-permute-start | bytes 811016 | tf_op jit(solution)/shard_map/ppermute | solution.py:262
  8.4 1.3 %collective-permute-start.2 = (bf16[32,4224]{1,0:T(8,128)(2,1)}, bf16[32,4224]{1,0:T(8,128)(2,1)S(1)}, u32[]{:S(2)}, u32[]{:S(2)}) collective-permute-start(bf16[32,4224]{1,0:T(8,128)(2,1)} %get-tuple-element.49), channel_id=1, source_target_pairs={{0,24},{8,0},{16,8},{24,16},{1,25},{9,1},{17,9},{25,17},{2,26},{10... | collective-permute-start | bytes 811016 | tf_op jit(solution)/shard_map/ppermute | solution.py:262
  9.7 2.6 %shard_map.137 = (bf16[128,128]{1,0:T(8,128)(2,1)}, bf16[32,4096]{1,0:T(8,128)(2,1)}, bf16[32,4096]{1,0:T(8,128)(2,1)}, bf16[32,4096]{1,0:T(8,128)(2,1)}, bf16[32,4096]{1,0:T(8,128)(2,1)}) custom-call(bf16[128,128]{1,0:T(8,128)(2,1)} %get-tuple-element.43.pos_ref, bf16[128,2048]{1,0:T(8,128)(2,1)} %refs_0_.3, bf16[128,2048]{1,0:T(8,128)(2,1)} %refs_1_.3), custom_call_target="tpu_custom_call" | custom-call | bytes 2162688 | tf_op jit(solution)/shard_map/pallas_call | solution.py:41
  12.3 0.7 collective-permute-start.3
  13.3 2.1 %collective-permute-done.refs_1_ = bf16[32,4224]{1,0:T(8,128)(2,1)S(1)} collective-permute-done((bf16[32,4224]{1,0:T(8,128)(2,1)}, bf16[32,4224]{1,0:T(8,128)(2,1)S(1)}, u32[]{:S(2)}, u32[]{:S(2)}) %collective-permute-start) | collective-permute-done | bytes 270368 | tf_op jit(solution)/shard_map/ppermute | solution.py:262
  15.5 2.5 %collective-permute-start.5 = (bf16[32,4096]{1,0:T(8,128)(2,1)}, bf16[32,4096]{1,0:T(8,128)(2,1)S(1)}, u32[]{:S(2)}, u32[]{:S(2)}) collective-permute-start(bf16[32,4096]{1,0:T(8,128)(2,1)} %get-tuple-element.56), channel_id=1, source_target_pairs={{0,24},{8,0},{16,8},{24,16},{1,25},{9,1},{17,9},{25,17},{2,26},{10... | collective-permute-start | bytes 786440 | tf_op jit(solution)/shard_map/ppermute | solution.py:262
  18.0 1.0 copy-done.2
  18.9 0.9 copy-done.4
  19.9 0.7 copy-done.8
  20.5 0.7 copy-done.9
  21.2 0.7 copy-done.10
  22.1 5.0 %collective-permute-done.1.refs_2_ = bf16[32,4224]{1,0:T(8,128)(2,1)S(1)} collective-permute-done((bf16[32,4224]{1,0:T(8,128)(2,1)}, bf16[32,4224]{1,0:T(8,128)(2,1)S(1)}, u32[]{:S(2)}, u32[]{:S(2)}) %collective-permute-start.1) | collective-permute-done | bytes 270368 | tf_op jit(solution)/shard_map/ppermute | solution.py:262
  27.2 1.5 %shard_map.140.probs_ref = bf16[16,128,128]{2,1,0:T(8,128)(2,1)S(1)} custom-call(bf16[128,128]{1,0:T(8,128)(2,1)S(1)} %get-tuple-element.50.place_ref, f32[128,128]{1,0:T(8,128)S(1)} %get-tuple-element.52.outside_ref, bf16[32,4224]{1,0:T(8,128)(2,1)S(1)} %get-tuple-element.46.refs_0_, bf16[32,4224]{1,0:T(8,128)(2,1)S(1)} %collective-permute-done.refs_1_, ...), custom_call_target="tpu_custom_call" | custom-call | bytes 1703936 | tf_op jit(solution)/shard_map/pallas_call | solution.py:41
  28.8 4.0 %collective-permute-done.3.refs_1_ = bf16[32,4096]{1,0:T(8,128)(2,1)S(1)} collective-permute-done((bf16[32,4096]{1,0:T(8,128)(2,1)}, bf16[32,4096]{1,0:T(8,128)(2,1)S(1)}, u32[]{:S(2)}, u32[]{:S(2)}) %collective-permute-start.3) | collective-permute-done | bytes 262176 | tf_op jit(solution)/shard_map/ppermute | solution.py:262
  32.7 16.2 %collective-permute-done.4.refs_2_ = bf16[32,4096]{1,0:T(8,128)(2,1)S(1)} collective-permute-done((bf16[32,4096]{1,0:T(8,128)(2,1)}, bf16[32,4096]{1,0:T(8,128)(2,1)S(1)}, u32[]{:S(2)}, u32[]{:S(2)}) %collective-permute-start.4) | collective-permute-done | bytes 262176 | tf_op jit(solution)/shard_map/ppermute | solution.py:262
  49.2 0.8 shard_map.142
  50.1 1.3 %collective-permute-done.6.other_ref = bf16[32,2048]{1,0:T(8,128)(2,1)S(1)} collective-permute-done((bf16[32,2048]{1,0:T(8,128)(2,1)S(1)}, bf16[32,2048]{1,0:T(8,128)(2,1)S(1)}, u32[]{:S(2)}, u32[]{:S(2)}) %collective-permute-start.6) | collective-permute-done | bytes 131104 | tf_op jit(solution)/shard_map/ppermute | solution.py:333
  51.5 1.6 %collective-permute-start.10 = (bf16[16,2048]{1,0:T(8,128)(2,1)S(1)}, bf16[16,2048]{1,0:T(8,128)(2,1)S(1)}, u32[]{:S(2)}, u32[]{:S(2)}) collective-permute-start(bf16[16,2048]{1,0:T(8,128)(2,1)S(1)} %get-tuple-element.65), channel_id=1, source_target_pairs={{0,4},{1,5},{2,6},{3,7},{4,0},{5,1},{6,2},{7,3},{8,12},{9,13},{10,... | collective-permute-start | bytes 196616 | tf_op jit(solution)/shard_map/ppermute | solution.py:333
  53.0 1.4 %collective-permute-start.11 = (bf16[16,2048]{1,0:T(8,128)(2,1)S(1)}, bf16[16,2048]{1,0:T(8,128)(2,1)S(1)}, u32[]{:S(2)}, u32[]{:S(2)}) collective-permute-start(bf16[16,2048]{1,0:T(8,128)(2,1)S(1)} %get-tuple-element.66), channel_id=1, source_target_pairs={{0,6},{1,7},{2,4},{3,5},{4,2},{5,3},{6,0},{7,1},{8,14},{9,15},{10,... | collective-permute-start | bytes 196616 | tf_op jit(solution)/shard_map/ppermute | solution.py:333
  54.5 0.5 collective-permute-start.7
  55.0 0.8 collective-permute-done.10.refs_0_
  55.8 3.0 %collective-permute-done.11.refs_1_ = bf16[16,2048]{1,0:T(8,128)(2,1)S(1)} collective-permute-done((bf16[16,2048]{1,0:T(8,128)(2,1)S(1)}, bf16[16,2048]{1,0:T(8,128)(2,1)S(1)}, u32[]{:S(2)}, u32[]{:S(2)}) %collective-permute-start.11) | collective-permute-done | bytes 65568 | tf_op jit(solution)/shard_map/ppermute | solution.py:333
  58.8 5.2 %collective-permute-start.12 = (bf16[32,2048]{1,0:T(8,128)(2,1)S(1)}, bf16[32,2048]{1,0:T(8,128)(2,1)S(1)}, u32[]{:S(2)}, u32[]{:S(2)}) collective-permute-start(bf16[32,2048]{1,0:T(8,128)(2,1)S(1)} %shard_map.146.refs_0_), channel_id=1, source_target_pairs={{0,16},{8,24},{16,0},{24,8},{1,17},{9,25},{17,1},{25,9},{2,18},{10... | collective-permute-start | bytes 393224 | tf_op jit(solution)/shard_map/ppermute | solution.py:333
  64.2 3.8 %collective-permute-start.8 = (bf16[32,2048]{1,0:T(8,128)(2,1)S(1)}, bf16[32,2048]{1,0:T(8,128)(2,1)S(1)}, u32[]{:S(2)}, u32[]{:S(2)}) collective-permute-start(bf16[32,2048]{1,0:T(8,128)(2,1)S(1)} %shard_map.144.refs_0_), channel_id=1, source_target_pairs={{0,8},{8,0},{16,24},{24,16},{1,9},{9,1},{17,25},{25,17},{2,10},{10... | collective-permute-start | bytes 393224 | tf_op jit(solution)/shard_map/ppermute | solution.py:333
  68.0 5.2 %collective-permute-done.12.refs_2_ = bf16[32,2048]{1,0:T(8,128)(2,1)S(1)} collective-permute-done((bf16[32,2048]{1,0:T(8,128)(2,1)S(1)}, bf16[32,2048]{1,0:T(8,128)(2,1)S(1)}, u32[]{:S(2)}, u32[]{:S(2)}) %collective-permute-start.12) | collective-permute-done | bytes 131104 | tf_op jit(solution)/shard_map/ppermute | solution.py:333
  73.2 2.1 %collective-permute-done.14.refs_3_ = bf16[32,2048]{1,0:T(8,128)(2,1)S(1)} collective-permute-done((bf16[32,2048]{1,0:T(8,128)(2,1)S(1)}, bf16[32,2048]{1,0:T(8,128)(2,1)S(1)}, u32[]{:S(2)}, u32[]{:S(2)}) %collective-permute-start.14) | collective-permute-done | bytes 131104 | tf_op jit(solution)/shard_map/ppermute | solution.py:333
  75.4 1.6 %shard_map.145 = (bf16[32,2048]{1,0:T(8,128)(2,1)S(1)}, bf16[32,2048]{1,0:T(8,128)(2,1)S(1)}) custom-call(f32[1,1024]{1,0:T(1,128)S(1)} %copy-done.5, bf16[1,2048,1024]{2,1,0:T(8,128)(2,1)S(1)} %copy-done, bf16[1,1024,2048]{2,1,0:T(8,128)(2,1)S(1)} %copy-done.1, bf16[32,2048]{1,0:T(8,128)(2,1)S(1)} %shard_map.144.refs_0_, ...), custom_call_target="tpu_custom_call" | custom-call | flops 536870912 | bytes 8916992 | tf_op jit(solution)/shard_map/pallas_call | solution.py:41
  77.0 1.6 %shard_map.147 = (bf16[32,2048]{1,0:T(8,128)(2,1)S(1)}, bf16[32,2048]{1,0:T(8,128)(2,1)S(1)}) custom-call(f32[1,1024]{1,0:T(1,128)S(1)} %copy-done.5, bf16[1,2048,1024]{2,1,0:T(8,128)(2,1)S(1)} %copy-done, bf16[1,1024,2048]{2,1,0:T(8,128)(2,1)S(1)} %copy-done.1, bf16[32,2048]{1,0:T(8,128)(2,1)S(1)} %shard_map.146.refs_0_, ...), custom_call_target="tpu_custom_call" | custom-call | flops 536870912 | bytes 9048064 | tf_op jit(solution)/shard_map/pallas_call | solution.py:41
  78.6 1.2 %collective-permute-done.13.refs_0_ = bf16[32,2048]{1,0:T(8,128)(2,1)S(1)} collective-permute-done((bf16[32,2048]{1,0:T(8,128)(2,1)S(1)}, bf16[32,2048]{1,0:T(8,128)(2,1)S(1)}, u32[]{:S(2)}, u32[]{:S(2)}) %collective-permute-start.13) | collective-permute-done | bytes 131104 | tf_op jit(solution)/shard_map/ppermute | solution.py:333
  79.8 1.5 %collective-permute-done.15.refs_1_ = bf16[32,2048]{1,0:T(8,128)(2,1)S(1)} collective-permute-done((bf16[32,2048]{1,0:T(8,128)(2,1)S(1)}, bf16[32,2048]{1,0:T(8,128)(2,1)S(1)}, u32[]{:S(2)}, u32[]{:S(2)}) %collective-permute-start.15) | collective-permute-done | bytes 131104 | tf_op jit(solution)/shard_map/ppermute | solution.py:333
  81.3 1.4 %shard_map.148 = (bf16[32,2048]{1,0:T(8,128)(2,1)S(1)}, bf16[32,2048]{1,0:T(8,128)(2,1)S(1)}, bf16[32,2048]{1,0:T(8,128)(2,1)S(1)}, bf16[32,2048]{1,0:T(8,128)(2,1)S(1)}) custom-call(f32[1,1024]{1,0:T(1,128)S(1)} %copy-done.5, bf16[1,2048,1024]{2,1,0:T(8,128)(2,1)S(1)} %copy-done, bf16[1,1024,2048]{2,1,0:T(8,128)(2,1)S(1)} %copy-done.1, ...), custom_call_target="tpu_custom_call" | custom-call | flops 1073741824 | bytes 9572352 | tf_op jit(solution)/shard_map/pallas_call | solution.py:41
  82.6 0.5 collective-permute-start.21
  83.1 1.6 %collective-permute-start.17 = (bf16[32,2048]{1,0:T(8,128)(2,1)S(1)}, bf16[32,2048]{1,0:T(8,128)(2,1)S(1)}, u32[]{:S(2)}, u32[]{:S(2)}) collective-permute-start(bf16[32,2048]{1,0:T(8,128)(2,1)S(1)} %get-tuple-element.68), channel_id=1, source_target_pairs={{0,8},{8,0},{16,24},{24,16},{1,9},{9,1},{17,25},{25,17},{2,10},{10... | collective-permute-start | bytes 393224 | tf_op jit(solution)/shard_map/ppermute | solution.py:333
  84.7 0.4 collective-permute-start.20
  85.1 5.4 %collective-permute-done.21.first_ref = bf16[32,2048]{1,0:T(8,128)(2,1)S(1)} collective-permute-done((bf16[32,2048]{1,0:T(8,128)(2,1)S(1)}, bf16[32,2048]{1,0:T(8,128)(2,1)S(1)}, u32[]{:S(2)}, u32[]{:S(2)}) %collective-permute-start.21) | collective-permute-done | bytes 131104 | tf_op jit(solution)/shard_map/ppermute | solution.py:333
  90.6 2.0 %collective-permute-start.22 = (bf16[32,2048]{1,0:T(8,128)(2,1)S(1)}, bf16[32,2048]{1,0:T(8,128)(2,1)S(1)}, u32[]{:S(2)}, u32[]{:S(2)}) collective-permute-start(bf16[32,2048]{1,0:T(8,128)(2,1)S(1)} %shard_map.151), channel_id=1, source_target_pairs={{0,16},{8,24},{16,0},{24,8},{1,17},{9,25},{17,1},{25,9},{2,18},{10... | collective-permute-start | bytes 393224 | tf_op jit(solution)/shard_map/ppermute | solution.py:333
  92.5 3.0 %collective-permute-start.9 = (bf16[32,2048]{1,0:T(8,128)(2,1)S(1)}, bf16[32,2048]{1,0:T(8,128)(2,1)S(1)}, u32[]{:S(2)}, u32[]{:S(2)}) collective-permute-start(bf16[32,2048]{1,0:T(8,128)(2,1)S(1)} %get-tuple-element.63), channel_id=1, source_target_pairs={{0,8},{8,0},{16,24},{24,16},{1,9},{9,1},{17,25},{25,17},{2,10},{10... | collective-permute-start | bytes 393224 | tf_op jit(solution)/shard_map/ppermute | solution.py:333
  95.5 1.7 %collective-permute-start.18 = (bf16[32,2048]{1,0:T(8,128)(2,1)S(1)}, bf16[32,2048]{1,0:T(8,128)(2,1)S(1)}, u32[]{:S(2)}, u32[]{:S(2)}) collective-permute-start(bf16[32,2048]{1,0:T(8,128)(2,1)S(1)} %shard_map.149), channel_id=1, source_target_pairs={{0,16},{8,24},{16,0},{24,8},{1,17},{9,25},{17,1},{25,9},{2,18},{10... | collective-permute-start | bytes 393224 | tf_op jit(solution)/shard_map/ppermute | solution.py:333
  97.3 0.8 collective-permute-done.20.near_ref
  98.2 0.8 collective-permute-start.23
  99.0 2.4 %collective-permute-start.24 = (bf16[16,2048]{1,0:T(8,128)(2,1)S(1)}, bf16[16,2048]{1,0:T(8,128)(2,1)S(1)}, u32[]{:S(2)}, u32[]{:S(2)}) collective-permute-start(bf16[16,2048]{1,0:T(8,128)(2,1)S(1)} %get-tuple-element.76), channel_id=1, source_target_pairs={{0,6},{1,7},{2,4},{3,5},{4,2},{5,3},{6,0},{7,1},{8,14},{9,15},{10,... | collective-permute-start | bytes 196616 | tf_op jit(solution)/shard_map/ppermute | solution.py:333
  101.7 1.7 %collective-permute-start.19 = (bf16[16,2048]{1,0:T(8,128)(2,1)S(1)}, bf16[16,2048]{1,0:T(8,128)(2,1)S(1)}, u32[]{:S(2)}, u32[]{:S(2)}) collective-permute-start(bf16[16,2048]{1,0:T(8,128)(2,1)S(1)} %get-tuple-element.71), channel_id=1, source_target_pairs={{0,2},{1,3},{2,0},{3,1},{4,6},{5,7},{6,4},{7,5},{8,10},{9,11},{10,... | collective-permute-start | bytes 196616 | tf_op jit(solution)/shard_map/ppermute | solution.py:333
  103.4 0.7 collective-permute-done.24.refs_3_
  104.1 1.9 %collective-permute-done.19.refs_1_ = bf16[16,2048]{1,0:T(8,128)(2,1)S(1)} collective-permute-done((bf16[16,2048]{1,0:T(8,128)(2,1)S(1)}, bf16[16,2048]{1,0:T(8,128)(2,1)S(1)}, u32[]{:S(2)}, u32[]{:S(2)}) %collective-permute-start.19) | collective-permute-done | bytes 65568 | tf_op jit(solution)/shard_map/ppermute | solution.py:333
  106.1 1.3 %collective-permute-done.25.refs_1_ = bf16[32,2048]{1,0:T(8,128)(2,1)S(1)} collective-permute-done((bf16[32,2048]{1,0:T(8,128)(2,1)S(1)}, bf16[32,2048]{1,0:T(8,128)(2,1)S(1)}, u32[]{:S(2)}, u32[]{:S(2)}) %collective-permute-start.25) | collective-permute-done | bytes 131104 | tf_op jit(solution)/shard_map/ppermute | solution.py:333
  107.5 1.1 shard_map.154
  (45 shorter events, 1.9 us)
Async XLA Ops:
  0.0 49.2 %copy-start.7 = (f32[2048]{0:T(1024)S(1)}, f32[2048]{0:T(1024)}, u32[]{:S(2)}) copy-start(f32[2048]{0:T(1024)} %param.23) | copy-start | bytes 24580
  0.0 49.2 %copy-start.6 = (f32[2048]{0:T(1024)S(1)}, f32[2048]{0:T(1024)}, u32[]{:S(2)}) copy-start(f32[2048]{0:T(1024)} %param.22) | copy-start | bytes 24580
  2.8 12.7 %collective-permute-start = (bf16[32,4224]{1,0:T(8,128)(2,1)}, bf16[32,4224]{1,0:T(8,128)(2,1)S(1)}, u32[]{:S(2)}, u32[]{:S(2)}) collective-permute-start(bf16[32,4224]{1,0:T(8,128)(2,1)} %get-tuple-element.47), channel_id=1, source_target_pairs={{0,8},{8,16},{16,24},{24,0},{1,9},{9,17},{17,25},{25,1},{2,10},{10... | collective-permute-start | bytes 811016 | tf_op jit(solution)/shard_map/ppermute | solution.py:262
  5.8 21.3 %collective-permute-start.1 = (bf16[32,4224]{1,0:T(8,128)(2,1)}, bf16[32,4224]{1,0:T(8,128)(2,1)S(1)}, u32[]{:S(2)}, u32[]{:S(2)}) collective-permute-start(bf16[32,4224]{1,0:T(8,128)(2,1)} %get-tuple-element.48), channel_id=1, source_target_pairs={{0,16},{8,24},{16,0},{24,8},{1,17},{9,25},{17,1},{25,9},{2,18},{10... | collective-permute-start | bytes 811016 | tf_op jit(solution)/shard_map/ppermute | solution.py:262
  8.4 18.7 %collective-permute-start.2 = (bf16[32,4224]{1,0:T(8,128)(2,1)}, bf16[32,4224]{1,0:T(8,128)(2,1)S(1)}, u32[]{:S(2)}, u32[]{:S(2)}) collective-permute-start(bf16[32,4224]{1,0:T(8,128)(2,1)} %get-tuple-element.49), channel_id=1, source_target_pairs={{0,24},{8,0},{16,8},{24,16},{1,25},{9,1},{17,9},{25,17},{2,26},{10... | collective-permute-start | bytes 811016 | tf_op jit(solution)/shard_map/ppermute | solution.py:262
  12.3 20.4 %collective-permute-start.3 = (bf16[32,4096]{1,0:T(8,128)(2,1)}, bf16[32,4096]{1,0:T(8,128)(2,1)S(1)}, u32[]{:S(2)}, u32[]{:S(2)}) collective-permute-start(bf16[32,4096]{1,0:T(8,128)(2,1)} %get-tuple-element.54), channel_id=1, source_target_pairs={{0,8},{8,16},{16,24},{24,0},{1,9},{9,17},{17,25},{25,1},{2,10},{10... | collective-permute-start | bytes 786440 | tf_op jit(solution)/shard_map/ppermute | solution.py:262
  13.0 35.9 %collective-permute-start.4 = (bf16[32,4096]{1,0:T(8,128)(2,1)}, bf16[32,4096]{1,0:T(8,128)(2,1)S(1)}, u32[]{:S(2)}, u32[]{:S(2)}) collective-permute-start(bf16[32,4096]{1,0:T(8,128)(2,1)} %get-tuple-element.55), channel_id=1, source_target_pairs={{0,16},{8,24},{16,0},{24,8},{1,17},{9,25},{17,1},{25,9},{2,18},{10... | collective-permute-start | bytes 786440 | tf_op jit(solution)/shard_map/ppermute | solution.py:262
  15.5 33.4 %collective-permute-start.5 = (bf16[32,4096]{1,0:T(8,128)(2,1)}, bf16[32,4096]{1,0:T(8,128)(2,1)S(1)}, u32[]{:S(2)}, u32[]{:S(2)}) collective-permute-start(bf16[32,4096]{1,0:T(8,128)(2,1)} %get-tuple-element.56), channel_id=1, source_target_pairs={{0,24},{8,0},{16,8},{24,16},{1,25},{9,1},{17,9},{25,17},{2,26},{10... | collective-permute-start | bytes 786440 | tf_op jit(solution)/shard_map/ppermute | solution.py:262
  18.0 1.0 copy-start.2
  18.9 0.9 copy-start.4
  19.9 0.7 copy-start.8
  20.5 0.7 copy-start.9
  21.2 0.7 copy-start.10
  27.1 48.2 %copy-start = (bf16[1,2048,1024]{2,1,0:T(8,128)(2,1)S(1)}, bf16[1,2048,1024]{2,1,0:T(8,128)(2,1)}, u32[]{:S(2)}) copy-start(bf16[1,2048,1024]{2,1,0:T(8,128)(2,1)} %w_in_ref.5) | copy-start | bytes 12582916
  27.1 48.3 %copy-start.1 = (bf16[1,1024,2048]{2,1,0:T(8,128)(2,1)S(1)}, bf16[1,1024,2048]{2,1,0:T(8,128)(2,1)}, u32[]{:S(2)}) copy-start(bf16[1,1024,2048]{2,1,0:T(8,128)(2,1)} %w_out_ref.5) | copy-start | bytes 12582916
  27.1 48.3 %copy-start.5 = (f32[1,1024]{1,0:T(1,128)S(1)}, f32[1,1024]{1,0:T(1,128)}, u32[]{:S(2)}) copy-start(f32[1,1024]{1,0:T(1,128)} %bias_ref.7) | copy-start | bytes 12292
  50.0 1.4 %collective-permute-start.6 = (bf16[32,2048]{1,0:T(8,128)(2,1)S(1)}, bf16[32,2048]{1,0:T(8,128)(2,1)S(1)}, u32[]{:S(2)}, u32[]{:S(2)}) collective-permute-start(bf16[32,2048]{1,0:T(8,128)(2,1)S(1)} %get-tuple-element.60), channel_id=1, source_target_pairs={{0,1},{1,0},{2,3},{3,2},{4,5},{5,4},{6,7},{7,6},{8,9},{9,8},{10,11... | collective-permute-start | bytes 393224 | tf_op jit(solution)/shard_map/ppermute | solution.py:333
  51.5 4.3 %collective-permute-start.10 = (bf16[16,2048]{1,0:T(8,128)(2,1)S(1)}, bf16[16,2048]{1,0:T(8,128)(2,1)S(1)}, u32[]{:S(2)}, u32[]{:S(2)}) collective-permute-start(bf16[16,2048]{1,0:T(8,128)(2,1)S(1)} %get-tuple-element.65), channel_id=1, source_target_pairs={{0,4},{1,5},{2,6},{3,7},{4,0},{5,1},{6,2},{7,3},{8,12},{9,13},{10,... | collective-permute-start | bytes 196616 | tf_op jit(solution)/shard_map/ppermute | solution.py:333
  53.0 5.8 %collective-permute-start.11 = (bf16[16,2048]{1,0:T(8,128)(2,1)S(1)}, bf16[16,2048]{1,0:T(8,128)(2,1)S(1)}, u32[]{:S(2)}, u32[]{:S(2)}) collective-permute-start(bf16[16,2048]{1,0:T(8,128)(2,1)S(1)} %get-tuple-element.66), channel_id=1, source_target_pairs={{0,6},{1,7},{2,4},{3,5},{4,2},{5,3},{6,0},{7,1},{8,14},{9,15},{10,... | collective-permute-start | bytes 196616 | tf_op jit(solution)/shard_map/ppermute | solution.py:333
  54.5 9.6 %collective-permute-start.7 = (bf16[16,2048]{1,0:T(8,128)(2,1)S(1)}, bf16[16,2048]{1,0:T(8,128)(2,1)S(1)}, u32[]{:S(2)}, u32[]{:S(2)}) collective-permute-start(bf16[16,2048]{1,0:T(8,128)(2,1)S(1)} %get-tuple-element.62), channel_id=1, source_target_pairs={{0,2},{1,3},{2,0},{3,1},{4,6},{5,7},{6,4},{7,5},{8,10},{9,11},{10,... | collective-permute-start | bytes 196616 | tf_op jit(solution)/shard_map/ppermute | solution.py:333
  58.8 14.4 %collective-permute-start.12 = (bf16[32,2048]{1,0:T(8,128)(2,1)S(1)}, bf16[32,2048]{1,0:T(8,128)(2,1)S(1)}, u32[]{:S(2)}, u32[]{:S(2)}) collective-permute-start(bf16[32,2048]{1,0:T(8,128)(2,1)S(1)} %shard_map.146.refs_0_), channel_id=1, source_target_pairs={{0,16},{8,24},{16,0},{24,8},{1,17},{9,25},{17,1},{25,9},{2,18},{10... | collective-permute-start | bytes 393224 | tf_op jit(solution)/shard_map/ppermute | solution.py:333
  64.1 11.3 %collective-permute-start.14 = (bf16[32,2048]{1,0:T(8,128)(2,1)S(1)}, bf16[32,2048]{1,0:T(8,128)(2,1)S(1)}, u32[]{:S(2)}, u32[]{:S(2)}) collective-permute-start(bf16[32,2048]{1,0:T(8,128)(2,1)S(1)} %shard_map.144.refs_0_), channel_id=1, source_target_pairs={{0,16},{8,24},{16,0},{24,8},{1,17},{9,25},{17,1},{25,9},{2,18},{10... | collective-permute-start | bytes 393224 | tf_op jit(solution)/shard_map/ppermute | solution.py:333
  64.2 11.2 %collective-permute-start.8 = (bf16[32,2048]{1,0:T(8,128)(2,1)S(1)}, bf16[32,2048]{1,0:T(8,128)(2,1)S(1)}, u32[]{:S(2)}, u32[]{:S(2)}) collective-permute-start(bf16[32,2048]{1,0:T(8,128)(2,1)S(1)} %shard_map.144.refs_0_), channel_id=1, source_target_pairs={{0,8},{8,0},{16,24},{24,16},{1,9},{9,1},{17,25},{25,17},{2,10},{10... | collective-permute-start | bytes 393224 | tf_op jit(solution)/shard_map/ppermute | solution.py:333
  68.0 9.0 %collective-permute-start.16 = (bf16[32,2048]{1,0:T(8,128)(2,1)S(1)}, bf16[32,2048]{1,0:T(8,128)(2,1)S(1)}, u32[]{:S(2)}, u32[]{:S(2)}) collective-permute-start(bf16[32,2048]{1,0:T(8,128)(2,1)S(1)} %shard_map.146.refs_0_), channel_id=1, source_target_pairs={{0,8},{8,0},{16,24},{24,16},{1,9},{9,1},{17,25},{25,17},{2,10},{10... | collective-permute-start | bytes 393224 | tf_op jit(solution)/shard_map/ppermute | solution.py:333
  73.2 6.6 %collective-permute-start.13 = (bf16[32,2048]{1,0:T(8,128)(2,1)S(1)}, bf16[32,2048]{1,0:T(8,128)(2,1)S(1)}, u32[]{:S(2)}, u32[]{:S(2)}) collective-permute-start(bf16[32,2048]{1,0:T(8,128)(2,1)S(1)} %collective-permute-done.12.refs_2_), channel_id=1, source_target_pairs={{0,8},{8,0},{16,24},{24,16},{1,9},{9,1},{17,25},{25,17},{2,10},{10... | collective-permute-start | bytes 393224 | tf_op jit(solution)/shard_map/ppermute | solution.py:333
  75.4 5.9 %collective-permute-start.15 = (bf16[32,2048]{1,0:T(8,128)(2,1)S(1)}, bf16[32,2048]{1,0:T(8,128)(2,1)S(1)}, u32[]{:S(2)}, u32[]{:S(2)}) collective-permute-start(bf16[32,2048]{1,0:T(8,128)(2,1)S(1)} %collective-permute-done.14.refs_3_), channel_id=1, source_target_pairs={{0,8},{8,0},{16,24},{24,16},{1,9},{9,1},{17,25},{25,17},{2,10},{10... | collective-permute-start | bytes 393224 | tf_op jit(solution)/shard_map/ppermute | solution.py:333
  81.3 16.8 %copy-start.3 = (f32[8,2048]{1,0:T(8,128)S(1)}, f32[8,2048]{1,0:T(8,128)}, u32[]{:S(2)}) copy-start(f32[8,2048]{1,0:T(8,128)} %bias_ref.9) | copy-start | bytes 196612
  82.6 7.9 %collective-permute-start.21 = (bf16[32,2048]{1,0:T(8,128)(2,1)S(1)}, bf16[32,2048]{1,0:T(8,128)(2,1)S(1)}, u32[]{:S(2)}, u32[]{:S(2)}) collective-permute-start(bf16[32,2048]{1,0:T(8,128)(2,1)S(1)} %get-tuple-element.73), channel_id=1, source_target_pairs={{0,8},{8,0},{16,24},{24,16},{1,9},{9,1},{17,25},{25,17},{2,10},{10... | collective-permute-start | bytes 393224 | tf_op jit(solution)/shard_map/ppermute | solution.py:333
  83.1 12.4 %collective-permute-start.17 = (bf16[32,2048]{1,0:T(8,128)(2,1)S(1)}, bf16[32,2048]{1,0:T(8,128)(2,1)S(1)}, u32[]{:S(2)}, u32[]{:S(2)}) collective-permute-start(bf16[32,2048]{1,0:T(8,128)(2,1)S(1)} %get-tuple-element.68), channel_id=1, source_target_pairs={{0,8},{8,0},{16,24},{24,16},{1,9},{9,1},{17,25},{25,17},{2,10},{10... | collective-permute-start | bytes 393224 | tf_op jit(solution)/shard_map/ppermute | solution.py:333
  84.7 13.4 %collective-permute-start.20 = (bf16[32,2048]{1,0:T(8,128)(2,1)S(1)}, bf16[32,2048]{1,0:T(8,128)(2,1)S(1)}, u32[]{:S(2)}, u32[]{:S(2)}) collective-permute-start(bf16[32,2048]{1,0:T(8,128)(2,1)S(1)} %get-tuple-element.72), channel_id=1, source_target_pairs={{0,8},{8,0},{16,24},{24,16},{1,9},{9,1},{17,25},{25,17},{2,10},{10... | collective-permute-start | bytes 393224 | tf_op jit(solution)/shard_map/ppermute | solution.py:333
  90.6 7.5 %collective-permute-start.22 = (bf16[32,2048]{1,0:T(8,128)(2,1)S(1)}, bf16[32,2048]{1,0:T(8,128)(2,1)S(1)}, u32[]{:S(2)}, u32[]{:S(2)}) collective-permute-start(bf16[32,2048]{1,0:T(8,128)(2,1)S(1)} %shard_map.151), channel_id=1, source_target_pairs={{0,16},{8,24},{16,0},{24,8},{1,17},{9,25},{17,1},{25,9},{2,18},{10... | collective-permute-start | bytes 393224 | tf_op jit(solution)/shard_map/ppermute | solution.py:333
  92.5 8.8 %collective-permute-start.9 = (bf16[32,2048]{1,0:T(8,128)(2,1)S(1)}, bf16[32,2048]{1,0:T(8,128)(2,1)S(1)}, u32[]{:S(2)}, u32[]{:S(2)}) collective-permute-start(bf16[32,2048]{1,0:T(8,128)(2,1)S(1)} %get-tuple-element.63), channel_id=1, source_target_pairs={{0,8},{8,0},{16,24},{24,16},{1,9},{9,1},{17,25},{25,17},{2,10},{10... | collective-permute-start | bytes 393224 | tf_op jit(solution)/shard_map/ppermute | solution.py:333
  95.5 6.1 %collective-permute-start.18 = (bf16[32,2048]{1,0:T(8,128)(2,1)S(1)}, bf16[32,2048]{1,0:T(8,128)(2,1)S(1)}, u32[]{:S(2)}, u32[]{:S(2)}) collective-permute-start(bf16[32,2048]{1,0:T(8,128)(2,1)S(1)} %shard_map.149), channel_id=1, source_target_pairs={{0,16},{8,24},{16,0},{24,8},{1,17},{9,25},{17,1},{25,9},{2,18},{10... | collective-permute-start | bytes 393224 | tf_op jit(solution)/shard_map/ppermute | solution.py:333
  98.2 5.2 %collective-permute-start.23 = (bf16[16,2048]{1,0:T(8,128)(2,1)S(1)}, bf16[16,2048]{1,0:T(8,128)(2,1)S(1)}, u32[]{:S(2)}, u32[]{:S(2)}) collective-permute-start(bf16[16,2048]{1,0:T(8,128)(2,1)S(1)} %get-tuple-element.75), channel_id=1, source_target_pairs={{0,4},{1,5},{2,6},{3,7},{4,0},{5,1},{6,2},{7,3},{8,12},{9,13},{10,... | collective-permute-start | bytes 196616 | tf_op jit(solution)/shard_map/ppermute | solution.py:333
  99.0 5.2 %collective-permute-start.24 = (bf16[16,2048]{1,0:T(8,128)(2,1)S(1)}, bf16[16,2048]{1,0:T(8,128)(2,1)S(1)}, u32[]{:S(2)}, u32[]{:S(2)}) collective-permute-start(bf16[16,2048]{1,0:T(8,128)(2,1)S(1)} %get-tuple-element.76), channel_id=1, source_target_pairs={{0,6},{1,7},{2,4},{3,5},{4,2},{5,3},{6,0},{7,1},{8,14},{9,15},{10,... | collective-permute-start | bytes 196616 | tf_op jit(solution)/shard_map/ppermute | solution.py:333
  101.7 4.3 %collective-permute-start.19 = (bf16[16,2048]{1,0:T(8,128)(2,1)S(1)}, bf16[16,2048]{1,0:T(8,128)(2,1)S(1)}, u32[]{:S(2)}, u32[]{:S(2)}) collective-permute-start(bf16[16,2048]{1,0:T(8,128)(2,1)S(1)} %get-tuple-element.71), channel_id=1, source_target_pairs={{0,2},{1,3},{2,0},{3,1},{4,6},{5,7},{6,4},{7,5},{8,10},{9,11},{10,... | collective-permute-start | bytes 196616 | tf_op jit(solution)/shard_map/ppermute | solution.py:333
  106.1 1.4 %collective-permute-start.25 = (bf16[32,2048]{1,0:T(8,128)(2,1)S(1)}, bf16[32,2048]{1,0:T(8,128)(2,1)S(1)}, u32[]{:S(2)}, u32[]{:S(2)}) collective-permute-start(bf16[32,2048]{1,0:T(8,128)(2,1)S(1)} %get-tuple-element.78), channel_id=1, source_target_pairs={{0,1},{1,0},{2,3},{3,2},{4,5},{5,4},{6,7},{7,6},{8,9},{9,8},{10,11... | collective-permute-start | bytes 393224 | tf_op jit(solution)/shard_map/ppermute | solution.py:333

commit v11 on v10

--- a/solution.py
+++ b/solution.py
@@ -180,8 +180,11 @@
         at += out_ref.shape[0]
 
 
-def add_kernel(first_ref, second_ref, out_ref):
-    out_ref[...] = (first_ref[...].astype(F32) + second_ref[...].astype(F32)).astype(BF16)
+def add_kernel(first_ref, second_ref, *refs):
+    count = len(refs) // 2
+    refs[count][...] = (first_ref[...].astype(F32) + second_ref[...].astype(F32)).astype(BF16)
+    for n in range(count):
+        refs[count + 1 + n][...] = refs[n][...]
 
 
 def result_kernel(lower, bias_ref, near_ref, *refs):
@@ -348,18 +351,22 @@
         last = last[0]
         *corner_share, far_first, far_second = apply([swap(x, 1) for x in far] + far, after=[last])
         far_shares = [far_first, far_second]
-        near_shares = [swap(x, 1) for x in near_shares]
-        backs = [None, None]
-        for n in (1, 0):
-            pair = swap(call(add_kernel, bf16(half), swap(corner_share[n], 1), far_shares[n]), 2)
-            backs[n] = call(
+        pairs = [None, None]
+        pairs[0], *near_shares = call(
+            add_kernel, (bf16(half),) * 3, swap(corner_share[0], 1), far_shares[0], *near_shares
+        )
+        (pairs[1],) = call(add_kernel, (bf16(half),), swap(corner_share[1], 1), far_shares[1])
+        backs = [
+            call(
                 functools.partial(result_kernel, 0),
                 (bf16(2 * cap),) * 2,
                 b_out,
-                near_shares[n],
+                swap(near_shares[n], 1),
                 own_share[n],
-                pair,
+                swap(pairs[n], 2),
             )
+            for n in range(2)
+        ]
         pieces = [x for n in (1, 0) for x in backs[n]]
         pieces = [swap(x, 2 * n, "expert") if n else x for n, x in enumerate(pieces)]
         mine, other = call(functools.partial(part_kernel, cap), (bf16(half),) * 2, *pieces)

time: 109 us -> 109 us (level)
  starting transfers between devices: 37.4 us -> 42.4 us
  waiting for transfers between devices: 52.9 us -> 48.1 us
    ppermute x20, starting transfers between devices: 26.9 us -> 31.9 us  [swap(): lax.ppermute(x, axis, [(i, i ^ distance) for i in range(lax.axis_size(axi...]
    ppermute x20, waiting for transfers between devices: 25.6 us -> 20.8 us  [swap(): lax.ppermute(x, axis, [(i, i ^ distance) for i in range(lax.axis_size(axi...]
  transfers between devices with their start and end apart: 26 -> 26, of which waited for: 17 -> 18; matrix products, arithmetic and copies ran while one was open for 0% -> 0% of each run, Pallas kernels for 7% -> 7%
where the time goes in v11:
time: 109 us
  waiting for transfers between devices  48.1 us (44%)
  starting transfers between devices  42.4 us (39%)
  Pallas kernels  14.1 us (13%)
  local copies, waits for them, and re-layouts  3.94 us (4%)
    ppermute x20, starting transfers between devices, swap(): lax.ppermute(x, axis, [(i, i ^ distance) for i in range(lax.axis_size(axi...  31.9 us
    ppermute x6, waiting for transfers between devices, spread(): lax.ppermute(part, 'dp', [(i, (i + n) % dp) for i in range(dp)])  27.3 us
    ppermute x20, waiting for transfers between devices, swap(): lax.ppermute(x, axis, [(i, i ^ distance) for i in range(lax.axis_size(axi...  20.8 us
    pallas_call x19, Pallas kernels, call(): pl.pallas_call(body, out_shape=out_shape, compiler_params=pltpu.CompilerP...  14.1 us
    ppermute x6, starting transfers between devices, spread(): lax.ppermute(part, 'dp', [(i, (i + n) % dp) for i in range(dp)])  10.5 us
    unnamed x22, local copies, waits for them, and re-layouts  3.94 us
  transfers between devices with their start and end apart: 26, of which 18 were waited for; matrix products, arithmetic and copies ran while one was open for 0% of the time, Pallas kernels for 7%

profile of v11, /device:TPU:0, one launch (start us, length us, event | category | flops | bytes accessed | tf_op | source)
XLA Modules:
  0.0 108.8 jit_solution(3359747482985641598)
XLA Ops:
  0.0 2.7 %shard_map.136 = (bf16[128,128]{1,0:T(8,128)(2,1)}, bf16[32,4224]{1,0:T(8,128)(2,1)}, bf16[32,4224]{1,0:T(8,128)(2,1)}, bf16[32,4224]{1,0:T(8,128)(2,1)}, bf16[32,4224]{1,0:T(8,128)(2,1)}) custom-call(s32[1,128]{1,0:T(1,128)} %bitcast.9, bf16[128,2048]{1,0:T(8,128)(2,1)} %refs_0_.2, bf16[128,2048]{1,0:T(8,128)(2,1)} %refs_1_.2), custom_call_target="tpu_custom_call" | custom-call | bytes 2163200 | tf_op jit(solution)/shard_map/pallas_call | solution.py:41
  2.8 3.0 %collective-permute-start = (bf16[32,4224]{1,0:T(8,128)(2,1)}, bf16[32,4224]{1,0:T(8,128)(2,1)S(1)}, u32[]{:S(2)}, u32[]{:S(2)}) collective-permute-start(bf16[32,4224]{1,0:T(8,128)(2,1)} %get-tuple-element.50), channel_id=1, source_target_pairs={{0,8},{8,16},{16,24},{24,0},{1,9},{9,17},{17,25},{25,1},{2,10},{10... | collective-permute-start | bytes 811016 | tf_op jit(solution)/shard_map/ppermute | solution.py:265
  5.8 2.6 %collective-permute-start.1 = (bf16[32,4224]{1,0:T(8,128)(2,1)}, bf16[32,4224]{1,0:T(8,128)(2,1)S(1)}, u32[]{:S(2)}, u32[]{:S(2)}) collective-permute-start(bf16[32,4224]{1,0:T(8,128)(2,1)} %get-tuple-element.51), channel_id=1, source_target_pairs={{0,16},{8,24},{16,0},{24,8},{1,17},{9,25},{17,1},{25,9},{2,18},{10... | collective-permute-start | bytes 811016 | tf_op jit(solution)/shard_map/ppermute | solution.py:265
  8.4 1.3 %collective-permute-start.2 = (bf16[32,4224]{1,0:T(8,128)(2,1)}, bf16[32,4224]{1,0:T(8,128)(2,1)S(1)}, u32[]{:S(2)}, u32[]{:S(2)}) collective-permute-start(bf16[32,4224]{1,0:T(8,128)(2,1)} %get-tuple-element.52), channel_id=1, source_target_pairs={{0,24},{8,0},{16,8},{24,16},{1,25},{9,1},{17,9},{25,17},{2,26},{10... | collective-permute-start | bytes 811016 | tf_op jit(solution)/shard_map/ppermute | solution.py:265
  9.7 2.6 %shard_map.137 = (bf16[128,128]{1,0:T(8,128)(2,1)}, bf16[32,4096]{1,0:T(8,128)(2,1)}, bf16[32,4096]{1,0:T(8,128)(2,1)}, bf16[32,4096]{1,0:T(8,128)(2,1)}, bf16[32,4096]{1,0:T(8,128)(2,1)}) custom-call(bf16[128,128]{1,0:T(8,128)(2,1)} %get-tuple-element.46.pos_ref, bf16[128,2048]{1,0:T(8,128)(2,1)} %refs_0_.3, bf16[128,2048]{1,0:T(8,128)(2,1)} %refs_1_.3), custom_call_target="tpu_custom_call" | custom-call | bytes 2162688 | tf_op jit(solution)/shard_map/pallas_call | solution.py:41
  12.3 0.7 collective-permute-start.3
  13.3 2.1 %collective-permute-done.refs_1_ = bf16[32,4224]{1,0:T(8,128)(2,1)S(1)} collective-permute-done((bf16[32,4224]{1,0:T(8,128)(2,1)}, bf16[32,4224]{1,0:T(8,128)(2,1)S(1)}, u32[]{:S(2)}, u32[]{:S(2)}) %collective-permute-start) | collective-permute-done | bytes 270368 | tf_op jit(solution)/shard_map/ppermute | solution.py:265
  15.5 2.5 %collective-permute-start.5 = (bf16[32,4096]{1,0:T(8,128)(2,1)}, bf16[32,4096]{1,0:T(8,128)(2,1)S(1)}, u32[]{:S(2)}, u32[]{:S(2)}) collective-permute-start(bf16[32,4096]{1,0:T(8,128)(2,1)} %get-tuple-element.59), channel_id=1, source_target_pairs={{0,24},{8,0},{16,8},{24,16},{1,25},{9,1},{17,9},{25,17},{2,26},{10... | collective-permute-start | bytes 786440 | tf_op jit(solution)/shard_map/ppermute | solution.py:265
  17.9 1.0 copy-done.2
  18.9 0.9 copy-done.4
  19.9 0.7 copy-done.8
  20.5 0.7 copy-done.9
  21.2 0.7 copy-done.10
  22.1 5.0 %collective-permute-done.1.refs_2_ = bf16[32,4224]{1,0:T(8,128)(2,1)S(1)} collective-permute-done((bf16[32,4224]{1,0:T(8,128)(2,1)}, bf16[32,4224]{1,0:T(8,128)(2,1)S(1)}, u32[]{:S(2)}, u32[]{:S(2)}) %collective-permute-start.1) | collective-permute-done | bytes 270368 | tf_op jit(solution)/shard_map/ppermute | solution.py:265
  27.2 1.5 %shard_map.140.probs_ref = bf16[16,128,128]{2,1,0:T(8,128)(2,1)S(1)} custom-call(bf16[128,128]{1,0:T(8,128)(2,1)S(1)} %get-tuple-element.53.place_ref, f32[128,128]{1,0:T(8,128)S(1)} %get-tuple-element.55.outside_ref, bf16[32,4224]{1,0:T(8,128)(2,1)S(1)} %get-tuple-element.49.refs_0_, bf16[32,4224]{1,0:T(8,128)(2,1)S(1)} %collective-permute-done.refs_1_, ...), custom_call_target="tpu_custom_call" | custom-call | bytes 1703936 | tf_op jit(solution)/shard_map/pallas_call | solution.py:41
  28.7 4.0 %collective-permute-done.3.refs_1_ = bf16[32,4096]{1,0:T(8,128)(2,1)S(1)} collective-permute-done((bf16[32,4096]{1,0:T(8,128)(2,1)}, bf16[32,4096]{1,0:T(8,128)(2,1)S(1)}, u32[]{:S(2)}, u32[]{:S(2)}) %collective-permute-start.3) | collective-permute-done | bytes 262176 | tf_op jit(solution)/shard_map/ppermute | solution.py:265
  32.7 16.2 %collective-permute-done.4.refs_2_ = bf16[32,4096]{1,0:T(8,128)(2,1)S(1)} collective-permute-done((bf16[32,4096]{1,0:T(8,128)(2,1)}, bf16[32,4096]{1,0:T(8,128)(2,1)S(1)}, u32[]{:S(2)}, u32[]{:S(2)}) %collective-permute-start.4) | collective-permute-done | bytes 262176 | tf_op jit(solution)/shard_map/ppermute | solution.py:265
  49.2 0.8 shard_map.142
  50.1 1.3 %collective-permute-done.6.other_ref = bf16[32,2048]{1,0:T(8,128)(2,1)S(1)} collective-permute-done((bf16[32,2048]{1,0:T(8,128)(2,1)S(1)}, bf16[32,2048]{1,0:T(8,128)(2,1)S(1)}, u32[]{:S(2)}, u32[]{:S(2)}) %collective-permute-start.6) | collective-permute-done | bytes 131104 | tf_op jit(solution)/shard_map/ppermute | solution.py:336
  51.4 1.6 %collective-permute-start.11 = (bf16[16,2048]{1,0:T(8,128)(2,1)S(1)}, bf16[16,2048]{1,0:T(8,128)(2,1)S(1)}, u32[]{:S(2)}, u32[]{:S(2)}) collective-permute-start(bf16[16,2048]{1,0:T(8,128)(2,1)S(1)} %get-tuple-element.67), channel_id=1, source_target_pairs={{0,2},{1,3},{2,0},{3,1},{4,6},{5,7},{6,4},{7,5},{8,10},{9,11},{10,... | collective-permute-start | bytes 196616 | tf_op jit(solution)/shard_map/ppermute | solution.py:336
  53.0 1.5 %collective-permute-start.7 = (bf16[16,2048]{1,0:T(8,128)(2,1)S(1)}, bf16[16,2048]{1,0:T(8,128)(2,1)S(1)}, u32[]{:S(2)}, u32[]{:S(2)}) collective-permute-start(bf16[16,2048]{1,0:T(8,128)(2,1)S(1)} %get-tuple-element.64), channel_id=1, source_target_pairs={{0,4},{1,5},{2,6},{3,7},{4,0},{5,1},{6,2},{7,3},{8,12},{9,13},{10,... | collective-permute-start | bytes 196616 | tf_op jit(solution)/shard_map/ppermute | solution.py:336
  54.5 0.5 collective-permute-start.8
  55.0 0.8 collective-permute-done.11.refs_1_
  55.8 5.2 %collective-permute-start.12 = (bf16[32,2048]{1,0:T(8,128)(2,1)S(1)}, bf16[32,2048]{1,0:T(8,128)(2,1)S(1)}, u32[]{:S(2)}, u32[]{:S(2)}) collective-permute-start(bf16[32,2048]{1,0:T(8,128)(2,1)S(1)} %shard_map.145.refs_0_), channel_id=1, source_target_pairs={{0,16},{8,24},{16,0},{24,8},{1,17},{9,25},{17,1},{25,9},{2,18},{10... | collective-permute-start | bytes 393224 | tf_op jit(solution)/shard_map/ppermute | solution.py:336
  61.0 3.9 %collective-permute-start.9 = (bf16[32,2048]{1,0:T(8,128)(2,1)S(1)}, bf16[32,2048]{1,0:T(8,128)(2,1)S(1)}, u32[]{:S(2)}, u32[]{:S(2)}) collective-permute-start(bf16[32,2048]{1,0:T(8,128)(2,1)S(1)} %shard_map.144.refs_0_), channel_id=1, source_target_pairs={{0,16},{8,24},{16,0},{24,8},{1,17},{9,25},{17,1},{25,9},{2,18},{10... | collective-permute-start | bytes 393224 | tf_op jit(solution)/shard_map/ppermute | solution.py:336
  64.9 2.5 %collective-permute-start.15 = (bf16[32,2048]{1,0:T(8,128)(2,1)S(1)}, bf16[32,2048]{1,0:T(8,128)(2,1)S(1)}, u32[]{:S(2)}, u32[]{:S(2)}) collective-permute-start(bf16[32,2048]{1,0:T(8,128)(2,1)S(1)} %shard_map.145.refs_0_), channel_id=1, source_target_pairs={{0,8},{8,0},{16,24},{24,16},{1,9},{9,1},{17,25},{25,17},{2,10},{10... | collective-permute-start | bytes 393224 | tf_op jit(solution)/shard_map/ppermute | solution.py:336
  67.5 3.2 %collective-permute-start.13 = (bf16[32,2048]{1,0:T(8,128)(2,1)S(1)}, bf16[32,2048]{1,0:T(8,128)(2,1)S(1)}, u32[]{:S(2)}, u32[]{:S(2)}) collective-permute-start(bf16[32,2048]{1,0:T(8,128)(2,1)S(1)} %collective-permute-done.12.refs_3_), channel_id=1, source_target_pairs={{0,8},{8,0},{16,24},{24,16},{1,9},{9,1},{17,25},{25,17},{2,10},{10... | collective-permute-start | bytes 393224 | tf_op jit(solution)/shard_map/ppermute | solution.py:336
  70.6 1.6 %collective-permute-done.9.refs_2_ = bf16[32,2048]{1,0:T(8,128)(2,1)S(1)} collective-permute-done((bf16[32,2048]{1,0:T(8,128)(2,1)S(1)}, bf16[32,2048]{1,0:T(8,128)(2,1)S(1)}, u32[]{:S(2)}, u32[]{:S(2)}) %collective-permute-start.9) | collective-permute-done | bytes 131104 | tf_op jit(solution)/shard_map/ppermute | solution.py:336
  72.3 0.9 collective-permute-start.10
  73.2 0.7 collective-permute-done.15.refs_1_
  73.9 1.6 %shard_map.146 = (bf16[32,2048]{1,0:T(8,128)(2,1)S(1)}, bf16[32,2048]{1,0:T(8,128)(2,1)S(1)}) custom-call(f32[1,1024]{1,0:T(1,128)S(1)} %copy-done.5, bf16[1,2048,1024]{2,1,0:T(8,128)(2,1)S(1)} %copy-done, bf16[1,1024,2048]{2,1,0:T(8,128)(2,1)S(1)} %copy-done.1, bf16[32,2048]{1,0:T(8,128)(2,1)S(1)} %shard_map.145.refs_0_, ...), custom_call_target="tpu_custom_call" | custom-call | flops 536870912 | bytes 8916992 | tf_op jit(solution)/shard_map/pallas_call | solution.py:41
  75.5 1.2 %collective-permute-done.14.refs_1_ = bf16[32,2048]{1,0:T(8,128)(2,1)S(1)} collective-permute-done((bf16[32,2048]{1,0:T(8,128)(2,1)S(1)}, bf16[32,2048]{1,0:T(8,128)(2,1)S(1)}, u32[]{:S(2)}, u32[]{:S(2)}) %collective-permute-start.14) | collective-permute-done | bytes 131104 | tf_op jit(solution)/shard_map/ppermute | solution.py:336
  76.7 1.6 %shard_map.147 = (bf16[32,2048]{1,0:T(8,128)(2,1)S(1)}, bf16[32,2048]{1,0:T(8,128)(2,1)S(1)}) custom-call(f32[1,1024]{1,0:T(1,128)S(1)} %copy-done.5, bf16[1,2048,1024]{2,1,0:T(8,128)(2,1)S(1)} %copy-done, bf16[1,1024,2048]{2,1,0:T(8,128)(2,1)S(1)} %copy-done.1, bf16[32,2048]{1,0:T(8,128)(2,1)S(1)} %shard_map.144.refs_0_, ...), custom_call_target="tpu_custom_call" | custom-call | flops 536870912 | bytes 9048064 | tf_op jit(solution)/shard_map/pallas_call | solution.py:41
  78.6 1.4 %collective-permute-done.10.refs_0_ = bf16[32,2048]{1,0:T(8,128)(2,1)S(1)} collective-permute-done((bf16[32,2048]{1,0:T(8,128)(2,1)S(1)}, bf16[32,2048]{1,0:T(8,128)(2,1)S(1)}, u32[]{:S(2)}, u32[]{:S(2)}) %collective-permute-start.10) | collective-permute-done | bytes 131104 | tf_op jit(solution)/shard_map/ppermute | solution.py:336
  80.0 1.3 %shard_map.148 = (bf16[32,2048]{1,0:T(8,128)(2,1)S(1)}, bf16[32,2048]{1,0:T(8,128)(2,1)S(1)}, bf16[32,2048]{1,0:T(8,128)(2,1)S(1)}, bf16[32,2048]{1,0:T(8,128)(2,1)S(1)}) custom-call(f32[1,1024]{1,0:T(1,128)S(1)} %copy-done.5, bf16[1,2048,1024]{2,1,0:T(8,128)(2,1)S(1)} %copy-done, bf16[1,1024,2048]{2,1,0:T(8,128)(2,1)S(1)} %copy-done.1, ...), custom_call_target="tpu_custom_call" | custom-call | flops 1073741824 | bytes 9572352 | tf_op jit(solution)/shard_map/pallas_call | solution.py:41
  81.3 0.9 collective-permute-start.16
  82.2 1.2 %collective-permute-start.18 = (bf16[32,2048]{1,0:T(8,128)(2,1)S(1)}, bf16[32,2048]{1,0:T(8,128)(2,1)S(1)}, u32[]{:S(2)}, u32[]{:S(2)}) collective-permute-start(bf16[32,2048]{1,0:T(8,128)(2,1)S(1)} %get-tuple-element.75), channel_id=1, source_target_pairs={{0,8},{8,0},{16,24},{24,16},{1,9},{9,1},{17,25},{25,17},{2,10},{10... | collective-permute-start | bytes 393224 | tf_op jit(solution)/shard_map/ppermute | solution.py:336
  83.4 3.7 %collective-permute-done.16.first_ref = bf16[32,2048]{1,0:T(8,128)(2,1)S(1)} collective-permute-done((bf16[32,2048]{1,0:T(8,128)(2,1)S(1)}, bf16[32,2048]{1,0:T(8,128)(2,1)S(1)}, u32[]{:S(2)}, u32[]{:S(2)}) %collective-permute-start.16) | collective-permute-done | bytes 131104 | tf_op jit(solution)/shard_map/ppermute | solution.py:336
  87.1 0.7 collective-permute-start.21
  87.8 5.4 %collective-permute-start.22 = (bf16[32,2048]{1,0:T(8,128)(2,1)S(1)}, bf16[32,2048]{1,0:T(8,128)(2,1)S(1)}, u32[]{:S(2)}, u32[]{:S(2)}) collective-permute-start(bf16[32,2048]{1,0:T(8,128)(2,1)S(1)} %get-tuple-element.80), channel_id=1, source_target_pairs={{0,16},{8,24},{16,0},{24,8},{1,17},{9,25},{17,1},{25,9},{2,18},{10... | collective-permute-start | bytes 393224 | tf_op jit(solution)/shard_map/ppermute | solution.py:336
  93.6 2.6 %collective-permute-start.19 = (bf16[32,2048]{1,0:T(8,128)(2,1)S(1)}, bf16[32,2048]{1,0:T(8,128)(2,1)S(1)}, u32[]{:S(2)}, u32[]{:S(2)}) collective-permute-start(bf16[32,2048]{1,0:T(8,128)(2,1)S(1)} %shard_map.150), channel_id=1, source_target_pairs={{0,16},{8,24},{16,0},{24,8},{1,17},{9,25},{17,1},{25,9},{2,18},{10... | collective-permute-start | bytes 393224 | tf_op jit(solution)/shard_map/ppermute | solution.py:336
  96.2 1.3 %collective-permute-done.21.near_ref = bf16[32,2048]{1,0:T(8,128)(2,1)S(1)} collective-permute-done((bf16[32,2048]{1,0:T(8,128)(2,1)S(1)}, bf16[32,2048]{1,0:T(8,128)(2,1)S(1)}, u32[]{:S(2)}, u32[]{:S(2)}) %collective-permute-start.21) | collective-permute-done | bytes 131104 | tf_op jit(solution)/shard_map/ppermute | solution.py:336
  97.6 1.2 %collective-permute-start.24 = (bf16[16,2048]{1,0:T(8,128)(2,1)S(1)}, bf16[16,2048]{1,0:T(8,128)(2,1)S(1)}, u32[]{:S(2)}, u32[]{:S(2)}) collective-permute-start(bf16[16,2048]{1,0:T(8,128)(2,1)S(1)} %get-tuple-element.82), channel_id=1, source_target_pairs={{0,6},{1,7},{2,4},{3,5},{4,2},{5,3},{6,0},{7,1},{8,14},{9,15},{10,... | collective-permute-start | bytes 196616 | tf_op jit(solution)/shard_map/ppermute | solution.py:336
  99.1 2.8 %collective-permute-done.19.refs_1_ = bf16[32,2048]{1,0:T(8,128)(2,1)S(1)} collective-permute-done((bf16[32,2048]{1,0:T(8,128)(2,1)S(1)}, bf16[32,2048]{1,0:T(8,128)(2,1)S(1)}, u32[]{:S(2)}, u32[]{:S(2)}) %collective-permute-start.19) | collective-permute-done | bytes 131104 | tf_op jit(solution)/shard_map/ppermute | solution.py:336
  102.0 0.9 collective-permute-done.24.refs_3_
  102.9 3.4 %collective-permute-done.20.refs_1_ = bf16[16,2048]{1,0:T(8,128)(2,1)S(1)} collective-permute-done((bf16[16,2048]{1,0:T(8,128)(2,1)S(1)}, bf16[16,2048]{1,0:T(8,128)(2,1)S(1)}, u32[]{:S(2)}, u32[]{:S(2)}) %collective-permute-start.20) | collective-permute-done | bytes 65568 | tf_op jit(solution)/shard_map/ppermute | solution.py:336
  106.4 1.3 %collective-permute-done.25.refs_1_ = bf16[32,2048]{1,0:T(8,128)(2,1)S(1)} collective-permute-done((bf16[32,2048]{1,0:T(8,128)(2,1)S(1)}, bf16[32,2048]{1,0:T(8,128)(2,1)S(1)}, u32[]{:S(2)}, u32[]{:S(2)}) %collective-permute-start.25) | collective-permute-done | bytes 131104 | tf_op jit(solution)/shard_map/ppermute | solution.py:336
  107.7 1.1 shard_map.154
  (45 shorter events, 2.5 us)
Async XLA Ops:
  0.0 49.2 %copy-start.7 = (f32[2048]{0:T(1024)S(1)}, f32[2048]{0:T(1024)}, u32[]{:S(2)}) copy-start(f32[2048]{0:T(1024)} %param.23) | copy-start | bytes 24580
  0.0 49.2 %copy-start.6 = (f32[2048]{0:T(1024)S(1)}, f32[2048]{0:T(1024)}, u32[]{:S(2)}) copy-start(f32[2048]{0:T(1024)} %param.22) | copy-start | bytes 24580
  2.8 12.7 %collective-permute-start = (bf16[32,4224]{1,0:T(8,128)(2,1)}, bf16[32,4224]{1,0:T(8,128)(2,1)S(1)}, u32[]{:S(2)}, u32[]{:S(2)}) collective-permute-start(bf16[32,4224]{1,0:T(8,128)(2,1)} %get-tuple-element.50), channel_id=1, source_target_pairs={{0,8},{8,16},{16,24},{24,0},{1,9},{9,17},{17,25},{25,1},{2,10},{10... | collective-permute-start | bytes 811016 | tf_op jit(solution)/shard_map/ppermute | solution.py:265
  5.8 21.3 %collective-permute-start.1 = (bf16[32,4224]{1,0:T(8,128)(2,1)}, bf16[32,4224]{1,0:T(8,128)(2,1)S(1)}, u32[]{:S(2)}, u32[]{:S(2)}) collective-permute-start(bf16[32,4224]{1,0:T(8,128)(2,1)} %get-tuple-element.51), channel_id=1, source_target_pairs={{0,16},{8,24},{16,0},{24,8},{1,17},{9,25},{17,1},{25,9},{2,18},{10... | collective-permute-start | bytes 811016 | tf_op jit(solution)/shard_map/ppermute | solution.py:265
  8.4 18.7 %collective-permute-start.2 = (bf16[32,4224]{1,0:T(8,128)(2,1)}, bf16[32,4224]{1,0:T(8,128)(2,1)S(1)}, u32[]{:S(2)}, u32[]{:S(2)}) collective-permute-start(bf16[32,4224]{1,0:T(8,128)(2,1)} %get-tuple-element.52), channel_id=1, source_target_pairs={{0,24},{8,0},{16,8},{24,16},{1,25},{9,1},{17,9},{25,17},{2,26},{10... | collective-permute-start | bytes 811016 | tf_op jit(solution)/shard_map/ppermute | solution.py:265
  12.3 20.4 %collective-permute-start.3 = (bf16[32,4096]{1,0:T(8,128)(2,1)}, bf16[32,4096]{1,0:T(8,128)(2,1)S(1)}, u32[]{:S(2)}, u32[]{:S(2)}) collective-permute-start(bf16[32,4096]{1,0:T(8,128)(2,1)} %get-tuple-element.57), channel_id=1, source_target_pairs={{0,8},{8,16},{16,24},{24,0},{1,9},{9,17},{17,25},{25,1},{2,10},{10... | collective-permute-start | bytes 786440 | tf_op jit(solution)/shard_map/ppermute | solution.py:265
  13.0 35.9 %collective-permute-start.4 = (bf16[32,4096]{1,0:T(8,128)(2,1)}, bf16[32,4096]{1,0:T(8,128)(2,1)S(1)}, u32[]{:S(2)}, u32[]{:S(2)}) collective-permute-start(bf16[32,4096]{1,0:T(8,128)(2,1)} %get-tuple-element.58), channel_id=1, source_target_pairs={{0,16},{8,24},{16,0},{24,8},{1,17},{9,25},{17,1},{25,9},{2,18},{10... | collective-permute-start | bytes 786440 | tf_op jit(solution)/shard_map/ppermute | solution.py:265
  15.5 33.4 %collective-permute-start.5 = (bf16[32,4096]{1,0:T(8,128)(2,1)}, bf16[32,4096]{1,0:T(8,128)(2,1)S(1)}, u32[]{:S(2)}, u32[]{:S(2)}) collective-permute-start(bf16[32,4096]{1,0:T(8,128)(2,1)} %get-tuple-element.59), channel_id=1, source_target_pairs={{0,24},{8,0},{16,8},{24,16},{1,25},{9,1},{17,9},{25,17},{2,26},{10... | collective-permute-start | bytes 786440 | tf_op jit(solution)/shard_map/ppermute | solution.py:265
  17.9 1.0 copy-start.2
  18.9 0.9 copy-start.4
  19.9 0.7 copy-start.8
  20.5 0.7 copy-start.9
  21.2 0.7 copy-start.10
  27.1 46.8 %copy-start = (bf16[1,2048,1024]{2,1,0:T(8,128)(2,1)S(1)}, bf16[1,2048,1024]{2,1,0:T(8,128)(2,1)}, u32[]{:S(2)}) copy-start(bf16[1,2048,1024]{2,1,0:T(8,128)(2,1)} %w_in_ref.5) | copy-start | bytes 12582916
  27.1 46.8 %copy-start.1 = (bf16[1,1024,2048]{2,1,0:T(8,128)(2,1)S(1)}, bf16[1,1024,2048]{2,1,0:T(8,128)(2,1)}, u32[]{:S(2)}) copy-start(bf16[1,1024,2048]{2,1,0:T(8,128)(2,1)} %w_out_ref.5) | copy-start | bytes 12582916
  27.1 46.8 %copy-start.5 = (f32[1,1024]{1,0:T(1,128)S(1)}, f32[1,1024]{1,0:T(1,128)}, u32[]{:S(2)}) copy-start(f32[1,1024]{1,0:T(1,128)} %bias_ref.7) | copy-start | bytes 12292
  50.0 1.4 %collective-permute-start.6 = (bf16[32,2048]{1,0:T(8,128)(2,1)S(1)}, bf16[32,2048]{1,0:T(8,128)(2,1)S(1)}, u32[]{:S(2)}, u32[]{:S(2)}) collective-permute-start(bf16[32,2048]{1,0:T(8,128)(2,1)S(1)} %get-tuple-element.63), channel_id=1, source_target_pairs={{0,1},{1,0},{2,3},{3,2},{4,5},{5,4},{6,7},{7,6},{8,9},{9,8},{10,11... | collective-permute-start | bytes 393224 | tf_op jit(solution)/shard_map/ppermute | solution.py:336
  51.4 4.3 %collective-permute-start.11 = (bf16[16,2048]{1,0:T(8,128)(2,1)S(1)}, bf16[16,2048]{1,0:T(8,128)(2,1)S(1)}, u32[]{:S(2)}, u32[]{:S(2)}) collective-permute-start(bf16[16,2048]{1,0:T(8,128)(2,1)S(1)} %get-tuple-element.67), channel_id=1, source_target_pairs={{0,2},{1,3},{2,0},{3,1},{4,6},{5,7},{6,4},{7,5},{8,10},{9,11},{10,... | collective-permute-start | bytes 196616 | tf_op jit(solution)/shard_map/ppermute | solution.py:336
  53.0 8.0 %collective-permute-start.7 = (bf16[16,2048]{1,0:T(8,128)(2,1)S(1)}, bf16[16,2048]{1,0:T(8,128)(2,1)S(1)}, u32[]{:S(2)}, u32[]{:S(2)}) collective-permute-start(bf16[16,2048]{1,0:T(8,128)(2,1)S(1)} %get-tuple-element.64), channel_id=1, source_target_pairs={{0,4},{1,5},{2,6},{3,7},{4,0},{5,1},{6,2},{7,3},{8,12},{9,13},{10,... | collective-permute-start | bytes 196616 | tf_op jit(solution)/shard_map/ppermute | solution.py:336
  54.5 6.5 %collective-permute-start.8 = (bf16[16,2048]{1,0:T(8,128)(2,1)S(1)}, bf16[16,2048]{1,0:T(8,128)(2,1)S(1)}, u32[]{:S(2)}, u32[]{:S(2)}) collective-permute-start(bf16[16,2048]{1,0:T(8,128)(2,1)S(1)} %get-tuple-element.65), channel_id=1, source_target_pairs={{0,6},{1,7},{2,4},{3,5},{4,2},{5,3},{6,0},{7,1},{8,14},{9,15},{10,... | collective-permute-start | bytes 196616 | tf_op jit(solution)/shard_map/ppermute | solution.py:336
  55.8 11.7 %collective-permute-start.12 = (bf16[32,2048]{1,0:T(8,128)(2,1)S(1)}, bf16[32,2048]{1,0:T(8,128)(2,1)S(1)}, u32[]{:S(2)}, u32[]{:S(2)}) collective-permute-start(bf16[32,2048]{1,0:T(8,128)(2,1)S(1)} %shard_map.145.refs_0_), channel_id=1, source_target_pairs={{0,16},{8,24},{16,0},{24,8},{1,17},{9,25},{17,1},{25,9},{2,18},{10... | collective-permute-start | bytes 393224 | tf_op jit(solution)/shard_map/ppermute | solution.py:336
  61.0 11.2 %collective-permute-start.9 = (bf16[32,2048]{1,0:T(8,128)(2,1)S(1)}, bf16[32,2048]{1,0:T(8,128)(2,1)S(1)}, u32[]{:S(2)}, u32[]{:S(2)}) collective-permute-start(bf16[32,2048]{1,0:T(8,128)(2,1)S(1)} %shard_map.144.refs_0_), channel_id=1, source_target_pairs={{0,16},{8,24},{16,0},{24,8},{1,17},{9,25},{17,1},{25,9},{2,18},{10... | collective-permute-start | bytes 393224 | tf_op jit(solution)/shard_map/ppermute | solution.py:336
  64.9 9.0 %collective-permute-start.15 = (bf16[32,2048]{1,0:T(8,128)(2,1)S(1)}, bf16[32,2048]{1,0:T(8,128)(2,1)S(1)}, u32[]{:S(2)}, u32[]{:S(2)}) collective-permute-start(bf16[32,2048]{1,0:T(8,128)(2,1)S(1)} %shard_map.145.refs_0_), channel_id=1, source_target_pairs={{0,8},{8,0},{16,24},{24,16},{1,9},{9,1},{17,25},{25,17},{2,10},{10... | collective-permute-start | bytes 393224 | tf_op jit(solution)/shard_map/ppermute | solution.py:336
  67.4 9.3 %collective-permute-start.14 = (bf16[32,2048]{1,0:T(8,128)(2,1)S(1)}, bf16[32,2048]{1,0:T(8,128)(2,1)S(1)}, u32[]{:S(2)}, u32[]{:S(2)}) collective-permute-start(bf16[32,2048]{1,0:T(8,128)(2,1)S(1)} %shard_map.144.refs_0_), channel_id=1, source_target_pairs={{0,8},{8,0},{16,24},{24,16},{1,9},{9,1},{17,25},{25,17},{2,10},{10... | collective-permute-start | bytes 393224 | tf_op jit(solution)/shard_map/ppermute | solution.py:336
  67.5 11.1 %collective-permute-start.13 = (bf16[32,2048]{1,0:T(8,128)(2,1)S(1)}, bf16[32,2048]{1,0:T(8,128)(2,1)S(1)}, u32[]{:S(2)}, u32[]{:S(2)}) collective-permute-start(bf16[32,2048]{1,0:T(8,128)(2,1)S(1)} %collective-permute-done.12.refs_3_), channel_id=1, source_target_pairs={{0,8},{8,0},{16,24},{24,16},{1,9},{9,1},{17,25},{25,17},{2,10},{10... | collective-permute-start | bytes 393224 | tf_op jit(solution)/shard_map/ppermute | solution.py:336
  72.3 7.7 %collective-permute-start.10 = (bf16[32,2048]{1,0:T(8,128)(2,1)S(1)}, bf16[32,2048]{1,0:T(8,128)(2,1)S(1)}, u32[]{:S(2)}, u32[]{:S(2)}) collective-permute-start(bf16[32,2048]{1,0:T(8,128)(2,1)S(1)} %collective-permute-done.9.refs_2_), channel_id=1, source_target_pairs={{0,8},{8,0},{16,24},{24,16},{1,9},{9,1},{17,25},{25,17},{2,10},{10... | collective-permute-start | bytes 393224 | tf_op jit(solution)/shard_map/ppermute | solution.py:336
  80.0 17.5 %copy-start.3 = (f32[8,2048]{1,0:T(8,128)S(1)}, f32[8,2048]{1,0:T(8,128)}, u32[]{:S(2)}) copy-start(f32[8,2048]{1,0:T(8,128)} %bias_ref.9) | copy-start | bytes 196612
  81.3 5.8 %collective-permute-start.16 = (bf16[32,2048]{1,0:T(8,128)(2,1)S(1)}, bf16[32,2048]{1,0:T(8,128)(2,1)S(1)}, u32[]{:S(2)}, u32[]{:S(2)}) collective-permute-start(bf16[32,2048]{1,0:T(8,128)(2,1)S(1)} %get-tuple-element.70), channel_id=1, source_target_pairs={{0,8},{8,0},{16,24},{24,16},{1,9},{9,1},{17,25},{25,17},{2,10},{10... | collective-permute-start | bytes 393224 | tf_op jit(solution)/shard_map/ppermute | solution.py:336
  82.2 11.4 %collective-permute-start.18 = (bf16[32,2048]{1,0:T(8,128)(2,1)S(1)}, bf16[32,2048]{1,0:T(8,128)(2,1)S(1)}, u32[]{:S(2)}, u32[]{:S(2)}) collective-permute-start(bf16[32,2048]{1,0:T(8,128)(2,1)S(1)} %get-tuple-element.75), channel_id=1, source_target_pairs={{0,8},{8,0},{16,24},{24,16},{1,9},{9,1},{17,25},{25,17},{2,10},{10... | collective-permute-start | bytes 393224 | tf_op jit(solution)/shard_map/ppermute | solution.py:336
  87.1 10.3 %collective-permute-start.21 = (bf16[32,2048]{1,0:T(8,128)(2,1)S(1)}, bf16[32,2048]{1,0:T(8,128)(2,1)S(1)}, u32[]{:S(2)}, u32[]{:S(2)}) collective-permute-start(bf16[32,2048]{1,0:T(8,128)(2,1)S(1)} %get-tuple-element.79), channel_id=1, source_target_pairs={{0,8},{8,0},{16,24},{24,16},{1,9},{9,1},{17,25},{25,17},{2,10},{10... | collective-permute-start | bytes 393224 | tf_op jit(solution)/shard_map/ppermute | solution.py:336
  87.8 9.7 %collective-permute-start.22 = (bf16[32,2048]{1,0:T(8,128)(2,1)S(1)}, bf16[32,2048]{1,0:T(8,128)(2,1)S(1)}, u32[]{:S(2)}, u32[]{:S(2)}) collective-permute-start(bf16[32,2048]{1,0:T(8,128)(2,1)S(1)} %get-tuple-element.80), channel_id=1, source_target_pairs={{0,16},{8,24},{16,0},{24,8},{1,17},{9,25},{17,1},{25,9},{2,18},{10... | collective-permute-start | bytes 393224 | tf_op jit(solution)/shard_map/ppermute | solution.py:336
  93.2 5.9 %collective-permute-start.17 = (bf16[32,2048]{1,0:T(8,128)(2,1)S(1)}, bf16[32,2048]{1,0:T(8,128)(2,1)S(1)}, u32[]{:S(2)}, u32[]{:S(2)}) collective-permute-start(bf16[32,2048]{1,0:T(8,128)(2,1)S(1)} %get-tuple-element.74), channel_id=1, source_target_pairs={{0,8},{8,0},{16,24},{24,16},{1,9},{9,1},{17,25},{25,17},{2,10},{10... | collective-permute-start | bytes 393224 | tf_op jit(solution)/shard_map/ppermute | solution.py:336
  93.6 8.2 %collective-permute-start.19 = (bf16[32,2048]{1,0:T(8,128)(2,1)S(1)}, bf16[32,2048]{1,0:T(8,128)(2,1)S(1)}, u32[]{:S(2)}, u32[]{:S(2)}) collective-permute-start(bf16[32,2048]{1,0:T(8,128)(2,1)S(1)} %shard_map.150), channel_id=1, source_target_pairs={{0,16},{8,24},{16,0},{24,8},{1,17},{9,25},{17,1},{25,9},{2,18},{10... | collective-permute-start | bytes 393224 | tf_op jit(solution)/shard_map/ppermute | solution.py:336
  97.6 4.5 %collective-permute-start.23 = (bf16[16,2048]{1,0:T(8,128)(2,1)S(1)}, bf16[16,2048]{1,0:T(8,128)(2,1)S(1)}, u32[]{:S(2)}, u32[]{:S(2)}) collective-permute-start(bf16[16,2048]{1,0:T(8,128)(2,1)S(1)} %get-tuple-element.81), channel_id=1, source_target_pairs={{0,4},{1,5},{2,6},{3,7},{4,0},{5,1},{6,2},{7,3},{8,12},{9,13},{10,... | collective-permute-start | bytes 196616 | tf_op jit(solution)/shard_map/ppermute | solution.py:336
  97.6 5.2 %collective-permute-start.24 = (bf16[16,2048]{1,0:T(8,128)(2,1)S(1)}, bf16[16,2048]{1,0:T(8,128)(2,1)S(1)}, u32[]{:S(2)}, u32[]{:S(2)}) collective-permute-start(bf16[16,2048]{1,0:T(8,128)(2,1)S(1)} %get-tuple-element.82), channel_id=1, source_target_pairs={{0,6},{1,7},{2,4},{3,5},{4,2},{5,3},{6,0},{7,1},{8,14},{9,15},{10,... | collective-permute-start | bytes 196616 | tf_op jit(solution)/shard_map/ppermute | solution.py:336
  101.9 4.3 %collective-permute-start.20 = (bf16[16,2048]{1,0:T(8,128)(2,1)S(1)}, bf16[16,2048]{1,0:T(8,128)(2,1)S(1)}, u32[]{:S(2)}, u32[]{:S(2)}) collective-permute-start(bf16[16,2048]{1,0:T(8,128)(2,1)S(1)} %get-tuple-element.78), channel_id=1, source_target_pairs={{0,2},{1,3},{2,0},{3,1},{4,6},{5,7},{6,4},{7,5},{8,10},{9,11},{10,... | collective-permute-start | bytes 196616 | tf_op jit(solution)/shard_map/ppermute | solution.py:336
  106.3 1.4 %collective-permute-start.25 = (bf16[32,2048]{1,0:T(8,128)(2,1)S(1)}, bf16[32,2048]{1,0:T(8,128)(2,1)S(1)}, u32[]{:S(2)}, u32[]{:S(2)}) collective-permute-start(bf16[32,2048]{1,0:T(8,128)(2,1)S(1)} %get-tuple-element.84), channel_id=1, source_target_pairs={{0,1},{1,0},{2,3},{3,2},{4,5},{5,4},{6,7},{7,6},{8,9},{9,8},{10,11... | collective-permute-start | bytes 393224 | tf_op jit(solution)/shard_map/ppermute | solution.py:336

commit v12 on v11

--- a/solution.py
+++ b/solution.py
@@ -169,8 +169,8 @@
         at += send_ref.shape[0]
 
 
-def expert_kernel(count, bias_ref, w_in_ref, w_out_ref, *refs):
-    x_refs, out_refs = refs[:count], refs[-count:]
+def expert_kernel(count, outs, bias_ref, w_in_ref, w_out_ref, *refs):
+    x_refs, out_refs = refs[:count], refs[-outs:]
     inner = jnp.dot(joined(x_refs), w_in_ref[0], preferred_element_type=F32)
     inner = jnp.maximum(inner + bias_ref[...], 0.0).astype(BF16)
     share = jnp.dot(inner, w_out_ref[0], preferred_element_type=F32).astype(BF16)
@@ -181,10 +181,13 @@
 
 
 def add_kernel(first_ref, second_ref, *refs):
-    count = len(refs) // 2
-    refs[count][...] = (first_ref[...].astype(F32) + second_ref[...].astype(F32)).astype(BF16)
+    count = len(refs) // 2 - 1
+    total = (first_ref[...].astype(F32) + second_ref[...].astype(F32)).astype(BF16)
+    half = total.shape[0] // 2
+    refs[count][...] = total[:half]
+    refs[count + 1][...] = total[half:]
     for n in range(count):
-        refs[count + 1 + n][...] = refs[n][...]
+        refs[count + 2 + n][...] = refs[n][...]
 
 
 def result_kernel(lower, bias_ref, near_ref, *refs):
@@ -319,11 +322,11 @@
     def bf16(rows):
         return jax.ShapeDtypeStruct((rows, width), BF16)
 
-    def apply(rows, after=()):
+    def apply(rows, outs, after=()):
         count = sum(x.shape[0] for x in rows)
         return call(
-            functools.partial(expert_kernel, len(rows)),
-            tuple(bf16(x.shape[0]) for x in rows),
+            functools.partial(expert_kernel, len(rows), outs),
+            (bf16(count // outs),) * outs,
             b_in,
             w_in,
             w_out,
@@ -346,16 +349,13 @@
         near = [swap(x, 1) for x in own]
         own_share, near_shares, last = [None, None], [None, None], ()
         for n in (1, 0):
-            own_share[n], near_shares[n] = apply([own[n], near[n]], after=last)
+            own_share[n], near_shares[n] = apply([own[n], near[n]], 2, after=last)
             last = own_share[n : n + 1]
         last = last[0]
-        *corner_share, far_first, far_second = apply([swap(x, 1) for x in far] + far, after=[last])
-        far_shares = [far_first, far_second]
-        pairs = [None, None]
-        pairs[0], *near_shares = call(
-            add_kernel, (bf16(half),) * 3, swap(corner_share[0], 1), far_shares[0], *near_shares
-        )
-        (pairs[1],) = call(add_kernel, (bf16(half),), swap(corner_share[1], 1), far_shares[1])
+        corner_share, far_share = apply([swap(x, 1) for x in far] + far, 2, after=[last])
+        *pairs, near_shares[0], near_shares[1] = call(
+            add_kernel, (bf16(half),) * 4, swap(corner_share, 1), far_share, *near_shares
+        )
         backs = [
             call(
                 functools.partial(result_kernel, 0),
@@ -373,7 +373,7 @@
         returned = [mine, swap(other, 1, "expert")]
     else:
         every = lax.all_gather(over_experts(send[0]), "dp", axis=0, tiled=True)
-        (share,) = apply([every])
+        (share,) = apply([every], 1)
         shares = lax.all_to_all(
             share.reshape(dp, slots, width), "dp", split_axis=0, concat_axis=0, tiled=True
         )

time: 109 us -> 111 us (1.018)
  waiting for transfers between devices: 48.1 us -> 52.2 us
  starting transfers between devices: 42.4 us -> 40.4 us
    ppermute x20 -> x19, waiting for transfers between devices: 20.8 us -> 24.9 us  [swap(): lax.ppermute(x, axis, [(i, i ^ distance) for i in range(lax.axis_size(axi...]
    ppermute x20 -> x19, starting transfers between devices: 31.9 us -> 29.9 us  [swap(): lax.ppermute(x, axis, [(i, i ^ distance) for i in range(lax.axis_size(axi...]
    pallas_call x19 -> x18, Pallas kernels: 14.1 us -> 14.1 us  [call(): pl.pallas_call(body, out_shape=out_shape, compiler_params=pltpu.CompilerP...]
  transfers between devices with their start and end apart: 26 -> 25, of which waited for: 18 -> 18; matrix products, arithmetic and copies ran while one was open for 0% -> 0% of each run, Pallas kernels for 7% -> 7%
where the time goes in v12:
time: 111 us
  waiting for transfers between devices  52.2 us (47%)
  starting transfers between devices  40.4 us (36%)
  Pallas kernels  14.1 us (13%)
  local copies, waits for them, and re-layouts  3.94 us (4%)
    ppermute x19, starting transfers between devices, swap(): lax.ppermute(x, axis, [(i, i ^ distance) for i in range(lax.axis_size(axi...  29.9 us
    ppermute x6, waiting for transfers between devices, spread(): lax.ppermute(part, 'dp', [(i, (i + n) % dp) for i in range(dp)])  27.3 us
    ppermute x19, waiting for transfers between devices, swap(): lax.ppermute(x, axis, [(i, i ^ distance) for i in range(lax.axis_size(axi...  24.9 us
    pallas_call x18, Pallas kernels, call(): pl.pallas_call(body, out_shape=out_shape, compiler_params=pltpu.CompilerP...  14.1 us
    ppermute x6, starting transfers between devices, spread(): lax.ppermute(part, 'dp', [(i, (i + n) % dp) for i in range(dp)])  10.5 us
    unnamed x22, local copies, waits for them, and re-layouts  3.94 us
  transfers between devices with their start and end apart: 25, of which 18 were waited for; matrix products, arithmetic and copies ran while one was open for 0% of the time, Pallas kernels for 7%

profile of v12, /device:TPU:0, one launch (start us, length us, event | category | flops | bytes accessed | tf_op | source)
XLA Modules:
  0.0 110.8 jit_solution(11997013078915591077)
XLA Ops:
  0.0 2.8 %shard_map.136 = (bf16[128,128]{1,0:T(8,128)(2,1)}, bf16[32,4224]{1,0:T(8,128)(2,1)}, bf16[32,4224]{1,0:T(8,128)(2,1)}, bf16[32,4224]{1,0:T(8,128)(2,1)}, bf16[32,4224]{1,0:T(8,128)(2,1)}) custom-call(s32[1,128]{1,0:T(1,128)} %bitcast.9, bf16[128,2048]{1,0:T(8,128)(2,1)} %refs_0_.2, bf16[128,2048]{1,0:T(8,128)(2,1)} %refs_1_.2), custom_call_target="tpu_custom_call" | custom-call | bytes 2163200 | tf_op jit(solution)/shard_map/pallas_call | solution.py:41
  2.8 3.0 %collective-permute-start = (bf16[32,4224]{1,0:T(8,128)(2,1)}, bf16[32,4224]{1,0:T(8,128)(2,1)S(1)}, u32[]{:S(2)}, u32[]{:S(2)}) collective-permute-start(bf16[32,4224]{1,0:T(8,128)(2,1)} %get-tuple-element.49), channel_id=1, source_target_pairs={{0,8},{8,16},{16,24},{24,0},{1,9},{9,17},{17,25},{25,1},{2,10},{10... | collective-permute-start | bytes 811016 | tf_op jit(solution)/shard_map/ppermute | solution.py:268
  5.8 2.6 %collective-permute-start.1 = (bf16[32,4224]{1,0:T(8,128)(2,1)}, bf16[32,4224]{1,0:T(8,128)(2,1)S(1)}, u32[]{:S(2)}, u32[]{:S(2)}) collective-permute-start(bf16[32,4224]{1,0:T(8,128)(2,1)} %get-tuple-element.50), channel_id=1, source_target_pairs={{0,16},{8,24},{16,0},{24,8},{1,17},{9,25},{17,1},{25,9},{2,18},{10... | collective-permute-start | bytes 811016 | tf_op jit(solution)/shard_map/ppermute | solution.py:268
  8.4 1.3 %collective-permute-start.2 = (bf16[32,4224]{1,0:T(8,128)(2,1)}, bf16[32,4224]{1,0:T(8,128)(2,1)S(1)}, u32[]{:S(2)}, u32[]{:S(2)}) collective-permute-start(bf16[32,4224]{1,0:T(8,128)(2,1)} %get-tuple-element.51), channel_id=1, source_target_pairs={{0,24},{8,0},{16,8},{24,16},{1,25},{9,1},{17,9},{25,17},{2,26},{10... | collective-permute-start | bytes 811016 | tf_op jit(solution)/shard_map/ppermute | solution.py:268
  9.7 2.6 %shard_map.137 = (bf16[128,128]{1,0:T(8,128)(2,1)}, bf16[32,4096]{1,0:T(8,128)(2,1)}, bf16[32,4096]{1,0:T(8,128)(2,1)}, bf16[32,4096]{1,0:T(8,128)(2,1)}, bf16[32,4096]{1,0:T(8,128)(2,1)}) custom-call(bf16[128,128]{1,0:T(8,128)(2,1)} %get-tuple-element.45.pos_ref, bf16[128,2048]{1,0:T(8,128)(2,1)} %refs_0_.3, bf16[128,2048]{1,0:T(8,128)(2,1)} %refs_1_.3), custom_call_target="tpu_custom_call" | custom-call | bytes 2162688 | tf_op jit(solution)/shard_map/pallas_call | solution.py:41
  12.3 0.7 collective-permute-start.3
  13.0 0.3 collective-permute-start.4
  13.3 2.1 %collective-permute-done.refs_1_ = bf16[32,4224]{1,0:T(8,128)(2,1)S(1)} collective-permute-done((bf16[32,4224]{1,0:T(8,128)(2,1)}, bf16[32,4224]{1,0:T(8,128)(2,1)S(1)}, u32[]{:S(2)}, u32[]{:S(2)}) %collective-permute-start) | collective-permute-done | bytes 270368 | tf_op jit(solution)/shard_map/ppermute | solution.py:268
  15.5 2.5 %collective-permute-start.5 = (bf16[32,4096]{1,0:T(8,128)(2,1)}, bf16[32,4096]{1,0:T(8,128)(2,1)S(1)}, u32[]{:S(2)}, u32[]{:S(2)}) collective-permute-start(bf16[32,4096]{1,0:T(8,128)(2,1)} %get-tuple-element.58), channel_id=1, source_target_pairs={{0,24},{8,0},{16,8},{24,16},{1,25},{9,1},{17,9},{25,17},{2,26},{10... | collective-permute-start | bytes 786440 | tf_op jit(solution)/shard_map/ppermute | solution.py:268
  18.0 1.0 copy-done.2
  18.9 0.9 copy-done.4
  19.9 0.7 copy-done.8
  20.5 0.7 copy-done.9
  21.2 0.7 copy-done.10
  22.1 5.0 %collective-permute-done.1.refs_2_ = bf16[32,4224]{1,0:T(8,128)(2,1)S(1)} collective-permute-done((bf16[32,4224]{1,0:T(8,128)(2,1)}, bf16[32,4224]{1,0:T(8,128)(2,1)S(1)}, u32[]{:S(2)}, u32[]{:S(2)}) %collective-permute-start.1) | collective-permute-done | bytes 270368 | tf_op jit(solution)/shard_map/ppermute | solution.py:268
  27.2 1.5 %shard_map.140.probs_ref = bf16[16,128,128]{2,1,0:T(8,128)(2,1)S(1)} custom-call(bf16[128,128]{1,0:T(8,128)(2,1)S(1)} %get-tuple-element.52.place_ref, f32[128,128]{1,0:T(8,128)S(1)} %get-tuple-element.54.outside_ref, bf16[32,4224]{1,0:T(8,128)(2,1)S(1)} %get-tuple-element.48.refs_0_, bf16[32,4224]{1,0:T(8,128)(2,1)S(1)} %collective-permute-done.refs_1_, ...), custom_call_target="tpu_custom_call" | custom-call | bytes 1703936 | tf_op jit(solution)/shard_map/pallas_call | solution.py:41
  28.8 4.0 %collective-permute-done.3.refs_1_ = bf16[32,4096]{1,0:T(8,128)(2,1)S(1)} collective-permute-done((bf16[32,4096]{1,0:T(8,128)(2,1)}, bf16[32,4096]{1,0:T(8,128)(2,1)S(1)}, u32[]{:S(2)}, u32[]{:S(2)}) %collective-permute-start.3) | collective-permute-done | bytes 262176 | tf_op jit(solution)/shard_map/ppermute | solution.py:268
  32.7 16.2 %collective-permute-done.4.refs_2_ = bf16[32,4096]{1,0:T(8,128)(2,1)S(1)} collective-permute-done((bf16[32,4096]{1,0:T(8,128)(2,1)}, bf16[32,4096]{1,0:T(8,128)(2,1)S(1)}, u32[]{:S(2)}, u32[]{:S(2)}) %collective-permute-start.4) | collective-permute-done | bytes 262176 | tf_op jit(solution)/shard_map/ppermute | solution.py:268
  49.2 0.8 shard_map.142
  50.1 1.3 %collective-permute-done.6.other_ref = bf16[32,2048]{1,0:T(8,128)(2,1)S(1)} collective-permute-done((bf16[32,2048]{1,0:T(8,128)(2,1)S(1)}, bf16[32,2048]{1,0:T(8,128)(2,1)S(1)}, u32[]{:S(2)}, u32[]{:S(2)}) %collective-permute-start.6) | collective-permute-done | bytes 131104 | tf_op jit(solution)/shard_map/ppermute | solution.py:339
  51.5 1.6 %collective-permute-start.11 = (bf16[16,2048]{1,0:T(8,128)(2,1)S(1)}, bf16[16,2048]{1,0:T(8,128)(2,1)S(1)}, u32[]{:S(2)}, u32[]{:S(2)}) collective-permute-start(bf16[16,2048]{1,0:T(8,128)(2,1)S(1)} %get-tuple-element.66), channel_id=1, source_target_pairs={{0,2},{1,3},{2,0},{3,1},{4,6},{5,7},{6,4},{7,5},{8,10},{9,11},{10,... | collective-permute-start | bytes 196616 | tf_op jit(solution)/shard_map/ppermute | solution.py:339
  53.0 1.5 %collective-permute-start.7 = (bf16[16,2048]{1,0:T(8,128)(2,1)S(1)}, bf16[16,2048]{1,0:T(8,128)(2,1)S(1)}, u32[]{:S(2)}, u32[]{:S(2)}) collective-permute-start(bf16[16,2048]{1,0:T(8,128)(2,1)S(1)} %get-tuple-element.63), channel_id=1, source_target_pairs={{0,4},{1,5},{2,6},{3,7},{4,0},{5,1},{6,2},{7,3},{8,12},{9,13},{10,... | collective-permute-start | bytes 196616 | tf_op jit(solution)/shard_map/ppermute | solution.py:339
  54.5 0.5 collective-permute-start.8
  55.0 0.8 collective-permute-done.11.refs_1_
  55.8 5.2 %collective-permute-start.12 = (bf16[32,2048]{1,0:T(8,128)(2,1)S(1)}, bf16[32,2048]{1,0:T(8,128)(2,1)S(1)}, u32[]{:S(2)}, u32[]{:S(2)}) collective-permute-start(bf16[32,2048]{1,0:T(8,128)(2,1)S(1)} %shard_map.145.refs_0_), channel_id=1, source_target_pairs={{0,16},{8,24},{16,0},{24,8},{1,17},{9,25},{17,1},{25,9},{2,18},{10... | collective-permute-start | bytes 393224 | tf_op jit(solution)/shard_map/ppermute | solution.py:339
  61.1 3.9 %collective-permute-start.9 = (bf16[32,2048]{1,0:T(8,128)(2,1)S(1)}, bf16[32,2048]{1,0:T(8,128)(2,1)S(1)}, u32[]{:S(2)}, u32[]{:S(2)}) collective-permute-start(bf16[32,2048]{1,0:T(8,128)(2,1)S(1)} %shard_map.144.refs_0_), channel_id=1, source_target_pairs={{0,16},{8,24},{16,0},{24,8},{1,17},{9,25},{17,1},{25,9},{2,18},{10... | collective-permute-start | bytes 393224 | tf_op jit(solution)/shard_map/ppermute | solution.py:339
  64.9 2.5 %collective-permute-start.15 = (bf16[32,2048]{1,0:T(8,128)(2,1)S(1)}, bf16[32,2048]{1,0:T(8,128)(2,1)S(1)}, u32[]{:S(2)}, u32[]{:S(2)}) collective-permute-start(bf16[32,2048]{1,0:T(8,128)(2,1)S(1)} %shard_map.145.refs_0_), channel_id=1, source_target_pairs={{0,8},{8,0},{16,24},{24,16},{1,9},{9,1},{17,25},{25,17},{2,10},{10... | collective-permute-start | bytes 393224 | tf_op jit(solution)/shard_map/ppermute | solution.py:339
  67.5 3.2 %collective-permute-start.13 = (bf16[32,2048]{1,0:T(8,128)(2,1)S(1)}, bf16[32,2048]{1,0:T(8,128)(2,1)S(1)}, u32[]{:S(2)}, u32[]{:S(2)}) collective-permute-start(bf16[32,2048]{1,0:T(8,128)(2,1)S(1)} %collective-permute-done.12.refs_3_), channel_id=1, source_target_pairs={{0,8},{8,0},{16,24},{24,16},{1,9},{9,1},{17,25},{25,17},{2,10},{10... | collective-permute-start | bytes 393224 | tf_op jit(solution)/shard_map/ppermute | solution.py:339
  70.7 1.6 %collective-permute-done.9.refs_2_ = bf16[32,2048]{1,0:T(8,128)(2,1)S(1)} collective-permute-done((bf16[32,2048]{1,0:T(8,128)(2,1)S(1)}, bf16[32,2048]{1,0:T(8,128)(2,1)S(1)}, u32[]{:S(2)}, u32[]{:S(2)}) %collective-permute-start.9) | collective-permute-done | bytes 131104 | tf_op jit(solution)/shard_map/ppermute | solution.py:339
  72.3 0.9 collective-permute-start.10
  73.2 0.7 collective-permute-done.15.refs_1_
  73.9 1.6 %shard_map.146 = (bf16[32,2048]{1,0:T(8,128)(2,1)S(1)}, bf16[32,2048]{1,0:T(8,128)(2,1)S(1)}) custom-call(f32[1,1024]{1,0:T(1,128)S(1)} %copy-done.5, bf16[1,2048,1024]{2,1,0:T(8,128)(2,1)S(1)} %copy-done, bf16[1,1024,2048]{2,1,0:T(8,128)(2,1)S(1)} %copy-done.1, bf16[32,2048]{1,0:T(8,128)(2,1)S(1)} %shard_map.145.refs_0_, ...), custom_call_target="tpu_custom_call" | custom-call | flops 536870912 | bytes 8916992 | tf_op jit(solution)/shard_map/pallas_call | solution.py:41
  75.5 1.2 %collective-permute-done.14.refs_1_ = bf16[32,2048]{1,0:T(8,128)(2,1)S(1)} collective-permute-done((bf16[32,2048]{1,0:T(8,128)(2,1)S(1)}, bf16[32,2048]{1,0:T(8,128)(2,1)S(1)}, u32[]{:S(2)}, u32[]{:S(2)}) %collective-permute-start.14) | collective-permute-done | bytes 131104 | tf_op jit(solution)/shard_map/ppermute | solution.py:339
  76.7 1.6 %shard_map.147 = (bf16[32,2048]{1,0:T(8,128)(2,1)S(1)}, bf16[32,2048]{1,0:T(8,128)(2,1)S(1)}) custom-call(f32[1,1024]{1,0:T(1,128)S(1)} %copy-done.5, bf16[1,2048,1024]{2,1,0:T(8,128)(2,1)S(1)} %copy-done, bf16[1,1024,2048]{2,1,0:T(8,128)(2,1)S(1)} %copy-done.1, bf16[32,2048]{1,0:T(8,128)(2,1)S(1)} %shard_map.144.refs_0_, ...), custom_call_target="tpu_custom_call" | custom-call | flops 536870912 | bytes 9048064 | tf_op jit(solution)/shard_map/pallas_call | solution.py:41
  78.6 1.4 %collective-permute-done.10.refs_0_ = bf16[32,2048]{1,0:T(8,128)(2,1)S(1)} collective-permute-done((bf16[32,2048]{1,0:T(8,128)(2,1)S(1)}, bf16[32,2048]{1,0:T(8,128)(2,1)S(1)}, u32[]{:S(2)}, u32[]{:S(2)}) %collective-permute-start.10) | collective-permute-done | bytes 131104 | tf_op jit(solution)/shard_map/ppermute | solution.py:339
  80.0 1.3 %shard_map.148 = (bf16[64,2048]{1,0:T(8,128)(2,1)S(1)}, bf16[64,2048]{1,0:T(8,128)(2,1)S(1)}) custom-call(f32[1,1024]{1,0:T(1,128)S(1)} %copy-done.5, bf16[1,2048,1024]{2,1,0:T(8,128)(2,1)S(1)} %copy-done, bf16[1,1024,2048]{2,1,0:T(8,128)(2,1)S(1)} %copy-done.1, bf16[32,2048]{1,0:T(8,128)(2,1)S(1)} %collective-permute-done.10.refs_0_, ...), custom_call_target="tpu_custom_call" | custom-call | flops 1073741824 | bytes 9572352 | tf_op jit(solution)/shard_map/pallas_call | solution.py:41
  81.4 0.9 collective-permute-start.16
  82.3 5.9 %collective-permute-done.16.first_ref = bf16[64,2048]{1,0:T(8,128)(2,1)S(1)} collective-permute-done((bf16[64,2048]{1,0:T(8,128)(2,1)S(1)}, bf16[64,2048]{1,0:T(8,128)(2,1)S(1)}, u32[]{:S(2)}, u32[]{:S(2)}) %collective-permute-start.16) | collective-permute-done | bytes 262176 | tf_op jit(solution)/shard_map/ppermute | solution.py:339
  88.3 0.8 collective-permute-start.17
  89.0 5.4 %collective-permute-start.18 = (bf16[32,2048]{1,0:T(8,128)(2,1)S(1)}, bf16[32,2048]{1,0:T(8,128)(2,1)S(1)}, u32[]{:S(2)}, u32[]{:S(2)}) collective-permute-start(bf16[32,2048]{1,0:T(8,128)(2,1)S(1)} %get-tuple-element.74), channel_id=1, source_target_pairs={{0,16},{8,24},{16,0},{24,8},{1,17},{9,25},{17,1},{25,9},{2,18},{10... | collective-permute-start | bytes 393224 | tf_op jit(solution)/shard_map/ppermute | solution.py:339
  94.8 4.0 %collective-permute-done.18.refs_1_ = bf16[32,2048]{1,0:T(8,128)(2,1)S(1)} collective-permute-done((bf16[32,2048]{1,0:T(8,128)(2,1)S(1)}, bf16[32,2048]{1,0:T(8,128)(2,1)S(1)}, u32[]{:S(2)}, u32[]{:S(2)}) %collective-permute-start.18) | collective-permute-done | bytes 131104 | tf_op jit(solution)/shard_map/ppermute | solution.py:339
  98.9 1.5 %collective-permute-start.19 = (bf16[16,2048]{1,0:T(8,128)(2,1)S(1)}, bf16[16,2048]{1,0:T(8,128)(2,1)S(1)}, u32[]{:S(2)}, u32[]{:S(2)}) collective-permute-start(bf16[16,2048]{1,0:T(8,128)(2,1)S(1)} %get-tuple-element.76), channel_id=1, source_target_pairs={{0,2},{1,3},{2,0},{3,1},{4,6},{5,7},{6,4},{7,5},{8,10},{9,11},{10,... | collective-permute-start | bytes 196616 | tf_op jit(solution)/shard_map/ppermute | solution.py:339
  100.4 2.6 %collective-permute-done.21.refs_1_ = bf16[32,2048]{1,0:T(8,128)(2,1)S(1)} collective-permute-done((bf16[32,2048]{1,0:T(8,128)(2,1)S(1)}, bf16[32,2048]{1,0:T(8,128)(2,1)S(1)}, u32[]{:S(2)}, u32[]{:S(2)}) %collective-permute-start.21) | collective-permute-done | bytes 131104 | tf_op jit(solution)/shard_map/ppermute | solution.py:339
  103.1 1.6 %collective-permute-start.23 = (bf16[16,2048]{1,0:T(8,128)(2,1)S(1)}, bf16[16,2048]{1,0:T(8,128)(2,1)S(1)}, u32[]{:S(2)}, u32[]{:S(2)}) collective-permute-start(bf16[16,2048]{1,0:T(8,128)(2,1)S(1)} %get-tuple-element.80), channel_id=1, source_target_pairs={{0,6},{1,7},{2,4},{3,5},{4,2},{5,3},{6,0},{7,1},{8,14},{9,15},{10,... | collective-permute-start | bytes 196616 | tf_op jit(solution)/shard_map/ppermute | solution.py:339
  104.7 2.7 %collective-permute-done.22.refs_2_ = bf16[16,2048]{1,0:T(8,128)(2,1)S(1)} collective-permute-done((bf16[16,2048]{1,0:T(8,128)(2,1)S(1)}, bf16[16,2048]{1,0:T(8,128)(2,1)S(1)}, u32[]{:S(2)}, u32[]{:S(2)}) %collective-permute-start.22) | collective-permute-done | bytes 65568 | tf_op jit(solution)/shard_map/ppermute | solution.py:339
  107.3 1.0 collective-permute-done.23.refs_3_
  108.4 1.3 %collective-permute-done.24.refs_1_ = bf16[32,2048]{1,0:T(8,128)(2,1)S(1)} collective-permute-done((bf16[32,2048]{1,0:T(8,128)(2,1)S(1)}, bf16[32,2048]{1,0:T(8,128)(2,1)S(1)}, u32[]{:S(2)}, u32[]{:S(2)}) %collective-permute-start.24) | collective-permute-done | bytes 131104 | tf_op jit(solution)/shard_map/ppermute | solution.py:339
  109.8 1.1 shard_map.153
  (42 shorter events, 1.9 us)
Async XLA Ops:
  0.0 49.2 %copy-start.7 = (f32[2048]{0:T(1024)S(1)}, f32[2048]{0:T(1024)}, u32[]{:S(2)}) copy-start(f32[2048]{0:T(1024)} %param.23) | copy-start | bytes 24580
  0.0 49.2 %copy-start.6 = (f32[2048]{0:T(1024)S(1)}, f32[2048]{0:T(1024)}, u32[]{:S(2)}) copy-start(f32[2048]{0:T(1024)} %param.22) | copy-start | bytes 24580
  2.8 12.7 %collective-permute-start = (bf16[32,4224]{1,0:T(8,128)(2,1)}, bf16[32,4224]{1,0:T(8,128)(2,1)S(1)}, u32[]{:S(2)}, u32[]{:S(2)}) collective-permute-start(bf16[32,4224]{1,0:T(8,128)(2,1)} %get-tuple-element.49), channel_id=1, source_target_pairs={{0,8},{8,16},{16,24},{24,0},{1,9},{9,17},{17,25},{25,1},{2,10},{10... | collective-permute-start | bytes 811016 | tf_op jit(solution)/shard_map/ppermute | solution.py:268
  5.8 21.3 %collective-permute-start.1 = (bf16[32,4224]{1,0:T(8,128)(2,1)}, bf16[32,4224]{1,0:T(8,128)(2,1)S(1)}, u32[]{:S(2)}, u32[]{:S(2)}) collective-permute-start(bf16[32,4224]{1,0:T(8,128)(2,1)} %get-tuple-element.50), channel_id=1, source_target_pairs={{0,16},{8,24},{16,0},{24,8},{1,17},{9,25},{17,1},{25,9},{2,18},{10... | collective-permute-start | bytes 811016 | tf_op jit(solution)/shard_map/ppermute | solution.py:268
  8.4 18.7 %collective-permute-start.2 = (bf16[32,4224]{1,0:T(8,128)(2,1)}, bf16[32,4224]{1,0:T(8,128)(2,1)S(1)}, u32[]{:S(2)}, u32[]{:S(2)}) collective-permute-start(bf16[32,4224]{1,0:T(8,128)(2,1)} %get-tuple-element.51), channel_id=1, source_target_pairs={{0,24},{8,0},{16,8},{24,16},{1,25},{9,1},{17,9},{25,17},{2,26},{10... | collective-permute-start | bytes 811016 | tf_op jit(solution)/shard_map/ppermute | solution.py:268
  12.3 20.4 %collective-permute-start.3 = (bf16[32,4096]{1,0:T(8,128)(2,1)}, bf16[32,4096]{1,0:T(8,128)(2,1)S(1)}, u32[]{:S(2)}, u32[]{:S(2)}) collective-permute-start(bf16[32,4096]{1,0:T(8,128)(2,1)} %get-tuple-element.56), channel_id=1, source_target_pairs={{0,8},{8,16},{16,24},{24,0},{1,9},{9,17},{17,25},{25,1},{2,10},{10... | collective-permute-start | bytes 786440 | tf_op jit(solution)/shard_map/ppermute | solution.py:268
  13.0 35.9 %collective-permute-start.4 = (bf16[32,4096]{1,0:T(8,128)(2,1)}, bf16[32,4096]{1,0:T(8,128)(2,1)S(1)}, u32[]{:S(2)}, u32[]{:S(2)}) collective-permute-start(bf16[32,4096]{1,0:T(8,128)(2,1)} %get-tuple-element.57), channel_id=1, source_target_pairs={{0,16},{8,24},{16,0},{24,8},{1,17},{9,25},{17,1},{25,9},{2,18},{10... | collective-permute-start | bytes 786440 | tf_op jit(solution)/shard_map/ppermute | solution.py:268
  15.5 33.4 %collective-permute-start.5 = (bf16[32,4096]{1,0:T(8,128)(2,1)}, bf16[32,4096]{1,0:T(8,128)(2,1)S(1)}, u32[]{:S(2)}, u32[]{:S(2)}) collective-permute-start(bf16[32,4096]{1,0:T(8,128)(2,1)} %get-tuple-element.58), channel_id=1, source_target_pairs={{0,24},{8,0},{16,8},{24,16},{1,25},{9,1},{17,9},{25,17},{2,26},{10... | collective-permute-start | bytes 786440 | tf_op jit(solution)/shard_map/ppermute | solution.py:268
  18.0 1.0 copy-start.2
  18.9 0.9 copy-start.4
  19.9 0.7 copy-start.8
  20.5 0.7 copy-start.9
  21.2 0.7 copy-start.10
  27.1 46.8 %copy-start = (bf16[1,2048,1024]{2,1,0:T(8,128)(2,1)S(1)}, bf16[1,2048,1024]{2,1,0:T(8,128)(2,1)}, u32[]{:S(2)}) copy-start(bf16[1,2048,1024]{2,1,0:T(8,128)(2,1)} %w_in_ref.5) | copy-start | bytes 12582916
  27.1 46.8 %copy-start.1 = (bf16[1,1024,2048]{2,1,0:T(8,128)(2,1)S(1)}, bf16[1,1024,2048]{2,1,0:T(8,128)(2,1)}, u32[]{:S(2)}) copy-start(bf16[1,1024,2048]{2,1,0:T(8,128)(2,1)} %w_out_ref.5) | copy-start | bytes 12582916
  27.1 46.8 %copy-start.5 = (f32[1,1024]{1,0:T(1,128)S(1)}, f32[1,1024]{1,0:T(1,128)}, u32[]{:S(2)}) copy-start(f32[1,1024]{1,0:T(1,128)} %bias_ref.7) | copy-start | bytes 12292
  50.0 1.4 %collective-permute-start.6 = (bf16[32,2048]{1,0:T(8,128)(2,1)S(1)}, bf16[32,2048]{1,0:T(8,128)(2,1)S(1)}, u32[]{:S(2)}, u32[]{:S(2)}) collective-permute-start(bf16[32,2048]{1,0:T(8,128)(2,1)S(1)} %get-tuple-element.62), channel_id=1, source_target_pairs={{0,1},{1,0},{2,3},{3,2},{4,5},{5,4},{6,7},{7,6},{8,9},{9,8},{10,11... | collective-permute-start | bytes 393224 | tf_op jit(solution)/shard_map/ppermute | solution.py:339
  51.5 4.3 %collective-permute-start.11 = (bf16[16,2048]{1,0:T(8,128)(2,1)S(1)}, bf16[16,2048]{1,0:T(8,128)(2,1)S(1)}, u32[]{:S(2)}, u32[]{:S(2)}) collective-permute-start(bf16[16,2048]{1,0:T(8,128)(2,1)S(1)} %get-tuple-element.66), channel_id=1, source_target_pairs={{0,2},{1,3},{2,0},{3,1},{4,6},{5,7},{6,4},{7,5},{8,10},{9,11},{10,... | collective-permute-start | bytes 196616 | tf_op jit(solution)/shard_map/ppermute | solution.py:339
  53.0 8.0 %collective-permute-start.7 = (bf16[16,2048]{1,0:T(8,128)(2,1)S(1)}, bf16[16,2048]{1,0:T(8,128)(2,1)S(1)}, u32[]{:S(2)}, u32[]{:S(2)}) collective-permute-start(bf16[16,2048]{1,0:T(8,128)(2,1)S(1)} %get-tuple-element.63), channel_id=1, source_target_pairs={{0,4},{1,5},{2,6},{3,7},{4,0},{5,1},{6,2},{7,3},{8,12},{9,13},{10,... | collective-permute-start | bytes 196616 | tf_op jit(solution)/shard_map/ppermute | solution.py:339
  54.5 6.5 %collective-permute-start.8 = (bf16[16,2048]{1,0:T(8,128)(2,1)S(1)}, bf16[16,2048]{1,0:T(8,128)(2,1)S(1)}, u32[]{:S(2)}, u32[]{:S(2)}) collective-permute-start(bf16[16,2048]{1,0:T(8,128)(2,1)S(1)} %get-tuple-element.64), channel_id=1, source_target_pairs={{0,6},{1,7},{2,4},{3,5},{4,2},{5,3},{6,0},{7,1},{8,14},{9,15},{10,... | collective-permute-start | bytes 196616 | tf_op jit(solution)/shard_map/ppermute | solution.py:339
  55.8 11.7 %collective-permute-start.12 = (bf16[32,2048]{1,0:T(8,128)(2,1)S(1)}, bf16[32,2048]{1,0:T(8,128)(2,1)S(1)}, u32[]{:S(2)}, u32[]{:S(2)}) collective-permute-start(bf16[32,2048]{1,0:T(8,128)(2,1)S(1)} %shard_map.145.refs_0_), channel_id=1, source_target_pairs={{0,16},{8,24},{16,0},{24,8},{1,17},{9,25},{17,1},{25,9},{2,18},{10... | collective-permute-start | bytes 393224 | tf_op jit(solution)/shard_map/ppermute | solution.py:339
  61.1 11.2 %collective-permute-start.9 = (bf16[32,2048]{1,0:T(8,128)(2,1)S(1)}, bf16[32,2048]{1,0:T(8,128)(2,1)S(1)}, u32[]{:S(2)}, u32[]{:S(2)}) collective-permute-start(bf16[32,2048]{1,0:T(8,128)(2,1)S(1)} %shard_map.144.refs_0_), channel_id=1, source_target_pairs={{0,16},{8,24},{16,0},{24,8},{1,17},{9,25},{17,1},{25,9},{2,18},{10... | collective-permute-start | bytes 393224 | tf_op jit(solution)/shard_map/ppermute | solution.py:339
  64.9 9.0 %collective-permute-start.15 = (bf16[32,2048]{1,0:T(8,128)(2,1)S(1)}, bf16[32,2048]{1,0:T(8,128)(2,1)S(1)}, u32[]{:S(2)}, u32[]{:S(2)}) collective-permute-start(bf16[32,2048]{1,0:T(8,128)(2,1)S(1)} %shard_map.145.refs_0_), channel_id=1, source_target_pairs={{0,8},{8,0},{16,24},{24,16},{1,9},{9,1},{17,25},{25,17},{2,10},{10... | collective-permute-start | bytes 393224 | tf_op jit(solution)/shard_map/ppermute | solution.py:339
  67.5 9.3 %collective-permute-start.14 = (bf16[32,2048]{1,0:T(8,128)(2,1)S(1)}, bf16[32,2048]{1,0:T(8,128)(2,1)S(1)}, u32[]{:S(2)}, u32[]{:S(2)}) collective-permute-start(bf16[32,2048]{1,0:T(8,128)(2,1)S(1)} %shard_map.144.refs_0_), channel_id=1, source_target_pairs={{0,8},{8,0},{16,24},{24,16},{1,9},{9,1},{17,25},{25,17},{2,10},{10... | collective-permute-start | bytes 393224 | tf_op jit(solution)/shard_map/ppermute | solution.py:339
  67.5 11.1 %collective-permute-start.13 = (bf16[32,2048]{1,0:T(8,128)(2,1)S(1)}, bf16[32,2048]{1,0:T(8,128)(2,1)S(1)}, u32[]{:S(2)}, u32[]{:S(2)}) collective-permute-start(bf16[32,2048]{1,0:T(8,128)(2,1)S(1)} %collective-permute-done.12.refs_3_), channel_id=1, source_target_pairs={{0,8},{8,0},{16,24},{24,16},{1,9},{9,1},{17,25},{25,17},{2,10},{10... | collective-permute-start | bytes 393224 | tf_op jit(solution)/shard_map/ppermute | solution.py:339
  72.3 7.7 %collective-permute-start.10 = (bf16[32,2048]{1,0:T(8,128)(2,1)S(1)}, bf16[32,2048]{1,0:T(8,128)(2,1)S(1)}, u32[]{:S(2)}, u32[]{:S(2)}) collective-permute-start(bf16[32,2048]{1,0:T(8,128)(2,1)S(1)} %collective-permute-done.9.refs_2_), channel_id=1, source_target_pairs={{0,8},{8,0},{16,24},{24,16},{1,9},{9,1},{17,25},{25,17},{2,10},{10... | collective-permute-start | bytes 393224 | tf_op jit(solution)/shard_map/ppermute | solution.py:339
  80.0 18.8 %copy-start.3 = (f32[8,2048]{1,0:T(8,128)S(1)}, f32[8,2048]{1,0:T(8,128)}, u32[]{:S(2)}) copy-start(f32[8,2048]{1,0:T(8,128)} %bias_ref.9) | copy-start | bytes 196612
  81.4 6.8 %collective-permute-start.16 = (bf16[64,2048]{1,0:T(8,128)(2,1)S(1)}, bf16[64,2048]{1,0:T(8,128)(2,1)S(1)}, u32[]{:S(2)}, u32[]{:S(2)}) collective-permute-start(bf16[64,2048]{1,0:T(8,128)(2,1)S(1)} %get-tuple-element.69), channel_id=1, source_target_pairs={{0,8},{8,0},{16,24},{24,16},{1,9},{9,1},{17,25},{25,17},{2,10},{10... | collective-permute-start | bytes 786440 | tf_op jit(solution)/shard_map/ppermute | solution.py:339
  88.3 6.6 %collective-permute-start.17 = (bf16[32,2048]{1,0:T(8,128)(2,1)S(1)}, bf16[32,2048]{1,0:T(8,128)(2,1)S(1)}, u32[]{:S(2)}, u32[]{:S(2)}) collective-permute-start(bf16[32,2048]{1,0:T(8,128)(2,1)S(1)} %get-tuple-element.73), channel_id=1, source_target_pairs={{0,8},{8,0},{16,24},{24,16},{1,9},{9,1},{17,25},{25,17},{2,10},{10... | collective-permute-start | bytes 393224 | tf_op jit(solution)/shard_map/ppermute | solution.py:339
  89.0 9.8 %collective-permute-start.18 = (bf16[32,2048]{1,0:T(8,128)(2,1)S(1)}, bf16[32,2048]{1,0:T(8,128)(2,1)S(1)}, u32[]{:S(2)}, u32[]{:S(2)}) collective-permute-start(bf16[32,2048]{1,0:T(8,128)(2,1)S(1)} %get-tuple-element.74), channel_id=1, source_target_pairs={{0,16},{8,24},{16,0},{24,8},{1,17},{9,25},{17,1},{25,9},{2,18},{10... | collective-permute-start | bytes 393224 | tf_op jit(solution)/shard_map/ppermute | solution.py:339
  94.4 6.0 %collective-permute-start.20 = (bf16[32,2048]{1,0:T(8,128)(2,1)S(1)}, bf16[32,2048]{1,0:T(8,128)(2,1)S(1)}, u32[]{:S(2)}, u32[]{:S(2)}) collective-permute-start(bf16[32,2048]{1,0:T(8,128)(2,1)S(1)} %get-tuple-element.77), channel_id=1, source_target_pairs={{0,8},{8,0},{16,24},{24,16},{1,9},{9,1},{17,25},{25,17},{2,10},{10... | collective-permute-start | bytes 393224 | tf_op jit(solution)/shard_map/ppermute | solution.py:339
  94.7 8.2 %collective-permute-start.21 = (bf16[32,2048]{1,0:T(8,128)(2,1)S(1)}, bf16[32,2048]{1,0:T(8,128)(2,1)S(1)}, u32[]{:S(2)}, u32[]{:S(2)}) collective-permute-start(bf16[32,2048]{1,0:T(8,128)(2,1)S(1)} %get-tuple-element.78), channel_id=1, source_target_pairs={{0,16},{8,24},{16,0},{24,8},{1,17},{9,25},{17,1},{25,9},{2,18},{10... | collective-permute-start | bytes 393224 | tf_op jit(solution)/shard_map/ppermute | solution.py:339
  98.9 5.8 %collective-permute-start.19 = (bf16[16,2048]{1,0:T(8,128)(2,1)S(1)}, bf16[16,2048]{1,0:T(8,128)(2,1)S(1)}, u32[]{:S(2)}, u32[]{:S(2)}) collective-permute-start(bf16[16,2048]{1,0:T(8,128)(2,1)S(1)} %get-tuple-element.76), channel_id=1, source_target_pairs={{0,2},{1,3},{2,0},{3,1},{4,6},{5,7},{6,4},{7,5},{8,10},{9,11},{10,... | collective-permute-start | bytes 196616 | tf_op jit(solution)/shard_map/ppermute | solution.py:339
  103.0 4.3 %collective-permute-start.22 = (bf16[16,2048]{1,0:T(8,128)(2,1)S(1)}, bf16[16,2048]{1,0:T(8,128)(2,1)S(1)}, u32[]{:S(2)}, u32[]{:S(2)}) collective-permute-start(bf16[16,2048]{1,0:T(8,128)(2,1)S(1)} %get-tuple-element.79), channel_id=1, source_target_pairs={{0,4},{1,5},{2,6},{3,7},{4,0},{5,1},{6,2},{7,3},{8,12},{9,13},{10,... | collective-permute-start | bytes 196616 | tf_op jit(solution)/shard_map/ppermute | solution.py:339
  103.1 5.2 %collective-permute-start.23 = (bf16[16,2048]{1,0:T(8,128)(2,1)S(1)}, bf16[16,2048]{1,0:T(8,128)(2,1)S(1)}, u32[]{:S(2)}, u32[]{:S(2)}) collective-permute-start(bf16[16,2048]{1,0:T(8,128)(2,1)S(1)} %get-tuple-element.80), channel_id=1, source_target_pairs={{0,6},{1,7},{2,4},{3,5},{4,2},{5,3},{6,0},{7,1},{8,14},{9,15},{10,... | collective-permute-start | bytes 196616 | tf_op jit(solution)/shard_map/ppermute | solution.py:339
  108.3 1.4 %collective-permute-start.24 = (bf16[32,2048]{1,0:T(8,128)(2,1)S(1)}, bf16[32,2048]{1,0:T(8,128)(2,1)S(1)}, u32[]{:S(2)}, u32[]{:S(2)}) collective-permute-start(bf16[32,2048]{1,0:T(8,128)(2,1)S(1)} %get-tuple-element.82), channel_id=1, source_target_pairs={{0,1},{1,0},{2,3},{3,2},{4,5},{5,4},{6,7},{7,6},{8,9},{9,8},{10,11... | collective-permute-start | bytes 393224 | tf_op jit(solution)/shard_map/ppermute | solution.py:339

commit v13 on v10

--- a/solution.py
+++ b/solution.py
@@ -144,21 +144,17 @@
         out_ref[h] = (terms / jnp.sum(terms, axis=1, keepdims=True)).astype(BF16)
 
 
-def mix_kernel(probs_ref, *refs):
-    *value_refs, out_ref = refs
-    width = out_ref.shape[1]
+def norm_kernel(parts, place_ref, taken_ref, gain_ref, bias_ref, probs_ref, *refs):
+    row_refs, hidden_ref, send_refs = refs[: -parts - 1], refs[-parts - 1], refs[-parts:]
+    width = hidden_ref.shape[1]
     for h in range(probs_ref.shape[0]):
         lo = h * HEAD_DIM
-        values = joined(value_refs, slice(lo, lo + HEAD_DIM))
-        out_ref[:, lo : lo + HEAD_DIM] = jnp.dot(probs_ref[h], values, preferred_element_type=F32)
-
-
-def norm_kernel(parts, place_ref, taken_ref, gain_ref, bias_ref, mixed_ref, *refs):
-    state_refs, hidden_ref, send_refs = refs[: -parts - 1], refs[-parts - 1], refs[-parts:]
-    hidden = mixed_ref[...] + jnp.dot(
-        place_ref[...], joined(state_refs, slice(mixed_ref.shape[1], None)), preferred_element_type=F32
-    )
-    hidden_ref[...] = hidden
+        values = joined(row_refs, slice(lo, lo + HEAD_DIM))
+        states = joined(row_refs, slice(width + lo, width + lo + HEAD_DIM))
+        hidden_ref[:, lo : lo + HEAD_DIM] = jnp.dot(
+            probs_ref[h], values, preferred_element_type=F32
+        ) + jnp.dot(place_ref[...], states, preferred_element_type=F32)
+    hidden = hidden_ref[...]
     centered = hidden - jnp.mean(hidden, axis=1, keepdims=True)
     variance = jnp.mean(centered * centered, axis=1, keepdims=True)
     normed = (centered * lax.rsqrt(variance + epsilon) * gain_ref[...] + bias_ref[...]).astype(BF16)
@@ -182,6 +178,13 @@
 
 def add_kernel(first_ref, second_ref, out_ref):
     out_ref[...] = (first_ref[...].astype(F32) + second_ref[...].astype(F32)).astype(BF16)
+
+
+def hand_kernel(first_ref, second_ref, _, *out_refs):
+    rows = out_refs[0].shape[0]
+    for n, out_ref in enumerate(out_refs):
+        source_ref = (first_ref, second_ref)[n // 2]
+        out_ref[...] = source_ref[n % 2 * rows : (n % 2 + 1) * rows]
 
 
 def result_kernel(lower, bias_ref, near_ref, *refs):
@@ -295,7 +298,6 @@
         outside,
         *rows,
     )
-    mixed = call(mix_kernel, jax.ShapeDtypeStruct((tok, width), F32), probs, *later)
     parts = 2 if relative else 1
     hidden_state, *send = call(
         functools.partial(norm_kernel, parts),
@@ -305,7 +307,7 @@
         taken,
         ln_gain.reshape(1, width),
         ln_bias.reshape(1, width),
-        mixed,
+        probs,
         *later,
     )
 
@@ -348,18 +350,23 @@
         last = last[0]
         *corner_share, far_first, far_second = apply([swap(x, 1) for x in far] + far, after=[last])
         far_shares = [far_first, far_second]
-        near_shares = [swap(x, 1) for x in near_shares]
-        backs = [None, None]
-        for n in (1, 0):
-            pair = swap(call(add_kernel, bf16(half), swap(corner_share[n], 1), far_shares[n]), 2)
-            backs[n] = call(
+        first_pair = call(add_kernel, bf16(half), swap(corner_share[0], 1), far_shares[0])
+        second_pair = call(add_kernel, bf16(half), swap(corner_share[1], 1), far_shares[1])
+        near_parts = call(hand_kernel, (bf16(half // 2),) * 4, *near_shares, first_pair)
+        near_parts = [swap(x, 1) for x in near_parts]
+        near_shares = [call(join_kernel, bf16(half), *near_parts[n : n + 2]) for n in (0, 2)]
+        pairs = [first_pair, second_pair]
+        backs = [
+            call(
                 functools.partial(result_kernel, 0),
                 (bf16(2 * cap),) * 2,
                 b_out,
                 near_shares[n],
                 own_share[n],
-                pair,
+                swap(pairs[n], 2),
             )
+            for n in range(2)
+        ]
         pieces = [x for n in (1, 0) for x in backs[n]]
         pieces = [swap(x, 2 * n, "expert") if n else x for n, x in enumerate(pieces)]
         mine, other = call(functools.partial(part_kernel, cap), (bf16(half),) * 2, *pieces)

time: 109 us -> 112 us (1.028)
  starting transfers between devices: 37.4 us -> 47.6 us
  waiting for transfers between devices: 52.9 us -> 44.2 us
  local copies, waits for them, and re-layouts: 3.94 us -> 6.12 us
    ppermute x20 -> x22, starting transfers between devices: 26.9 us -> 37.1 us  [swap(): lax.ppermute(x, axis, [(i, i ^ distance) for i in range(lax.axis_size(axi...]
    ppermute x20 -> x22, waiting for transfers between devices: 25.6 us -> 16.9 us  [swap(): lax.ppermute(x, axis, [(i, i ^ distance) for i in range(lax.axis_size(axi...]
    unnamed x22, local copies, waits for them, and re-layouts: 3.94 us -> 6.12 us
    pallas_call x19 -> x21, Pallas kernels: 14.2 us -> 14 us  [call(): pl.pallas_call(body, out_shape=out_shape, compiler_params=pltpu.CompilerP...]
  transfers between devices with their start and end apart: 26 -> 28, of which waited for: 17 -> 17; matrix products, arithmetic and copies ran while one was open for 0% -> 0% of each run, Pallas kernels for 7% -> 7%
where the time goes in v13:
time: 112 us
  starting transfers between devices  47.6 us (42%)
  waiting for transfers between devices  44.2 us (39%)
  Pallas kernels  14 us (12%)
  local copies, waits for them, and re-layouts  6.12 us (5%)
    ppermute x22, starting transfers between devices, swap(): lax.ppermute(x, axis, [(i, i ^ distance) for i in range(lax.axis_size(axi...  37.1 us
    ppermute x6, waiting for transfers between devices, spread(): lax.ppermute(part, 'dp', [(i, (i + n) % dp) for i in range(dp)])  27.3 us
    ppermute x22, waiting for transfers between devices, swap(): lax.ppermute(x, axis, [(i, i ^ distance) for i in range(lax.axis_size(axi...  16.9 us
    pallas_call x21, Pallas kernels, call(): pl.pallas_call(body, out_shape=out_shape, compiler_params=pltpu.CompilerP...  14 us
    ppermute x6, starting transfers between devices, spread(): lax.ppermute(part, 'dp', [(i, (i + n) % dp) for i in range(dp)])  10.5 us
    unnamed x22, local copies, waits for them, and re-layouts  6.12 us
  transfers between devices with their start and end apart: 28, of which 17 were waited for; matrix products, arithmetic and copies ran while one was open for 0% of the time, Pallas kernels for 7%

profile of v13, /device:TPU:0, one launch (start us, length us, event | category | flops | bytes accessed | tf_op | source)
XLA Modules:
  0.0 112.1 jit_solution(8101739309623858105)
XLA Ops:
  0.0 2.7 %shard_map.136 = (bf16[128,128]{1,0:T(8,128)(2,1)}, bf16[32,4224]{1,0:T(8,128)(2,1)}, bf16[32,4224]{1,0:T(8,128)(2,1)}, bf16[32,4224]{1,0:T(8,128)(2,1)}, bf16[32,4224]{1,0:T(8,128)(2,1)}) custom-call(s32[1,128]{1,0:T(1,128)} %bitcast.9, bf16[128,2048]{1,0:T(8,128)(2,1)} %refs_0_.2, bf16[128,2048]{1,0:T(8,128)(2,1)} %refs_1_.2), custom_call_target="tpu_custom_call" | custom-call | bytes 2163200 | tf_op jit(solution)/shard_map/pallas_call | solution.py:41
  2.8 3.0 %collective-permute-start = (bf16[32,4224]{1,0:T(8,128)(2,1)}, bf16[32,4224]{1,0:T(8,128)(2,1)S(1)}, u32[]{:S(2)}, u32[]{:S(2)}) collective-permute-start(bf16[32,4224]{1,0:T(8,128)(2,1)} %get-tuple-element.51), channel_id=1, source_target_pairs={{0,8},{8,16},{16,24},{24,0},{1,9},{9,17},{17,25},{25,1},{2,10},{10... | collective-permute-start | bytes 811016 | tf_op jit(solution)/shard_map/ppermute | solution.py:265
  5.8 2.6 %collective-permute-start.1 = (bf16[32,4224]{1,0:T(8,128)(2,1)}, bf16[32,4224]{1,0:T(8,128)(2,1)S(1)}, u32[]{:S(2)}, u32[]{:S(2)}) collective-permute-start(bf16[32,4224]{1,0:T(8,128)(2,1)} %get-tuple-element.52), channel_id=1, source_target_pairs={{0,16},{8,24},{16,0},{24,8},{1,17},{9,25},{17,1},{25,9},{2,18},{10... | collective-permute-start | bytes 811016 | tf_op jit(solution)/shard_map/ppermute | solution.py:265
  8.4 1.3 %collective-permute-start.2 = (bf16[32,4224]{1,0:T(8,128)(2,1)}, bf16[32,4224]{1,0:T(8,128)(2,1)S(1)}, u32[]{:S(2)}, u32[]{:S(2)}) collective-permute-start(bf16[32,4224]{1,0:T(8,128)(2,1)} %get-tuple-element.53), channel_id=1, source_target_pairs={{0,24},{8,0},{16,8},{24,16},{1,25},{9,1},{17,9},{25,17},{2,26},{10... | collective-permute-start | bytes 811016 | tf_op jit(solution)/shard_map/ppermute | solution.py:265
  9.7 2.6 %shard_map.137 = (bf16[128,128]{1,0:T(8,128)(2,1)}, bf16[32,4096]{1,0:T(8,128)(2,1)}, bf16[32,4096]{1,0:T(8,128)(2,1)}, bf16[32,4096]{1,0:T(8,128)(2,1)}, bf16[32,4096]{1,0:T(8,128)(2,1)}) custom-call(bf16[128,128]{1,0:T(8,128)(2,1)} %get-tuple-element.47.pos_ref, bf16[128,2048]{1,0:T(8,128)(2,1)} %refs_0_.3, bf16[128,2048]{1,0:T(8,128)(2,1)} %refs_1_.3), custom_call_target="tpu_custom_call" | custom-call | bytes 2162688 | tf_op jit(solution)/shard_map/pallas_call | solution.py:41
  12.3 0.7 collective-permute-start.3
  13.3 2.1 %collective-permute-done.refs_1_ = bf16[32,4224]{1,0:T(8,128)(2,1)S(1)} collective-permute-done((bf16[32,4224]{1,0:T(8,128)(2,1)}, bf16[32,4224]{1,0:T(8,128)(2,1)S(1)}, u32[]{:S(2)}, u32[]{:S(2)}) %collective-permute-start) | collective-permute-done | bytes 270368 | tf_op jit(solution)/shard_map/ppermute | solution.py:265
  15.5 2.5 %collective-permute-start.5 = (bf16[32,4096]{1,0:T(8,128)(2,1)}, bf16[32,4096]{1,0:T(8,128)(2,1)S(1)}, u32[]{:S(2)}, u32[]{:S(2)}) collective-permute-start(bf16[32,4096]{1,0:T(8,128)(2,1)} %get-tuple-element.60), channel_id=1, source_target_pairs={{0,24},{8,0},{16,8},{24,16},{1,25},{9,1},{17,9},{25,17},{2,26},{10... | collective-permute-start | bytes 786440 | tf_op jit(solution)/shard_map/ppermute | solution.py:265
  18.0 1.0 copy-done.2
  18.9 0.9 copy-done.4
  19.9 0.7 copy-done.8
  20.5 0.7 copy-done.9
  22.1 5.0 %collective-permute-done.1.refs_2_ = bf16[32,4224]{1,0:T(8,128)(2,1)S(1)} collective-permute-done((bf16[32,4224]{1,0:T(8,128)(2,1)}, bf16[32,4224]{1,0:T(8,128)(2,1)S(1)}, u32[]{:S(2)}, u32[]{:S(2)}) %collective-permute-start.1) | collective-permute-done | bytes 270368 | tf_op jit(solution)/shard_map/ppermute | solution.py:265
  27.2 1.5 %shard_map.140.probs_ref = bf16[16,128,128]{2,1,0:T(8,128)(2,1)S(1)} custom-call(bf16[128,128]{1,0:T(8,128)(2,1)S(1)} %get-tuple-element.54.place_ref, f32[128,128]{1,0:T(8,128)S(1)} %get-tuple-element.56.outside_ref, bf16[32,4224]{1,0:T(8,128)(2,1)S(1)} %get-tuple-element.50.refs_0_, bf16[32,4224]{1,0:T(8,128)(2,1)S(1)} %collective-permute-done.refs_1_, ...), custom_call_target="tpu_custom_call" | custom-call | bytes 1703936 | tf_op jit(solution)/shard_map/pallas_call | solution.py:41
  28.7 4.0 %collective-permute-done.3.refs_1_ = bf16[32,4096]{1,0:T(8,128)(2,1)S(1)} collective-permute-done((bf16[32,4096]{1,0:T(8,128)(2,1)}, bf16[32,4096]{1,0:T(8,128)(2,1)S(1)}, u32[]{:S(2)}, u32[]{:S(2)}) %collective-permute-start.3) | collective-permute-done | bytes 262176 | tf_op jit(solution)/shard_map/ppermute | solution.py:265
  32.7 16.2 %collective-permute-done.4.refs_2_ = bf16[32,4096]{1,0:T(8,128)(2,1)S(1)} collective-permute-done((bf16[32,4096]{1,0:T(8,128)(2,1)}, bf16[32,4096]{1,0:T(8,128)(2,1)S(1)}, u32[]{:S(2)}, u32[]{:S(2)}) %collective-permute-start.4) | collective-permute-done | bytes 262176 | tf_op jit(solution)/shard_map/ppermute | solution.py:265
  48.9 0.9 shard_map.141
  49.9 1.3 %collective-permute-done.6.other_ref = bf16[32,2048]{1,0:T(8,128)(2,1)S(1)} collective-permute-done((bf16[32,2048]{1,0:T(8,128)(2,1)S(1)}, bf16[32,2048]{1,0:T(8,128)(2,1)S(1)}, u32[]{:S(2)}, u32[]{:S(2)}) %collective-permute-start.6) | collective-permute-done | bytes 131104 | tf_op jit(solution)/shard_map/ppermute | solution.py:335
  51.3 1.6 %collective-permute-start.10 = (bf16[16,2048]{1,0:T(8,128)(2,1)S(1)}, bf16[16,2048]{1,0:T(8,128)(2,1)S(1)}, u32[]{:S(2)}, u32[]{:S(2)}) collective-permute-start(bf16[16,2048]{1,0:T(8,128)(2,1)S(1)} %get-tuple-element.68), channel_id=1, source_target_pairs={{0,2},{1,3},{2,0},{3,1},{4,6},{5,7},{6,4},{7,5},{8,10},{9,11},{10,... | collective-permute-start | bytes 196616 | tf_op jit(solution)/shard_map/ppermute | solution.py:335
  52.9 1.5 %collective-permute-start.7 = (bf16[16,2048]{1,0:T(8,128)(2,1)S(1)}, bf16[16,2048]{1,0:T(8,128)(2,1)S(1)}, u32[]{:S(2)}, u32[]{:S(2)}) collective-permute-start(bf16[16,2048]{1,0:T(8,128)(2,1)S(1)} %get-tuple-element.65), channel_id=1, source_target_pairs={{0,4},{1,5},{2,6},{3,7},{4,0},{5,1},{6,2},{7,3},{8,12},{9,13},{10,... | collective-permute-start | bytes 196616 | tf_op jit(solution)/shard_map/ppermute | solution.py:335
  54.8 0.8 collective-permute-done.10.refs_1_
  55.6 5.2 %collective-permute-start.14 = (bf16[32,2048]{1,0:T(8,128)(2,1)S(1)}, bf16[32,2048]{1,0:T(8,128)(2,1)S(1)}, u32[]{:S(2)}, u32[]{:S(2)}) collective-permute-start(bf16[32,2048]{1,0:T(8,128)(2,1)S(1)} %shard_map.144.refs_0_), channel_id=1, source_target_pairs={{0,16},{8,24},{16,0},{24,8},{1,17},{9,25},{17,1},{25,9},{2,18},{10... | collective-permute-start | bytes 393224 | tf_op jit(solution)/shard_map/ppermute | solution.py:335
  60.9 3.9 %collective-permute-start.12 = (bf16[32,2048]{1,0:T(8,128)(2,1)S(1)}, bf16[32,2048]{1,0:T(8,128)(2,1)S(1)}, u32[]{:S(2)}, u32[]{:S(2)}) collective-permute-start(bf16[32,2048]{1,0:T(8,128)(2,1)S(1)} %shard_map.143.refs_0_), channel_id=1, source_target_pairs={{0,16},{8,24},{16,0},{24,8},{1,17},{9,25},{17,1},{25,9},{2,18},{10... | collective-permute-start | bytes 393224 | tf_op jit(solution)/shard_map/ppermute | solution.py:335
  64.8 2.5 %collective-permute-start.11 = (bf16[32,2048]{1,0:T(8,128)(2,1)S(1)}, bf16[32,2048]{1,0:T(8,128)(2,1)S(1)}, u32[]{:S(2)}, u32[]{:S(2)}) collective-permute-start(bf16[32,2048]{1,0:T(8,128)(2,1)S(1)} %shard_map.144.refs_0_), channel_id=1, source_target_pairs={{0,8},{8,0},{16,24},{24,16},{1,9},{9,1},{17,25},{25,17},{2,10},{10... | collective-permute-start | bytes 393224 | tf_op jit(solution)/shard_map/ppermute | solution.py:335
  67.3 3.2 %collective-permute-start.15 = (bf16[32,2048]{1,0:T(8,128)(2,1)S(1)}, bf16[32,2048]{1,0:T(8,128)(2,1)S(1)}, u32[]{:S(2)}, u32[]{:S(2)}) collective-permute-start(bf16[32,2048]{1,0:T(8,128)(2,1)S(1)} %collective-permute-done.14.refs_3_), channel_id=1, source_target_pairs={{0,8},{8,0},{16,24},{24,16},{1,9},{9,1},{17,25},{25,17},{2,10},{10... | collective-permute-start | bytes 393224 | tf_op jit(solution)/shard_map/ppermute | solution.py:335
  70.5 1.6 %collective-permute-done.12.refs_2_ = bf16[32,2048]{1,0:T(8,128)(2,1)S(1)} collective-permute-done((bf16[32,2048]{1,0:T(8,128)(2,1)S(1)}, bf16[32,2048]{1,0:T(8,128)(2,1)S(1)}, u32[]{:S(2)}, u32[]{:S(2)}) %collective-permute-start.12) | collective-permute-done | bytes 131104 | tf_op jit(solution)/shard_map/ppermute | solution.py:335
  72.1 0.9 collective-permute-start.13
  73.0 0.7 collective-permute-done.11.refs_1_
  73.8 2.2 %copy-done.1 = bf16[1,1024,2048]{2,1,0:T(8,128)(2,1)S(1)} copy-done((bf16[1,1024,2048]{2,1,0:T(8,128)(2,1)S(1)}, bf16[1,1024,2048]{2,1,0:T(8,128)(2,1)}, u32[]{:S(2)}) %copy-start.1) | copy-done | bytes 4194328
  75.9 1.6 %shard_map.145 = (bf16[32,2048]{1,0:T(8,128)(2,1)S(1)}, bf16[32,2048]{1,0:T(8,128)(2,1)S(1)}) custom-call(f32[1,1024]{1,0:T(1,128)S(1)} %copy-done.5, bf16[1,2048,1024]{2,1,0:T(8,128)(2,1)S(1)} %copy-done, bf16[1,1024,2048]{2,1,0:T(8,128)(2,1)S(1)} %copy-done.1, bf16[32,2048]{1,0:T(8,128)(2,1)S(1)} %shard_map.144.refs_0_, ...), custom_call_target="tpu_custom_call" | custom-call | flops 536870912 | bytes 8916992 | tf_op jit(solution)/shard_map/pallas_call | solution.py:41
  77.6 1.6 %shard_map.146 = (bf16[32,2048]{1,0:T(8,128)(2,1)S(1)}, bf16[32,2048]{1,0:T(8,128)(2,1)S(1)}) custom-call(f32[1,1024]{1,0:T(1,128)S(1)} %copy-done.5, bf16[1,2048,1024]{2,1,0:T(8,128)(2,1)S(1)} %copy-done, bf16[1,1024,2048]{2,1,0:T(8,128)(2,1)S(1)} %copy-done.1, bf16[32,2048]{1,0:T(8,128)(2,1)S(1)} %shard_map.143.refs_0_, ...), custom_call_target="tpu_custom_call" | custom-call | flops 536870912 | bytes 9048064 | tf_op jit(solution)/shard_map/pallas_call | solution.py:41
  79.8 1.3 %shard_map.147 = (bf16[32,2048]{1,0:T(8,128)(2,1)S(1)}, bf16[32,2048]{1,0:T(8,128)(2,1)S(1)}, bf16[32,2048]{1,0:T(8,128)(2,1)S(1)}, bf16[32,2048]{1,0:T(8,128)(2,1)S(1)}) custom-call(f32[1,1024]{1,0:T(1,128)S(1)} %copy-done.5, bf16[1,2048,1024]{2,1,0:T(8,128)(2,1)S(1)} %copy-done, bf16[1,1024,2048]{2,1,0:T(8,128)(2,1)S(1)} %copy-done.1, ...), custom_call_target="tpu_custom_call" | custom-call | flops 1073741824 | bytes 9572352 | tf_op jit(solution)/shard_map/pallas_call | solution.py:41
  81.2 0.9 collective-permute-start.16
  82.1 1.2 %collective-permute-start.19 = (bf16[32,2048]{1,0:T(8,128)(2,1)S(1)}, bf16[32,2048]{1,0:T(8,128)(2,1)S(1)}, u32[]{:S(2)}, u32[]{:S(2)}) collective-permute-start(bf16[32,2048]{1,0:T(8,128)(2,1)S(1)} %get-tuple-element.77), channel_id=1, source_target_pairs={{0,8},{8,0},{16,24},{24,16},{1,9},{9,1},{17,25},{25,17},{2,10},{10... | collective-permute-start | bytes 393224 | tf_op jit(solution)/shard_map/ppermute | solution.py:335
  83.3 3.6 %collective-permute-done.16.first_ref = bf16[32,2048]{1,0:T(8,128)(2,1)S(1)} collective-permute-done((bf16[32,2048]{1,0:T(8,128)(2,1)S(1)}, bf16[32,2048]{1,0:T(8,128)(2,1)S(1)}, u32[]{:S(2)}, u32[]{:S(2)}) %collective-permute-start.16) | collective-permute-done | bytes 131104 | tf_op jit(solution)/shard_map/ppermute | solution.py:335
  87.6 5.4 %collective-permute-start.24 = (bf16[32,2048]{1,0:T(8,128)(2,1)S(1)}, bf16[32,2048]{1,0:T(8,128)(2,1)S(1)}, u32[]{:S(2)}, u32[]{:S(2)}) collective-permute-start(bf16[32,2048]{1,0:T(8,128)(2,1)S(1)} %shard_map.148._), channel_id=1, source_target_pairs={{0,16},{8,24},{16,0},{24,8},{1,17},{9,25},{17,1},{25,9},{2,18},{10... | collective-permute-start | bytes 393224 | tf_op jit(solution)/shard_map/ppermute | solution.py:335
  93.1 1.4 %collective-permute-start.20 = (bf16[32,2048]{1,0:T(8,128)(2,1)S(1)}, bf16[32,2048]{1,0:T(8,128)(2,1)S(1)}, u32[]{:S(2)}, u32[]{:S(2)}) collective-permute-start(bf16[32,2048]{1,0:T(8,128)(2,1)S(1)} %shard_map.151), channel_id=1, source_target_pairs={{0,16},{8,24},{16,0},{24,8},{1,17},{9,25},{17,1},{25,9},{2,18},{10... | collective-permute-start | bytes 393224 | tf_op jit(solution)/shard_map/ppermute | solution.py:335
  94.5 2.5 %collective-permute-start.18 = (bf16[16,2048]{1,0:T(8,128)(2,1)S(1)}, bf16[16,2048]{1,0:T(8,128)(2,1)S(1)}, u32[]{:S(2)}, u32[]{:S(2)}) collective-permute-start(bf16[16,2048]{1,0:T(8,128)(2,1)S(1)} %get-tuple-element.76), channel_id=1, source_target_pairs={{0,8},{8,0},{16,24},{24,16},{1,9},{9,1},{17,25},{25,17},{2,10},{10... | collective-permute-start | bytes 196616 | tf_op jit(solution)/shard_map/ppermute | solution.py:335
  97.0 2.0 %collective-permute-start.23 = (bf16[16,2048]{1,0:T(8,128)(2,1)S(1)}, bf16[16,2048]{1,0:T(8,128)(2,1)S(1)}, u32[]{:S(2)}, u32[]{:S(2)}) collective-permute-start(bf16[16,2048]{1,0:T(8,128)(2,1)S(1)} %get-tuple-element.82), channel_id=1, source_target_pairs={{0,8},{8,0},{16,24},{24,16},{1,9},{9,1},{17,25},{25,17},{2,10},{10... | collective-permute-start | bytes 196616 | tf_op jit(solution)/shard_map/ppermute | solution.py:335
  99.0 0.9 collective-permute-done.18.refs_1_
  99.9 2.4 %collective-permute-done.22.refs_0_ = bf16[16,2048]{1,0:T(8,128)(2,1)S(1)} collective-permute-done((bf16[16,2048]{1,0:T(8,128)(2,1)S(1)}, bf16[16,2048]{1,0:T(8,128)(2,1)S(1)}, u32[]{:S(2)}, u32[]{:S(2)}) %collective-permute-start.22) | collective-permute-done | bytes 65568 | tf_op jit(solution)/shard_map/ppermute | solution.py:335
  102.3 0.7 collective-permute-done.23.refs_1_
  103.4 1.2 %collective-permute-start.26 = (bf16[16,2048]{1,0:T(8,128)(2,1)S(1)}, bf16[16,2048]{1,0:T(8,128)(2,1)S(1)}, u32[]{:S(2)}, u32[]{:S(2)}) collective-permute-start(bf16[16,2048]{1,0:T(8,128)(2,1)S(1)} %get-tuple-element.84), channel_id=1, source_target_pairs={{0,6},{1,7},{2,4},{3,5},{4,2},{5,3},{6,0},{7,1},{8,14},{9,15},{10,... | collective-permute-start | bytes 196616 | tf_op jit(solution)/shard_map/ppermute | solution.py:335
  104.7 2.1 %collective-permute-start.21 = (bf16[16,2048]{1,0:T(8,128)(2,1)S(1)}, bf16[16,2048]{1,0:T(8,128)(2,1)S(1)}, u32[]{:S(2)}, u32[]{:S(2)}) collective-permute-start(bf16[16,2048]{1,0:T(8,128)(2,1)S(1)} %get-tuple-element.80), channel_id=1, source_target_pairs={{0,2},{1,3},{2,0},{3,1},{4,6},{5,7},{6,4},{7,5},{8,10},{9,11},{10,... | collective-permute-start | bytes 196616 | tf_op jit(solution)/shard_map/ppermute | solution.py:335
  107.4 1.1 %collective-permute-done.26.refs_3_ = bf16[16,2048]{1,0:T(8,128)(2,1)S(1)} collective-permute-done((bf16[16,2048]{1,0:T(8,128)(2,1)S(1)}, bf16[16,2048]{1,0:T(8,128)(2,1)S(1)}, u32[]{:S(2)}, u32[]{:S(2)}) %collective-permute-start.26) | collective-permute-done | bytes 65568 | tf_op jit(solution)/shard_map/ppermute | solution.py:335
  108.6 1.0 collective-permute-done.21.refs_1_
  109.7 1.3 %collective-permute-done.27.refs_1_ = bf16[32,2048]{1,0:T(8,128)(2,1)S(1)} collective-permute-done((bf16[32,2048]{1,0:T(8,128)(2,1)S(1)}, bf16[32,2048]{1,0:T(8,128)(2,1)S(1)}, u32[]{:S(2)}, u32[]{:S(2)}) %collective-permute-start.27) | collective-permute-done | bytes 131104 | tf_op jit(solution)/shard_map/ppermute | solution.py:335
  111.0 1.1 shard_map.156
  (51 shorter events, 4.7 us)
Async XLA Ops:
  0.0 48.9 %copy-start.7 = (f32[2048]{0:T(1024)S(1)}, f32[2048]{0:T(1024)}, u32[]{:S(2)}) copy-start(f32[2048]{0:T(1024)} %param.23) | copy-start | bytes 24580
  0.0 48.9 %copy-start.6 = (f32[2048]{0:T(1024)S(1)}, f32[2048]{0:T(1024)}, u32[]{:S(2)}) copy-start(f32[2048]{0:T(1024)} %param.22) | copy-start | bytes 24580
  0.0 73.8 %copy-start.5 = (f32[1,1024]{1,0:T(1,128)S(1)}, f32[1,1024]{1,0:T(1,128)}, u32[]{:S(2)}) copy-start(f32[1,1024]{1,0:T(1,128)} %bias_ref.7) | copy-start | bytes 12292
  2.8 12.7 %collective-permute-start = (bf16[32,4224]{1,0:T(8,128)(2,1)}, bf16[32,4224]{1,0:T(8,128)(2,1)S(1)}, u32[]{:S(2)}, u32[]{:S(2)}) collective-permute-start(bf16[32,4224]{1,0:T(8,128)(2,1)} %get-tuple-element.51), channel_id=1, source_target_pairs={{0,8},{8,16},{16,24},{24,0},{1,9},{9,17},{17,25},{25,1},{2,10},{10... | collective-permute-start | bytes 811016 | tf_op jit(solution)/shard_map/ppermute | solution.py:265
  5.8 21.3 %collective-permute-start.1 = (bf16[32,4224]{1,0:T(8,128)(2,1)}, bf16[32,4224]{1,0:T(8,128)(2,1)S(1)}, u32[]{:S(2)}, u32[]{:S(2)}) collective-permute-start(bf16[32,4224]{1,0:T(8,128)(2,1)} %get-tuple-element.52), channel_id=1, source_target_pairs={{0,16},{8,24},{16,0},{24,8},{1,17},{9,25},{17,1},{25,9},{2,18},{10... | collective-permute-start | bytes 811016 | tf_op jit(solution)/shard_map/ppermute | solution.py:265
  8.4 18.7 %collective-permute-start.2 = (bf16[32,4224]{1,0:T(8,128)(2,1)}, bf16[32,4224]{1,0:T(8,128)(2,1)S(1)}, u32[]{:S(2)}, u32[]{:S(2)}) collective-permute-start(bf16[32,4224]{1,0:T(8,128)(2,1)} %get-tuple-element.53), channel_id=1, source_target_pairs={{0,24},{8,0},{16,8},{24,16},{1,25},{9,1},{17,9},{25,17},{2,26},{10... | collective-permute-start | bytes 811016 | tf_op jit(solution)/shard_map/ppermute | solution.py:265
  12.3 61.4 %copy-start = (bf16[1,2048,1024]{2,1,0:T(8,128)(2,1)S(1)}, bf16[1,2048,1024]{2,1,0:T(8,128)(2,1)}, u32[]{:S(2)}) copy-start(bf16[1,2048,1024]{2,1,0:T(8,128)(2,1)} %w_in_ref.5) | copy-start | bytes 12582916
  12.3 20.4 %collective-permute-start.3 = (bf16[32,4096]{1,0:T(8,128)(2,1)}, bf16[32,4096]{1,0:T(8,128)(2,1)S(1)}, u32[]{:S(2)}, u32[]{:S(2)}) collective-permute-start(bf16[32,4096]{1,0:T(8,128)(2,1)} %get-tuple-element.58), channel_id=1, source_target_pairs={{0,8},{8,16},{16,24},{24,0},{1,9},{9,17},{17,25},{25,1},{2,10},{10... | collective-permute-start | bytes 786440 | tf_op jit(solution)/shard_map/ppermute | solution.py:265
  13.0 35.9 %collective-permute-start.4 = (bf16[32,4096]{1,0:T(8,128)(2,1)}, bf16[32,4096]{1,0:T(8,128)(2,1)S(1)}, u32[]{:S(2)}, u32[]{:S(2)}) collective-permute-start(bf16[32,4096]{1,0:T(8,128)(2,1)} %get-tuple-element.59), channel_id=1, source_target_pairs={{0,16},{8,24},{16,0},{24,8},{1,17},{9,25},{17,1},{25,9},{2,18},{10... | collective-permute-start | bytes 786440 | tf_op jit(solution)/shard_map/ppermute | solution.py:265
  15.5 33.4 %collective-permute-start.5 = (bf16[32,4096]{1,0:T(8,128)(2,1)}, bf16[32,4096]{1,0:T(8,128)(2,1)S(1)}, u32[]{:S(2)}, u32[]{:S(2)}) collective-permute-start(bf16[32,4096]{1,0:T(8,128)(2,1)} %get-tuple-element.60), channel_id=1, source_target_pairs={{0,24},{8,0},{16,8},{24,16},{1,25},{9,1},{17,9},{25,17},{2,26},{10... | collective-permute-start | bytes 786440 | tf_op jit(solution)/shard_map/ppermute | solution.py:265
  18.0 1.0 copy-start.2
  18.9 0.9 copy-start.4
  19.9 0.7 copy-start.8
  20.5 0.7 copy-start.9
  21.2 0.7 copy-start.10
  49.9 1.4 %collective-permute-start.6 = (bf16[32,2048]{1,0:T(8,128)(2,1)S(1)}, bf16[32,2048]{1,0:T(8,128)(2,1)S(1)}, u32[]{:S(2)}, u32[]{:S(2)}) collective-permute-start(bf16[32,2048]{1,0:T(8,128)(2,1)S(1)} %get-tuple-element.64), channel_id=1, source_target_pairs={{0,1},{1,0},{2,3},{3,2},{4,5},{5,4},{6,7},{7,6},{8,9},{9,8},{10,11... | collective-permute-start | bytes 393224 | tf_op jit(solution)/shard_map/ppermute | solution.py:335
  51.3 4.3 %collective-permute-start.10 = (bf16[16,2048]{1,0:T(8,128)(2,1)S(1)}, bf16[16,2048]{1,0:T(8,128)(2,1)S(1)}, u32[]{:S(2)}, u32[]{:S(2)}) collective-permute-start(bf16[16,2048]{1,0:T(8,128)(2,1)S(1)} %get-tuple-element.68), channel_id=1, source_target_pairs={{0,2},{1,3},{2,0},{3,1},{4,6},{5,7},{6,4},{7,5},{8,10},{9,11},{10,... | collective-permute-start | bytes 196616 | tf_op jit(solution)/shard_map/ppermute | solution.py:335
  52.9 8.0 %collective-permute-start.7 = (bf16[16,2048]{1,0:T(8,128)(2,1)S(1)}, bf16[16,2048]{1,0:T(8,128)(2,1)S(1)}, u32[]{:S(2)}, u32[]{:S(2)}) collective-permute-start(bf16[16,2048]{1,0:T(8,128)(2,1)S(1)} %get-tuple-element.65), channel_id=1, source_target_pairs={{0,4},{1,5},{2,6},{3,7},{4,0},{5,1},{6,2},{7,3},{8,12},{9,13},{10,... | collective-permute-start | bytes 196616 | tf_op jit(solution)/shard_map/ppermute | solution.py:335
  54.4 6.5 %collective-permute-start.8 = (bf16[16,2048]{1,0:T(8,128)(2,1)S(1)}, bf16[16,2048]{1,0:T(8,128)(2,1)S(1)}, u32[]{:S(2)}, u32[]{:S(2)}) collective-permute-start(bf16[16,2048]{1,0:T(8,128)(2,1)S(1)} %get-tuple-element.66), channel_id=1, source_target_pairs={{0,6},{1,7},{2,4},{3,5},{4,2},{5,3},{6,0},{7,1},{8,14},{9,15},{10,... | collective-permute-start | bytes 196616 | tf_op jit(solution)/shard_map/ppermute | solution.py:335
  55.6 11.7 %collective-permute-start.14 = (bf16[32,2048]{1,0:T(8,128)(2,1)S(1)}, bf16[32,2048]{1,0:T(8,128)(2,1)S(1)}, u32[]{:S(2)}, u32[]{:S(2)}) collective-permute-start(bf16[32,2048]{1,0:T(8,128)(2,1)S(1)} %shard_map.144.refs_0_), channel_id=1, source_target_pairs={{0,16},{8,24},{16,0},{24,8},{1,17},{9,25},{17,1},{25,9},{2,18},{10... | collective-permute-start | bytes 393224 | tf_op jit(solution)/shard_map/ppermute | solution.py:335
  60.9 11.2 %collective-permute-start.12 = (bf16[32,2048]{1,0:T(8,128)(2,1)S(1)}, bf16[32,2048]{1,0:T(8,128)(2,1)S(1)}, u32[]{:S(2)}, u32[]{:S(2)}) collective-permute-start(bf16[32,2048]{1,0:T(8,128)(2,1)S(1)} %shard_map.143.refs_0_), channel_id=1, source_target_pairs={{0,16},{8,24},{16,0},{24,8},{1,17},{9,25},{17,1},{25,9},{2,18},{10... | collective-permute-start | bytes 393224 | tf_op jit(solution)/shard_map/ppermute | solution.py:335
  64.8 9.0 %collective-permute-start.11 = (bf16[32,2048]{1,0:T(8,128)(2,1)S(1)}, bf16[32,2048]{1,0:T(8,128)(2,1)S(1)}, u32[]{:S(2)}, u32[]{:S(2)}) collective-permute-start(bf16[32,2048]{1,0:T(8,128)(2,1)S(1)} %shard_map.144.refs_0_), channel_id=1, source_target_pairs={{0,8},{8,0},{16,24},{24,16},{1,9},{9,1},{17,25},{25,17},{2,10},{10... | collective-permute-start | bytes 393224 | tf_op jit(solution)/shard_map/ppermute | solution.py:335
  67.3 10.3 %collective-permute-start.9 = (bf16[32,2048]{1,0:T(8,128)(2,1)S(1)}, bf16[32,2048]{1,0:T(8,128)(2,1)S(1)}, u32[]{:S(2)}, u32[]{:S(2)}) collective-permute-start(bf16[32,2048]{1,0:T(8,128)(2,1)S(1)} %shard_map.143.refs_0_), channel_id=1, source_target_pairs={{0,8},{8,0},{16,24},{24,16},{1,9},{9,1},{17,25},{25,17},{2,10},{10... | collective-permute-start | bytes 393224 | tf_op jit(solution)/shard_map/ppermute | solution.py:335
  67.3 11.8 %collective-permute-start.15 = (bf16[32,2048]{1,0:T(8,128)(2,1)S(1)}, bf16[32,2048]{1,0:T(8,128)(2,1)S(1)}, u32[]{:S(2)}, u32[]{:S(2)}) collective-permute-start(bf16[32,2048]{1,0:T(8,128)(2,1)S(1)} %collective-permute-done.14.refs_3_), channel_id=1, source_target_pairs={{0,8},{8,0},{16,24},{24,16},{1,9},{9,1},{17,25},{25,17},{2,10},{10... | collective-permute-start | bytes 393224 | tf_op jit(solution)/shard_map/ppermute | solution.py:335
  72.1 7.7 %collective-permute-start.13 = (bf16[32,2048]{1,0:T(8,128)(2,1)S(1)}, bf16[32,2048]{1,0:T(8,128)(2,1)S(1)}, u32[]{:S(2)}, u32[]{:S(2)}) collective-permute-start(bf16[32,2048]{1,0:T(8,128)(2,1)S(1)} %collective-permute-done.12.refs_2_), channel_id=1, source_target_pairs={{0,8},{8,0},{16,24},{24,16},{1,9},{9,1},{17,25},{25,17},{2,10},{10... | collective-permute-start | bytes 393224 | tf_op jit(solution)/shard_map/ppermute | solution.py:335
  73.8 2.2 %copy-start.1 = (bf16[1,1024,2048]{2,1,0:T(8,128)(2,1)S(1)}, bf16[1,1024,2048]{2,1,0:T(8,128)(2,1)}, u32[]{:S(2)}) copy-start(bf16[1,1024,2048]{2,1,0:T(8,128)(2,1)} %w_out_ref.5) | copy-start | bytes 12582916
  79.8 23.2 %copy-start.3 = (f32[8,2048]{1,0:T(8,128)S(1)}, f32[8,2048]{1,0:T(8,128)}, u32[]{:S(2)}) copy-start(f32[8,2048]{1,0:T(8,128)} %bias_ref.9) | copy-start | bytes 196612
  81.2 5.7 %collective-permute-start.16 = (bf16[32,2048]{1,0:T(8,128)(2,1)S(1)}, bf16[32,2048]{1,0:T(8,128)(2,1)S(1)}, u32[]{:S(2)}, u32[]{:S(2)}) collective-permute-start(bf16[32,2048]{1,0:T(8,128)(2,1)S(1)} %get-tuple-element.73), channel_id=1, source_target_pairs={{0,8},{8,0},{16,24},{24,16},{1,9},{9,1},{17,25},{25,17},{2,10},{10... | collective-permute-start | bytes 393224 | tf_op jit(solution)/shard_map/ppermute | solution.py:335
  82.1 10.9 %collective-permute-start.19 = (bf16[32,2048]{1,0:T(8,128)(2,1)S(1)}, bf16[32,2048]{1,0:T(8,128)(2,1)S(1)}, u32[]{:S(2)}, u32[]{:S(2)}) collective-permute-start(bf16[32,2048]{1,0:T(8,128)(2,1)S(1)} %get-tuple-element.77), channel_id=1, source_target_pairs={{0,8},{8,0},{16,24},{24,16},{1,9},{9,1},{17,25},{25,17},{2,10},{10... | collective-permute-start | bytes 393224 | tf_op jit(solution)/shard_map/ppermute | solution.py:335
  87.0 10.0 %collective-permute-start.17 = (bf16[16,2048]{1,0:T(8,128)(2,1)S(1)}, bf16[16,2048]{1,0:T(8,128)(2,1)S(1)}, u32[]{:S(2)}, u32[]{:S(2)}) collective-permute-start(bf16[16,2048]{1,0:T(8,128)(2,1)S(1)} %get-tuple-element.75), channel_id=1, source_target_pairs={{0,8},{8,0},{16,24},{24,16},{1,9},{9,1},{17,25},{25,17},{2,10},{10... | collective-permute-start | bytes 196616 | tf_op jit(solution)/shard_map/ppermute | solution.py:335
  87.6 15.4 %collective-permute-start.24 = (bf16[32,2048]{1,0:T(8,128)(2,1)S(1)}, bf16[32,2048]{1,0:T(8,128)(2,1)S(1)}, u32[]{:S(2)}, u32[]{:S(2)}) collective-permute-start(bf16[32,2048]{1,0:T(8,128)(2,1)S(1)} %shard_map.148._), channel_id=1, source_target_pairs={{0,16},{8,24},{16,0},{24,8},{1,17},{9,25},{17,1},{25,9},{2,18},{10... | collective-permute-start | bytes 393224 | tf_op jit(solution)/shard_map/ppermute | solution.py:335
  93.1 11.5 %collective-permute-start.20 = (bf16[32,2048]{1,0:T(8,128)(2,1)S(1)}, bf16[32,2048]{1,0:T(8,128)(2,1)S(1)}, u32[]{:S(2)}, u32[]{:S(2)}) collective-permute-start(bf16[32,2048]{1,0:T(8,128)(2,1)S(1)} %shard_map.151), channel_id=1, source_target_pairs={{0,16},{8,24},{16,0},{24,8},{1,17},{9,25},{17,1},{25,9},{2,18},{10... | collective-permute-start | bytes 393224 | tf_op jit(solution)/shard_map/ppermute | solution.py:335
  94.5 5.4 %collective-permute-start.18 = (bf16[16,2048]{1,0:T(8,128)(2,1)S(1)}, bf16[16,2048]{1,0:T(8,128)(2,1)S(1)}, u32[]{:S(2)}, u32[]{:S(2)}) collective-permute-start(bf16[16,2048]{1,0:T(8,128)(2,1)S(1)} %get-tuple-element.76), channel_id=1, source_target_pairs={{0,8},{8,0},{16,24},{24,16},{1,9},{9,1},{17,25},{25,17},{2,10},{10... | collective-permute-start | bytes 196616 | tf_op jit(solution)/shard_map/ppermute | solution.py:335
  97.0 5.3 %collective-permute-start.22 = (bf16[16,2048]{1,0:T(8,128)(2,1)S(1)}, bf16[16,2048]{1,0:T(8,128)(2,1)S(1)}, u32[]{:S(2)}, u32[]{:S(2)}) collective-permute-start(bf16[16,2048]{1,0:T(8,128)(2,1)S(1)} %get-tuple-element.81), channel_id=1, source_target_pairs={{0,8},{8,0},{16,24},{24,16},{1,9},{9,1},{17,25},{25,17},{2,10},{10... | collective-permute-start | bytes 196616 | tf_op jit(solution)/shard_map/ppermute | solution.py:335
  97.0 6.0 %collective-permute-start.23 = (bf16[16,2048]{1,0:T(8,128)(2,1)S(1)}, bf16[16,2048]{1,0:T(8,128)(2,1)S(1)}, u32[]{:S(2)}, u32[]{:S(2)}) collective-permute-start(bf16[16,2048]{1,0:T(8,128)(2,1)S(1)} %get-tuple-element.82), channel_id=1, source_target_pairs={{0,8},{8,0},{16,24},{24,16},{1,9},{9,1},{17,25},{25,17},{2,10},{10... | collective-permute-start | bytes 196616 | tf_op jit(solution)/shard_map/ppermute | solution.py:335
  103.1 4.3 %collective-permute-start.25 = (bf16[16,2048]{1,0:T(8,128)(2,1)S(1)}, bf16[16,2048]{1,0:T(8,128)(2,1)S(1)}, u32[]{:S(2)}, u32[]{:S(2)}) collective-permute-start(bf16[16,2048]{1,0:T(8,128)(2,1)S(1)} %get-tuple-element.83), channel_id=1, source_target_pairs={{0,4},{1,5},{2,6},{3,7},{4,0},{5,1},{6,2},{7,3},{8,12},{9,13},{10,... | collective-permute-start | bytes 196616 | tf_op jit(solution)/shard_map/ppermute | solution.py:335
  103.4 5.2 %collective-permute-start.26 = (bf16[16,2048]{1,0:T(8,128)(2,1)S(1)}, bf16[16,2048]{1,0:T(8,128)(2,1)S(1)}, u32[]{:S(2)}, u32[]{:S(2)}) collective-permute-start(bf16[16,2048]{1,0:T(8,128)(2,1)S(1)} %get-tuple-element.84), channel_id=1, source_target_pairs={{0,6},{1,7},{2,4},{3,5},{4,2},{5,3},{6,0},{7,1},{8,14},{9,15},{10,... | collective-permute-start | bytes 196616 | tf_op jit(solution)/shard_map/ppermute | solution.py:335
  104.7 4.9 %collective-permute-start.21 = (bf16[16,2048]{1,0:T(8,128)(2,1)S(1)}, bf16[16,2048]{1,0:T(8,128)(2,1)S(1)}, u32[]{:S(2)}, u32[]{:S(2)}) collective-permute-start(bf16[16,2048]{1,0:T(8,128)(2,1)S(1)} %get-tuple-element.80), channel_id=1, source_target_pairs={{0,2},{1,3},{2,0},{3,1},{4,6},{5,7},{6,4},{7,5},{8,10},{9,11},{10,... | collective-permute-start | bytes 196616 | tf_op jit(solution)/shard_map/ppermute | solution.py:335
  109.6 1.4 %collective-permute-start.27 = (bf16[32,2048]{1,0:T(8,128)(2,1)S(1)}, bf16[32,2048]{1,0:T(8,128)(2,1)S(1)}, u32[]{:S(2)}, u32[]{:S(2)}) collective-permute-start(bf16[32,2048]{1,0:T(8,128)(2,1)S(1)} %get-tuple-element.86), channel_id=1, source_target_pairs={{0,1},{1,0},{2,3},{3,2},{4,5},{5,4},{6,7},{7,6},{8,9},{9,8},{10,11... | collective-permute-start | bytes 393224 | tf_op jit(solution)/shard_map/ppermute | solution.py:335

commit v14 on v13

--- a/solution.py
+++ b/solution.py
@@ -11,6 +11,7 @@
 HEAD_DIM = 128
 ROUNDS = 4
 LANES = 128
+OUT_PARTS = 4
 
 epsilon = 1e-05
 mask_fill = -1e30
@@ -180,13 +181,6 @@
     out_ref[...] = (first_ref[...].astype(F32) + second_ref[...].astype(F32)).astype(BF16)
 
 
-def hand_kernel(first_ref, second_ref, _, *out_refs):
-    rows = out_refs[0].shape[0]
-    for n, out_ref in enumerate(out_refs):
-        source_ref = (first_ref, second_ref)[n // 2]
-        out_ref[...] = source_ref[n % 2 * rows : (n % 2 + 1) * rows]
-
-
 def result_kernel(lower, bias_ref, near_ref, *refs):
     count = refs[0].shape[0]
     outs = next(n for n in range(1, len(refs)) if sum(r.shape[0] for r in refs[-n:]) == count)
@@ -220,11 +214,19 @@
     other_ref[...] = jnp.concatenate([piece[cap:] for piece in pieces], axis=0).astype(BF16)
 
 
-def combine_kernel(hidden_ref, give_ref, *refs):
-    *result_refs, out_ref = refs
+def combine_kernel(count, hidden_ref, give_ref, *refs):
+    result_refs, out_ref, buf, sem = refs[:count], refs[count], refs[count + 1], refs[count + 2]
     result = joined(list(result_refs) * 2)
-    added = jnp.dot(give_ref[...], result, preferred_element_type=F32)
-    out_ref[...] = (hidden_ref[...] + added).astype(BF16)
+    rows = buf.shape[0] // OUT_PARTS
+    copies = []
+    for n in range(OUT_PARTS):
+        part = slice(n * rows, (n + 1) * rows)
+        added = jnp.dot(give_ref[part, :], result, preferred_element_type=F32)
+        buf[part, :] = (hidden_ref[part, :] + added).astype(BF16)
+        copies.append(pltpu.make_async_copy(buf.at[part, :], out_ref.at[part, :], sem.at[n]))
+        copies[n].start()
+    for copy in copies:
+        copy.wait()
 
 
 def per_device(
@@ -350,23 +352,18 @@
         last = last[0]
         *corner_share, far_first, far_second = apply([swap(x, 1) for x in far] + far, after=[last])
         far_shares = [far_first, far_second]
-        first_pair = call(add_kernel, bf16(half), swap(corner_share[0], 1), far_shares[0])
-        second_pair = call(add_kernel, bf16(half), swap(corner_share[1], 1), far_shares[1])
-        near_parts = call(hand_kernel, (bf16(half // 2),) * 4, *near_shares, first_pair)
-        near_parts = [swap(x, 1) for x in near_parts]
-        near_shares = [call(join_kernel, bf16(half), *near_parts[n : n + 2]) for n in (0, 2)]
-        pairs = [first_pair, second_pair]
-        backs = [
-            call(
+        near_shares = [swap(x, 1) for x in near_shares]
+        backs = [None, None]
+        for n in (1, 0):
+            pair = swap(call(add_kernel, bf16(half), swap(corner_share[n], 1), far_shares[n]), 2)
+            backs[n] = call(
                 functools.partial(result_kernel, 0),
                 (bf16(2 * cap),) * 2,
                 b_out,
                 near_shares[n],
                 own_share[n],
-                swap(pairs[n], 2),
+                pair,
             )
-            for n in range(2)
-        ]
         pieces = [x for n in (1, 0) for x in backs[n]]
         pieces = [swap(x, 2 * n, "expert") if n else x for n, x in enumerate(pieces)]
         mine, other = call(functools.partial(part_kernel, cap), (bf16(half),) * 2, *pieces)
@@ -381,9 +378,14 @@
             functools.partial(result_kernel, 0), (bf16(slots),), b_out, *[shares[n] for n in range(dp)]
         )
         returned = [over_experts(results)]
-    return call(
-        combine_kernel, jax.ShapeDtypeStruct((tok, width), BF16), hidden_state, give, *returned
-    )
+    return pl.pallas_call(
+        functools.partial(combine_kernel, len(returned)),
+        out_shape=jax.ShapeDtypeStruct((tok, width), BF16),
+        in_specs=[pl.BlockSpec(memory_space=pltpu.VMEM)] * (2 + len(returned)),
+        out_specs=pl.BlockSpec(memory_space=pl.ANY),
+        scratch_shapes=[pltpu.VMEM((tok, width), BF16), pltpu.SemaphoreType.DMA((OUT_PARTS,))],
+        compiler_params=pltpu.CompilerParams(vmem_limit_bytes=VMEM_BYTES),
+    )(hidden_state, give, *returned)
 
 
 def solution(mesh):

time: 112 us -> 111 us (level)
  starting transfers between devices: 47.6 us -> 40.1 us
  waiting for transfers between devices: 44.2 us -> 50.2 us
    ppermute x22 -> x20, starting transfers between devices: 37.1 us -> 29.6 us  [swap(): lax.ppermute(x, axis, [(i, i ^ distance) for i in range(lax.axis_size(axi...]
    ppermute x22 -> x20, waiting for transfers between devices: 16.9 us -> 22.9 us  [swap(): lax.ppermute(x, axis, [(i, i ^ distance) for i in range(lax.axis_size(axi...]
    pallas_call x21 -> x17, Pallas kernels: 14 us -> 12.9 us  [call(): pl.pallas_call(body, out_shape=out_shape, compiler_params=pltpu.CompilerP...]
  transfers between devices with their start and end apart: 28 -> 26, of which waited for: 17 -> 15; matrix products, arithmetic and copies ran while one was open for 0% -> 0% of each run, Pallas kernels for 7% -> 7%
where the time goes in v14:
time: 111 us
  waiting for transfers between devices  50.2 us (45%)
  starting transfers between devices  40.1 us (36%)
  Pallas kernels  14 us (13%)
  local copies, waits for them, and re-layouts  6.11 us (6%)
    ppermute x20, starting transfers between devices, swap(): lax.ppermute(x, axis, [(i, i ^ distance) for i in range(lax.axis_size(axi...  29.6 us
    ppermute x6, waiting for transfers between devices, spread(): lax.ppermute(part, 'dp', [(i, (i + n) % dp) for i in range(dp)])  27.3 us
    ppermute x20, waiting for transfers between devices, swap(): lax.ppermute(x, axis, [(i, i ^ distance) for i in range(lax.axis_size(axi...  22.9 us
    pallas_call x17, Pallas kernels, call(): pl.pallas_call(body, out_shape=out_shape, compiler_params=pltpu.CompilerP...  12.9 us
    ppermute x6, starting transfers between devices, spread(): lax.ppermute(part, 'dp', [(i, (i + n) % dp) for i in range(dp)])  10.5 us
    unnamed x22, local copies, waits for them, and re-layouts  6.11 us
  transfers between devices with their start and end apart: 26, of which 15 were waited for; matrix products, arithmetic and copies ran while one was open for 0% of the time, Pallas kernels for 7%

profile of v14, /device:TPU:0, one launch (start us, length us, event | category | flops | bytes accessed | tf_op | source)
XLA Modules:
  0.0 110.6 jit_solution(10554469255868617537)
XLA Ops:
  0.0 2.8 %shard_map.136 = (bf16[128,128]{1,0:T(8,128)(2,1)}, bf16[32,4224]{1,0:T(8,128)(2,1)}, bf16[32,4224]{1,0:T(8,128)(2,1)}, bf16[32,4224]{1,0:T(8,128)(2,1)}, bf16[32,4224]{1,0:T(8,128)(2,1)}) custom-call(s32[1,128]{1,0:T(1,128)} %bitcast.9, bf16[128,2048]{1,0:T(8,128)(2,1)} %refs_0_.2, bf16[128,2048]{1,0:T(8,128)(2,1)} %refs_1_.2), custom_call_target="tpu_custom_call" | custom-call | bytes 2163200 | tf_op jit(solution)/shard_map/pallas_call | solution.py:42
  2.8 3.0 %collective-permute-start = (bf16[32,4224]{1,0:T(8,128)(2,1)}, bf16[32,4224]{1,0:T(8,128)(2,1)S(1)}, u32[]{:S(2)}, u32[]{:S(2)}) collective-permute-start(bf16[32,4224]{1,0:T(8,128)(2,1)} %get-tuple-element.47), channel_id=1, source_target_pairs={{0,8},{8,16},{16,24},{24,0},{1,9},{9,17},{17,25},{25,1},{2,10},{10... | collective-permute-start | bytes 811016 | tf_op jit(solution)/shard_map/ppermute | solution.py:267
  5.8 2.6 %collective-permute-start.1 = (bf16[32,4224]{1,0:T(8,128)(2,1)}, bf16[32,4224]{1,0:T(8,128)(2,1)S(1)}, u32[]{:S(2)}, u32[]{:S(2)}) collective-permute-start(bf16[32,4224]{1,0:T(8,128)(2,1)} %get-tuple-element.48), channel_id=1, source_target_pairs={{0,16},{8,24},{16,0},{24,8},{1,17},{9,25},{17,1},{25,9},{2,18},{10... | collective-permute-start | bytes 811016 | tf_op jit(solution)/shard_map/ppermute | solution.py:267
  8.4 1.3 %collective-permute-start.2 = (bf16[32,4224]{1,0:T(8,128)(2,1)}, bf16[32,4224]{1,0:T(8,128)(2,1)S(1)}, u32[]{:S(2)}, u32[]{:S(2)}) collective-permute-start(bf16[32,4224]{1,0:T(8,128)(2,1)} %get-tuple-element.49), channel_id=1, source_target_pairs={{0,24},{8,0},{16,8},{24,16},{1,25},{9,1},{17,9},{25,17},{2,26},{10... | collective-permute-start | bytes 811016 | tf_op jit(solution)/shard_map/ppermute | solution.py:267
  9.7 2.6 %shard_map.137 = (bf16[128,128]{1,0:T(8,128)(2,1)}, bf16[32,4096]{1,0:T(8,128)(2,1)}, bf16[32,4096]{1,0:T(8,128)(2,1)}, bf16[32,4096]{1,0:T(8,128)(2,1)}, bf16[32,4096]{1,0:T(8,128)(2,1)}) custom-call(bf16[128,128]{1,0:T(8,128)(2,1)} %get-tuple-element.43.pos_ref, bf16[128,2048]{1,0:T(8,128)(2,1)} %refs_0_.3, bf16[128,2048]{1,0:T(8,128)(2,1)} %refs_1_.3), custom_call_target="tpu_custom_call" | custom-call | bytes 2162688 | tf_op jit(solution)/shard_map/pallas_call | solution.py:42
  12.3 0.7 collective-permute-start.3
  13.4 2.1 %collective-permute-done.refs_1_ = bf16[32,4224]{1,0:T(8,128)(2,1)S(1)} collective-permute-done((bf16[32,4224]{1,0:T(8,128)(2,1)}, bf16[32,4224]{1,0:T(8,128)(2,1)S(1)}, u32[]{:S(2)}, u32[]{:S(2)}) %collective-permute-start) | collective-permute-done | bytes 270368 | tf_op jit(solution)/shard_map/ppermute | solution.py:267
  15.5 2.5 %collective-permute-start.5 = (bf16[32,4096]{1,0:T(8,128)(2,1)}, bf16[32,4096]{1,0:T(8,128)(2,1)S(1)}, u32[]{:S(2)}, u32[]{:S(2)}) collective-permute-start(bf16[32,4096]{1,0:T(8,128)(2,1)} %get-tuple-element.56), channel_id=1, source_target_pairs={{0,24},{8,0},{16,8},{24,16},{1,25},{9,1},{17,9},{25,17},{2,26},{10... | collective-permute-start | bytes 786440 | tf_op jit(solution)/shard_map/ppermute | solution.py:267
  18.0 1.0 copy-done.2
  18.9 0.9 copy-done.4
  19.9 0.7 copy-done.8
  20.6 0.7 copy-done.9
  21.2 0.7 copy-done.10
  22.1 5.0 %collective-permute-done.1.refs_2_ = bf16[32,4224]{1,0:T(8,128)(2,1)S(1)} collective-permute-done((bf16[32,4224]{1,0:T(8,128)(2,1)}, bf16[32,4224]{1,0:T(8,128)(2,1)S(1)}, u32[]{:S(2)}, u32[]{:S(2)}) %collective-permute-start.1) | collective-permute-done | bytes 270368 | tf_op jit(solution)/shard_map/ppermute | solution.py:267
  27.3 1.5 %shard_map.140.probs_ref = bf16[16,128,128]{2,1,0:T(8,128)(2,1)S(1)} custom-call(bf16[128,128]{1,0:T(8,128)(2,1)S(1)} %get-tuple-element.50.place_ref, f32[128,128]{1,0:T(8,128)S(1)} %get-tuple-element.52.outside_ref, bf16[32,4224]{1,0:T(8,128)(2,1)S(1)} %get-tuple-element.46.refs_0_, bf16[32,4224]{1,0:T(8,128)(2,1)S(1)} %collective-permute-done.refs_1_, ...), custom_call_target="tpu_custom_call" | custom-call | bytes 1703936 | tf_op jit(solution)/shard_map/pallas_call | solution.py:42
  28.8 4.0 %collective-permute-done.3.refs_1_ = bf16[32,4096]{1,0:T(8,128)(2,1)S(1)} collective-permute-done((bf16[32,4096]{1,0:T(8,128)(2,1)}, bf16[32,4096]{1,0:T(8,128)(2,1)S(1)}, u32[]{:S(2)}, u32[]{:S(2)}) %collective-permute-start.3) | collective-permute-done | bytes 262176 | tf_op jit(solution)/shard_map/ppermute | solution.py:267
  32.7 16.2 %collective-permute-done.4.refs_2_ = bf16[32,4096]{1,0:T(8,128)(2,1)S(1)} collective-permute-done((bf16[32,4096]{1,0:T(8,128)(2,1)}, bf16[32,4096]{1,0:T(8,128)(2,1)S(1)}, u32[]{:S(2)}, u32[]{:S(2)}) %collective-permute-start.4) | collective-permute-done | bytes 262176 | tf_op jit(solution)/shard_map/ppermute | solution.py:267
  48.9 0.9 shard_map.141
  50.0 1.3 %collective-permute-done.6.other_ref = bf16[32,2048]{1,0:T(8,128)(2,1)S(1)} collective-permute-done((bf16[32,2048]{1,0:T(8,128)(2,1)S(1)}, bf16[32,2048]{1,0:T(8,128)(2,1)S(1)}, u32[]{:S(2)}, u32[]{:S(2)}) %collective-permute-start.6) | collective-permute-done | bytes 131104 | tf_op jit(solution)/shard_map/ppermute | solution.py:337
  51.3 1.6 %collective-permute-start.10 = (bf16[16,2048]{1,0:T(8,128)(2,1)S(1)}, bf16[16,2048]{1,0:T(8,128)(2,1)S(1)}, u32[]{:S(2)}, u32[]{:S(2)}) collective-permute-start(bf16[16,2048]{1,0:T(8,128)(2,1)S(1)} %get-tuple-element.65), channel_id=1, source_target_pairs={{0,4},{1,5},{2,6},{3,7},{4,0},{5,1},{6,2},{7,3},{8,12},{9,13},{10,... | collective-permute-start | bytes 196616 | tf_op jit(solution)/shard_map/ppermute | solution.py:337
  52.9 1.4 %collective-permute-start.11 = (bf16[16,2048]{1,0:T(8,128)(2,1)S(1)}, bf16[16,2048]{1,0:T(8,128)(2,1)S(1)}, u32[]{:S(2)}, u32[]{:S(2)}) collective-permute-start(bf16[16,2048]{1,0:T(8,128)(2,1)S(1)} %get-tuple-element.66), channel_id=1, source_target_pairs={{0,6},{1,7},{2,4},{3,5},{4,2},{5,3},{6,0},{7,1},{8,14},{9,15},{10,... | collective-permute-start | bytes 196616 | tf_op jit(solution)/shard_map/ppermute | solution.py:337
  54.3 0.5 collective-permute-start.7
  54.9 0.8 collective-permute-done.10.refs_0_
  55.7 3.0 %collective-permute-done.11.refs_1_ = bf16[16,2048]{1,0:T(8,128)(2,1)S(1)} collective-permute-done((bf16[16,2048]{1,0:T(8,128)(2,1)S(1)}, bf16[16,2048]{1,0:T(8,128)(2,1)S(1)}, u32[]{:S(2)}, u32[]{:S(2)}) %collective-permute-start.11) | collective-permute-done | bytes 65568 | tf_op jit(solution)/shard_map/ppermute | solution.py:337
  58.7 5.2 %collective-permute-start.12 = (bf16[32,2048]{1,0:T(8,128)(2,1)S(1)}, bf16[32,2048]{1,0:T(8,128)(2,1)S(1)}, u32[]{:S(2)}, u32[]{:S(2)}) collective-permute-start(bf16[32,2048]{1,0:T(8,128)(2,1)S(1)} %shard_map.145.refs_0_), channel_id=1, source_target_pairs={{0,16},{8,24},{16,0},{24,8},{1,17},{9,25},{17,1},{25,9},{2,18},{10... | collective-permute-start | bytes 393224 | tf_op jit(solution)/shard_map/ppermute | solution.py:337
  64.0 3.8 %collective-permute-start.8 = (bf16[32,2048]{1,0:T(8,128)(2,1)S(1)}, bf16[32,2048]{1,0:T(8,128)(2,1)S(1)}, u32[]{:S(2)}, u32[]{:S(2)}) collective-permute-start(bf16[32,2048]{1,0:T(8,128)(2,1)S(1)} %shard_map.143.refs_0_), channel_id=1, source_target_pairs={{0,8},{8,0},{16,24},{24,16},{1,9},{9,1},{17,25},{25,17},{2,10},{10... | collective-permute-start | bytes 393224 | tf_op jit(solution)/shard_map/ppermute | solution.py:337
  67.9 5.2 %collective-permute-done.12.refs_2_ = bf16[32,2048]{1,0:T(8,128)(2,1)S(1)} collective-permute-done((bf16[32,2048]{1,0:T(8,128)(2,1)S(1)}, bf16[32,2048]{1,0:T(8,128)(2,1)S(1)}, u32[]{:S(2)}, u32[]{:S(2)}) %collective-permute-start.12) | collective-permute-done | bytes 131104 | tf_op jit(solution)/shard_map/ppermute | solution.py:337
  73.1 2.2 %collective-permute-done.14.refs_3_ = bf16[32,2048]{1,0:T(8,128)(2,1)S(1)} collective-permute-done((bf16[32,2048]{1,0:T(8,128)(2,1)S(1)}, bf16[32,2048]{1,0:T(8,128)(2,1)S(1)}, u32[]{:S(2)}, u32[]{:S(2)}) %collective-permute-start.14) | collective-permute-done | bytes 131104 | tf_op jit(solution)/shard_map/ppermute | solution.py:337
  75.3 2.2 %copy-done.1 = bf16[1,1024,2048]{2,1,0:T(8,128)(2,1)S(1)} copy-done((bf16[1,1024,2048]{2,1,0:T(8,128)(2,1)S(1)}, bf16[1,1024,2048]{2,1,0:T(8,128)(2,1)}, u32[]{:S(2)}) %copy-start.1) | copy-done | bytes 4194328
  77.5 1.6 %shard_map.144 = (bf16[32,2048]{1,0:T(8,128)(2,1)S(1)}, bf16[32,2048]{1,0:T(8,128)(2,1)S(1)}) custom-call(f32[1,1024]{1,0:T(1,128)S(1)} %copy-done.5, bf16[1,2048,1024]{2,1,0:T(8,128)(2,1)S(1)} %copy-done, bf16[1,1024,2048]{2,1,0:T(8,128)(2,1)S(1)} %copy-done.1, bf16[32,2048]{1,0:T(8,128)(2,1)S(1)} %shard_map.143.refs_0_, ...), custom_call_target="tpu_custom_call" | custom-call | flops 536870912 | bytes 8916992 | tf_op jit(solution)/shard_map/pallas_call | solution.py:42
  79.1 1.6 %shard_map.146 = (bf16[32,2048]{1,0:T(8,128)(2,1)S(1)}, bf16[32,2048]{1,0:T(8,128)(2,1)S(1)}) custom-call(f32[1,1024]{1,0:T(1,128)S(1)} %copy-done.5, bf16[1,2048,1024]{2,1,0:T(8,128)(2,1)S(1)} %copy-done, bf16[1,1024,2048]{2,1,0:T(8,128)(2,1)S(1)} %copy-done.1, bf16[32,2048]{1,0:T(8,128)(2,1)S(1)} %shard_map.145.refs_0_, ...), custom_call_target="tpu_custom_call" | custom-call | flops 536870912 | bytes 9048064 | tf_op jit(solution)/shard_map/pallas_call | solution.py:42
  80.7 0.4 collective-permute-done.15.refs_1_
  81.1 1.3 %shard_map.147 = (bf16[32,2048]{1,0:T(8,128)(2,1)S(1)}, bf16[32,2048]{1,0:T(8,128)(2,1)S(1)}, bf16[32,2048]{1,0:T(8,128)(2,1)S(1)}, bf16[32,2048]{1,0:T(8,128)(2,1)S(1)}) custom-call(f32[1,1024]{1,0:T(1,128)S(1)} %copy-done.5, bf16[1,2048,1024]{2,1,0:T(8,128)(2,1)S(1)} %copy-done, bf16[1,1024,2048]{2,1,0:T(8,128)(2,1)S(1)} %copy-done.1, ...), custom_call_target="tpu_custom_call" | custom-call | flops 1073741824 | bytes 9572352 | tf_op jit(solution)/shard_map/pallas_call | solution.py:42
  82.5 1.7 %collective-permute-start.21 = (bf16[32,2048]{1,0:T(8,128)(2,1)S(1)}, bf16[32,2048]{1,0:T(8,128)(2,1)S(1)}, u32[]{:S(2)}, u32[]{:S(2)}) collective-permute-start(bf16[32,2048]{1,0:T(8,128)(2,1)S(1)} %get-tuple-element.73), channel_id=1, source_target_pairs={{0,8},{8,0},{16,24},{24,16},{1,9},{9,1},{17,25},{25,17},{2,10},{10... | collective-permute-start | bytes 393224 | tf_op jit(solution)/shard_map/ppermute | solution.py:337
  84.1 0.4 collective-permute-start.17
  84.5 1.6 %collective-permute-start.20 = (bf16[32,2048]{1,0:T(8,128)(2,1)S(1)}, bf16[32,2048]{1,0:T(8,128)(2,1)S(1)}, u32[]{:S(2)}, u32[]{:S(2)}) collective-permute-start(bf16[32,2048]{1,0:T(8,128)(2,1)S(1)} %get-tuple-element.72), channel_id=1, source_target_pairs={{0,8},{8,0},{16,24},{24,16},{1,9},{9,1},{17,25},{25,17},{2,10},{10... | collective-permute-start | bytes 393224 | tf_op jit(solution)/shard_map/ppermute | solution.py:337
  86.2 2.8 %collective-permute-done.21.first_ref = bf16[32,2048]{1,0:T(8,128)(2,1)S(1)} collective-permute-done((bf16[32,2048]{1,0:T(8,128)(2,1)S(1)}, bf16[32,2048]{1,0:T(8,128)(2,1)S(1)}, u32[]{:S(2)}, u32[]{:S(2)}) %collective-permute-start.21) | collective-permute-done | bytes 131104 | tf_op jit(solution)/shard_map/ppermute | solution.py:337
  89.0 3.8 %collective-permute-start.22 = (bf16[32,2048]{1,0:T(8,128)(2,1)S(1)}, bf16[32,2048]{1,0:T(8,128)(2,1)S(1)}, u32[]{:S(2)}, u32[]{:S(2)}) collective-permute-start(bf16[32,2048]{1,0:T(8,128)(2,1)S(1)} %shard_map.150), channel_id=1, source_target_pairs={{0,16},{8,24},{16,0},{24,8},{1,17},{9,25},{17,1},{25,9},{2,18},{10... | collective-permute-start | bytes 393224 | tf_op jit(solution)/shard_map/ppermute | solution.py:337
  92.8 3.0 %collective-permute-start.9 = (bf16[32,2048]{1,0:T(8,128)(2,1)S(1)}, bf16[32,2048]{1,0:T(8,128)(2,1)S(1)}, u32[]{:S(2)}, u32[]{:S(2)}) collective-permute-start(bf16[32,2048]{1,0:T(8,128)(2,1)S(1)} %get-tuple-element.63), channel_id=1, source_target_pairs={{0,8},{8,0},{16,24},{24,16},{1,9},{9,1},{17,25},{25,17},{2,10},{10... | collective-permute-start | bytes 393224 | tf_op jit(solution)/shard_map/ppermute | solution.py:337
  95.8 1.3 %collective-permute-start.18 = (bf16[32,2048]{1,0:T(8,128)(2,1)S(1)}, bf16[32,2048]{1,0:T(8,128)(2,1)S(1)}, u32[]{:S(2)}, u32[]{:S(2)}) collective-permute-start(bf16[32,2048]{1,0:T(8,128)(2,1)S(1)} %shard_map.148), channel_id=1, source_target_pairs={{0,16},{8,24},{16,0},{24,8},{1,17},{9,25},{17,1},{25,9},{2,18},{10... | collective-permute-start | bytes 393224 | tf_op jit(solution)/shard_map/ppermute | solution.py:337
  97.1 0.8 collective-permute-done.20.near_ref
  98.0 0.8 collective-permute-start.23
  98.8 2.4 %collective-permute-start.24 = (bf16[16,2048]{1,0:T(8,128)(2,1)S(1)}, bf16[16,2048]{1,0:T(8,128)(2,1)S(1)}, u32[]{:S(2)}, u32[]{:S(2)}) collective-permute-start(bf16[16,2048]{1,0:T(8,128)(2,1)S(1)} %get-tuple-element.76), channel_id=1, source_target_pairs={{0,6},{1,7},{2,4},{3,5},{4,2},{5,3},{6,0},{7,1},{8,14},{9,15},{10,... | collective-permute-start | bytes 196616 | tf_op jit(solution)/shard_map/ppermute | solution.py:337
  101.2 2.4 %collective-permute-done.18.refs_1_ = bf16[32,2048]{1,0:T(8,128)(2,1)S(1)} collective-permute-done((bf16[32,2048]{1,0:T(8,128)(2,1)S(1)}, bf16[32,2048]{1,0:T(8,128)(2,1)S(1)}, u32[]{:S(2)}, u32[]{:S(2)}) %collective-permute-start.18) | collective-permute-done | bytes 131104 | tf_op jit(solution)/shard_map/ppermute | solution.py:337
  103.7 1.7 %collective-permute-start.19 = (bf16[16,2048]{1,0:T(8,128)(2,1)S(1)}, bf16[16,2048]{1,0:T(8,128)(2,1)S(1)}, u32[]{:S(2)}, u32[]{:S(2)}) collective-permute-start(bf16[16,2048]{1,0:T(8,128)(2,1)S(1)} %get-tuple-element.71), channel_id=1, source_target_pairs={{0,2},{1,3},{2,0},{3,1},{4,6},{5,7},{6,4},{7,5},{8,10},{9,11},{10,... | collective-permute-start | bytes 196616 | tf_op jit(solution)/shard_map/ppermute | solution.py:337
  105.4 2.6 %collective-permute-done.19.refs_1_ = bf16[16,2048]{1,0:T(8,128)(2,1)S(1)} collective-permute-done((bf16[16,2048]{1,0:T(8,128)(2,1)S(1)}, bf16[16,2048]{1,0:T(8,128)(2,1)S(1)}, u32[]{:S(2)}, u32[]{:S(2)}) %collective-permute-start.19) | collective-permute-done | bytes 65568 | tf_op jit(solution)/shard_map/ppermute | solution.py:337
  108.1 1.3 %collective-permute-done.25.refs_1_ = bf16[32,2048]{1,0:T(8,128)(2,1)S(1)} collective-permute-done((bf16[32,2048]{1,0:T(8,128)(2,1)S(1)}, bf16[32,2048]{1,0:T(8,128)(2,1)S(1)}, u32[]{:S(2)}, u32[]{:S(2)}) %collective-permute-start.25) | collective-permute-done | bytes 131104 | tf_op jit(solution)/shard_map/ppermute | solution.py:337
  109.5 1.1 shard_map.153
  (44 shorter events, 1.3 us)
Async XLA Ops:
  0.0 48.9 %copy-start.7 = (f32[2048]{0:T(1024)S(1)}, f32[2048]{0:T(1024)}, u32[]{:S(2)}) copy-start(f32[2048]{0:T(1024)} %param.23) | copy-start | bytes 24580
  0.0 48.9 %copy-start.6 = (f32[2048]{0:T(1024)S(1)}, f32[2048]{0:T(1024)}, u32[]{:S(2)}) copy-start(f32[2048]{0:T(1024)} %param.22) | copy-start | bytes 24580
  0.0 75.3 %copy-start.5 = (f32[1,1024]{1,0:T(1,128)S(1)}, f32[1,1024]{1,0:T(1,128)}, u32[]{:S(2)}) copy-start(f32[1,1024]{1,0:T(1,128)} %bias_ref.7) | copy-start | bytes 12292
  2.8 12.7 %collective-permute-start = (bf16[32,4224]{1,0:T(8,128)(2,1)}, bf16[32,4224]{1,0:T(8,128)(2,1)S(1)}, u32[]{:S(2)}, u32[]{:S(2)}) collective-permute-start(bf16[32,4224]{1,0:T(8,128)(2,1)} %get-tuple-element.47), channel_id=1, source_target_pairs={{0,8},{8,16},{16,24},{24,0},{1,9},{9,17},{17,25},{25,1},{2,10},{10... | collective-permute-start | bytes 811016 | tf_op jit(solution)/shard_map/ppermute | solution.py:267
  5.8 21.3 %collective-permute-start.1 = (bf16[32,4224]{1,0:T(8,128)(2,1)}, bf16[32,4224]{1,0:T(8,128)(2,1)S(1)}, u32[]{:S(2)}, u32[]{:S(2)}) collective-permute-start(bf16[32,4224]{1,0:T(8,128)(2,1)} %get-tuple-element.48), channel_id=1, source_target_pairs={{0,16},{8,24},{16,0},{24,8},{1,17},{9,25},{17,1},{25,9},{2,18},{10... | collective-permute-start | bytes 811016 | tf_op jit(solution)/shard_map/ppermute | solution.py:267
  8.4 18.7 %collective-permute-start.2 = (bf16[32,4224]{1,0:T(8,128)(2,1)}, bf16[32,4224]{1,0:T(8,128)(2,1)S(1)}, u32[]{:S(2)}, u32[]{:S(2)}) collective-permute-start(bf16[32,4224]{1,0:T(8,128)(2,1)} %get-tuple-element.49), channel_id=1, source_target_pairs={{0,24},{8,0},{16,8},{24,16},{1,25},{9,1},{17,9},{25,17},{2,26},{10... | collective-permute-start | bytes 811016 | tf_op jit(solution)/shard_map/ppermute | solution.py:267
  12.3 62.9 %copy-start = (bf16[1,2048,1024]{2,1,0:T(8,128)(2,1)S(1)}, bf16[1,2048,1024]{2,1,0:T(8,128)(2,1)}, u32[]{:S(2)}) copy-start(bf16[1,2048,1024]{2,1,0:T(8,128)(2,1)} %w_in_ref.5) | copy-start | bytes 12582916
  12.3 20.4 %collective-permute-start.3 = (bf16[32,4096]{1,0:T(8,128)(2,1)}, bf16[32,4096]{1,0:T(8,128)(2,1)S(1)}, u32[]{:S(2)}, u32[]{:S(2)}) collective-permute-start(bf16[32,4096]{1,0:T(8,128)(2,1)} %get-tuple-element.54), channel_id=1, source_target_pairs={{0,8},{8,16},{16,24},{24,0},{1,9},{9,17},{17,25},{25,1},{2,10},{10... | collective-permute-start | bytes 786440 | tf_op jit(solution)/shard_map/ppermute | solution.py:267
  13.0 35.9 %collective-permute-start.4 = (bf16[32,4096]{1,0:T(8,128)(2,1)}, bf16[32,4096]{1,0:T(8,128)(2,1)S(1)}, u32[]{:S(2)}, u32[]{:S(2)}) collective-permute-start(bf16[32,4096]{1,0:T(8,128)(2,1)} %get-tuple-element.55), channel_id=1, source_target_pairs={{0,16},{8,24},{16,0},{24,8},{1,17},{9,25},{17,1},{25,9},{2,18},{10... | collective-permute-start | bytes 786440 | tf_op jit(solution)/shard_map/ppermute | solution.py:267
  15.5 33.4 %collective-permute-start.5 = (bf16[32,4096]{1,0:T(8,128)(2,1)}, bf16[32,4096]{1,0:T(8,128)(2,1)S(1)}, u32[]{:S(2)}, u32[]{:S(2)}) collective-permute-start(bf16[32,4096]{1,0:T(8,128)(2,1)} %get-tuple-element.56), channel_id=1, source_target_pairs={{0,24},{8,0},{16,8},{24,16},{1,25},{9,1},{17,9},{25,17},{2,26},{10... | collective-permute-start | bytes 786440 | tf_op jit(solution)/shard_map/ppermute | solution.py:267
  18.0 1.0 copy-start.2
  18.9 0.9 copy-start.4
  19.9 0.7 copy-start.8
  20.6 0.7 copy-start.9
  21.2 0.7 copy-start.10
  49.9 1.4 %collective-permute-start.6 = (bf16[32,2048]{1,0:T(8,128)(2,1)S(1)}, bf16[32,2048]{1,0:T(8,128)(2,1)S(1)}, u32[]{:S(2)}, u32[]{:S(2)}) collective-permute-start(bf16[32,2048]{1,0:T(8,128)(2,1)S(1)} %get-tuple-element.60), channel_id=1, source_target_pairs={{0,1},{1,0},{2,3},{3,2},{4,5},{5,4},{6,7},{7,6},{8,9},{9,8},{10,11... | collective-permute-start | bytes 393224 | tf_op jit(solution)/shard_map/ppermute | solution.py:337
  51.3 4.3 %collective-permute-start.10 = (bf16[16,2048]{1,0:T(8,128)(2,1)S(1)}, bf16[16,2048]{1,0:T(8,128)(2,1)S(1)}, u32[]{:S(2)}, u32[]{:S(2)}) collective-permute-start(bf16[16,2048]{1,0:T(8,128)(2,1)S(1)} %get-tuple-element.65), channel_id=1, source_target_pairs={{0,4},{1,5},{2,6},{3,7},{4,0},{5,1},{6,2},{7,3},{8,12},{9,13},{10,... | collective-permute-start | bytes 196616 | tf_op jit(solution)/shard_map/ppermute | solution.py:337
  52.9 5.8 %collective-permute-start.11 = (bf16[16,2048]{1,0:T(8,128)(2,1)S(1)}, bf16[16,2048]{1,0:T(8,128)(2,1)S(1)}, u32[]{:S(2)}, u32[]{:S(2)}) collective-permute-start(bf16[16,2048]{1,0:T(8,128)(2,1)S(1)} %get-tuple-element.66), channel_id=1, source_target_pairs={{0,6},{1,7},{2,4},{3,5},{4,2},{5,3},{6,0},{7,1},{8,14},{9,15},{10,... | collective-permute-start | bytes 196616 | tf_op jit(solution)/shard_map/ppermute | solution.py:337
  54.3 9.6 %collective-permute-start.7 = (bf16[16,2048]{1,0:T(8,128)(2,1)S(1)}, bf16[16,2048]{1,0:T(8,128)(2,1)S(1)}, u32[]{:S(2)}, u32[]{:S(2)}) collective-permute-start(bf16[16,2048]{1,0:T(8,128)(2,1)S(1)} %get-tuple-element.62), channel_id=1, source_target_pairs={{0,2},{1,3},{2,0},{3,1},{4,6},{5,7},{6,4},{7,5},{8,10},{9,11},{10,... | collective-permute-start | bytes 196616 | tf_op jit(solution)/shard_map/ppermute | solution.py:337
  58.7 14.4 %collective-permute-start.12 = (bf16[32,2048]{1,0:T(8,128)(2,1)S(1)}, bf16[32,2048]{1,0:T(8,128)(2,1)S(1)}, u32[]{:S(2)}, u32[]{:S(2)}) collective-permute-start(bf16[32,2048]{1,0:T(8,128)(2,1)S(1)} %shard_map.145.refs_0_), channel_id=1, source_target_pairs={{0,16},{8,24},{16,0},{24,8},{1,17},{9,25},{17,1},{25,9},{2,18},{10... | collective-permute-start | bytes 393224 | tf_op jit(solution)/shard_map/ppermute | solution.py:337
  63.9 11.3 %collective-permute-start.14 = (bf16[32,2048]{1,0:T(8,128)(2,1)S(1)}, bf16[32,2048]{1,0:T(8,128)(2,1)S(1)}, u32[]{:S(2)}, u32[]{:S(2)}) collective-permute-start(bf16[32,2048]{1,0:T(8,128)(2,1)S(1)} %shard_map.143.refs_0_), channel_id=1, source_target_pairs={{0,16},{8,24},{16,0},{24,8},{1,17},{9,25},{17,1},{25,9},{2,18},{10... | collective-permute-start | bytes 393224 | tf_op jit(solution)/shard_map/ppermute | solution.py:337
  64.0 11.3 %collective-permute-start.8 = (bf16[32,2048]{1,0:T(8,128)(2,1)S(1)}, bf16[32,2048]{1,0:T(8,128)(2,1)S(1)}, u32[]{:S(2)}, u32[]{:S(2)}) collective-permute-start(bf16[32,2048]{1,0:T(8,128)(2,1)S(1)} %shard_map.143.refs_0_), channel_id=1, source_target_pairs={{0,8},{8,0},{16,24},{24,16},{1,9},{9,1},{17,25},{25,17},{2,10},{10... | collective-permute-start | bytes 393224 | tf_op jit(solution)/shard_map/ppermute | solution.py:337
  67.8 11.2 %collective-permute-start.16 = (bf16[32,2048]{1,0:T(8,128)(2,1)S(1)}, bf16[32,2048]{1,0:T(8,128)(2,1)S(1)}, u32[]{:S(2)}, u32[]{:S(2)}) collective-permute-start(bf16[32,2048]{1,0:T(8,128)(2,1)S(1)} %shard_map.145.refs_0_), channel_id=1, source_target_pairs={{0,8},{8,0},{16,24},{24,16},{1,9},{9,1},{17,25},{25,17},{2,10},{10... | collective-permute-start | bytes 393224 | tf_op jit(solution)/shard_map/ppermute | solution.py:337
  73.1 7.6 %collective-permute-start.13 = (bf16[32,2048]{1,0:T(8,128)(2,1)S(1)}, bf16[32,2048]{1,0:T(8,128)(2,1)S(1)}, u32[]{:S(2)}, u32[]{:S(2)}) collective-permute-start(bf16[32,2048]{1,0:T(8,128)(2,1)S(1)} %collective-permute-done.12.refs_2_), channel_id=1, source_target_pairs={{0,8},{8,0},{16,24},{24,16},{1,9},{9,1},{17,25},{25,17},{2,10},{10... | collective-permute-start | bytes 393224 | tf_op jit(solution)/shard_map/ppermute | solution.py:337
  75.3 5.8 %collective-permute-start.15 = (bf16[32,2048]{1,0:T(8,128)(2,1)S(1)}, bf16[32,2048]{1,0:T(8,128)(2,1)S(1)}, u32[]{:S(2)}, u32[]{:S(2)}) collective-permute-start(bf16[32,2048]{1,0:T(8,128)(2,1)S(1)} %collective-permute-done.14.refs_3_), channel_id=1, source_target_pairs={{0,8},{8,0},{16,24},{24,16},{1,9},{9,1},{17,25},{25,17},{2,10},{10... | collective-permute-start | bytes 393224 | tf_op jit(solution)/shard_map/ppermute | solution.py:337
  75.3 2.2 %copy-start.1 = (bf16[1,1024,2048]{2,1,0:T(8,128)(2,1)S(1)}, bf16[1,1024,2048]{2,1,0:T(8,128)(2,1)}, u32[]{:S(2)}) copy-start(bf16[1,1024,2048]{2,1,0:T(8,128)(2,1)} %w_out_ref.5) | copy-start | bytes 12582916
  81.1 16.8 %copy-start.3 = (f32[8,2048]{1,0:T(8,128)S(1)}, f32[8,2048]{1,0:T(8,128)}, u32[]{:S(2)}) copy-start(f32[8,2048]{1,0:T(8,128)} %bias_ref.9) | copy-start | bytes 196612
  82.5 6.5 %collective-permute-start.21 = (bf16[32,2048]{1,0:T(8,128)(2,1)S(1)}, bf16[32,2048]{1,0:T(8,128)(2,1)S(1)}, u32[]{:S(2)}, u32[]{:S(2)}) collective-permute-start(bf16[32,2048]{1,0:T(8,128)(2,1)S(1)} %get-tuple-element.73), channel_id=1, source_target_pairs={{0,8},{8,0},{16,24},{24,16},{1,9},{9,1},{17,25},{25,17},{2,10},{10... | collective-permute-start | bytes 393224 | tf_op jit(solution)/shard_map/ppermute | solution.py:337
  84.1 11.7 %collective-permute-start.17 = (bf16[32,2048]{1,0:T(8,128)(2,1)S(1)}, bf16[32,2048]{1,0:T(8,128)(2,1)S(1)}, u32[]{:S(2)}, u32[]{:S(2)}) collective-permute-start(bf16[32,2048]{1,0:T(8,128)(2,1)S(1)} %get-tuple-element.68), channel_id=1, source_target_pairs={{0,8},{8,0},{16,24},{24,16},{1,9},{9,1},{17,25},{25,17},{2,10},{10... | collective-permute-start | bytes 393224 | tf_op jit(solution)/shard_map/ppermute | solution.py:337
  84.5 13.4 %collective-permute-start.20 = (bf16[32,2048]{1,0:T(8,128)(2,1)S(1)}, bf16[32,2048]{1,0:T(8,128)(2,1)S(1)}, u32[]{:S(2)}, u32[]{:S(2)}) collective-permute-start(bf16[32,2048]{1,0:T(8,128)(2,1)S(1)} %get-tuple-element.72), channel_id=1, source_target_pairs={{0,8},{8,0},{16,24},{24,16},{1,9},{9,1},{17,25},{25,17},{2,10},{10... | collective-permute-start | bytes 393224 | tf_op jit(solution)/shard_map/ppermute | solution.py:337
  89.0 8.9 %collective-permute-start.22 = (bf16[32,2048]{1,0:T(8,128)(2,1)S(1)}, bf16[32,2048]{1,0:T(8,128)(2,1)S(1)}, u32[]{:S(2)}, u32[]{:S(2)}) collective-permute-start(bf16[32,2048]{1,0:T(8,128)(2,1)S(1)} %shard_map.150), channel_id=1, source_target_pairs={{0,16},{8,24},{16,0},{24,8},{1,17},{9,25},{17,1},{25,9},{2,18},{10... | collective-permute-start | bytes 393224 | tf_op jit(solution)/shard_map/ppermute | solution.py:337
  92.8 8.4 %collective-permute-start.9 = (bf16[32,2048]{1,0:T(8,128)(2,1)S(1)}, bf16[32,2048]{1,0:T(8,128)(2,1)S(1)}, u32[]{:S(2)}, u32[]{:S(2)}) collective-permute-start(bf16[32,2048]{1,0:T(8,128)(2,1)S(1)} %get-tuple-element.63), channel_id=1, source_target_pairs={{0,8},{8,0},{16,24},{24,16},{1,9},{9,1},{17,25},{25,17},{2,10},{10... | collective-permute-start | bytes 393224 | tf_op jit(solution)/shard_map/ppermute | solution.py:337
  95.8 7.8 %collective-permute-start.18 = (bf16[32,2048]{1,0:T(8,128)(2,1)S(1)}, bf16[32,2048]{1,0:T(8,128)(2,1)S(1)}, u32[]{:S(2)}, u32[]{:S(2)}) collective-permute-start(bf16[32,2048]{1,0:T(8,128)(2,1)S(1)} %shard_map.148), channel_id=1, source_target_pairs={{0,16},{8,24},{16,0},{24,8},{1,17},{9,25},{17,1},{25,9},{2,18},{10... | collective-permute-start | bytes 393224 | tf_op jit(solution)/shard_map/ppermute | solution.py:337
  98.0 7.4 %collective-permute-start.23 = (bf16[16,2048]{1,0:T(8,128)(2,1)S(1)}, bf16[16,2048]{1,0:T(8,128)(2,1)S(1)}, u32[]{:S(2)}, u32[]{:S(2)}) collective-permute-start(bf16[16,2048]{1,0:T(8,128)(2,1)S(1)} %get-tuple-element.75), channel_id=1, source_target_pairs={{0,4},{1,5},{2,6},{3,7},{4,0},{5,1},{6,2},{7,3},{8,12},{9,13},{10,... | collective-permute-start | bytes 196616 | tf_op jit(solution)/shard_map/ppermute | solution.py:337
  98.8 6.7 %collective-permute-start.24 = (bf16[16,2048]{1,0:T(8,128)(2,1)S(1)}, bf16[16,2048]{1,0:T(8,128)(2,1)S(1)}, u32[]{:S(2)}, u32[]{:S(2)}) collective-permute-start(bf16[16,2048]{1,0:T(8,128)(2,1)S(1)} %get-tuple-element.76), channel_id=1, source_target_pairs={{0,6},{1,7},{2,4},{3,5},{4,2},{5,3},{6,0},{7,1},{8,14},{9,15},{10,... | collective-permute-start | bytes 196616 | tf_op jit(solution)/shard_map/ppermute | solution.py:337
  103.7 4.3 %collective-permute-start.19 = (bf16[16,2048]{1,0:T(8,128)(2,1)S(1)}, bf16[16,2048]{1,0:T(8,128)(2,1)S(1)}, u32[]{:S(2)}, u32[]{:S(2)}) collective-permute-start(bf16[16,2048]{1,0:T(8,128)(2,1)S(1)} %get-tuple-element.71), channel_id=1, source_target_pairs={{0,2},{1,3},{2,0},{3,1},{4,6},{5,7},{6,4},{7,5},{8,10},{9,11},{10,... | collective-permute-start | bytes 196616 | tf_op jit(solution)/shard_map/ppermute | solution.py:337
  108.1 1.4 %collective-permute-start.25 = (bf16[32,2048]{1,0:T(8,128)(2,1)S(1)}, bf16[32,2048]{1,0:T(8,128)(2,1)S(1)}, u32[]{:S(2)}, u32[]{:S(2)}) collective-permute-start(bf16[32,2048]{1,0:T(8,128)(2,1)S(1)} %get-tuple-element.78), channel_id=1, source_target_pairs={{0,1},{1,0},{2,3},{3,2},{4,5},{5,4},{6,7},{7,6},{8,9},{9,8},{10,11... | collective-permute-start | bytes 393224 | tf_op jit(solution)/shard_map/ppermute | solution.py:337

commit v15 on v13

--- a/solution.py
+++ b/solution.py
@@ -178,13 +178,6 @@
 
 def add_kernel(first_ref, second_ref, out_ref):
     out_ref[...] = (first_ref[...].astype(F32) + second_ref[...].astype(F32)).astype(BF16)
-
-
-def hand_kernel(first_ref, second_ref, _, *out_refs):
-    rows = out_refs[0].shape[0]
-    for n, out_ref in enumerate(out_refs):
-        source_ref = (first_ref, second_ref)[n // 2]
-        out_ref[...] = source_ref[n % 2 * rows : (n % 2 + 1) * rows]
 
 
 def result_kernel(lower, bias_ref, near_ref, *refs):
@@ -350,23 +343,18 @@
         last = last[0]
         *corner_share, far_first, far_second = apply([swap(x, 1) for x in far] + far, after=[last])
         far_shares = [far_first, far_second]
-        first_pair = call(add_kernel, bf16(half), swap(corner_share[0], 1), far_shares[0])
-        second_pair = call(add_kernel, bf16(half), swap(corner_share[1], 1), far_shares[1])
-        near_parts = call(hand_kernel, (bf16(half // 2),) * 4, *near_shares, first_pair)
-        near_parts = [swap(x, 1) for x in near_parts]
-        near_shares = [call(join_kernel, bf16(half), *near_parts[n : n + 2]) for n in (0, 2)]
-        pairs = [first_pair, second_pair]
-        backs = [
-            call(
+        near_shares = [swap(x, 1) for x in near_shares]
+        backs = [None, None]
+        for n in (1, 0):
+            pair = swap(call(add_kernel, bf16(half), swap(corner_share[n], 1), far_shares[n]), 2)
+            backs[n] = call(
                 functools.partial(result_kernel, 0),
                 (bf16(2 * cap),) * 2,
                 b_out,
                 near_shares[n],
                 own_share[n],
-                swap(pairs[n], 2),
+                pair,
             )
-            for n in range(2)
-        ]
         pieces = [x for n in (1, 0) for x in backs[n]]
         pieces = [swap(x, 2 * n, "expert") if n else x for n, x in enumerate(pieces)]
         mine, other = call(functools.partial(part_kernel, cap), (bf16(half),) * 2, *pieces)

time: 112 us -> 111 us (level)
  starting transfers between devices: 47.6 us -> 40.1 us
  waiting for transfers between devices: 44.2 us -> 50.2 us
    ppermute x22 -> x20, starting transfers between devices: 37.1 us -> 29.6 us  [swap(): lax.ppermute(x, axis, [(i, i ^ distance) for i in range(lax.axis_size(axi...]
    ppermute x22 -> x20, waiting for transfers between devices: 16.9 us -> 22.9 us  [swap(): lax.ppermute(x, axis, [(i, i ^ distance) for i in range(lax.axis_size(axi...]
    pallas_call x21 -> x18, Pallas kernels: 14 us -> 14 us  [call(): pl.pallas_call(body, out_shape=out_shape, compiler_params=pltpu.CompilerP...]
  transfers between devices with their start and end apart: 28 -> 26, of which waited for: 17 -> 15; matrix products, arithmetic and copies ran while one was open for 0% -> 0% of each run, Pallas kernels for 7% -> 7%
where the time goes in v15:
time: 111 us
  waiting for transfers between devices  50.2 us (45%)
  starting transfers between devices  40.1 us (36%)
  Pallas kernels  14 us (13%)
  local copies, waits for them, and re-layouts  6.11 us (6%)
    ppermute x20, starting transfers between devices, swap(): lax.ppermute(x, axis, [(i, i ^ distance) for i in range(lax.axis_size(axi...  29.6 us
    ppermute x6, waiting for transfers between devices, spread(): lax.ppermute(part, 'dp', [(i, (i + n) % dp) for i in range(dp)])  27.3 us
    ppermute x20, waiting for transfers between devices, swap(): lax.ppermute(x, axis, [(i, i ^ distance) for i in range(lax.axis_size(axi...  22.9 us
    pallas_call x18, Pallas kernels, call(): pl.pallas_call(body, out_shape=out_shape, compiler_params=pltpu.CompilerP...  14 us
    ppermute x6, starting transfers between devices, spread(): lax.ppermute(part, 'dp', [(i, (i + n) % dp) for i in range(dp)])  10.5 us
    unnamed x22, local copies, waits for them, and re-layouts  6.11 us
  transfers between devices with their start and end apart: 26, of which 15 were waited for; matrix products, arithmetic and copies ran while one was open for 0% of the time, Pallas kernels for 7%

profile of v15, /device:TPU:0, one launch (start us, length us, event | category | flops | bytes accessed | tf_op | source)
XLA Modules:
  0.0 110.5 jit_solution(12362418202855545520)
XLA Ops:
  0.0 2.8 %shard_map.136 = (bf16[128,128]{1,0:T(8,128)(2,1)}, bf16[32,4224]{1,0:T(8,128)(2,1)}, bf16[32,4224]{1,0:T(8,128)(2,1)}, bf16[32,4224]{1,0:T(8,128)(2,1)}, bf16[32,4224]{1,0:T(8,128)(2,1)}) custom-call(s32[1,128]{1,0:T(1,128)} %bitcast.9, bf16[128,2048]{1,0:T(8,128)(2,1)} %refs_0_.2, bf16[128,2048]{1,0:T(8,128)(2,1)} %refs_1_.2), custom_call_target="tpu_custom_call" | custom-call | bytes 2163200 | tf_op jit(solution)/shard_map/pallas_call | solution.py:41
  2.8 3.0 %collective-permute-start = (bf16[32,4224]{1,0:T(8,128)(2,1)}, bf16[32,4224]{1,0:T(8,128)(2,1)S(1)}, u32[]{:S(2)}, u32[]{:S(2)}) collective-permute-start(bf16[32,4224]{1,0:T(8,128)(2,1)} %get-tuple-element.47), channel_id=1, source_target_pairs={{0,8},{8,16},{16,24},{24,0},{1,9},{9,17},{17,25},{25,1},{2,10},{10... | collective-permute-start | bytes 811016 | tf_op jit(solution)/shard_map/ppermute | solution.py:258
  5.8 2.6 %collective-permute-start.1 = (bf16[32,4224]{1,0:T(8,128)(2,1)}, bf16[32,4224]{1,0:T(8,128)(2,1)S(1)}, u32[]{:S(2)}, u32[]{:S(2)}) collective-permute-start(bf16[32,4224]{1,0:T(8,128)(2,1)} %get-tuple-element.48), channel_id=1, source_target_pairs={{0,16},{8,24},{16,0},{24,8},{1,17},{9,25},{17,1},{25,9},{2,18},{10... | collective-permute-start | bytes 811016 | tf_op jit(solution)/shard_map/ppermute | solution.py:258
  8.4 1.3 %collective-permute-start.2 = (bf16[32,4224]{1,0:T(8,128)(2,1)}, bf16[32,4224]{1,0:T(8,128)(2,1)S(1)}, u32[]{:S(2)}, u32[]{:S(2)}) collective-permute-start(bf16[32,4224]{1,0:T(8,128)(2,1)} %get-tuple-element.49), channel_id=1, source_target_pairs={{0,24},{8,0},{16,8},{24,16},{1,25},{9,1},{17,9},{25,17},{2,26},{10... | collective-permute-start | bytes 811016 | tf_op jit(solution)/shard_map/ppermute | solution.py:258
  9.7 2.6 %shard_map.137 = (bf16[128,128]{1,0:T(8,128)(2,1)}, bf16[32,4096]{1,0:T(8,128)(2,1)}, bf16[32,4096]{1,0:T(8,128)(2,1)}, bf16[32,4096]{1,0:T(8,128)(2,1)}, bf16[32,4096]{1,0:T(8,128)(2,1)}) custom-call(bf16[128,128]{1,0:T(8,128)(2,1)} %get-tuple-element.43.pos_ref, bf16[128,2048]{1,0:T(8,128)(2,1)} %refs_0_.3, bf16[128,2048]{1,0:T(8,128)(2,1)} %refs_1_.3), custom_call_target="tpu_custom_call" | custom-call | bytes 2162688 | tf_op jit(solution)/shard_map/pallas_call | solution.py:41
  12.3 0.7 collective-permute-start.3
  13.4 2.1 %collective-permute-done.refs_1_ = bf16[32,4224]{1,0:T(8,128)(2,1)S(1)} collective-permute-done((bf16[32,4224]{1,0:T(8,128)(2,1)}, bf16[32,4224]{1,0:T(8,128)(2,1)S(1)}, u32[]{:S(2)}, u32[]{:S(2)}) %collective-permute-start) | collective-permute-done | bytes 270368 | tf_op jit(solution)/shard_map/ppermute | solution.py:258
  15.5 2.5 %collective-permute-start.5 = (bf16[32,4096]{1,0:T(8,128)(2,1)}, bf16[32,4096]{1,0:T(8,128)(2,1)S(1)}, u32[]{:S(2)}, u32[]{:S(2)}) collective-permute-start(bf16[32,4096]{1,0:T(8,128)(2,1)} %get-tuple-element.56), channel_id=1, source_target_pairs={{0,24},{8,0},{16,8},{24,16},{1,25},{9,1},{17,9},{25,17},{2,26},{10... | collective-permute-start | bytes 786440 | tf_op jit(solution)/shard_map/ppermute | solution.py:258
  18.0 1.0 copy-done.2
  18.9 0.9 copy-done.4
  19.9 0.7 copy-done.8
  20.6 0.7 copy-done.9
  21.2 0.7 copy-done.10
  22.1 5.0 %collective-permute-done.1.refs_2_ = bf16[32,4224]{1,0:T(8,128)(2,1)S(1)} collective-permute-done((bf16[32,4224]{1,0:T(8,128)(2,1)}, bf16[32,4224]{1,0:T(8,128)(2,1)S(1)}, u32[]{:S(2)}, u32[]{:S(2)}) %collective-permute-start.1) | collective-permute-done | bytes 270368 | tf_op jit(solution)/shard_map/ppermute | solution.py:258
  27.3 1.5 %shard_map.140.probs_ref = bf16[16,128,128]{2,1,0:T(8,128)(2,1)S(1)} custom-call(bf16[128,128]{1,0:T(8,128)(2,1)S(1)} %get-tuple-element.50.place_ref, f32[128,128]{1,0:T(8,128)S(1)} %get-tuple-element.52.outside_ref, bf16[32,4224]{1,0:T(8,128)(2,1)S(1)} %get-tuple-element.46.refs_0_, bf16[32,4224]{1,0:T(8,128)(2,1)S(1)} %collective-permute-done.refs_1_, ...), custom_call_target="tpu_custom_call" | custom-call | bytes 1703936 | tf_op jit(solution)/shard_map/pallas_call | solution.py:41
  28.8 4.0 %collective-permute-done.3.refs_1_ = bf16[32,4096]{1,0:T(8,128)(2,1)S(1)} collective-permute-done((bf16[32,4096]{1,0:T(8,128)(2,1)}, bf16[32,4096]{1,0:T(8,128)(2,1)S(1)}, u32[]{:S(2)}, u32[]{:S(2)}) %collective-permute-start.3) | collective-permute-done | bytes 262176 | tf_op jit(solution)/shard_map/ppermute | solution.py:258
  32.7 16.2 %collective-permute-done.4.refs_2_ = bf16[32,4096]{1,0:T(8,128)(2,1)S(1)} collective-permute-done((bf16[32,4096]{1,0:T(8,128)(2,1)}, bf16[32,4096]{1,0:T(8,128)(2,1)S(1)}, u32[]{:S(2)}, u32[]{:S(2)}) %collective-permute-start.4) | collective-permute-done | bytes 262176 | tf_op jit(solution)/shard_map/ppermute | solution.py:258
  48.9 0.9 shard_map.141
  50.0 1.3 %collective-permute-done.6.other_ref = bf16[32,2048]{1,0:T(8,128)(2,1)S(1)} collective-permute-done((bf16[32,2048]{1,0:T(8,128)(2,1)S(1)}, bf16[32,2048]{1,0:T(8,128)(2,1)S(1)}, u32[]{:S(2)}, u32[]{:S(2)}) %collective-permute-start.6) | collective-permute-done | bytes 131104 | tf_op jit(solution)/shard_map/ppermute | solution.py:328
  51.3 1.6 %collective-permute-start.10 = (bf16[16,2048]{1,0:T(8,128)(2,1)S(1)}, bf16[16,2048]{1,0:T(8,128)(2,1)S(1)}, u32[]{:S(2)}, u32[]{:S(2)}) collective-permute-start(bf16[16,2048]{1,0:T(8,128)(2,1)S(1)} %get-tuple-element.65), channel_id=1, source_target_pairs={{0,4},{1,5},{2,6},{3,7},{4,0},{5,1},{6,2},{7,3},{8,12},{9,13},{10,... | collective-permute-start | bytes 196616 | tf_op jit(solution)/shard_map/ppermute | solution.py:328
  52.9 1.4 %collective-permute-start.11 = (bf16[16,2048]{1,0:T(8,128)(2,1)S(1)}, bf16[16,2048]{1,0:T(8,128)(2,1)S(1)}, u32[]{:S(2)}, u32[]{:S(2)}) collective-permute-start(bf16[16,2048]{1,0:T(8,128)(2,1)S(1)} %get-tuple-element.66), channel_id=1, source_target_pairs={{0,6},{1,7},{2,4},{3,5},{4,2},{5,3},{6,0},{7,1},{8,14},{9,15},{10,... | collective-permute-start | bytes 196616 | tf_op jit(solution)/shard_map/ppermute | solution.py:328
  54.3 0.5 collective-permute-start.7
  54.9 0.8 collective-permute-done.10.refs_0_
  55.7 3.0 %collective-permute-done.11.refs_1_ = bf16[16,2048]{1,0:T(8,128)(2,1)S(1)} collective-permute-done((bf16[16,2048]{1,0:T(8,128)(2,1)S(1)}, bf16[16,2048]{1,0:T(8,128)(2,1)S(1)}, u32[]{:S(2)}, u32[]{:S(2)}) %collective-permute-start.11) | collective-permute-done | bytes 65568 | tf_op jit(solution)/shard_map/ppermute | solution.py:328
  58.7 5.2 %collective-permute-start.12 = (bf16[32,2048]{1,0:T(8,128)(2,1)S(1)}, bf16[32,2048]{1,0:T(8,128)(2,1)S(1)}, u32[]{:S(2)}, u32[]{:S(2)}) collective-permute-start(bf16[32,2048]{1,0:T(8,128)(2,1)S(1)} %shard_map.145.refs_0_), channel_id=1, source_target_pairs={{0,16},{8,24},{16,0},{24,8},{1,17},{9,25},{17,1},{25,9},{2,18},{10... | collective-permute-start | bytes 393224 | tf_op jit(solution)/shard_map/ppermute | solution.py:328
  64.0 3.8 %collective-permute-start.8 = (bf16[32,2048]{1,0:T(8,128)(2,1)S(1)}, bf16[32,2048]{1,0:T(8,128)(2,1)S(1)}, u32[]{:S(2)}, u32[]{:S(2)}) collective-permute-start(bf16[32,2048]{1,0:T(8,128)(2,1)S(1)} %shard_map.143.refs_0_), channel_id=1, source_target_pairs={{0,8},{8,0},{16,24},{24,16},{1,9},{9,1},{17,25},{25,17},{2,10},{10... | collective-permute-start | bytes 393224 | tf_op jit(solution)/shard_map/ppermute | solution.py:328
  67.9 5.2 %collective-permute-done.12.refs_2_ = bf16[32,2048]{1,0:T(8,128)(2,1)S(1)} collective-permute-done((bf16[32,2048]{1,0:T(8,128)(2,1)S(1)}, bf16[32,2048]{1,0:T(8,128)(2,1)S(1)}, u32[]{:S(2)}, u32[]{:S(2)}) %collective-permute-start.12) | collective-permute-done | bytes 131104 | tf_op jit(solution)/shard_map/ppermute | solution.py:328
  73.1 2.2 %collective-permute-done.14.refs_3_ = bf16[32,2048]{1,0:T(8,128)(2,1)S(1)} collective-permute-done((bf16[32,2048]{1,0:T(8,128)(2,1)S(1)}, bf16[32,2048]{1,0:T(8,128)(2,1)S(1)}, u32[]{:S(2)}, u32[]{:S(2)}) %collective-permute-start.14) | collective-permute-done | bytes 131104 | tf_op jit(solution)/shard_map/ppermute | solution.py:328
  75.3 2.2 %copy-done.1 = bf16[1,1024,2048]{2,1,0:T(8,128)(2,1)S(1)} copy-done((bf16[1,1024,2048]{2,1,0:T(8,128)(2,1)S(1)}, bf16[1,1024,2048]{2,1,0:T(8,128)(2,1)}, u32[]{:S(2)}) %copy-start.1) | copy-done | bytes 4194328
  77.5 1.6 %shard_map.144 = (bf16[32,2048]{1,0:T(8,128)(2,1)S(1)}, bf16[32,2048]{1,0:T(8,128)(2,1)S(1)}) custom-call(f32[1,1024]{1,0:T(1,128)S(1)} %copy-done.5, bf16[1,2048,1024]{2,1,0:T(8,128)(2,1)S(1)} %copy-done, bf16[1,1024,2048]{2,1,0:T(8,128)(2,1)S(1)} %copy-done.1, bf16[32,2048]{1,0:T(8,128)(2,1)S(1)} %shard_map.143.refs_0_, ...), custom_call_target="tpu_custom_call" | custom-call | flops 536870912 | bytes 8916992 | tf_op jit(solution)/shard_map/pallas_call | solution.py:41
  79.1 1.6 %shard_map.146 = (bf16[32,2048]{1,0:T(8,128)(2,1)S(1)}, bf16[32,2048]{1,0:T(8,128)(2,1)S(1)}) custom-call(f32[1,1024]{1,0:T(1,128)S(1)} %copy-done.5, bf16[1,2048,1024]{2,1,0:T(8,128)(2,1)S(1)} %copy-done, bf16[1,1024,2048]{2,1,0:T(8,128)(2,1)S(1)} %copy-done.1, bf16[32,2048]{1,0:T(8,128)(2,1)S(1)} %shard_map.145.refs_0_, ...), custom_call_target="tpu_custom_call" | custom-call | flops 536870912 | bytes 9048064 | tf_op jit(solution)/shard_map/pallas_call | solution.py:41
  80.7 0.4 collective-permute-done.15.refs_1_
  81.1 1.3 %shard_map.147 = (bf16[32,2048]{1,0:T(8,128)(2,1)S(1)}, bf16[32,2048]{1,0:T(8,128)(2,1)S(1)}, bf16[32,2048]{1,0:T(8,128)(2,1)S(1)}, bf16[32,2048]{1,0:T(8,128)(2,1)S(1)}) custom-call(f32[1,1024]{1,0:T(1,128)S(1)} %copy-done.5, bf16[1,2048,1024]{2,1,0:T(8,128)(2,1)S(1)} %copy-done, bf16[1,1024,2048]{2,1,0:T(8,128)(2,1)S(1)} %copy-done.1, ...), custom_call_target="tpu_custom_call" | custom-call | flops 1073741824 | bytes 9572352 | tf_op jit(solution)/shard_map/pallas_call | solution.py:41
  82.5 1.7 %collective-permute-start.21 = (bf16[32,2048]{1,0:T(8,128)(2,1)S(1)}, bf16[32,2048]{1,0:T(8,128)(2,1)S(1)}, u32[]{:S(2)}, u32[]{:S(2)}) collective-permute-start(bf16[32,2048]{1,0:T(8,128)(2,1)S(1)} %get-tuple-element.73), channel_id=1, source_target_pairs={{0,8},{8,0},{16,24},{24,16},{1,9},{9,1},{17,25},{25,17},{2,10},{10... | collective-permute-start | bytes 393224 | tf_op jit(solution)/shard_map/ppermute | solution.py:328
  84.1 0.4 collective-permute-start.17
  84.5 1.6 %collective-permute-start.20 = (bf16[32,2048]{1,0:T(8,128)(2,1)S(1)}, bf16[32,2048]{1,0:T(8,128)(2,1)S(1)}, u32[]{:S(2)}, u32[]{:S(2)}) collective-permute-start(bf16[32,2048]{1,0:T(8,128)(2,1)S(1)} %get-tuple-element.72), channel_id=1, source_target_pairs={{0,8},{8,0},{16,24},{24,16},{1,9},{9,1},{17,25},{25,17},{2,10},{10... | collective-permute-start | bytes 393224 | tf_op jit(solution)/shard_map/ppermute | solution.py:328
  86.2 2.8 %collective-permute-done.21.first_ref = bf16[32,2048]{1,0:T(8,128)(2,1)S(1)} collective-permute-done((bf16[32,2048]{1,0:T(8,128)(2,1)S(1)}, bf16[32,2048]{1,0:T(8,128)(2,1)S(1)}, u32[]{:S(2)}, u32[]{:S(2)}) %collective-permute-start.21) | collective-permute-done | bytes 131104 | tf_op jit(solution)/shard_map/ppermute | solution.py:328
  89.0 3.8 %collective-permute-start.22 = (bf16[32,2048]{1,0:T(8,128)(2,1)S(1)}, bf16[32,2048]{1,0:T(8,128)(2,1)S(1)}, u32[]{:S(2)}, u32[]{:S(2)}) collective-permute-start(bf16[32,2048]{1,0:T(8,128)(2,1)S(1)} %shard_map.150), channel_id=1, source_target_pairs={{0,16},{8,24},{16,0},{24,8},{1,17},{9,25},{17,1},{25,9},{2,18},{10... | collective-permute-start | bytes 393224 | tf_op jit(solution)/shard_map/ppermute | solution.py:328
  92.8 3.0 %collective-permute-start.9 = (bf16[32,2048]{1,0:T(8,128)(2,1)S(1)}, bf16[32,2048]{1,0:T(8,128)(2,1)S(1)}, u32[]{:S(2)}, u32[]{:S(2)}) collective-permute-start(bf16[32,2048]{1,0:T(8,128)(2,1)S(1)} %get-tuple-element.63), channel_id=1, source_target_pairs={{0,8},{8,0},{16,24},{24,16},{1,9},{9,1},{17,25},{25,17},{2,10},{10... | collective-permute-start | bytes 393224 | tf_op jit(solution)/shard_map/ppermute | solution.py:328
  95.8 1.3 %collective-permute-start.18 = (bf16[32,2048]{1,0:T(8,128)(2,1)S(1)}, bf16[32,2048]{1,0:T(8,128)(2,1)S(1)}, u32[]{:S(2)}, u32[]{:S(2)}) collective-permute-start(bf16[32,2048]{1,0:T(8,128)(2,1)S(1)} %shard_map.148), channel_id=1, source_target_pairs={{0,16},{8,24},{16,0},{24,8},{1,17},{9,25},{17,1},{25,9},{2,18},{10... | collective-permute-start | bytes 393224 | tf_op jit(solution)/shard_map/ppermute | solution.py:328
  97.1 0.8 collective-permute-done.20.near_ref
  98.0 0.8 collective-permute-start.23
  98.8 2.4 %collective-permute-start.24 = (bf16[16,2048]{1,0:T(8,128)(2,1)S(1)}, bf16[16,2048]{1,0:T(8,128)(2,1)S(1)}, u32[]{:S(2)}, u32[]{:S(2)}) collective-permute-start(bf16[16,2048]{1,0:T(8,128)(2,1)S(1)} %get-tuple-element.76), channel_id=1, source_target_pairs={{0,6},{1,7},{2,4},{3,5},{4,2},{5,3},{6,0},{7,1},{8,14},{9,15},{10,... | collective-permute-start | bytes 196616 | tf_op jit(solution)/shard_map/ppermute | solution.py:328
  101.2 2.4 %collective-permute-done.18.refs_1_ = bf16[32,2048]{1,0:T(8,128)(2,1)S(1)} collective-permute-done((bf16[32,2048]{1,0:T(8,128)(2,1)S(1)}, bf16[32,2048]{1,0:T(8,128)(2,1)S(1)}, u32[]{:S(2)}, u32[]{:S(2)}) %collective-permute-start.18) | collective-permute-done | bytes 131104 | tf_op jit(solution)/shard_map/ppermute | solution.py:328
  103.7 1.7 %collective-permute-start.19 = (bf16[16,2048]{1,0:T(8,128)(2,1)S(1)}, bf16[16,2048]{1,0:T(8,128)(2,1)S(1)}, u32[]{:S(2)}, u32[]{:S(2)}) collective-permute-start(bf16[16,2048]{1,0:T(8,128)(2,1)S(1)} %get-tuple-element.71), channel_id=1, source_target_pairs={{0,2},{1,3},{2,0},{3,1},{4,6},{5,7},{6,4},{7,5},{8,10},{9,11},{10,... | collective-permute-start | bytes 196616 | tf_op jit(solution)/shard_map/ppermute | solution.py:328
  105.4 2.6 %collective-permute-done.19.refs_1_ = bf16[16,2048]{1,0:T(8,128)(2,1)S(1)} collective-permute-done((bf16[16,2048]{1,0:T(8,128)(2,1)S(1)}, bf16[16,2048]{1,0:T(8,128)(2,1)S(1)}, u32[]{:S(2)}, u32[]{:S(2)}) %collective-permute-start.19) | collective-permute-done | bytes 65568 | tf_op jit(solution)/shard_map/ppermute | solution.py:328
  108.1 1.3 %collective-permute-done.25.refs_1_ = bf16[32,2048]{1,0:T(8,128)(2,1)S(1)} collective-permute-done((bf16[32,2048]{1,0:T(8,128)(2,1)S(1)}, bf16[32,2048]{1,0:T(8,128)(2,1)S(1)}, u32[]{:S(2)}, u32[]{:S(2)}) %collective-permute-start.25) | collective-permute-done | bytes 131104 | tf_op jit(solution)/shard_map/ppermute | solution.py:328
  109.5 1.1 shard_map.153
  (44 shorter events, 1.3 us)
Async XLA Ops:
  0.0 48.9 %copy-start.7 = (f32[2048]{0:T(1024)S(1)}, f32[2048]{0:T(1024)}, u32[]{:S(2)}) copy-start(f32[2048]{0:T(1024)} %param.23) | copy-start | bytes 24580
  0.0 48.9 %copy-start.6 = (f32[2048]{0:T(1024)S(1)}, f32[2048]{0:T(1024)}, u32[]{:S(2)}) copy-start(f32[2048]{0:T(1024)} %param.22) | copy-start | bytes 24580
  0.0 75.3 %copy-start.5 = (f32[1,1024]{1,0:T(1,128)S(1)}, f32[1,1024]{1,0:T(1,128)}, u32[]{:S(2)}) copy-start(f32[1,1024]{1,0:T(1,128)} %bias_ref.7) | copy-start | bytes 12292
  2.8 12.7 %collective-permute-start = (bf16[32,4224]{1,0:T(8,128)(2,1)}, bf16[32,4224]{1,0:T(8,128)(2,1)S(1)}, u32[]{:S(2)}, u32[]{:S(2)}) collective-permute-start(bf16[32,4224]{1,0:T(8,128)(2,1)} %get-tuple-element.47), channel_id=1, source_target_pairs={{0,8},{8,16},{16,24},{24,0},{1,9},{9,17},{17,25},{25,1},{2,10},{10... | collective-permute-start | bytes 811016 | tf_op jit(solution)/shard_map/ppermute | solution.py:258
  5.8 21.3 %collective-permute-start.1 = (bf16[32,4224]{1,0:T(8,128)(2,1)}, bf16[32,4224]{1,0:T(8,128)(2,1)S(1)}, u32[]{:S(2)}, u32[]{:S(2)}) collective-permute-start(bf16[32,4224]{1,0:T(8,128)(2,1)} %get-tuple-element.48), channel_id=1, source_target_pairs={{0,16},{8,24},{16,0},{24,8},{1,17},{9,25},{17,1},{25,9},{2,18},{10... | collective-permute-start | bytes 811016 | tf_op jit(solution)/shard_map/ppermute | solution.py:258
  8.4 18.7 %collective-permute-start.2 = (bf16[32,4224]{1,0:T(8,128)(2,1)}, bf16[32,4224]{1,0:T(8,128)(2,1)S(1)}, u32[]{:S(2)}, u32[]{:S(2)}) collective-permute-start(bf16[32,4224]{1,0:T(8,128)(2,1)} %get-tuple-element.49), channel_id=1, source_target_pairs={{0,24},{8,0},{16,8},{24,16},{1,25},{9,1},{17,9},{25,17},{2,26},{10... | collective-permute-start | bytes 811016 | tf_op jit(solution)/shard_map/ppermute | solution.py:258
  12.3 62.9 %copy-start = (bf16[1,2048,1024]{2,1,0:T(8,128)(2,1)S(1)}, bf16[1,2048,1024]{2,1,0:T(8,128)(2,1)}, u32[]{:S(2)}) copy-start(bf16[1,2048,1024]{2,1,0:T(8,128)(2,1)} %w_in_ref.5) | copy-start | bytes 12582916
  12.3 20.4 %collective-permute-start.3 = (bf16[32,4096]{1,0:T(8,128)(2,1)}, bf16[32,4096]{1,0:T(8,128)(2,1)S(1)}, u32[]{:S(2)}, u32[]{:S(2)}) collective-permute-start(bf16[32,4096]{1,0:T(8,128)(2,1)} %get-tuple-element.54), channel_id=1, source_target_pairs={{0,8},{8,16},{16,24},{24,0},{1,9},{9,17},{17,25},{25,1},{2,10},{10... | collective-permute-start | bytes 786440 | tf_op jit(solution)/shard_map/ppermute | solution.py:258
  13.0 35.9 %collective-permute-start.4 = (bf16[32,4096]{1,0:T(8,128)(2,1)}, bf16[32,4096]{1,0:T(8,128)(2,1)S(1)}, u32[]{:S(2)}, u32[]{:S(2)}) collective-permute-start(bf16[32,4096]{1,0:T(8,128)(2,1)} %get-tuple-element.55), channel_id=1, source_target_pairs={{0,16},{8,24},{16,0},{24,8},{1,17},{9,25},{17,1},{25,9},{2,18},{10... | collective-permute-start | bytes 786440 | tf_op jit(solution)/shard_map/ppermute | solution.py:258
  15.5 33.4 %collective-permute-start.5 = (bf16[32,4096]{1,0:T(8,128)(2,1)}, bf16[32,4096]{1,0:T(8,128)(2,1)S(1)}, u32[]{:S(2)}, u32[]{:S(2)}) collective-permute-start(bf16[32,4096]{1,0:T(8,128)(2,1)} %get-tuple-element.56), channel_id=1, source_target_pairs={{0,24},{8,0},{16,8},{24,16},{1,25},{9,1},{17,9},{25,17},{2,26},{10... | collective-permute-start | bytes 786440 | tf_op jit(solution)/shard_map/ppermute | solution.py:258
  18.0 1.0 copy-start.2
  18.9 0.9 copy-start.4
  19.9 0.7 copy-start.8
  20.6 0.7 copy-start.9
  21.2 0.7 copy-start.10
  49.9 1.4 %collective-permute-start.6 = (bf16[32,2048]{1,0:T(8,128)(2,1)S(1)}, bf16[32,2048]{1,0:T(8,128)(2,1)S(1)}, u32[]{:S(2)}, u32[]{:S(2)}) collective-permute-start(bf16[32,2048]{1,0:T(8,128)(2,1)S(1)} %get-tuple-element.60), channel_id=1, source_target_pairs={{0,1},{1,0},{2,3},{3,2},{4,5},{5,4},{6,7},{7,6},{8,9},{9,8},{10,11... | collective-permute-start | bytes 393224 | tf_op jit(solution)/shard_map/ppermute | solution.py:328
  51.3 4.3 %collective-permute-start.10 = (bf16[16,2048]{1,0:T(8,128)(2,1)S(1)}, bf16[16,2048]{1,0:T(8,128)(2,1)S(1)}, u32[]{:S(2)}, u32[]{:S(2)}) collective-permute-start(bf16[16,2048]{1,0:T(8,128)(2,1)S(1)} %get-tuple-element.65), channel_id=1, source_target_pairs={{0,4},{1,5},{2,6},{3,7},{4,0},{5,1},{6,2},{7,3},{8,12},{9,13},{10,... | collective-permute-start | bytes 196616 | tf_op jit(solution)/shard_map/ppermute | solution.py:328
  52.9 5.8 %collective-permute-start.11 = (bf16[16,2048]{1,0:T(8,128)(2,1)S(1)}, bf16[16,2048]{1,0:T(8,128)(2,1)S(1)}, u32[]{:S(2)}, u32[]{:S(2)}) collective-permute-start(bf16[16,2048]{1,0:T(8,128)(2,1)S(1)} %get-tuple-element.66), channel_id=1, source_target_pairs={{0,6},{1,7},{2,4},{3,5},{4,2},{5,3},{6,0},{7,1},{8,14},{9,15},{10,... | collective-permute-start | bytes 196616 | tf_op jit(solution)/shard_map/ppermute | solution.py:328
  54.3 9.6 %collective-permute-start.7 = (bf16[16,2048]{1,0:T(8,128)(2,1)S(1)}, bf16[16,2048]{1,0:T(8,128)(2,1)S(1)}, u32[]{:S(2)}, u32[]{:S(2)}) collective-permute-start(bf16[16,2048]{1,0:T(8,128)(2,1)S(1)} %get-tuple-element.62), channel_id=1, source_target_pairs={{0,2},{1,3},{2,0},{3,1},{4,6},{5,7},{6,4},{7,5},{8,10},{9,11},{10,... | collective-permute-start | bytes 196616 | tf_op jit(solution)/shard_map/ppermute | solution.py:328
  58.7 14.4 %collective-permute-start.12 = (bf16[32,2048]{1,0:T(8,128)(2,1)S(1)}, bf16[32,2048]{1,0:T(8,128)(2,1)S(1)}, u32[]{:S(2)}, u32[]{:S(2)}) collective-permute-start(bf16[32,2048]{1,0:T(8,128)(2,1)S(1)} %shard_map.145.refs_0_), channel_id=1, source_target_pairs={{0,16},{8,24},{16,0},{24,8},{1,17},{9,25},{17,1},{25,9},{2,18},{10... | collective-permute-start | bytes 393224 | tf_op jit(solution)/shard_map/ppermute | solution.py:328
  63.9 11.3 %collective-permute-start.14 = (bf16[32,2048]{1,0:T(8,128)(2,1)S(1)}, bf16[32,2048]{1,0:T(8,128)(2,1)S(1)}, u32[]{:S(2)}, u32[]{:S(2)}) collective-permute-start(bf16[32,2048]{1,0:T(8,128)(2,1)S(1)} %shard_map.143.refs_0_), channel_id=1, source_target_pairs={{0,16},{8,24},{16,0},{24,8},{1,17},{9,25},{17,1},{25,9},{2,18},{10... | collective-permute-start | bytes 393224 | tf_op jit(solution)/shard_map/ppermute | solution.py:328
  64.0 11.3 %collective-permute-start.8 = (bf16[32,2048]{1,0:T(8,128)(2,1)S(1)}, bf16[32,2048]{1,0:T(8,128)(2,1)S(1)}, u32[]{:S(2)}, u32[]{:S(2)}) collective-permute-start(bf16[32,2048]{1,0:T(8,128)(2,1)S(1)} %shard_map.143.refs_0_), channel_id=1, source_target_pairs={{0,8},{8,0},{16,24},{24,16},{1,9},{9,1},{17,25},{25,17},{2,10},{10... | collective-permute-start | bytes 393224 | tf_op jit(solution)/shard_map/ppermute | solution.py:328
  67.8 11.2 %collective-permute-start.16 = (bf16[32,2048]{1,0:T(8,128)(2,1)S(1)}, bf16[32,2048]{1,0:T(8,128)(2,1)S(1)}, u32[]{:S(2)}, u32[]{:S(2)}) collective-permute-start(bf16[32,2048]{1,0:T(8,128)(2,1)S(1)} %shard_map.145.refs_0_), channel_id=1, source_target_pairs={{0,8},{8,0},{16,24},{24,16},{1,9},{9,1},{17,25},{25,17},{2,10},{10... | collective-permute-start | bytes 393224 | tf_op jit(solution)/shard_map/ppermute | solution.py:328
  73.1 7.6 %collective-permute-start.13 = (bf16[32,2048]{1,0:T(8,128)(2,1)S(1)}, bf16[32,2048]{1,0:T(8,128)(2,1)S(1)}, u32[]{:S(2)}, u32[]{:S(2)}) collective-permute-start(bf16[32,2048]{1,0:T(8,128)(2,1)S(1)} %collective-permute-done.12.refs_2_), channel_id=1, source_target_pairs={{0,8},{8,0},{16,24},{24,16},{1,9},{9,1},{17,25},{25,17},{2,10},{10... | collective-permute-start | bytes 393224 | tf_op jit(solution)/shard_map/ppermute | solution.py:328
  75.3 5.8 %collective-permute-start.15 = (bf16[32,2048]{1,0:T(8,128)(2,1)S(1)}, bf16[32,2048]{1,0:T(8,128)(2,1)S(1)}, u32[]{:S(2)}, u32[]{:S(2)}) collective-permute-start(bf16[32,2048]{1,0:T(8,128)(2,1)S(1)} %collective-permute-done.14.refs_3_), channel_id=1, source_target_pairs={{0,8},{8,0},{16,24},{24,16},{1,9},{9,1},{17,25},{25,17},{2,10},{10... | collective-permute-start | bytes 393224 | tf_op jit(solution)/shard_map/ppermute | solution.py:328
  75.3 2.2 %copy-start.1 = (bf16[1,1024,2048]{2,1,0:T(8,128)(2,1)S(1)}, bf16[1,1024,2048]{2,1,0:T(8,128)(2,1)}, u32[]{:S(2)}) copy-start(bf16[1,1024,2048]{2,1,0:T(8,128)(2,1)} %w_out_ref.5) | copy-start | bytes 12582916
  81.1 16.8 %copy-start.3 = (f32[8,2048]{1,0:T(8,128)S(1)}, f32[8,2048]{1,0:T(8,128)}, u32[]{:S(2)}) copy-start(f32[8,2048]{1,0:T(8,128)} %bias_ref.9) | copy-start | bytes 196612
  82.5 6.5 %collective-permute-start.21 = (bf16[32,2048]{1,0:T(8,128)(2,1)S(1)}, bf16[32,2048]{1,0:T(8,128)(2,1)S(1)}, u32[]{:S(2)}, u32[]{:S(2)}) collective-permute-start(bf16[32,2048]{1,0:T(8,128)(2,1)S(1)} %get-tuple-element.73), channel_id=1, source_target_pairs={{0,8},{8,0},{16,24},{24,16},{1,9},{9,1},{17,25},{25,17},{2,10},{10... | collective-permute-start | bytes 393224 | tf_op jit(solution)/shard_map/ppermute | solution.py:328
  84.1 11.7 %collective-permute-start.17 = (bf16[32,2048]{1,0:T(8,128)(2,1)S(1)}, bf16[32,2048]{1,0:T(8,128)(2,1)S(1)}, u32[]{:S(2)}, u32[]{:S(2)}) collective-permute-start(bf16[32,2048]{1,0:T(8,128)(2,1)S(1)} %get-tuple-element.68), channel_id=1, source_target_pairs={{0,8},{8,0},{16,24},{24,16},{1,9},{9,1},{17,25},{25,17},{2,10},{10... | collective-permute-start | bytes 393224 | tf_op jit(solution)/shard_map/ppermute | solution.py:328
  84.5 13.4 %collective-permute-start.20 = (bf16[32,2048]{1,0:T(8,128)(2,1)S(1)}, bf16[32,2048]{1,0:T(8,128)(2,1)S(1)}, u32[]{:S(2)}, u32[]{:S(2)}) collective-permute-start(bf16[32,2048]{1,0:T(8,128)(2,1)S(1)} %get-tuple-element.72), channel_id=1, source_target_pairs={{0,8},{8,0},{16,24},{24,16},{1,9},{9,1},{17,25},{25,17},{2,10},{10... | collective-permute-start | bytes 393224 | tf_op jit(solution)/shard_map/ppermute | solution.py:328
  89.0 8.9 %collective-permute-start.22 = (bf16[32,2048]{1,0:T(8,128)(2,1)S(1)}, bf16[32,2048]{1,0:T(8,128)(2,1)S(1)}, u32[]{:S(2)}, u32[]{:S(2)}) collective-permute-start(bf16[32,2048]{1,0:T(8,128)(2,1)S(1)} %shard_map.150), channel_id=1, source_target_pairs={{0,16},{8,24},{16,0},{24,8},{1,17},{9,25},{17,1},{25,9},{2,18},{10... | collective-permute-start | bytes 393224 | tf_op jit(solution)/shard_map/ppermute | solution.py:328
  92.8 8.4 %collective-permute-start.9 = (bf16[32,2048]{1,0:T(8,128)(2,1)S(1)}, bf16[32,2048]{1,0:T(8,128)(2,1)S(1)}, u32[]{:S(2)}, u32[]{:S(2)}) collective-permute-start(bf16[32,2048]{1,0:T(8,128)(2,1)S(1)} %get-tuple-element.63), channel_id=1, source_target_pairs={{0,8},{8,0},{16,24},{24,16},{1,9},{9,1},{17,25},{25,17},{2,10},{10... | collective-permute-start | bytes 393224 | tf_op jit(solution)/shard_map/ppermute | solution.py:328
  95.8 7.8 %collective-permute-start.18 = (bf16[32,2048]{1,0:T(8,128)(2,1)S(1)}, bf16[32,2048]{1,0:T(8,128)(2,1)S(1)}, u32[]{:S(2)}, u32[]{:S(2)}) collective-permute-start(bf16[32,2048]{1,0:T(8,128)(2,1)S(1)} %shard_map.148), channel_id=1, source_target_pairs={{0,16},{8,24},{16,0},{24,8},{1,17},{9,25},{17,1},{25,9},{2,18},{10... | collective-permute-start | bytes 393224 | tf_op jit(solution)/shard_map/ppermute | solution.py:328
  98.0 7.4 %collective-permute-start.23 = (bf16[16,2048]{1,0:T(8,128)(2,1)S(1)}, bf16[16,2048]{1,0:T(8,128)(2,1)S(1)}, u32[]{:S(2)}, u32[]{:S(2)}) collective-permute-start(bf16[16,2048]{1,0:T(8,128)(2,1)S(1)} %get-tuple-element.75), channel_id=1, source_target_pairs={{0,4},{1,5},{2,6},{3,7},{4,0},{5,1},{6,2},{7,3},{8,12},{9,13},{10,... | collective-permute-start | bytes 196616 | tf_op jit(solution)/shard_map/ppermute | solution.py:328
  98.8 6.7 %collective-permute-start.24 = (bf16[16,2048]{1,0:T(8,128)(2,1)S(1)}, bf16[16,2048]{1,0:T(8,128)(2,1)S(1)}, u32[]{:S(2)}, u32[]{:S(2)}) collective-permute-start(bf16[16,2048]{1,0:T(8,128)(2,1)S(1)} %get-tuple-element.76), channel_id=1, source_target_pairs={{0,6},{1,7},{2,4},{3,5},{4,2},{5,3},{6,0},{7,1},{8,14},{9,15},{10,... | collective-permute-start | bytes 196616 | tf_op jit(solution)/shard_map/ppermute | solution.py:328
  103.7 4.3 %collective-permute-start.19 = (bf16[16,2048]{1,0:T(8,128)(2,1)S(1)}, bf16[16,2048]{1,0:T(8,128)(2,1)S(1)}, u32[]{:S(2)}, u32[]{:S(2)}) collective-permute-start(bf16[16,2048]{1,0:T(8,128)(2,1)S(1)} %get-tuple-element.71), channel_id=1, source_target_pairs={{0,2},{1,3},{2,0},{3,1},{4,6},{5,7},{6,4},{7,5},{8,10},{9,11},{10,... | collective-permute-start | bytes 196616 | tf_op jit(solution)/shard_map/ppermute | solution.py:328
  108.1 1.4 %collective-permute-start.25 = (bf16[32,2048]{1,0:T(8,128)(2,1)S(1)}, bf16[32,2048]{1,0:T(8,128)(2,1)S(1)}, u32[]{:S(2)}, u32[]{:S(2)}) collective-permute-start(bf16[32,2048]{1,0:T(8,128)(2,1)S(1)} %get-tuple-element.78), channel_id=1, source_target_pairs={{0,1},{1,0},{2,3},{3,2},{4,5},{5,4},{6,7},{7,6},{8,9},{9,8},{10,11... | collective-permute-start | bytes 393224 | tf_op jit(solution)/shard_map/ppermute | solution.py:328
